TPU v7x, 32 devices: a whole 2x2x4 slice. The times are simulated.
32 devices in a mesh: batch: 8 (over y, x, core), frame: 4 (over z).
Axes of the slice: x: 2, y: 2, z: 4, core: 2. Of those that a mesh axis runs over, the one named last changes fastest.
Arguments:
- tokens: bfloat16 [4, 6304, 768], P('frame', 'batch'), may hold values from -6 to 6
- size_tag: int32 [8], P('batch'), may hold values from 196 to 784, as said below
- cotangent: bfloat16 [4, 6304, 768], P('frame', 'batch'), may hold values from -6 to 6
- time_project: bfloat16 [768, 2304], P('batch'), may hold values from -0.21875 to 0.21875
- time_output: bfloat16 [768, 768], P('batch'), may hold values from -0.4375 to 0.4375
- time_vector: bfloat16 [5, 768], P(None, 'batch'), may hold values from -1.25 to 1.4
- space_project: bfloat16 [768, 2304], P('batch'), may hold values from -0.21875 to 0.21875
- space_output: bfloat16 [768, 768], P('batch'), may hold values from -1.25 to 1.25
- space_vector: bfloat16 [5, 768], P(None, 'batch'), may hold values from -1.25 to 1.4
- feed_inner: bfloat16 [768, 3072], P('batch'), may hold values from -0.21875 to 0.21875
- feed_bias: bfloat16 [3072], P('batch'), may hold values from -1.796875 to 1.796875
- feed_outer: bfloat16 [3072, 768], P('batch'), may hold values from -0.109375 to 0.109375
- feed_vector: bfloat16 [3, 768], P(None, 'batch'), may hold values from -1.25 to 1.4
Outputs:
- block_out: bfloat16 [4, 6304, 768], P('frame', 'batch')
- grad_tokens: float32 [4, 6304, 768], P('frame', 'batch')
- grad_time_project: float32 [768, 2304], replicated
- grad_time_output: float32 [768, 768], replicated
- grad_time_vector: float32 [5, 768], replicated
- grad_space_project: float32 [768, 2304], replicated
- grad_space_output: float32 [768, 768], replicated
- grad_space_vector: float32 [5, 768], replicated
- grad_feed_inner: float32 [768, 3072], replicated
- grad_feed_bias: float32 [3072], replicated
- grad_feed_outer: float32 [3072, 768], replicated
- grad_feed_vector: float32 [3, 768], replicated
Inputs may be any that keep to these rules, and one draw needn't show every extreme that they name: `size_tag`: A batch index with tag 196 holds 4 clips of 196 patches a frame, one with tag 4 * 196 holds 1 clips of 784; both tags occur in every draw.
All inputs are finite; a program needn't handle non-finite values.
Results may differ from a plain program's by a relative error of at most 0.019.
Values may be sent and summed in bfloat16 or wider, within the bound.
No kernel may reach another device: no remote copies, remote signals or barrier semaphores. Data moves between devices by JAX's collectives and lax.ppermute only.
A program may use at most 384 MiB of HBM per device.

v0:
```python
import jax
import jax.numpy as jnp
from jax import lax
from jax.sharding import PartitionSpec as P

HEADS = 12
UNITS = 4
PATCHES = 784


def norm_rows(values, norm_gain, norm_shift):
    average = jnp.mean(values, axis=-1, keepdims=True)
    centered = values - average
    variance = jnp.mean(centered * centered, axis=-1, keepdims=True)
    return centered * lax.rsqrt(variance + 1e-06) * norm_gain + norm_shift


def gelu_exact(hidden):
    return jax.nn.gelu(hidden, approximate=False)


def forward_dot(operand, partner):
    return jnp.dot(operand, partner, preferred_element_type=jnp.float32)


def inner_rows(operand, partner):
    return lax.dot_general(
        operand, partner, (((0,), (0,)), ((), ())), preferred_element_type=jnp.float32
    )


def times_back(operand, partner):
    return lax.dot_general(
        operand, partner, (((1,), (1,)), ((), ())), preferred_element_type=jnp.float32
    )


def split_frames(array):
    frame_count, row_count, feature_count = array.shape
    return array.reshape(frame_count, row_count, HEADS, feature_count // HEADS)


def frame_scores(queries, key_rows):
    head_size = queries.shape[2] // HEADS
    scores = jnp.einsum(
        "frhd,grhd->rhfg",
        split_frames(queries),
        split_frames(key_rows),
        preferred_element_type=jnp.float32,
    )
    return scores * head_size ** (-0.5)


def frame_forward(queries, key_rows, values):
    scores = frame_scores(queries, key_rows)
    log_total = jax.nn.logsumexp(scores, axis=-1)
    rounded = jnp.exp(scores - log_total[..., None]).astype(jnp.bfloat16)
    mixture = jnp.einsum(
        "rhfg,grhd->frhd", rounded, split_frames(values), preferred_element_type=jnp.float32
    )
    return (mixture.reshape(queries.shape).astype(jnp.bfloat16), log_total)


def frame_backward(queries, key_rows, values, log_total, grad_mixture):
    head_size = queries.shape[2] // HEADS
    scores = frame_scores(queries, key_rows)
    probability = jnp.exp(scores - log_total[..., None])
    rounded = probability.astype(jnp.bfloat16)
    grad_split = split_frames(grad_mixture)
    grad_weights = jnp.einsum(
        "frhd,grhd->rhfg", grad_split, split_frames(values), preferred_element_type=jnp.float32
    )
    grad_scores = probability * (
        grad_weights - jnp.sum(grad_weights * probability, axis=-1, keepdims=True)
    )
    grad_scores = grad_scores.astype(jnp.bfloat16)
    scaling = head_size ** (-0.5)
    grad_query = (
        jnp.einsum(
            "rhfg,grhd->frhd",
            grad_scores,
            split_frames(key_rows),
            preferred_element_type=jnp.float32,
        )
        * scaling
    )
    grad_keys = (
        jnp.einsum(
            "rhfg,frhd->grhd",
            grad_scores,
            split_frames(queries),
            preferred_element_type=jnp.float32,
        )
        * scaling
    )
    grad_values = jnp.einsum(
        "rhfg,frhd->grhd", rounded, grad_split, preferred_element_type=jnp.float32
    )
    return (
        grad_query.reshape(queries.shape),
        grad_keys.reshape(key_rows.shape),
        grad_values.reshape(values.shape),
    )


def space_scores(queries, key_rows, linked):
    row_count, feature_count = queries.shape
    head_size = feature_count // HEADS
    query_split = queries.reshape(row_count, HEADS, head_size)
    key_split = key_rows.reshape(row_count, HEADS, head_size)
    scores = jnp.einsum(
        "qhd,khd->hqk", query_split, key_split, preferred_element_type=jnp.float32
    ) * head_size ** (-0.5)
    return jnp.where(linked[None], scores, -1e30)


def body(
    tokens,
    size_tag,
    cotangent,
    time_project,
    time_output,
    time_vector,
    space_project,
    space_output,
    space_vector,
    feed_inner,
    feed_bias,
    feed_outer,
    feed_vector,
):
    gathered = (
        lax.all_gather(time_project, "batch", axis=0, tiled=True),
        lax.all_gather(time_output, "batch", axis=0, tiled=True),
        lax.all_gather(time_vector, "batch", axis=1, tiled=True),
        lax.all_gather(space_project, "batch", axis=0, tiled=True),
        lax.all_gather(space_output, "batch", axis=0, tiled=True),
        lax.all_gather(space_vector, "batch", axis=1, tiled=True),
        lax.all_gather(feed_inner, "batch", axis=0, tiled=True),
        lax.all_gather(feed_bias, "batch", axis=0, tiled=True),
        lax.all_gather(feed_outer, "batch", axis=0, tiled=True),
        lax.all_gather(feed_vector, "batch", axis=1, tiled=True),
    )
    (
        time_project_full,
        time_output_full,
        time_vector_full,
        space_project_full,
        space_output_full,
        space_vector_full,
        feed_inner_full,
        feed_bias_full,
        feed_outer_full,
        feed_vector_full,
    ) = gathered
    feature_count = tokens.shape[2]
    row_count = tokens.shape[1]
    head_size = feature_count // HEADS
    inputs = tokens[0].astype(jnp.float32)
    patches = inputs[:PATCHES]
    time_rows = time_vector_full.astype(jnp.float32)
    normed_time, time_norm_back = jax.vjp(norm_rows, patches, time_rows[0], time_rows[1])
    first_input = normed_time.astype(jnp.bfloat16)
    joined = forward_dot(first_input, time_project_full)
    query_time = (joined[:, :feature_count] + time_rows[2]).astype(jnp.bfloat16)
    key_time = joined[:, feature_count : 2 * feature_count].astype(jnp.bfloat16)
    value_time = (joined[:, 2 * feature_count :] + time_rows[3]).astype(jnp.bfloat16)
    keys_all, values_all = (
        lax.all_gather(key_time[None], "frame", axis=0, tiled=True),
        lax.all_gather(value_time[None], "frame", axis=0, tiled=True),
    )
    mixture, time_total = frame_forward(query_time[None], keys_all, values_all)
    mixture_time = mixture[0]
    after_time = jnp.concatenate(
        [patches + forward_dot(mixture_time, time_output_full) + time_rows[4], inputs[PATCHES:]],
        axis=0,
    )
    space_rows = space_vector_full.astype(jnp.float32)
    normed_space, space_norm_back = jax.vjp(norm_rows, after_time, space_rows[0], space_rows[1])
    second_input = normed_space.astype(jnp.bfloat16)
    joined = forward_dot(second_input, space_project_full)
    query_space = (joined[:, :feature_count] + space_rows[2]).astype(jnp.bfloat16)
    key_space = joined[:, feature_count : 2 * feature_count].astype(jnp.bfloat16)
    value_space = (joined[:, 2 * feature_count :] + space_rows[3]).astype(jnp.bfloat16)
    clip_tag = size_tag[0]
    clip_number = jnp.concatenate(
        [jnp.arange(PATCHES, dtype=jnp.int32) // clip_tag, jnp.arange(UNITS, dtype=jnp.int32)]
    )
    linked = clip_number[:, None] == clip_number[None, :]
    scores = space_scores(query_space, key_space, linked)
    space_total = jax.nn.logsumexp(scores, axis=-1)
    rounded = jnp.exp(scores - space_total[..., None]).astype(jnp.bfloat16)
    value_split = value_space.reshape(row_count, HEADS, head_size)
    mixture_space = jnp.einsum(
        "hqk,khd->qhd", rounded, value_split, preferred_element_type=jnp.float32
    )
    mixture_space = mixture_space.reshape(row_count, feature_count).astype(jnp.bfloat16)
    after_space = after_time + forward_dot(mixture_space, space_output_full) + space_rows[4]
    feed_rows = feed_vector_full.astype(jnp.float32)
    normed_feed, feed_norm_back = jax.vjp(norm_rows, after_space, feed_rows[0], feed_rows[1])
    third_input = normed_feed.astype(jnp.bfloat16)
    hidden = forward_dot(third_input, feed_inner_full) + feed_bias_full.astype(jnp.float32)
    active_float, gelu_back = jax.vjp(gelu_exact, hidden)
    active = active_float.astype(jnp.bfloat16)
    block_out = (after_space + forward_dot(active, feed_outer_full) + feed_rows[2]).astype(
        jnp.bfloat16
    )
    grad_result = cotangent[0]
    grad_top = grad_result.astype(jnp.float32)
    grad_feed_outer = inner_rows(active, grad_result)
    feed_out_sum = jnp.sum(grad_top, axis=0)
    (grad_hidden,) = gelu_back(times_back(grad_result, feed_outer_full))
    grad_hidden = grad_hidden.astype(jnp.bfloat16)
    grad_feed_inner = inner_rows(third_input, grad_hidden)
    grad_feed_bias = jnp.sum(grad_hidden.astype(jnp.float32), axis=0)
    grad_second, feed_gain, feed_shift = feed_norm_back(times_back(grad_hidden, feed_inner_full))
    grad_second = grad_second + grad_top
    grad_feed_vector = jnp.stack([feed_gain, feed_shift, feed_out_sum])
    grad_branch = grad_second.astype(jnp.bfloat16)
    grad_space_output = inner_rows(mixture_space, grad_branch)
    space_out_sum = jnp.sum(grad_branch.astype(jnp.float32), axis=0)
    grad_mixture = times_back(grad_branch, space_output_full).astype(jnp.bfloat16)
    scores = space_scores(query_space, key_space, linked)
    probability = jnp.exp(scores - space_total[..., None])
    grad_split = grad_mixture.reshape(row_count, HEADS, head_size)
    grad_weights = jnp.einsum(
        "qhd,khd->hqk", grad_split, value_split, preferred_element_type=jnp.float32
    )
    grad_scores = probability * (
        grad_weights - jnp.sum(grad_weights * probability, axis=-1, keepdims=True)
    )
    grad_scores = grad_scores.astype(jnp.bfloat16)
    scaling = head_size ** (-0.5)
    query_split = query_space.reshape(row_count, HEADS, head_size)
    key_split = key_space.reshape(row_count, HEADS, head_size)
    grad_query = (
        jnp.einsum("hqk,khd->qhd", grad_scores, key_split, preferred_element_type=jnp.float32)
        * scaling
    )
    grad_keys = (
        jnp.einsum("hqk,qhd->khd", grad_scores, query_split, preferred_element_type=jnp.float32)
        * scaling
    )
    grad_values = jnp.einsum(
        "hqk,qhd->khd",
        probability.astype(jnp.bfloat16),
        grad_split,
        preferred_element_type=jnp.float32,
    )
    grad_query = grad_query.reshape(row_count, feature_count).astype(jnp.bfloat16)
    grad_keys = grad_keys.reshape(row_count, feature_count).astype(jnp.bfloat16)
    grad_values = grad_values.reshape(row_count, feature_count).astype(jnp.bfloat16)
    grad_joined = jnp.concatenate([grad_query, grad_keys, grad_values], axis=1)
    grad_space_project = inner_rows(second_input, grad_joined)
    grad_first, space_gain, space_shift = space_norm_back(
        times_back(grad_joined, space_project_full)
    )
    grad_first = grad_first + grad_second
    grad_space_vector = jnp.stack(
        [
            space_gain,
            space_shift,
            jnp.sum(grad_query.astype(jnp.float32), axis=0),
            jnp.sum(grad_values.astype(jnp.float32), axis=0),
            space_out_sum,
        ]
    )
    grad_patch = grad_first[:PATCHES].astype(jnp.bfloat16)
    grad_time_output = inner_rows(mixture_time, grad_patch)
    time_out_sum = jnp.sum(grad_patch.astype(jnp.float32), axis=0)
    grad_mixture_time = times_back(grad_patch, time_output_full).astype(jnp.bfloat16)
    grad_query_all, grad_keys_all, grad_values_all = frame_backward(
        query_time[None], keys_all, values_all, time_total, grad_mixture_time[None]
    )
    grad_keys_own, grad_values_own = (
        lax.psum_scatter(grad_keys_all, "frame", scatter_dimension=0, tiled=True),
        lax.psum_scatter(grad_values_all, "frame", scatter_dimension=0, tiled=True),
    )
    grad_query_time = grad_query_all[0].astype(jnp.bfloat16)
    grad_key_time = grad_keys_own[0].astype(jnp.bfloat16)
    grad_value_time = grad_values_own[0].astype(jnp.bfloat16)
    grad_joined_time = jnp.concatenate([grad_query_time, grad_key_time, grad_value_time], axis=1)
    grad_time_project = inner_rows(first_input, grad_joined_time)
    grad_patches, time_gain, time_shift = time_norm_back(
        times_back(grad_joined_time, time_project_full)
    )
    grad_tokens = grad_first + jnp.pad(grad_patches, ((0, UNITS), (0, 0)))
    grad_time_vector = jnp.stack(
        [
            time_gain,
            time_shift,
            jnp.sum(grad_query_time.astype(jnp.float32), axis=0),
            jnp.sum(grad_value_time.astype(jnp.float32), axis=0),
            time_out_sum,
        ]
    )
    local_grads = (
        grad_time_project,
        grad_time_output,
        grad_time_vector,
        grad_space_project,
        grad_space_output,
        grad_space_vector,
        grad_feed_inner,
        grad_feed_bias,
        grad_feed_outer,
        grad_feed_vector,
    )
    parts = (
        lax.psum_scatter(
            local_grads[0].astype(jnp.bfloat16), "batch", scatter_dimension=0, tiled=True
        ).astype(jnp.float32),
        lax.psum_scatter(
            local_grads[1].astype(jnp.bfloat16), "batch", scatter_dimension=0, tiled=True
        ).astype(jnp.float32),
        lax.psum_scatter(
            local_grads[2].astype(jnp.bfloat16), "batch", scatter_dimension=1, tiled=True
        ).astype(jnp.float32),
        lax.psum_scatter(
            local_grads[3].astype(jnp.bfloat16), "batch", scatter_dimension=0, tiled=True
        ).astype(jnp.float32),
        lax.psum_scatter(
            local_grads[4].astype(jnp.bfloat16), "batch", scatter_dimension=0, tiled=True
        ).astype(jnp.float32),
        lax.psum_scatter(
            local_grads[5].astype(jnp.bfloat16), "batch", scatter_dimension=1, tiled=True
        ).astype(jnp.float32),
        lax.psum_scatter(
            local_grads[6].astype(jnp.bfloat16), "batch", scatter_dimension=0, tiled=True
        ).astype(jnp.float32),
        lax.psum_scatter(
            local_grads[7].astype(jnp.bfloat16), "batch", scatter_dimension=0, tiled=True
        ).astype(jnp.float32),
        lax.psum_scatter(
            local_grads[8].astype(jnp.bfloat16), "batch", scatter_dimension=0, tiled=True
        ).astype(jnp.float32),
        lax.psum_scatter(
            local_grads[9].astype(jnp.bfloat16), "batch", scatter_dimension=1, tiled=True
        ).astype(jnp.float32),
    )
    totals = (
        lax.psum(parts[0].astype(jnp.bfloat16), "frame").astype(jnp.float32),
        lax.psum(parts[1].astype(jnp.bfloat16), "frame").astype(jnp.float32),
        lax.psum(parts[2].astype(jnp.bfloat16), "frame").astype(jnp.float32),
        lax.psum(parts[3].astype(jnp.bfloat16), "frame").astype(jnp.float32),
        lax.psum(parts[4].astype(jnp.bfloat16), "frame").astype(jnp.float32),
        lax.psum(parts[5].astype(jnp.bfloat16), "frame").astype(jnp.float32),
        lax.psum(parts[6].astype(jnp.bfloat16), "frame").astype(jnp.float32),
        lax.psum(parts[7].astype(jnp.bfloat16), "frame").astype(jnp.float32),
        lax.psum(parts[8].astype(jnp.bfloat16), "frame").astype(jnp.float32),
        lax.psum(parts[9].astype(jnp.bfloat16), "frame").astype(jnp.float32),
    )
    whole = (
        lax.all_gather(totals[0].astype(jnp.bfloat16), "batch", axis=0, tiled=True).astype(
            jnp.float32
        ),
        lax.all_gather(totals[1].astype(jnp.bfloat16), "batch", axis=0, tiled=True).astype(
            jnp.float32
        ),
        lax.all_gather(totals[2].astype(jnp.bfloat16), "batch", axis=1, tiled=True).astype(
            jnp.float32
        ),
        lax.all_gather(totals[3].astype(jnp.bfloat16), "batch", axis=0, tiled=True).astype(
            jnp.float32
        ),
        lax.all_gather(totals[4].astype(jnp.bfloat16), "batch", axis=0, tiled=True).astype(
            jnp.float32
        ),
        lax.all_gather(totals[5].astype(jnp.bfloat16), "batch", axis=1, tiled=True).astype(
            jnp.float32
        ),
        lax.all_gather(totals[6].astype(jnp.bfloat16), "batch", axis=0, tiled=True).astype(
            jnp.float32
        ),
        lax.all_gather(totals[7].astype(jnp.bfloat16), "batch", axis=0, tiled=True).astype(
            jnp.float32
        ),
        lax.all_gather(totals[8].astype(jnp.bfloat16), "batch", axis=0, tiled=True).astype(
            jnp.float32
        ),
        lax.all_gather(totals[9].astype(jnp.bfloat16), "batch", axis=1, tiled=True).astype(
            jnp.float32
        ),
    )
    return (
        block_out[None],
        grad_tokens[None],
        whole[0],
        whole[1],
        whole[2],
        whole[3],
        whole[4],
        whole[5],
        whole[6],
        whole[7],
        whole[8],
        whole[9],
    )


def solution(mesh):
    placed = (
        P("frame", "batch", None),
        P("batch"),
        P("frame", "batch", None),
        P("batch", None),
        P("batch", None),
        P(None, "batch"),
        P("batch", None),
        P("batch", None),
        P(None, "batch"),
        P("batch", None),
        P("batch"),
        P("batch", None),
        P(None, "batch"),
    )
    return jax.shard_map(
        body,
        mesh=mesh,
        in_specs=placed,
        out_specs=(
            P("frame", "batch", None),
            P("frame", "batch", None),
            P(),
            P(),
            P(),
            P(),
            P(),
            P(),
            P(),
            P(),
            P(),
            P(),
        ),
        check_vma=False,
    )
```

profile of v0, /device:TPU:0, one launch (start us, length us, event | category | flops | bytes accessed | tf_op | source)
XLA Modules:
  0.0 1664.7 jit_solution(4334301094544702178)
XLA Ops:
  21.5 25.1 %all-gather.25.cloned.1.call-done = bf16[768,2304]{1,0:T(8,128)(2,1)} async-done(((bf16[96,2304]{1,0:T(8,128)(2,1)}), bf16[768,2304]{1,0:T(8,128)(2,1)}) %all-gather.25.cloned.1.call-update) | async-done | bytes 3538960 | tf_op jit(solution)/shard_map/all_gather | solution.py:133
  95.4 51.4 %all-gather.49.cloned.1.call-done = bf16[3136,768]{1,0:T(8,128)(2,1)} async-done(((bf16[784,768]{1,0:T(8,128)(2,1)}), bf16[3136,768]{1,0:T(8,128)(2,1)}) %all-gather.49.cloned.1.call-update) | async-done | bytes 4816912 | tf_op jit(solution)/shard_map/all_gather | solution.py:170
  166.1 72.3 %all-gather.51.cloned.1.call-done = bf16[3136,768]{1,0:T(8,128)(2,1)} async-done(((bf16[784,768]{1,0:T(8,128)(2,1)}), bf16[3136,768]{1,0:T(8,128)(2,1)}) %all-gather.51.cloned.1.call-update) | async-done | bytes 4816912 | tf_op jit(solution)/shard_map/all_gather | solution.py:169
  328.5 15.6 exponential_reduce_fusion
  344.2 17.1 %convolution_convert_fusion.5 = bf16[12,64,788]{2,1,0:T(8,128)(2,1)} fusion(bf16[788,12,64]{0,2,1:T(8,128)(2,1)S(1)} %bitcast.165, f32[12,788,788]{1,2,0:T(8,128)} %get-tuple-element.121, f32[12,788]{1,0:T(8,128)S(1)} %log_add_fusion, pred[788,788]{0,1:T(8,128)(4,1)S(1)} %broadcast_compare_fusion), kind=kOutput, calls=%fused_computation.78 | convolution fusion | flops 984180480 | bytes 32884816 | tf_op jit(solution)/shard_map/hqk,khd->qhd/dot_general | solution.py:194
  366.2 30.9 %multiply_convert_fusion.1 = (bf16[788,3072]{1,0:T(8,128)(2,1)}, f32[788,3072]{1,0:T(8,128)}, f32[788,3072]{1,0:T(8,128)}) fusion(f32[3072]{0:T(1024)S(1)} %bitcast.189, bf16[768,3072]{1,0:T(8,128)(2,1)} %all-gather.33.cloned.1.call-done, f32[788,768]{1,0:T(8,128)} %copy-done.17, f32[768]{0:T(1024)S(1)} %get-tuple-element.92, ...), kind=kOutput, calls=%fused_computation.15 | convolution fusion | flops 3881044992 | bytes 31371424 | tf_op jit(solution)/shard_map/dot_general | solution.py:23
  435.7 16.8 %fusion.62 = (bf16[12,64]{1,0:T(8,128)(2,1)}, bf16[12,64,788]{2,1,0:T(8,128)(2,1)}) fusion(bf16[788,12,64]{0,2,1:T(8,128)(2,1)} %bitcast.166, f32[12,788,788]{1,2,0:T(8,128)} %get-tuple-element.121, f32[12,788]{1,0:T(8,128)S(1)} %log_add_fusion, pred[788,788]{0,1:T(8,128)(4,1)S(1)} %broadcast_compare_fusion), kind=kOutput, calls=%fused_computation.173 | convolution fusion | flops 984784896 | bytes 32886352 | tf_op jit(solution)/shard_map/hqk,qhd->khd/dot_general | solution.py:244
  452.6 28.5 %multiply_reduce_fusion = (f32[12,788]{1,0:T(8,128)S(1)}, f32[12,788,788]{1,2,0:T(8,128)}) fusion(f32[12,788,788]{1,2,0:T(8,128)} %get-tuple-element.121, f32[12,788]{1,0:T(8,128)S(1)} %log_add_fusion, pred[788,788]{0,1:T(8,128)(4,1)S(1)} %broadcast_compare_fusion, bf16[788,12,64]{0,2,1:T(8,128)(2,1)} %bitcast.167, bf16[788,12,64]{0,2,1:T(8,128)(2,1)} %bitcast.164), kind=kOutput, calls=%fused_computation.1 | convolution fusion | flops 991017152 | bytes 62727952 | tf_op jit(solution)/shard_map/qhd,khd->hqk/dot_general | solution.py:226
  481.1 28.6 %multiply_convert_fusion = bf16[12,788,788]{1,2,0:T(8,128)(2,1)} fusion(f32[12,788,788]{1,2,0:T(8,128)} %get-tuple-element.127, f32[12,788,788]{1,2,0:T(8,128)} %get-tuple-element.121, f32[12,788]{1,0:T(8,128)S(1)} %get-tuple-element.126, f32[12,788]{1,0:T(8,128)S(1)} %log_add_fusion, pred[788,788]{0,1:T(8,128)(4,1)S(1)} %broadcast_compare_fusion), kind=kLoop, calls=%fused_computation | loop fusion | flops 44707968 | bytes 75209872 | tf_op jit(solution)/shard_map/convert_element_type | solution.py:232
  615.5 127.4 %reduce-scatter.18.cloned.1.call-done = f32[1,784,768]{1,2,0:T(8,128)} async-done(((f32[4,784,768]{1,2,0:T(8,128)}), f32[1,784,768]{1,2,0:T(8,128)}) %reduce-scatter.18.cloned.1.call-update) | async-done | bytes 2408464 | tf_op jit(solution)/shard_map/reduce_scatter | solution.py:276
  745.8 186.7 %reduce-scatter.20.cloned.1.call-done = f32[1,784,768]{1,2,0:T(8,128)} async-done(((f32[4,784,768]{1,2,0:T(8,128)}), f32[1,784,768]{1,2,0:T(8,128)}) %reduce-scatter.20.cloned.1.call-update) | async-done | bytes 2408464 | tf_op jit(solution)/shard_map/reduce_scatter | solution.py:277
  943.4 30.2 %reduce-scatter.28.cloned.1.call-done = bf16[96,768]{1,0:T(8,128)(2,1)} async-done(((bf16[768,768]{1,0:T(8,128)(2,1)}), bf16[96,768]{1,0:T(8,128)(2,1)}) %reduce-scatter.28.cloned.1.call-update) | async-done | bytes 147472 | tf_op jit(solution)/shard_map/reduce_scatter | solution.py:322
  973.7 40.8 %reduce-scatter.24.cloned.1.call-done = bf16[96,768]{1,0:T(8,128)(2,1)} async-done(((bf16[768,768]{1,0:T(8,128)(2,1)}), bf16[96,768]{1,0:T(8,128)(2,1)}) %reduce-scatter.24.cloned.1.call-update) | async-done | bytes 147472 | tf_op jit(solution)/shard_map/reduce_scatter | solution.py:313
  1014.5 51.6 %reduce-scatter.26.cloned.1.call-done = bf16[96,2304]{1,0:T(8,128)(2,1)} async-done(((bf16[768,2304]{1,0:T(8,128)(2,1)}), bf16[96,2304]{1,0:T(8,128)(2,1)}) %reduce-scatter.26.cloned.1.call-update) | async-done | bytes 442384 | tf_op jit(solution)/shard_map/reduce_scatter | solution.py:319
  1066.1 57.8 %reduce-scatter.30.cloned.1.call-done = bf16[96,3072]{1,0:T(8,128)(2,1)} async-done(((bf16[768,3072]{1,0:T(8,128)(2,1)}), bf16[96,3072]{1,0:T(8,128)(2,1)}) %reduce-scatter.30.cloned.1.call-update) | async-done | bytes 589840 | tf_op jit(solution)/shard_map/reduce_scatter | solution.py:328
  1123.9 58.2 %reduce-scatter.32.cloned.1.call-done = bf16[384,768]{1,0:T(8,128)(2,1)} async-done(((bf16[3072,768]{1,0:T(8,128)(2,1)}), bf16[384,768]{1,0:T(8,128)(2,1)}) %reduce-scatter.32.cloned.1.call-update) | async-done | bytes 589840 | tf_op jit(solution)/shard_map/reduce_scatter | solution.py:334
  1182.0 52.0 %reduce-scatter.22.cloned.1.call-done = bf16[96,2304]{1,0:T(8,128)(2,1)} async-done(((bf16[768,2304]{1,0:T(8,128)(2,1)}), bf16[96,2304]{1,0:T(8,128)(2,1)}) %reduce-scatter.22.cloned.1.call-update) | async-done | bytes 442384 | tf_op jit(solution)/shard_map/reduce_scatter | solution.py:310
  1250.1 84.1 %all-reduce.6.cloned.1.call-done = (bf16[96,2304]{1,0:T(8,128)(2,1)}, bf16[96,768]{1,0:T(8,128)(2,1)}, bf16[96,2304]{1,0:T(8,128)(2,1)}, bf16[96,768]{1,0:T(8,12...) async-done(((bf16[96,2304]{1,0:T(8,128)(2,1)}, bf16[96,768]{1,0:T(8,128)(2,1)}, bf16[96,2304]{1,0:T(8,128)(2,1)}, bf16[96,768]{1,0:T(8,128)(2,1)}, ...) | async-done | bytes 2359312 | tf_op jit(solution)/shard_map/psum | solution.py:342
  1370.9 36.7 %reduce-scatter.36.cloned.1.call-done = bf16[96,5]{1,0:T(8,128)(2,1)} async-done(((bf16[768,5]{1,0:T(8,128)(2,1)}), bf16[96,5]{1,0:T(8,128)(2,1)}) %reduce-scatter.36.cloned.1.call-update) | async-done | bytes 976
  1417.0 27.6 %reduce-scatter.34.cloned.1.call-done = bf16[96,5]{1,0:T(8,128)(2,1)} async-done(((bf16[768,5]{1,0:T(8,128)(2,1)}), bf16[96,5]{1,0:T(8,128)(2,1)}) %reduce-scatter.34.cloned.1.call-update) | async-done | bytes 976
  1499.7 33.2 %all-gather.41.cloned.1.call-done = bf16[768,2304]{1,0:T(8,128)(2,1)} async-done(((bf16[96,2304]{1,0:T(8,128)(2,1)}), bf16[768,2304]{1,0:T(8,128)(2,1)}) %all-gather.41.cloned.1.call-update) | async-done | bytes 3538960 | tf_op jit(solution)/shard_map/all_gather | solution.py:363
  1538.4 30.4 %all-gather.37.cloned.1.call-done = bf16[768,2304]{1,0:T(8,128)(2,1)} async-done(((bf16[96,2304]{1,0:T(8,128)(2,1)}), bf16[768,2304]{1,0:T(8,128)(2,1)}) %all-gather.37.cloned.1.call-update) | async-done | bytes 3538960 | tf_op jit(solution)/shard_map/all_gather | solution.py:354
  1574.3 35.5 %all-gather.47.cloned.1.call-done = bf16[3072,768]{1,0:T(8,128)(2,1)} async-done(((bf16[384,768]{1,0:T(8,128)(2,1)}), bf16[3072,768]{1,0:T(8,128)(2,1)}) %all-gather.47.cloned.1.call-update) | async-done | bytes 4718608 | tf_op jit(solution)/shard_map/all_gather | solution.py:378
  1616.6 34.0 %all-gather.45.cloned.1.call-done = bf16[768,3072]{1,0:T(8,128)(2,1)} async-done(((bf16[96,3072]{1,0:T(8,128)(2,1)}), bf16[768,3072]{1,0:T(8,128)(2,1)}) %all-gather.45.cloned.1.call-update) | async-done | bytes 4718608 | tf_op jit(solution)/shard_map/all_gather | solution.py:372
  (355 shorter events, 475.5 us)
Async XLA Ops:
  7.9 138.9 %all-gather.49.cloned.1.call-start = ((), (), s32[]{:S(2)}) async-start(), calls=%async_computation.31 | async-start | bytes 6021120 | tf_op jit(solution)/shard_map/all_gather | solution.py:170
  55.6 182.8 %all-gather.51.cloned.1.call-start = ((), (), s32[]{:S(2)}) async-start(), calls=%async_computation.32 | async-start | bytes 6021120 | tf_op jit(solution)/shard_map/all_gather | solution.py:169
  58.5 219.0 %all-gather.27.cloned.1.call-start = ((), (), s32[]{:S(2)}) async-start(), calls=%async_computation.12 | async-start | bytes 1327104 | tf_op jit(solution)/shard_map/all_gather | solution.py:134
  59.1 239.3 %all-gather.29.cloned.1.call-start = ((), (), s32[]{:S(2)}) async-start(), calls=%async_computation.13 | async-start | bytes 3981312 | tf_op jit(solution)/shard_map/all_gather | solution.py:136
  59.7 301.5 %all-gather.31.cloned.1.call-start = ((), (), s32[]{:S(2)}) async-start(), calls=%async_computation.14 | async-start | bytes 1327104 | tf_op jit(solution)/shard_map/all_gather | solution.py:137
  60.2 305.9 %all-gather.33.cloned.1.call-start = ((), (), s32[]{:S(2)}) async-start(), calls=%async_computation.15 | async-start | bytes 5308416 | tf_op jit(solution)/shard_map/all_gather | solution.py:139
  61.0 344.9 %all-gather.35.cloned.1.call-start = ((), (), s32[]{:S(2)}) async-start(), calls=%async_computation.16 | async-start | bytes 5308416 | tf_op jit(solution)/shard_map/all_gather | solution.py:141
  61.7 681.1 %reduce-scatter.18.cloned.1.call-start = ((), (), s32[]{:S(2)}) async-start(), calls=%async_computation.17 | async-start | bytes 13762560 | tf_op jit(solution)/shard_map/reduce_scatter | solution.py:276
  556.2 376.4 %reduce-scatter.20.cloned.1.call-start = ((), (), s32[]{:S(2)}) async-start(), calls=%async_computation.18 | async-start | bytes 13762560 | tf_op jit(solution)/shard_map/reduce_scatter | solution.py:277
  564.0 409.7 %reduce-scatter.28.cloned.1.call-start = ((), (), s32[]{:S(2)}) async-start(), calls=%async_computation.25 | async-start | bytes 1327104 | tf_op jit(solution)/shard_map/reduce_scatter | solution.py:322
  568.1 446.4 %reduce-scatter.24.cloned.1.call-start = ((), (), s32[]{:S(2)}) async-start(), calls=%async_computation.21 | async-start | bytes 1327104 | tf_op jit(solution)/shard_map/reduce_scatter | solution.py:313
  572.8 493.2 %reduce-scatter.26.cloned.1.call-start = ((), (), s32[]{:S(2)}) async-start(), calls=%async_computation.23 | async-start | bytes 3981312 | tf_op jit(solution)/shard_map/reduce_scatter | solution.py:319
  581.5 542.4 %reduce-scatter.30.cloned.1.call-start = ((), (), s32[]{:S(2)}) async-start(), calls=%async_computation.27 | async-start | bytes 5308416 | tf_op jit(solution)/shard_map/reduce_scatter | solution.py:328
  592.6 589.4 %reduce-scatter.32.cloned.1.call-start = ((), (), s32[]{:S(2)}) async-start(), calls=%async_computation.29 | async-start | bytes 5308416 | tf_op jit(solution)/shard_map/reduce_scatter | solution.py:334
  603.4 630.6 %reduce-scatter.22.cloned.1.call-start = ((), (), s32[]{:S(2)}) async-start(), calls=%async_computation.19 | async-start | bytes 3981312 | tf_op jit(solution)/shard_map/reduce_scatter | solution.py:310
  943.4 390.9 %all-reduce.6.cloned.1.call-start = ((), (), s32[]{:S(2)}) async-start(), calls=%async_computation.36 | async-start | bytes 4718592 | tf_op jit(solution)/shard_map/psum | solution.py:342
  1236.6 170.9 %reduce-scatter.36.cloned.1.call-start = ((), (), s32[]{:S(2)}) async-start(), calls=%async_computation.34 | async-start | bytes 221184
  1239.7 204.8 %reduce-scatter.34.cloned.1.call-start = ((), (), s32[]{:S(2)}) async-start(), calls=%async_computation.33 | async-start | bytes 221184
  1250.1 243.4 %all-gather.43.cloned.1.call-start = ((), (), s32[]{:S(2)}) async-start(), calls=%async_computation.26 | async-start | bytes 1327104 | tf_op jit(solution)/shard_map/all_gather | solution.py:366
  1334.3 162.6 %all-gather.39.cloned.1.call-start = ((), (), s32[]{:S(2)}) async-start(), calls=%async_computation.22 | async-start | bytes 1327104 | tf_op jit(solution)/shard_map/all_gather | solution.py:357
  1335.0 197.9 %all-gather.41.cloned.1.call-start = ((), (), s32[]{:S(2)}) async-start(), calls=%async_computation.24 | async-start | bytes 3981312 | tf_op jit(solution)/shard_map/all_gather | solution.py:363
  1335.8 233.0 %all-gather.37.cloned.1.call-start = ((), (), s32[]{:S(2)}) async-start(), calls=%async_computation.20 | async-start | bytes 3981312 | tf_op jit(solution)/shard_map/all_gather | solution.py:354
  1336.3 273.5 %all-gather.47.cloned.1.call-start = ((), (), s32[]{:S(2)}) async-start(), calls=%async_computation.30 | async-start | bytes 5308416 | tf_op jit(solution)/shard_map/all_gather | solution.py:378
  1337.1 313.6 %all-gather.45.cloned.1.call-start = ((), (), s32[]{:S(2)}) async-start(), calls=%async_computation.28 | async-start | bytes 5308416 | tf_op jit(solution)/shard_map/all_gather | solution.py:372
  (75 other events, 3815.3 us)
Sparse Core Ops, SparseCore 0:
  9.9 36.6 all-gather.24
  55.7 91.0 all-gather.48
  148.9 89.4 all-gather.50
  264.4 33.9 all-gather.28
  326.1 38.9 all-gather.32
  367.0 38.9 all-gather.34
  556.3 186.4 reduce-scatter.17
  745.0 187.4 reduce-scatter.19
  935.8 37.8 reduce-scatter.27
  977.6 36.7 reduce-scatter.23
  1018.0 48.0 reduce-scatter.25
  1070.0 53.8 reduce-scatter.29
  1128.1 53.8 reduce-scatter.31
  1185.9 48.0 reduce-scatter.21
  1236.7 97.4 all-reduce.5
  1337.7 32.3 reduce-scatter.37
  1373.9 33.5 reduce-scatter.35
  1411.0 33.5 reduce-scatter.33
  1446.6 24.0 all-gather.42
  1472.7 24.0 all-gather.38
  1498.9 33.9 all-gather.40
  1534.8 33.9 all-gather.36
  1570.8 38.9 all-gather.46
  1611.7 38.9 all-gather.44
  (2 shorter events, 46.4 us)
where the time goes:
time: 1670 us; the launch traced here: 1660 us
  waiting for transfers between devices  1060 us (63%)
  matrix products  249 us (15%)
  other arithmetic  151 us (9%)
  blocking collectives  95.4 us (6%)
  local copies, waits for them, and re-layouts  86.3 us (5%)
  between operations  16.7 us (1%)
    reduce_scatter x1, waiting for transfers between devices, body(): lax.psum_scatter(grad_values_all, 'frame', scatter_dimension=0, tiled=True)  187 us
    reduce_scatter x1, waiting for transfers between devices, body(): lax.psum_scatter(grad_keys_all, 'frame', scatter_dimension=0, tiled=True)  127 us
    psum x1, waiting for transfers between devices, body(): lax.psum(parts[0].astype(jnp.bfloat16), 'frame').astype(jnp.float32)  84.1 us
    unnamed x29, waiting for transfers between devices  78.9 us
    all_gather x1, waiting for transfers between devices, body(): lax.all_gather(key_time[None], 'frame', axis=0, tiled=True)  72.3 us
    dot_general x6, matrix products, forward_dot(): return jnp.dot(operand, partner, preferred_element_type=jnp.float32)  68.6 us
    reduce_scatter x1, waiting for transfers between devices, body(): lax.psum_scatter(local_grads[8].astype(jnp.bfloat16), 'batch', scatter_di...  58.2 us
    reduce_scatter x1, waiting for transfers between devices, body(): lax.psum_scatter(local_grads[6].astype(jnp.bfloat16), 'batch', scatter_di...  57.8 us
  transfers between devices with their start and end apart: 26, of which 22 were waited for; matrix products, arithmetic and copies ran while one was open for 18% of the time, Pallas kernels for 0%

commit v1 on v0

v1 whole, which is shorter than its diff:
```python
import jax
import jax.numpy as jnp
from jax import lax
from jax.sharding import PartitionSpec as P

HEADS = 12
UNITS = 4
PATCHES = 784


def norm_rows(values, norm_gain, norm_shift):
    average = jnp.mean(values, axis=-1, keepdims=True)
    centered = values - average
    variance = jnp.mean(centered * centered, axis=-1, keepdims=True)
    return centered * lax.rsqrt(variance + 1e-06) * norm_gain + norm_shift


def gelu_exact(hidden):
    return jax.nn.gelu(hidden, approximate=False)


def forward_dot(operand, partner):
    return jnp.dot(operand, partner, preferred_element_type=jnp.float32)


def inner_rows(operand, partner):
    return lax.dot_general(
        operand, partner, (((0,), (0,)), ((), ())), preferred_element_type=jnp.float32
    )


def times_back(operand, partner):
    return lax.dot_general(
        operand, partner, (((1,), (1,)), ((), ())), preferred_element_type=jnp.float32
    )


def split_frames(array):
    frame_count, row_count, feature_count = array.shape
    return array.reshape(frame_count, row_count, HEADS, feature_count // HEADS)


def frame_scores(queries, key_rows):
    head_size = queries.shape[2] // HEADS
    scores = jnp.einsum(
        "frhd,grhd->rhfg",
        split_frames(queries),
        split_frames(key_rows),
        preferred_element_type=jnp.float32,
    )
    return scores * head_size ** (-0.5)


def frame_forward(queries, key_rows, values):
    scores = frame_scores(queries, key_rows)
    log_total = jax.nn.logsumexp(scores, axis=-1)
    rounded = jnp.exp(scores - log_total[..., None]).astype(jnp.bfloat16)
    mixture = jnp.einsum(
        "rhfg,grhd->frhd", rounded, split_frames(values), preferred_element_type=jnp.float32
    )
    return (mixture.reshape(queries.shape).astype(jnp.bfloat16), log_total)


def frame_backward(queries, key_rows, values, log_total, grad_mixture):
    head_size = queries.shape[2] // HEADS
    scores = frame_scores(queries, key_rows)
    probability = jnp.exp(scores - log_total[..., None])
    rounded = probability.astype(jnp.bfloat16)
    grad_split = split_frames(grad_mixture)
    grad_weights = jnp.einsum(
        "frhd,grhd->rhfg", grad_split, split_frames(values), preferred_element_type=jnp.float32
    )
    grad_scores = probability * (
        grad_weights - jnp.sum(grad_weights * probability, axis=-1, keepdims=True)
    )
    grad_scores = grad_scores.astype(jnp.bfloat16)
    scaling = head_size ** (-0.5)
    grad_query = (
        jnp.einsum(
            "rhfg,grhd->frhd",
            grad_scores,
            split_frames(key_rows),
            preferred_element_type=jnp.float32,
        )
        * scaling
    )
    grad_keys = (
        jnp.einsum(
            "rhfg,frhd->grhd",
            grad_scores,
            split_frames(queries),
            preferred_element_type=jnp.float32,
        )
        * scaling
    )
    grad_values = jnp.einsum(
        "rhfg,frhd->grhd", rounded, grad_split, preferred_element_type=jnp.float32
    )
    return (
        grad_query.reshape(queries.shape),
        grad_keys.reshape(key_rows.shape),
        grad_values.reshape(values.shape),
    )


def round_up(count, step):
    return -(-count // step) * step


def shift_frames(block, frame_count, shift):
    if shift % frame_count == 0:
        return block
    pairs = [(index, (index + shift) % frame_count) for index in range(frame_count)]
    return lax.ppermute(block, "frame", pairs)


def rows_to_frames(rows, frame_count, frame_index):
    part = rows.shape[0] // frame_count
    slots = []
    for shift in range(frame_count):
        owner = (frame_index + shift) % frame_count
        block = lax.dynamic_slice_in_dim(rows, owner * part, part, 0)
        slots.append(shift_frames(block, frame_count, shift))
    return slots


def frames_to_rows(slots, frame_count, frame_index):
    part = slots[0].shape[0]
    rows = jnp.zeros((part * frame_count, slots[0].shape[1]), slots[0].dtype)
    for shift in range(frame_count):
        owner = (frame_index + shift) % frame_count
        block = shift_frames(slots[shift], frame_count, -shift)
        rows = lax.dynamic_update_slice_in_dim(rows, block, owner * part, 0)
    return rows


def swap_bit(block, axis, size, bit):
    pairs = [(index, index ^ (1 << bit)) for index in range(size)]
    return lax.ppermute(block, axis, pairs)


def halve_sum(block, axis, size, bit, index):
    half = block.shape[0] // 2
    own = (index >> bit) & 1
    sent = lax.dynamic_slice_in_dim(block, (1 - own) * half, half, 0)
    kept = lax.dynamic_slice_in_dim(block, own * half, half, 0)
    arrived = swap_bit(sent, axis, size, bit)
    return (kept.astype(jnp.float32) + arrived.astype(jnp.float32)).astype(jnp.bfloat16)


def double_rows(block, axis, size, bit, index):
    arrived = swap_bit(block, axis, size, bit)
    own = ((index >> bit) & 1) == 1
    return jnp.concatenate(
        [jnp.where(own, arrived, block), jnp.where(own, block, arrived)], axis=0
    )


def sum_everywhere(blocks, sizes, indices):
    batch_size, frame_size = sizes
    batch_index, frame_index = indices
    batch_bits = batch_size.bit_length() - 1
    frame_bits = frame_size.bit_length() - 1
    results = []
    for order, block in enumerate(blocks):
        wide = list(range(1, batch_bits))
        if order % 2:
            wide = wide[::-1]
        stages = [("batch", batch_size, bit, batch_index) for bit in [0] + wide]
        stages += [("frame", frame_size, bit, frame_index) for bit in range(frame_bits)]
        for stage in stages:
            block = halve_sum(block, *stage)
        for stage in stages[::-1]:
            block = double_rows(block, *stage)
        results.append(block)
    return results

def space_scores(queries, key_rows, linked):
    row_count, feature_count = queries.shape
    head_size = feature_count // HEADS
    query_split = queries.reshape(row_count, HEADS, head_size)
    key_split = key_rows.reshape(row_count, HEADS, head_size)
    scores = jnp.einsum(
        "qhd,khd->hqk", query_split, key_split, preferred_element_type=jnp.float32
    ) * head_size ** (-0.5)
    return jnp.where(linked[None], scores, -1e30)


def body(
    tokens,
    size_tag,
    cotangent,
    time_project,
    time_output,
    time_vector,
    space_project,
    space_output,
    space_vector,
    feed_inner,
    feed_bias,
    feed_outer,
    feed_vector,
):
    frame_count = lax.axis_size("frame")
    batch_count = lax.axis_size("batch")
    frame_index = lax.axis_index("frame")
    batch_index = lax.axis_index("batch")
    feature_count = tokens.shape[2]
    row_count = tokens.shape[1]
    head_size = feature_count // HEADS
    part = round_up(-(-PATCHES // frame_count), 16)
    padded = part * frame_count
    token_rows = jnp.pad(tokens[0], ((0, padded - row_count), (0, 0)))
    grad_result = jnp.pad(cotangent[0], ((0, padded - row_count), (0, 0)))
    row_number = jnp.arange(padded, dtype=jnp.int32)[:, None]
    is_patch = row_number < PATCHES

    vectors = jnp.concatenate(
        [time_vector, space_vector, feed_vector, feed_bias.reshape(-1, time_vector.shape[1])], axis=0
    )
    vectors = lax.all_gather(vectors, "batch", axis=0)
    vectors_full = vectors[:, :13].transpose(1, 0, 2).reshape(13, feature_count)
    feed_bias_full = vectors[:, 13:].reshape(-1)
    time_rows = vectors_full[0:5].astype(jnp.float32)
    space_rows = vectors_full[5:10].astype(jnp.float32)
    feed_rows = vectors_full[10:13].astype(jnp.float32)
    time_packed = lax.all_gather(
        jnp.concatenate([time_project, time_output], axis=1), "batch", axis=0, tiled=True
    )
    space_packed = lax.all_gather(
        jnp.concatenate([space_project, space_output], axis=1), "batch", axis=0, tiled=True
    )
    feed_inner_full = lax.all_gather(feed_inner, "batch", axis=0, tiled=True)
    feed_outer_full = lax.all_gather(feed_outer, "batch", axis=0, tiled=True)
    time_project_full = time_packed[:, : 3 * feature_count]
    time_output_full = time_packed[:, 3 * feature_count :]
    space_project_full = space_packed[:, : 3 * feature_count]
    space_output_full = space_packed[:, 3 * feature_count :]

    inputs = token_rows.astype(jnp.float32)
    patches = jnp.concatenate(rows_to_frames(token_rows, frame_count, frame_index), axis=0).astype(
        jnp.float32
    )
    normed_time, time_norm_back = jax.vjp(norm_rows, patches, time_rows[0], time_rows[1])
    first_input = normed_time.astype(jnp.bfloat16)
    joined = forward_dot(first_input, time_project_full)
    query_time = (joined[:, :feature_count] + time_rows[2]).astype(jnp.bfloat16)
    key_time = joined[:, feature_count : 2 * feature_count].astype(jnp.bfloat16)
    value_time = (joined[:, 2 * feature_count :] + time_rows[3]).astype(jnp.bfloat16)
    query_time, key_time, value_time = (
        array.reshape(frame_count, part, feature_count)
        for array in (query_time, key_time, value_time)
    )
    mixture, time_total = frame_forward(query_time, key_time, value_time)
    mixture_time = frames_to_rows(list(mixture), frame_count, frame_index)
    after_time = inputs + jnp.where(
        is_patch, forward_dot(mixture_time, time_output_full) + time_rows[4], 0.0
    )
    normed_space, space_norm_back = jax.vjp(norm_rows, after_time, space_rows[0], space_rows[1])
    second_input = normed_space.astype(jnp.bfloat16)
    joined = forward_dot(second_input, space_project_full)
    query_space = (joined[:, :feature_count] + space_rows[2]).astype(jnp.bfloat16)
    key_space = joined[:, feature_count : 2 * feature_count].astype(jnp.bfloat16)
    value_space = (joined[:, 2 * feature_count :] + space_rows[3]).astype(jnp.bfloat16)
    clip_tag = size_tag[0]
    clip_number = jnp.concatenate(
        [
            jnp.arange(PATCHES, dtype=jnp.int32) // clip_tag,
            jnp.arange(UNITS, dtype=jnp.int32),
            jnp.full((padded - PATCHES - UNITS,), -1, jnp.int32),
        ]
    )
    linked = clip_number[:, None] == clip_number[None, :]
    scores = space_scores(query_space, key_space, linked)
    space_total = jax.nn.logsumexp(scores, axis=-1)
    rounded = jnp.exp(scores - space_total[..., None]).astype(jnp.bfloat16)
    value_split = value_space.reshape(padded, HEADS, head_size)
    mixture_space = jnp.einsum(
        "hqk,khd->qhd", rounded, value_split, preferred_element_type=jnp.float32
    )
    mixture_space = mixture_space.reshape(padded, feature_count).astype(jnp.bfloat16)
    after_space = after_time + forward_dot(mixture_space, space_output_full) + space_rows[4]
    normed_feed, feed_norm_back = jax.vjp(norm_rows, after_space, feed_rows[0], feed_rows[1])
    third_input = normed_feed.astype(jnp.bfloat16)
    hidden = forward_dot(third_input, feed_inner_full) + feed_bias_full.astype(jnp.float32)
    active_float, gelu_back = jax.vjp(gelu_exact, hidden)
    active = active_float.astype(jnp.bfloat16)
    block_out = (after_space + forward_dot(active, feed_outer_full) + feed_rows[2]).astype(
        jnp.bfloat16
    )
    grad_top = grad_result.astype(jnp.float32)
    grad_feed_outer = inner_rows(active, grad_result)
    feed_out_sum = jnp.sum(grad_top, axis=0)
    (grad_hidden,) = gelu_back(times_back(grad_result, feed_outer_full))
    grad_hidden = grad_hidden.astype(jnp.bfloat16)
    grad_feed_inner = inner_rows(third_input, grad_hidden)
    grad_feed_bias = jnp.sum(grad_hidden.astype(jnp.float32), axis=0)
    grad_second, feed_gain, feed_shift = feed_norm_back(times_back(grad_hidden, feed_inner_full))
    grad_second = grad_second + grad_top
    grad_feed_vector = jnp.stack([feed_gain, feed_shift, feed_out_sum])
    grad_branch = grad_second.astype(jnp.bfloat16)
    grad_space_output = inner_rows(mixture_space, grad_branch)
    space_out_sum = jnp.sum(grad_branch.astype(jnp.float32), axis=0)
    grad_mixture = times_back(grad_branch, space_output_full).astype(jnp.bfloat16)
    scores = space_scores(query_space, key_space, linked)
    probability = jnp.exp(scores - space_total[..., None])
    grad_split = grad_mixture.reshape(padded, HEADS, head_size)
    grad_weights = jnp.einsum(
        "qhd,khd->hqk", grad_split, value_split, preferred_element_type=jnp.float32
    )
    grad_scores = probability * (
        grad_weights - jnp.sum(grad_weights * probability, axis=-1, keepdims=True)
    )
    grad_scores = grad_scores.astype(jnp.bfloat16)
    scaling = head_size ** (-0.5)
    query_split = query_space.reshape(padded, HEADS, head_size)
    key_split = key_space.reshape(padded, HEADS, head_size)
    grad_query = (
        jnp.einsum("hqk,khd->qhd", grad_scores, key_split, preferred_element_type=jnp.float32)
        * scaling
    )
    grad_keys = (
        jnp.einsum("hqk,qhd->khd", grad_scores, query_split, preferred_element_type=jnp.float32)
        * scaling
    )
    grad_values = jnp.einsum(
        "hqk,qhd->khd",
        probability.astype(jnp.bfloat16),
        grad_split,
        preferred_element_type=jnp.float32,
    )
    grad_query = grad_query.reshape(padded, feature_count).astype(jnp.bfloat16)
    grad_keys = grad_keys.reshape(padded, feature_count).astype(jnp.bfloat16)
    grad_values = grad_values.reshape(padded, feature_count).astype(jnp.bfloat16)
    grad_joined = jnp.concatenate([grad_query, grad_keys, grad_values], axis=1)
    grad_space_project = inner_rows(second_input, grad_joined)
    grad_first, space_gain, space_shift = space_norm_back(
        times_back(grad_joined, space_project_full)
    )
    grad_first = grad_first + grad_second
    grad_space_vector = jnp.stack(
        [
            space_gain,
            space_shift,
            jnp.sum(grad_query.astype(jnp.float32), axis=0),
            jnp.sum(grad_values.astype(jnp.float32), axis=0),
            space_out_sum,
        ]
    )
    grad_patch = jnp.where(is_patch, grad_first, 0.0).astype(jnp.bfloat16)
    grad_time_output = inner_rows(mixture_time, grad_patch)
    time_out_sum = jnp.sum(grad_patch.astype(jnp.float32), axis=0)
    grad_mixture_time = times_back(grad_patch, time_output_full).astype(jnp.bfloat16)
    grad_mixture_slots = rows_to_frames(grad_mixture_time, frame_count, frame_index)
    grads_time = frame_backward(
        query_time, key_time, value_time, time_total, jnp.stack(grad_mixture_slots)
    )
    grad_query_time, grad_key_time, grad_value_time = (
        array.reshape(padded, feature_count).astype(jnp.bfloat16) for array in grads_time
    )
    grad_joined_time = jnp.concatenate([grad_query_time, grad_key_time, grad_value_time], axis=1)
    grad_time_project = inner_rows(first_input, grad_joined_time)
    grad_patches, time_gain, time_shift = time_norm_back(
        times_back(grad_joined_time, time_project_full)
    )
    grad_slots = list(grad_patches.astype(jnp.bfloat16).reshape(frame_count, part, feature_count))
    grad_tokens = grad_first + frames_to_rows(grad_slots, frame_count, frame_index).astype(
        jnp.float32
    )
    grad_time_vector = jnp.stack(
        [
            time_gain,
            time_shift,
            jnp.sum(grad_query_time.astype(jnp.float32), axis=0),
            jnp.sum(grad_value_time.astype(jnp.float32), axis=0),
            time_out_sum,
        ]
    )
    sizes = (batch_count, frame_count)
    indices = (batch_index, frame_index)
    low = jnp.bfloat16
    vector_grads = jnp.concatenate(
        [grad_time_vector, grad_space_vector, grad_feed_vector, grad_feed_bias.reshape(-1, feature_count)]
    )
    vector_grads = lax.psum(vector_grads, ("batch", "frame"))
    grad_feed_inner, grad_feed_outer = lax.psum(
        (grad_feed_inner.astype(low), grad_feed_outer.astype(low)), ("batch", "frame")
    )
    (space_sum,) = sum_everywhere(
        [jnp.concatenate([grad_space_project.astype(low), grad_space_output.astype(low)], axis=1)],
        sizes,
        indices,
    )
    (time_sum,) = sum_everywhere(
        [jnp.concatenate([grad_time_project.astype(low), grad_time_output.astype(low)], axis=1)],
        sizes,
        indices,
    )
    space_sum = space_sum.astype(jnp.float32)
    time_sum = time_sum.astype(jnp.float32)
    return (
        block_out[None, :row_count],
        grad_tokens[None, :row_count],
        time_sum[:, : 3 * feature_count],
        time_sum[:, 3 * feature_count :],
        vector_grads[0:5],
        space_sum[:, : 3 * feature_count],
        space_sum[:, 3 * feature_count :],
        vector_grads[5:10],
        grad_feed_inner.astype(jnp.float32),
        vector_grads[13:].reshape(-1),
        grad_feed_outer.astype(jnp.float32),
        vector_grads[10:13],
    )


def solution(mesh):
    placed = (
        P("frame", "batch", None),
        P("batch"),
        P("frame", "batch", None),
        P("batch", None),
        P("batch", None),
        P(None, "batch"),
        P("batch", None),
        P("batch", None),
        P(None, "batch"),
        P("batch", None),
        P("batch"),
        P("batch", None),
        P(None, "batch"),
    )
    return jax.shard_map(
        body,
        mesh=mesh,
        in_specs=placed,
        out_specs=(
            P("frame", "batch", None),
            P("frame", "batch", None),
            P(),
            P(),
            P(),
            P(),
            P(),
            P(),
            P(),
            P(),
            P(),
            P(),
        ),
        check_vma=False,
    )
```

time: 1670 us -> 833 us (0.50)
  waiting for transfers between devices: 1060 us -> 182 us
  blocking collectives: 95.4 us -> 49.5 us
  starting transfers between devices: 1.62 us -> 46 us
  local copies, waits for them, and re-layouts: 86.3 us -> 129 us
  matrix products: 249 us -> 283 us
  other arithmetic: 151 us -> 118 us
    reduce_scatter x8 -> x0, waiting for transfers between devices: 605 us -> none  [the longest x1 187 us: body(): lax.psum_scatter(grad_values_all, 'frame', scatter_dimension=0, tiled=True)]
    all_gather x14 -> x4, waiting for transfers between devices: 296 us -> 6.21 us  [the longest x1 6.19 us: body(): lax.all_gather(jnp.concatenate([time_project, time_output], axis=1), 'bat...]
    ppermute x0 -> x32, waiting for transfers between devices: none -> 175 us  [the longest x20 145 us: swap_bit(): return lax.ppermute(block, axis, pairs)]
    psum x1, waiting for transfers between devices: 84.1 us -> 0.01 us  [body(): lax.psum((grad_feed_inner.astype(low), grad_feed_outer.astype(low)), ('ba...]
    unnamed x29 -> x5, waiting for transfers between devices: 78.9 us -> 0.75 us
    all_gather x8 -> x1, blocking collectives: 69.7 us -> 9.2 us  [body(): vectors = lax.all_gather(vectors, 'batch', axis=0)]
    dot_general x0 -> x6, matrix products: none -> 60 us  [the longest x1 20 us: frame_backward(): jnp.einsum('frhd,grhd->rhfg', grad_split, split_frames(values), preferred...]
    ppermute x0 -> x32, starting transfers between devices: none -> 45.8 us  [the longest x20 27.5 us: swap_bit(): return lax.ppermute(block, axis, pairs)]
  transfers between devices with their start and end apart: 26 -> 37, of which waited for: 22 -> 16; matrix products, arithmetic and copies ran while one was open for 18% -> 43% of each run, Pallas kernels for 0% -> 0%
where the time goes in v1:
time: 833 us; the launch traced here: 824 us
  matrix products  283 us (34%)
  waiting for transfers between devices  182 us (22%)
  local copies, waits for them, and re-layouts  129 us (15%)
  other arithmetic  118 us (14%)
  blocking collectives  49.5 us (6%)
  starting transfers between devices  46 us (6%)
  between operations  16.7 us (2%)
    ppermute x20, waiting for transfers between devices, swap_bit(): return lax.ppermute(block, axis, pairs)  145 us
    dot_general x6, matrix products, forward_dot(): return jnp.dot(operand, partner, preferred_element_type=jnp.float32)  55.3 us
    psum x1, blocking collectives, body(): vector_grads = lax.psum(vector_grads, ('batch', 'frame'))  40.3 us
    dot_general x6, matrix products, inner_rows(): lax.dot_general(operand, partner, (((0,), (0,)), ((), ())), preferred_ele...  35.5 us
    dot_general x6, matrix products, times_back(): lax.dot_general(operand, partner, (((1,), (1,)), ((), ())), preferred_ele...  35.4 us
    ppermute x12, waiting for transfers between devices, shift_frames(): return lax.ppermute(block, 'frame', pairs)  30.2 us
    dot_general x1, matrix products, body(): jnp.einsum('qhd,khd->hqk', grad_split, value_split, preferred_element_typ...  29.9 us
    convert_element_type x1, other arithmetic, body(): grad_scores = grad_scores.astype(jnp.bfloat16)  29.8 us
  transfers between devices with their start and end apart: 37, of which 16 were waited for; matrix products, arithmetic and copies ran while one was open for 43% of the time, Pallas kernels for 0%

profile of v1, /device:TPU:0, one launch (start us, length us, event | category | flops | bytes accessed | tf_op | source)
XLA Modules:
  0.0 824.3 jit_solution(4556105770847598200)
XLA Ops:
  19.2 9.2 %all-gather.1 = bf16[8,17,96]{2,1,0:T(8,128)(2,1)S(1)} all-gather(bf16[1,17,96]{2,1,0:T(8,128)(2,1)S(1)} %maximum_bitcast_fusion), channel_id=2, replica_groups=mesh['batch'=8,'frame'=4] {'batch'}, dimensions={0}, use_global_device_ids=true | all-gather | bytes 29376 | tf_op jit(solution)/shard_map/all_gather | solution.py:221
  30.9 14.3 %collective-permute-done.1 = bf16[208,768]{1,0:T(8,128)(2,1)S(1)} collective-permute-done((bf16[208,768]{1,0:T(8,128)(2,1)S(1)}, bf16[208,768]{1,0:T(8,128)(2,1)S(1)}, u32[]{:S(2)}, u32[]{:S(2)}) %collective-permute-start.1) | collective-permute-done | bytes 319520 | tf_op jit(solution)/shard_map/ppermute | solution.py:114
  71.5 11.1 %multiply_reduce_fusion.2 = (f32[208,12,4]{2,1,0:T(8,128)S(1)}, f32[208,12,4,4]{2,3,1,0:T(4,128)}) fusion(bf16[4,208,12,64]{3,2,1,0:T(8,128)(2,1)} %reshape.315, bf16[4,208,12,64]{3,2,1,0:T(8,128)(2,1)} %reshape.314), kind=kOutput, calls=%fused_computation.51 | convolution fusion | flops 5181696 | bytes 2755584 | tf_op jit(solution)/shard_map/frhd,grhd->rhfg/dot_general | solution.py:45
  83.9 8.5 %exponential_reduce_fusion.1 = f32[208,12,4]{2,1,0:T(8,128)S(1)} fusion(f32[208,12,4,4]{2,3,1,0:T(4,128)} %get-tuple-element.131, f32[208,12,4]{2,1,0:T(8,128)} %is-finite_select_fusion), kind=kLoop, calls=%fused_computation.36 | loop fusion | flops 109824 | bytes 239616 | tf_op jit(solution)/shard_map/reduce_sum | solution.py:56
  127.5 15.9 %collective-permute-done.4 = bf16[208,768]{1,0:T(8,128)(2,1)} collective-permute-done((bf16[208,768]{1,0:T(8,128)(2,1)}, bf16[208,768]{1,0:T(8,128)(2,1)}, u32[]{:S(2)}, u32[]{:S(2)}) %collective-permute-start.4) | collective-permute-done | bytes 319520 | tf_op jit(solution)/shard_map/ppermute | solution.py:114
  161.3 14.9 %fusion = (f32[12,832]{1,0:T(8,128)S(1)}, f32[12,832,832]{1,2,0:T(8,128)}) fusion(pred[832,832]{0,1:T(8,128)(4,1)S(1)} %broadcast_compare_fusion, bf16[832,12,64]{0,2,1:T(8,128)(2,1)S(1)} %bitcast.79, bf16[832,12,64]{0,2,1:T(8,128)(2,1)S(1)} %bitcast.81), kind=kOutput, calls=%fused_computation.5 | convolution fusion | flops 1088166144 | bytes 36514816 | tf_op jit(solution)/shard_map/qhd,khd->hqk/dot_general | solution.py:183
  176.2 16.1 %exponential_reduce_fusion = f32[12,832]{1,0:T(8,128)S(1)} fusion(f32[12,832,832]{1,2,0:T(8,128)} %get-tuple-element.135, f32[12,832]{1,0:T(8,128)S(1)} %is-finite_select_fusion.1, pred[832,832]{0,1:T(8,128)(4,1)S(1)} %broadcast_compare_fusion), kind=kLoop, calls=%fused_computation.3 | loop fusion | flops 33216768 | bytes 33998848 | tf_op jit(solution)/shard_map/reduce_sum | solution.py:275
  192.3 16.7 %convolution_convert_fusion.6 = bf16[12,64,832]{2,1,0:T(8,128)(2,1)} fusion(bf16[832,12,64]{0,2,1:T(8,128)(2,1)S(1)} %bitcast.87, f32[12,832,832]{1,2,0:T(8,128)} %get-tuple-element.135, f32[12,832]{1,0:T(8,128)S(1)} %log_add_fusion.1, pred[832,832]{0,1:T(8,128)(4,1)S(1)} %broadcast_compare_fusion), kind=kOutput, calls=%fused_computation.130 | convolution fusion | flops 1097121792 | bytes 36514816 | tf_op jit(solution)/shard_map/hqk,khd->qhd/dot_general | solution.py:278
  213.8 30.0 %multiply_convert_fusion.1 = (bf16[832,3072]{1,0:T(8,128)(2,1)}, f32[832,3072]{1,0:T(8,128)}, f32[832,3072]{1,0:T(8,128)}) fusion(f32[3072]{0:T(1024)S(1)} %copy-done.75, bf16[768,3072]{1,0:T(8,128)(2,1)} %all-gather.11.cloned.1.call-done, f32[832,768]{1,0:T(8,128)S(1)} %get-tuple-element.137, f32[768]{0:T(1024)S(1)} %copy-done.84, f32[768]{0:T(1024)S(1)} %copy-done.62, ...), kind=kOutput, calls=%fused_computation.11 | convolution fusion | flops 4097753088 | bytes 32858624 | tf_op jit(solution)/shard_map/dot_general | solution.py:23
  243.8 14.8 %convert_reduce_fusion = (f32[3072]{0:T(1024)}, bf16[832,3072]{1,0:T(8,128)(2,1)S(1)}) fusion(f32[832,3072]{1,0:T(8,128)} %get-tuple-element.84, bf16[3072,768]{1,0:T(8,128)(2,1)} %all-gather.13.cloned.1.call-done, bf16[788,768]{1,0:T(8,128)(2,1)} %bitcast.91, f32[832,3072]{1,0:T(8,128)} %get-tuple-element.138, f32[3072]{0:T(1024)S(1)} %copy-done.75), kind=kOutput, calls=%fused_computation.9 | convolution fusion | flops 3969315840 | bytes 31512576 | tf_op jit(solution)/shard_map/dot_general | solution.py:33
  273.2 17.0 %convert_reduce_fusion.5 = (f32[12,64]{1,0:T(8,128)}, bf16[12,64,832]{2,1,0:T(8,128)(2,1)}) fusion(bf16[832,12,64]{0,2,1:T(8,128)(2,1)S(1)} %bitcast.89, f32[12,832,832]{1,2,0:T(8,128)} %get-tuple-element.135, f32[12,832]{1,0:T(8,128)S(1)} %log_add_fusion.1, pred[832,832]{0,1:T(8,128)(4,1)S(1)} %broadcast_compare_fusion), kind=kOutput, calls=%fused_computation.73 | convolution fusion | flops 1098398976 | bytes 36517888 | tf_op jit(solution)/shard_map/hqk,qhd->khd/dot_general | solution.py:326
  290.2 29.9 %multiply_reduce_fusion = (f32[12,832]{1,0:T(8,128)}, f32[12,832,832]{1,2,0:T(8,128)}) fusion(f32[12,832,832]{1,2,0:T(8,128)} %get-tuple-element.135, f32[12,832]{1,0:T(8,128)S(1)} %log_add_fusion.1, pred[832,832]{0,1:T(8,128)(4,1)S(1)} %broadcast_compare_fusion, bf16[832,12,64]{0,2,1:T(8,128)(2,1)S(1)} %bitcast.90, bf16[832,12,64]{0,2,1:T(8,128)(2,1)S(1)} %bitcast.88), kind=kOutput, calls=%fused_computation.1 | convolution fusion | flops 1104779520 | bytes 69781504 | tf_op jit(solution)/shard_map/qhd,khd->hqk/dot_general | solution.py:308
  320.1 29.8 %multiply_convert_fusion = bf16[12,832,832]{1,2,0:T(8,128)(2,1)} fusion(f32[12,832,832]{1,2,0:T(8,128)} %get-tuple-element.141, f32[12,832,832]{1,2,0:T(8,128)} %get-tuple-element.135, f32[12,832]{1,0:T(8,128)} %get-tuple-element.140, f32[12,832]{1,0:T(8,128)S(1)} %log_add_fusion.1, pred[832,832]{0,1:T(8,128)(4,1)S(1)} %broadcast_compare_fusion), kind=kLoop, calls=%fused_computation | loop fusion | flops 49840128 | bytes 83838976 | tf_op jit(solution)/shard_map/convert_element_type | solution.py:314
  350.0 9.2 %multiply_convert_fusion.5 = bf16[12,64,832]{2,1,0:T(8,128)(2,1)S(1)} fusion(bf16[832,12,64]{0,2,1:T(8,128)(2,1)S(1)} %bitcast.80, bf16[12,832,832]{1,2,0:T(8,128)(2,1)} %multiply_convert_fusion), kind=kOutput, calls=%fused_computation.75 | convolution fusion | flops 1064534016 | bytes 19169280 | tf_op jit(solution)/shard_map/hqk,qhd->khd/dot_general | solution.py:323
  359.3 9.4 %convert_reduce_fusion.6 = (f32[12,64]{1,0:T(8,128)S(1)}, bf16[12,64,832]{2,1,0:T(8,128)(2,1)S(1)}) fusion(bf16[832,12,64]{0,2,1:T(8,128)(2,1)S(1)} %bitcast.82, bf16[12,832,832]{1,2,0:T(8,128)(2,1)} %multiply_convert_fusion), kind=kOutput, calls=%fused_computation.74 | convolution fusion | flops 1065811200 | bytes 19172352 | tf_op jit(solution)/shard_map/hqk,khd->qhd/dot_general | solution.py:319
  371.3 7.7 convolution_convert_fusion.1
  410.9 9.3 %convolution_convert_fusion = bf16[3072,768]{1,0:T(8,128)(2,1)} fusion(bf16[832,3072]{1,0:T(8,128)(2,1)} %get-tuple-element.83, bf16[788,768]{1,0:T(8,128)(2,1)S(1)} %bitcast.94), kind=kOutput, calls=%fused_computation.38 | convolution fusion | flops 3928227840 | bytes 11040768 | tf_op jit(solution)/shard_map/dot_general | solution.py:27
  443.2 20.0 %multiply_reduce_fusion.1 = (f32[208,12,4]{2,1,0:T(8,128)}, f32[208,12,4,4]{2,3,1,0:T(4,128)}) fusion(f32[208,12,4]{2,1,0:T(8,128)S(1)} %copy-done.16, f32[208,12,4,4]{2,3,1,0:T(4,128)} %get-tuple-element.131, bf16[4,208,12,64]{3,2,1,0:T(8,128)(2,1)} %reshape.313, bf16[1,208,12,64]{3,0,2,1:T(2,128)(2,1)} %copy.122, bf16[1,208,12,64]{3,0,2,1:T(2,128)(2,1)} %copy.121, ...), kind=kOutput, calls=%fused_computation.34 | convolution fusion | flops 10373376 | bytes 2955264 | tf_op jit(solution)/shard_map/frhd,grhd->rhfg/dot_general | solution.py:70
  479.8 13.7 %convert_reduce_fusion.1 = (f32[12,64]{1,0:T(8,128)}, bf16[208,12,64,4]{2,3,1,0:T(4,128)(2,1)}) fusion(f32[208,12,4]{2,1,0:T(8,128)S(1)} %copy-done.16, f32[208,12,4,4]{2,3,1,0:T(4,128)S(1)} %bitcast.86, bf16[1,208,12,64]{3,0,2,1:T(2,128)(2,1)} %copy.122, bf16[1,208,12,64]{3,0,2,1:T(2,128)(2,1)} %copy.121, bf16[1,208,12,64]{3,0,2,1:T(2,128)(2,1)} %copy.120, ...), kind=kOutput, calls=%fused_computation.29 | convolution fusion | flops 12259584 | bytes 2758656 | tf_op jit(solution)/shard_map/rhfg,frhd->grhd/dot_general | solution.py:96
  538.5 32.2 %collective-permute-done.23 = bf16[192,3072]{1,0:T(8,128)(2,1)S(1)} collective-permute-done((bf16[192,3072]{1,0:T(8,128)(2,1)S(1)}, bf16[192,3072]{1,0:T(8,128)(2,1)S(1)}, u32[]{:S(2)}, u32[]{:S(2)}) %collective-permute-start.23) | collective-permute-done | bytes 1179680 | tf_op jit(solution)/shard_map/ppermute | solution.py:139
  572.6 40.6 %collective-permute-done.13 = bf16[192,3072]{1,0:T(8,128)(2,1)S(1)} collective-permute-done((bf16[192,3072]{1,0:T(8,128)(2,1)S(1)}, bf16[192,3072]{1,0:T(8,128)(2,1)S(1)}, u32[]{:S(2)}, u32[]{:S(2)}) %collective-permute-start.13) | collective-permute-done | bytes 1179680 | tf_op jit(solution)/shard_map/ppermute | solution.py:139
  615.7 13.8 %collective-permute-done.25 = bf16[48,3072]{1,0:T(8,128)(2,1)S(1)} collective-permute-done((bf16[48,3072]{1,0:T(8,128)(2,1)S(1)}, bf16[48,3072]{1,0:T(8,128)(2,1)S(1)}, u32[]{:S(2)}, u32[]{:S(2)}) %collective-permute-start.25) | collective-permute-done | bytes 294944 | tf_op jit(solution)/shard_map/ppermute | solution.py:139
  691.4 19.3 %collective-permute-done.30 = bf16[192,3072]{1,0:T(8,128)(2,1)S(1)} collective-permute-done((bf16[192,3072]{1,0:T(8,128)(2,1)S(1)}, bf16[192,3072]{1,0:T(8,128)(2,1)S(1)}, u32[]{:S(2)}, u32[]{:S(2)}) %collective-permute-start.30) | collective-permute-done | bytes 1179680 | tf_op jit(solution)/shard_map/ppermute | solution.py:139
  728.7 40.3 %psum.21 = f32[17,768]{1,0:T(8,128)} all-reduce(f32[17,768]{1,0:T(8,128)} %concatenate.74), channel_id=1, replica_groups=mesh['batch'=8,'frame'=4] {'batch','frame'}, use_global_device_ids=true, to_apply=%region_32.33 | all-reduce | flops 13056 | bytes 104448 | tf_op jit(solution)/shard_map/psum | solution.py:385
  (483 shorter events, 363.7 us)
Async XLA Ops:
  7.2 45.1 %all-gather.7.cloned.1.call-start = ((), (), s32[]{:S(2)}) async-start(), calls=%async_computation | async-start | bytes 5308416 | tf_op jit(solution)/shard_map/all_gather | solution.py:227
  9.3 139.7 %all-gather.9.cloned.1.call-start = ((), (), s32[]{:S(2)}) async-start(), calls=%async_computation.1 | async-start | bytes 5308416 | tf_op jit(solution)/shard_map/all_gather | solution.py:230
  11.4 202.2 %all-gather.11.cloned.1.call-start = ((), (), s32[]{:S(2)}) async-start(), calls=%async_computation.2 | async-start | bytes 5308416 | tf_op jit(solution)/shard_map/all_gather | solution.py:233
  12.1 231.7 %all-gather.13.cloned.1.call-start = ((), (), s32[]{:S(2)}) async-start(), calls=%async_computation.3 | async-start | bytes 5308416 | tf_op jit(solution)/shard_map/all_gather | solution.py:234
  18.0 27.2 %collective-permute-start.1 = (bf16[208,768]{1,0:T(8,128)(2,1)S(1)}, bf16[208,768]{1,0:T(8,128)(2,1)S(1)}, u32[]{:S(2)}, u32[]{:S(2)}) collective-permute-start(bf16[208,768]{1,0:T(8,128)(2,1)S(1)} %get-tuple-element.112), channel_id=1, source_target_pairs={{0,2},{1,3},{2,0},{3,1},{4,6},{5,7},{6,4},{7,5},{8,10},{9,11},{10,... | collective-permute-start | bytes 958472 | tf_op jit(solution)/shard_map/ppermute | solution.py:114
  18.0 27.2 %collective-permute-start = (bf16[208,768]{1,0:T(8,128)(2,1)S(1)}, bf16[208,768]{1,0:T(8,128)(2,1)S(1)}, u32[]{:S(2)}, u32[]{:S(2)}) collective-permute-start(bf16[208,768]{1,0:T(8,128)(2,1)S(1)} %get-tuple-element.111), channel_id=1, source_target_pairs={{0,1},{1,2},{2,3},{3,0},{4,5},{5,6},{6,7},{7,4},{8,9},{9,10},{10,1... | collective-permute-start | bytes 958472 | tf_op jit(solution)/shard_map/ppermute | solution.py:114
  19.0 767.9 %all-reduce.5.cloned.1.call-start = ((), (), s32[]{:S(2)}) async-start(), calls=%async_computation.4 | async-start | bytes 18874368 | tf_op jit(solution)/shard_map/psum | solution.py:386
  121.0 22.4 %collective-permute-start.4 = (bf16[208,768]{1,0:T(8,128)(2,1)}, bf16[208,768]{1,0:T(8,128)(2,1)}, u32[]{:S(2)}, u32[]{:S(2)}) collective-permute-start(bf16[208,768]{1,0:T(8,128)(2,1)} %copy.104), channel_id=1, source_target_pairs={{0,2},{1,3},{2,0},{3,1},{4,6},{5,7},{6,4},{7,5},{8,10},{9,11},{10,... | collective-permute-start | bytes 958472 | tf_op jit(solution)/shard_map/ppermute | solution.py:114
  125.3 19.1 %collective-permute-start.5 = (bf16[208,768]{1,0:T(8,128)(2,1)S(1)}, bf16[208,768]{1,0:T(8,128)(2,1)S(1)}, u32[]{:S(2)}, u32[]{:S(2)}) collective-permute-start(bf16[208,768]{1,0:T(8,128)(2,1)S(1)} %copy.106), channel_id=1, source_target_pairs={{0,1},{1,2},{2,3},{3,0},{4,5},{5,6},{6,7},{7,4},{8,9},{9,10},{10,1... | collective-permute-start | bytes 958472 | tf_op jit(solution)/shard_map/ppermute | solution.py:114
  397.9 35.2 %collective-permute-start.8 = (bf16[208,768]{1,0:T(8,128)(2,1)}, bf16[208,768]{1,0:T(8,128)(2,1)}, u32[]{:S(2)}, u32[]{:S(2)}) collective-permute-start(bf16[208,768]{1,0:T(8,128)(2,1)} %get-tuple-element.106), channel_id=1, source_target_pairs={{0,3},{1,0},{2,1},{3,2},{4,7},{5,4},{6,5},{7,6},{8,11},{9,8},{10,9... | collective-permute-start | bytes 958472 | tf_op jit(solution)/shard_map/ppermute | solution.py:114
  397.9 38.5 %collective-permute-start.7 = (bf16[208,768]{1,0:T(8,128)(2,1)}, bf16[208,768]{1,0:T(8,128)(2,1)}, u32[]{:S(2)}, u32[]{:S(2)}) collective-permute-start(bf16[208,768]{1,0:T(8,128)(2,1)} %get-tuple-element.107), channel_id=1, source_target_pairs={{0,2},{1,3},{2,0},{3,1},{4,6},{5,7},{6,4},{7,5},{8,10},{9,11},{10,... | collective-permute-start | bytes 958472 | tf_op jit(solution)/shard_map/ppermute | solution.py:114
  398.3 41.6 %collective-permute-start.6 = (bf16[208,768]{1,0:T(8,128)(2,1)}, bf16[208,768]{1,0:T(8,128)(2,1)}, u32[]{:S(2)}, u32[]{:S(2)}) collective-permute-start(bf16[208,768]{1,0:T(8,128)(2,1)} %get-tuple-element.108), channel_id=1, source_target_pairs={{0,1},{1,2},{2,3},{3,0},{4,5},{5,6},{6,7},{7,4},{8,9},{9,10},{10,1... | collective-permute-start | bytes 958472 | tf_op jit(solution)/shard_map/ppermute | solution.py:114
  410.9 120.9 %collective-permute-start.22 = (bf16[384,3072]{1,0:T(8,128)(2,1)}, bf16[384,3072]{1,0:T(8,128)(2,1)}, u32[]{:S(2)}, u32[]{:S(2)}) collective-permute-start(bf16[384,3072]{1,0:T(8,128)(2,1)} %fusion.35), channel_id=1, source_target_pairs={{0,4},{4,0},{8,12},{12,8},{16,20},{20,16},{24,28},{28,24},{1,5},{5... | collective-permute-start | bytes 7077896 | tf_op jit(solution)/shard_map/ppermute | solution.py:139
  535.6 35.1 %collective-permute-start.23 = (bf16[192,3072]{1,0:T(8,128)(2,1)S(1)}, bf16[192,3072]{1,0:T(8,128)(2,1)S(1)}, u32[]{:S(2)}, u32[]{:S(2)}) collective-permute-start(bf16[192,3072]{1,0:T(8,128)(2,1)S(1)} %constant_dynamic-slice_fusion.3), channel_id=1, source_target_pairs={{0,8},{4,12},{8,0},{12,4},{16,24},{20,28},{24,16},{28,20},{1,9},{5... | collective-permute-start | bytes 3538952 | tf_op jit(solution)/shard_map/ppermute | solution.py:139
  537.8 75.3 %collective-permute-start.13 = (bf16[192,3072]{1,0:T(8,128)(2,1)S(1)}, bf16[192,3072]{1,0:T(8,128)(2,1)S(1)}, u32[]{:S(2)}, u32[]{:S(2)}) collective-permute-start(bf16[192,3072]{1,0:T(8,128)(2,1)S(1)} %constant_dynamic-slice_fusion.7), channel_id=1, source_target_pairs={{0,8},{4,12},{8,0},{12,4},{16,24},{20,28},{24,16},{28,20},{1,9},{5... | collective-permute-start | bytes 3538952 | tf_op jit(solution)/shard_map/ppermute | solution.py:139
  571.2 42.4 %collective-permute-start.24 = (bf16[96,3072]{1,0:T(8,128)(2,1)S(1)}, bf16[96,3072]{1,0:T(8,128)(2,1)S(1)}, u32[]{:S(2)}, u32[]{:S(2)}) collective-permute-start(bf16[96,3072]{1,0:T(8,128)(2,1)S(1)} %constant_dynamic-slice_fusion.2), channel_id=1, source_target_pairs={{0,16},{4,20},{8,24},{12,28},{16,0},{20,4},{24,8},{28,12},{1,17},{... | collective-permute-start | bytes 1769480 | tf_op jit(solution)/shard_map/ppermute | solution.py:139
  671.7 18.4 %collective-permute-start.19 = (bf16[96,3072]{1,0:T(8,128)(2,1)S(1)}, bf16[96,3072]{1,0:T(8,128)(2,1)S(1)}, u32[]{:S(2)}, u32[]{:S(2)}) collective-permute-start(bf16[96,3072]{1,0:T(8,128)(2,1)S(1)} %pad_maximum_fusion.11), channel_id=1, source_target_pairs={{0,16},{4,20},{8,24},{12,28},{16,0},{20,4},{24,8},{28,12},{1,17},{... | collective-permute-start | bytes 1769480 | tf_op jit(solution)/shard_map/ppermute | solution.py:139
  681.8 29.0 %collective-permute-start.30 = (bf16[192,3072]{1,0:T(8,128)(2,1)S(1)}, bf16[192,3072]{1,0:T(8,128)(2,1)S(1)}, u32[]{:S(2)}, u32[]{:S(2)}) collective-permute-start(bf16[192,3072]{1,0:T(8,128)(2,1)S(1)} %pad_maximum_fusion.8), channel_id=1, source_target_pairs={{0,8},{4,12},{8,0},{12,4},{16,24},{20,28},{24,16},{28,20},{1,9},{5... | collective-permute-start | bytes 3538952 | tf_op jit(solution)/shard_map/ppermute | solution.py:139
  690.5 78.4 %collective-permute-start.20 = (bf16[192,3072]{1,0:T(8,128)(2,1)S(1)}, bf16[192,3072]{1,0:T(8,128)(2,1)}, u32[]{:S(2)}, u32[]{:S(2)}) collective-permute-start(bf16[192,3072]{1,0:T(8,128)(2,1)S(1)} %pad_maximum_fusion.7), channel_id=1, source_target_pairs={{0,8},{4,12},{8,0},{12,4},{16,24},{20,28},{24,16},{28,20},{1,9},{5... | collective-permute-start | bytes 3538952 | tf_op jit(solution)/shard_map/ppermute | solution.py:139
  712.9 86.0 %collective-permute-start.31 = (bf16[384,3072]{1,0:T(8,128)(2,1)}, bf16[384,3072]{1,0:T(8,128)(2,1)}, u32[]{:S(2)}, u32[]{:S(2)}) collective-permute-start(bf16[384,3072]{1,0:T(8,128)(2,1)} %pad_maximum_fusion.3), channel_id=1, source_target_pairs={{0,4},{4,0},{8,12},{12,8},{16,20},{20,16},{24,28},{28,24},{1,5},{5... | collective-permute-start | bytes 7077896 | tf_op jit(solution)/shard_map/ppermute | solution.py:139
  715.1 60.5 %collective-permute-start.9 = (bf16[208,768]{1,0:T(8,128)(2,1)}, bf16[208,768]{1,0:T(8,128)(2,1)}, u32[]{:S(2)}, u32[]{:S(2)}) collective-permute-start(bf16[208,768]{1,0:T(8,128)(2,1)} %get-tuple-element.103), channel_id=1, source_target_pairs={{0,3},{1,0},{2,1},{3,2},{4,7},{5,4},{6,5},{7,6},{8,11},{9,8},{10,9... | collective-permute-start | bytes 958472 | tf_op jit(solution)/shard_map/ppermute | solution.py:114
  718.0 59.3 %collective-permute-start.10 = (bf16[208,768]{1,0:T(8,128)(2,1)}, bf16[208,768]{1,0:T(8,128)(2,1)}, u32[]{:S(2)}, u32[]{:S(2)}) collective-permute-start(bf16[208,768]{1,0:T(8,128)(2,1)} %get-tuple-element.102), channel_id=1, source_target_pairs={{0,2},{1,3},{2,0},{3,1},{4,6},{5,7},{6,4},{7,5},{8,10},{9,11},{10,... | collective-permute-start | bytes 958472 | tf_op jit(solution)/shard_map/ppermute | solution.py:114
  718.6 60.4 %collective-permute-start.11 = (bf16[208,768]{1,0:T(8,128)(2,1)}, bf16[208,768]{1,0:T(8,128)(2,1)}, u32[]{:S(2)}, u32[]{:S(2)}) collective-permute-start(bf16[208,768]{1,0:T(8,128)(2,1)} %get-tuple-element.101), channel_id=1, source_target_pairs={{0,1},{1,2},{2,3},{3,0},{4,5},{5,6},{6,7},{7,4},{8,9},{9,10},{10,1... | collective-permute-start | bytes 958472 | tf_op jit(solution)/shard_map/ppermute | solution.py:114
  773.7 34.3 %collective-permute-start.21 = (bf16[384,3072]{1,0:T(8,128)(2,1)}, bf16[384,3072]{1,0:T(8,128)(2,1)}, u32[]{:S(2)}, u32[]{:S(2)}) collective-permute-start(bf16[384,3072]{1,0:T(8,128)(2,1)} %pad_maximum_fusion.2), channel_id=1, source_target_pairs={{0,4},{4,0},{8,12},{12,8},{16,20},{20,16},{24,28},{28,24},{1,5},{5... | collective-permute-start | bytes 7077896 | tf_op jit(solution)/shard_map/ppermute | solution.py:139
  (120 other events, 1220.5 us)
Sparse Core Ops, SparseCore 0:
  10.5 41.7 all-gather.6
  54.7 38.9 all-gather.8
  95.5 38.9 all-gather.10
  136.2 38.9 all-gather.12
  429.1 208.4 all-reduce.4

commit v2 on v1

v2 whole, which is shorter than its diff:
```python
import functools
import math

import jax
import jax.numpy as jnp
from jax import lax
from jax.experimental import pallas as pl
from jax.experimental.pallas import tpu as pltpu
from jax.sharding import PartitionSpec as P

HEADS = 12
UNITS = 4
PATCHES = 784
LOG2E = 1.4426950408889634

def round_up(count, step):
    return -(-count // step) * step


def shift_frames(block, frame_count, shift):
    if shift % frame_count == 0:
        return block
    pairs = [(index, (index + shift) % frame_count) for index in range(frame_count)]
    return lax.ppermute(block, "frame", pairs)


def rows_to_frames(rows, frame_count, frame_index):
    part = rows.shape[0] // frame_count
    slots = []
    for shift in range(frame_count):
        owner = (frame_index + shift) % frame_count
        block = lax.dynamic_slice_in_dim(rows, owner * part, part, 0)
        slots.append(shift_frames(block, frame_count, shift))
    return slots


def frames_to_rows(slots, frame_count, frame_index):
    part = slots[0].shape[0]
    rows = jnp.zeros((part * frame_count, slots[0].shape[1]), slots[0].dtype)
    for shift in range(frame_count):
        owner = (frame_index + shift) % frame_count
        block = shift_frames(slots[shift], frame_count, -shift)
        rows = lax.dynamic_update_slice_in_dim(rows, block, owner * part, 0)
    return rows


def swap_bit(block, axis, size, bit):
    pairs = [(index, index ^ (1 << bit)) for index in range(size)]
    return lax.ppermute(block, axis, pairs)


def halve_sum(block, axis, size, bit, index):
    half = block.shape[0] // 2
    own = (index >> bit) & 1
    sent = lax.dynamic_slice_in_dim(block, (1 - own) * half, half, 0)
    kept = lax.dynamic_slice_in_dim(block, own * half, half, 0)
    arrived = swap_bit(sent, axis, size, bit)
    return (kept.astype(jnp.float32) + arrived.astype(jnp.float32)).astype(jnp.bfloat16)


def double_rows(block, axis, size, bit, index):
    arrived = swap_bit(block, axis, size, bit)
    own = ((index >> bit) & 1) == 1
    return jnp.concatenate(
        [jnp.where(own, arrived, block), jnp.where(own, block, arrived)], axis=0
    )


def sum_everywhere(blocks, sizes, indices):
    batch_size, frame_size = sizes
    batch_index, frame_index = indices
    batch_bits = batch_size.bit_length() - 1
    frame_bits = frame_size.bit_length() - 1
    results = []
    for order, block in enumerate(blocks):
        wide = list(range(1, batch_bits))
        if order % 2:
            wide = wide[::-1]
        stages = [("batch", batch_size, bit, batch_index) for bit in [0] + wide]
        stages += [("frame", frame_size, bit, frame_index) for bit in range(frame_bits)]
        for stage in stages:
            block = halve_sum(block, *stage)
        for stage in stages[::-1]:
            block = double_rows(block, *stage)
        results.append(block)
    return results

def contract(x,y,dims):
    return lax.dot_general(x,y,((dims[0:1],dims[1:2]),((),())),preferred_element_type=jnp.float32)

def widen_rows(values, wide):
    rows, width = values.shape
    if wide == rows:
        return values
    return jnp.concatenate([values, jnp.zeros((wide - rows, width), values.dtype)])


def head_halves(width):
    lane = lax.broadcasted_iota(jnp.int32, (1, width), 1)
    return [lane < width // 2, lane >= width // 2]

def space_forward_kernel(scale, tile, column_ref, row_ref, q_ref, k_ref, v_ref, mixture_ref, total_ref, bias_ref, k_wide, v_wide):
    rows, width = q_ref.shape
    wide = k_wide.shape[0]
    @pl.when(pl.program_id(0) == 0)
    def _():
        bias_ref[...] = jnp.where(column_ref[...] == row_ref[...], 0.0, -1e30)
        if wide > rows:
            k_wide[rows:] = jnp.zeros((wide - rows, width), k_wide.dtype)
            v_wide[rows:] = jnp.zeros((wide - rows, width), v_wide.dtype)
    k_wide[:rows] = k_ref[...]
    v_wide[:rows] = v_ref[...]
    halves = head_halves(width)
    zero, one = jnp.zeros((), q_ref.dtype), jnp.ones((), q_ref.dtype)
    filled = [jnp.where(half, v_wide[...], one) for half in halves]
    for start in range(0, rows, tile):
        span = slice(start, start + tile)
        outs, tops = [], []
        for half, values in zip(halves, filled):
            queries = jnp.where(half, q_ref[span], zero)
            scores = contract(queries, k_wide[...], (1, 1)) * (scale * LOG2E) + bias_ref[span]
            top = jnp.max(scores, axis=1, keepdims=True)
            weights = jnp.exp2(scores - top)
            outs.append(contract(weights.astype(jnp.bfloat16), values, (1, 0)))
            tops.append(top)
        mass = pltpu.roll(jnp.where(halves[0], outs[1], outs[0]), width // 2, 1)
        mixture = jnp.where(halves[0], outs[0], outs[1]) / mass
        mixture_ref[span] = mixture.astype(mixture_ref.dtype)
        total_ref[span] = jnp.where(halves[0], tops[0], tops[1]) + jnp.log2(mass)


def space_forward(qkv, clip, features):
    rows = qkv.shape[0]
    pairs = HEADS // 2
    width = features // pairs
    wide = round_up(rows, 128)
    scale = (features // HEADS) ** -0.5
    tile = rows
    column = clip[:, None]
    row = jnp.pad(clip, (0, wide - rows), constant_values=-2)[None]
    blocks = [pl.BlockSpec((rows, width), lambda i, o=o: (0, o + i)) for o in (0, pairs, 2 * pairs)]
    out = pl.BlockSpec((rows, width), lambda i: (0, i))
    return pl.pallas_call(
        functools.partial(space_forward_kernel, scale, tile),
        grid=(pairs,),
        in_specs=[pl.BlockSpec((rows, 1), lambda i: (0, 0)), pl.BlockSpec((1, wide), lambda i: (0, 0))] + blocks,
        out_specs=[out, out],
        out_shape=[jax.ShapeDtypeStruct((rows, features), jnp.bfloat16), jax.ShapeDtypeStruct((rows, features), jnp.float32)],
        scratch_shapes=[pltpu.VMEM((rows, wide), jnp.float32), pltpu.VMEM((wide, width), jnp.bfloat16), pltpu.VMEM((wide, width), jnp.bfloat16)],
        compiler_params=pltpu.CompilerParams(vmem_limit_bytes=48 << 20),
    )(column, row, qkv, qkv, qkv)

def space_backward_kernel(scale, tile, column_ref, row_ref, q_ref, k_ref, v_ref, mixture_ref, total_ref, grad_ref, dq_ref, dk_ref, dv_ref, bias_ref, q_wide, g_wide, dq_wide):
    rows, width = q_ref.shape
    wide = q_wide.shape[0]
    @pl.when(pl.program_id(0) == 0)
    def _():
        bias_ref[...] = jnp.where(column_ref[...] == row_ref[...], 0.0, -1e30)
        if wide > rows:
            q_wide[rows:] = jnp.zeros((wide - rows, width), q_wide.dtype)
            g_wide[rows:] = jnp.zeros((wide - rows, width), g_wide.dtype)
    q_wide[:rows] = q_ref[...]
    g_wide[:rows] = grad_ref[...]
    halves = head_halves(width)
    zero = jnp.zeros((), q_ref.dtype)
    product = grad_ref[...].astype(jnp.float32) * mixture_ref[...].astype(jnp.float32)
    sums = [jnp.sum(jnp.where(half, product, 0.0), axis=1, keepdims=True) for half in halves]
    delta = widen_rows(jnp.where(halves[0], sums[0], sums[1]), wide).T
    total = widen_rows(total_ref[...], wide).T
    dq_parts = [None, None]
    for start in range(0, rows, tile):
        span = slice(start, start + tile)
        dk, dv = [], []
        for index, half in enumerate(halves):
            at = index * (width // 2)
            keys = jnp.where(half, k_ref[span], zero)
            values = jnp.where(half, v_ref[span], zero)
            scores = contract(keys, q_wide[...], (1, 1)) * (scale * LOG2E)
            weights = jnp.exp2(scores + (bias_ref[span] - total[at:at + 1]))
            slopes = contract(values, g_wide[...], (1, 1))
            slopes = (weights * (slopes - delta[at:at + 1])).astype(jnp.bfloat16)
            dv.append(contract(weights.astype(jnp.bfloat16), g_wide[...], (1, 0)))
            dk.append(contract(slopes, q_wide[...], (1, 0)))
            part = contract(slopes, keys, (0, 0))
            dq_parts[index] = part if start == 0 else dq_parts[index] + part
        dk_ref[span] = (jnp.where(halves[0], dk[0], dk[1]) * scale).astype(dk_ref.dtype)
        dv_ref[span] = jnp.where(halves[0], dv[0], dv[1]).astype(dv_ref.dtype)
    dq_ref[...] = ((dq_parts[0] + dq_parts[1])[:rows] * scale).astype(dq_ref.dtype)

def space_backward(qkv, mixture, total, grad, clip, features):
    rows = qkv.shape[0]
    pairs = HEADS // 2
    width = features // pairs
    wide = round_up(rows, 128)
    scale = (features // HEADS) ** -0.5
    tile = rows
    column = clip[:, None]
    row = jnp.pad(clip, (0, wide - rows), constant_values=-2)[None]
    blocks = [pl.BlockSpec((rows, width), lambda i, o=o: (0, o + i)) for o in (0, pairs, 2 * pairs)]
    out = pl.BlockSpec((rows, width), lambda i: (0, i))
    shape = jax.ShapeDtypeStruct((rows, features), jnp.bfloat16)
    return pl.pallas_call(
        functools.partial(space_backward_kernel, scale, tile),
        grid=(pairs,),
        in_specs=[pl.BlockSpec((rows, 1), lambda i: (0, 0)), pl.BlockSpec((1, wide), lambda i: (0, 0))] + blocks + [out, out, out],
        out_specs=[out, out, out],
        out_shape=[shape, shape, shape],
        scratch_shapes=[pltpu.VMEM((rows, wide), jnp.float32), pltpu.VMEM((wide, width), jnp.bfloat16), pltpu.VMEM((wide, width), jnp.bfloat16), pltpu.VMEM((wide, width), jnp.float32)],
        compiler_params=pltpu.CompilerParams(vmem_limit_bytes=48 << 20),
    )(column, row, qkv, qkv, qkv, mixture, total, grad)

def norm_parts(values):
    average = jnp.mean(values, axis=1, keepdims=True)
    centered = values - average
    spread = lax.rsqrt(jnp.mean(centered * centered, axis=1, keepdims=True) + 1e-06)
    return centered * spread, spread
def norm_back(grad, normed, spread, gain):
    scaled = grad * gain
    return spread * (scaled - jnp.mean(scaled, axis=1, keepdims=True) - normed * jnp.mean(scaled * normed, axis=1, keepdims=True))
def column_sum(values):
    return jnp.sum(values, axis=0, keepdims=True)

def feed_kernel(chunks, x1_ref, mixture_ref, dz_ref, so_ref, fi_ref, fo_ref, fb_ref, vec_ref,
                out_ref, dx2_ref, dys_ref, dos_ref, gfi_ref, gfo_ref, gfb_ref, gso_ref, gvec_ref,
                x2_s, a3_s, a3t_s, acc_s, da_s, g_s, dh_s):
    step = pl.program_id(0)
    rows = x1_ref.shape[0]
    @pl.when(step == 0)
    def _():
        x2 = x1_ref[...] + contract(mixture_ref[...], so_ref[...], (1, 0)) + vec_ref[9:10]
        x2_s[...] = x2
        normed, _ = norm_parts(x2)
        a3 = (normed * vec_ref[10:11] + vec_ref[11:12]).astype(jnp.bfloat16)
        a3_s[...] = a3
        a3t_s[...] = a3.T
        acc_s[...] = x2 + vec_ref[12:13]
        da_s[...] = jnp.zeros_like(da_s)
    part = rows // chunks
    for chunk in range(chunks):
        span = slice(chunk * part, (chunk + 1) * part)
        hidden = contract(a3_s[span], fi_ref[...], (1, 0)) + fb_ref[...]
        cdf = 0.5 + 0.5 * lax.erf(hidden * math.sqrt(0.5))
        slope = cdf + hidden * jnp.exp(hidden * hidden * -0.5) * (1.0 / math.sqrt(2.0 * math.pi))
        active = (hidden * cdf).astype(jnp.bfloat16)
        g_s[span] = active
        dh = (contract(dz_ref[span], fo_ref[...], (1, 1)) * slope).astype(jnp.bfloat16)
        dh_s[span] = dh
        acc_s[span] += contract(active, fo_ref[...], (1, 0))
        da_s[span] += contract(dh, fi_ref[...], (1, 1))
    gfo_ref[...] = contract(g_s[...], dz_ref[...], (0, 0)).astype(gfo_ref.dtype)
    gfi_ref[...] = contract(a3t_s[...], dh_s[...], (1, 0)).astype(gfi_ref.dtype)
    gfb_ref[...] = column_sum(dh_s[...].astype(jnp.float32))
    @pl.when(step == pl.num_programs(0) - 1)
    def _():
        out_ref[...] = acc_s[...].astype(out_ref.dtype)
        normed, spread = norm_parts(x2_s[...])
        grad = da_s[...]
        dz = dz_ref[...].astype(jnp.float32)
        dx2 = dz + norm_back(grad, normed, spread, vec_ref[10:11])
        dx2_ref[...] = dx2
        dys = dx2.astype(jnp.bfloat16)
        dys_ref[...] = dys
        dos_ref[...] = contract(dys, so_ref[...], (1, 1)).astype(dos_ref.dtype)
        gso_ref[...] = contract(mixture_ref[...], dys, (0, 0)).astype(gso_ref.dtype)
        gvec_ref[0:1] = column_sum(grad * normed)
        gvec_ref[1:2] = column_sum(grad)
        gvec_ref[2:3] = column_sum(dz)
        gvec_ref[3:4] = column_sum(dys.astype(jnp.float32))
        gvec_ref[4:8] = jnp.zeros((4, gvec_ref.shape[1]), jnp.float32)

def feed_block(x1, mixture, dz, space_packed, fi, fo, fb, vec, tile, chunks):
    rows, features = x1.shape
    hidden = fi.shape[1]
    whole = pl.BlockSpec((rows, features), lambda j: (0, 0))
    square = pl.BlockSpec((features, features), lambda j: (0, 0))
    fi_spec = pl.BlockSpec((features, tile), lambda j: (0, j))
    fo_spec = pl.BlockSpec((tile, features), lambda j: (j, 0))
    fb_spec = pl.BlockSpec((1, tile), lambda j: (0, j))
    vec_spec = pl.BlockSpec(vec.shape, lambda j: (0, 0))
    sum_spec = pl.BlockSpec((8, features), lambda j: (0, 0))
    low, full = jnp.bfloat16, jnp.float32
    shape = jax.ShapeDtypeStruct
    return pl.pallas_call(
        functools.partial(feed_kernel, chunks),
        grid=(hidden // tile,),
        in_specs=[whole, whole, whole, pl.BlockSpec((features, features), lambda j: (0, space_packed.shape[1] // features - 1)), fi_spec, fo_spec, fb_spec, vec_spec],
        out_specs=[whole, whole, whole, whole, fi_spec, fo_spec, fb_spec, square, sum_spec],
        out_shape=[shape((rows, features), low), shape((rows, features), full), shape((rows, features), low), shape((rows, features), low),
                   shape(fi.shape, low), shape(fo.shape, low), shape((1, hidden), full), shape((features, features), low), shape((8, features), full)],
        scratch_shapes=[pltpu.VMEM((rows, features), full), pltpu.VMEM((rows, features), low), pltpu.VMEM((features, rows), low),
                        pltpu.VMEM((rows, features), full), pltpu.VMEM((rows, features), full), pltpu.VMEM((rows, tile), low), pltpu.VMEM((rows, tile), low)],
        compiler_params=pltpu.CompilerParams(vmem_limit_bytes=56 << 20),
    )(x1, mixture, dz, space_packed, fi, fo, fb, vec)

def middle_kernel(token_ref, mixture_ref, to_ref, sp_ref, vec_ref, x1_ref, a2_ref, qkv_ref):
    rows, features = token_ref.shape
    number = lax.broadcasted_iota(jnp.int32, (rows, 1), 0)
    branch = contract(mixture_ref[...], to_ref[...], (1, 0)) + vec_ref[4:5]
    x1 = token_ref[...].astype(jnp.float32) + jnp.where(number < PATCHES, branch, 0.0)
    x1_ref[...] = x1
    normed, _ = norm_parts(x1)
    a2 = (normed * vec_ref[5:6] + vec_ref[6:7]).astype(jnp.bfloat16)
    a2_ref[...] = a2
    for third in range(3):
        span = slice(third * features, (third + 1) * features)
        joined = contract(a2, sp_ref[:, span], (1, 0))
        if third != 1:
            joined = joined + vec_ref[7 + third // 2 : 8 + third // 2]
        qkv_ref[:, span] = joined.astype(jnp.bfloat16)


def middle_forward(tokens, mixture, time_packed, space_packed, vec):
    rows, features = tokens.shape
    whole = pl.BlockSpec((rows, features), lambda i: (0, 0))
    shape = jax.ShapeDtypeStruct
    return pl.pallas_call(
        middle_kernel,
        grid=(1,),
        in_specs=[
            whole,
            whole,
            pl.BlockSpec((features, features), lambda i: (0, 3)),
            pl.BlockSpec((features, 3 * features), lambda i: (0, 0)),
            pl.BlockSpec(vec.shape, lambda i: (0, 0)),
        ],
        out_specs=[whole, whole, pl.BlockSpec((rows, 3 * features), lambda i: (0, 0))],
        out_shape=[
            shape((rows, features), jnp.float32),
            shape((rows, features), jnp.bfloat16),
            shape((rows, 3 * features), jnp.bfloat16),
        ],
        compiler_params=pltpu.CompilerParams(vmem_limit_bytes=56 << 20),
    )(tokens, mixture, time_packed, space_packed, vec)


def middle_back_kernel(dq_ref, dk_ref, dv_ref, x1_ref, dx2_ref, to_ref, sp_ref, vec_ref, dx1_ref, dyt_ref, dot_ref, sums_ref):
    rows, features = x1_ref.shape
    grad = 0.0
    for third, piece in enumerate((dq_ref, dk_ref, dv_ref)):
        span = slice(third * features, (third + 1) * features)
        grad = grad + contract(piece[...], sp_ref[:, span], (1, 1))
    normed, spread = norm_parts(x1_ref[...])
    dx1 = dx2_ref[...] + norm_back(grad, normed, spread, vec_ref[5:6])
    dx1_ref[...] = dx1
    number = lax.broadcasted_iota(jnp.int32, (rows, 1), 0)
    dyt = jnp.where(number < PATCHES, dx1, 0.0).astype(jnp.bfloat16)
    dyt_ref[...] = dyt
    dot_ref[...] = contract(dyt, to_ref[...], (1, 1)).astype(dot_ref.dtype)
    sums_ref[0:1] = column_sum(grad * normed)
    sums_ref[1:2] = column_sum(grad)
    sums_ref[2:3] = column_sum(dq_ref[...].astype(jnp.float32))
    sums_ref[3:4] = column_sum(dv_ref[...].astype(jnp.float32))
    sums_ref[4:5] = column_sum(dyt.astype(jnp.float32))
    sums_ref[5:8] = jnp.zeros((3, features), jnp.float32)


def middle_backward(dq, dk, dv, x1, dx2, time_packed, space_packed, vec):
    rows, features = x1.shape
    whole = pl.BlockSpec((rows, features), lambda i: (0, 0))
    shape = jax.ShapeDtypeStruct
    return pl.pallas_call(
        middle_back_kernel,
        grid=(1,),
        in_specs=[whole] * 5
        + [
            pl.BlockSpec((features, features), lambda i: (0, 3)),
            pl.BlockSpec((features, 3 * features), lambda i: (0, 0)),
            pl.BlockSpec(vec.shape, lambda i: (0, 0)),
        ],
        out_specs=[whole, whole, whole, pl.BlockSpec((8, features), lambda i: (0, 0))],
        out_shape=[
            shape((rows, features), jnp.float32),
            shape((rows, features), jnp.bfloat16),
            shape((rows, features), jnp.bfloat16),
            shape((8, features), jnp.float32),
        ],
        compiler_params=pltpu.CompilerParams(vmem_limit_bytes=56 << 20),
    )(dq, dk, dv, x1, dx2, time_packed, space_packed, vec)


def middle_weights_kernel(a2_ref, dq_ref, dk_ref, dv_ref, mixture_ref, dyt_ref, gsp_ref, gto_ref):
    features = a2_ref.shape[1]
    turned = a2_ref[...].T
    for third, piece in enumerate((dq_ref, dk_ref, dv_ref)):
        span = slice(third * features, (third + 1) * features)
        gsp_ref[:, span] = contract(turned, piece[...], (1, 0)).astype(gsp_ref.dtype)
    gto_ref[...] = contract(mixture_ref[...], dyt_ref[...], (0, 0)).astype(gto_ref.dtype)


def middle_weights(a2, dq, dk, dv, mixture, dyt):
    features = a2.shape[1]
    vmem = pl.BlockSpec(memory_space=pltpu.VMEM)
    shape = jax.ShapeDtypeStruct
    return pl.pallas_call(
        middle_weights_kernel,
        in_specs=[vmem] * 6,
        out_specs=[vmem] * 2,
        out_shape=[
            shape((features, 3 * features), jnp.bfloat16),
            shape((features, features), jnp.bfloat16),
        ],
        compiler_params=pltpu.CompilerParams(vmem_limit_bytes=56 << 20),
    )(a2, dq, dk, dv, mixture, dyt)

CHUNK=16
def head_map(features, lanes=128):
    head = jnp.arange(features, dtype=jnp.int32) // (features // HEADS)
    return (head[:, None] == jnp.arange(lanes, dtype=jnp.int32)[None]).astype(jnp.bfloat16)

def pair_sums(left, right, gather_ref, pair_s):
    count = len(left)
    for f in range(count):
        for g in range(count):
            at = (f * count + g) * CHUNK
            pair_s[at:at + CHUNK] = (left[f] * right[g]).astype(jnp.bfloat16)
    return contract(pair_s[...], gather_ref[...], (1, 0))

def time_forward_kernel(count, scale, *refs):
    slots, (tp_ref, vec_ref, gather_ref, spread_ref) = refs[:count], refs[count:count + 4]
    outs, (qkv_ref, prob_ref, a1_ref) = refs[count + 4:2 * count + 4], refs[2 * count + 4:2 * count + 7]
    pair_s, weight_s = refs[2 * count + 7:]
    part, features = slots[0].shape
    for s in range(count):
        normed, _ = norm_parts(slots[s][...].astype(jnp.float32))
        a1_ref[s * part:(s + 1) * part] = (normed * vec_ref[0:1] + vec_ref[1:2]).astype(jnp.bfloat16)
    for third in range(3):
        span = slice(third * features, (third + 1) * features)
        joined = contract(a1_ref[...], tp_ref[:, span], (1, 0))
        if third != 1:
            joined = joined + vec_ref[2 + third // 2:3 + third // 2]
        qkv_ref[:, span] = joined.astype(jnp.bfloat16)

    def chunk_step(index, carry):
        def rows_of(s, third):
            start = pl.multiple_of(s * part + index * CHUNK, CHUNK)
            return qkv_ref[pl.ds(start, CHUNK), third * features:(third + 1) * features].astype(jnp.float32)
        queries, keys, values = ([rows_of(s, third) for s in range(count)] for third in range(3))
        scores = pair_sums(queries, keys, gather_ref, pair_s) * (scale * LOG2E)
        place = pl.ds(pl.multiple_of(index * CHUNK, CHUNK), CHUNK)
        for f in range(count):
            row = [scores[(f * count + g) * CHUNK:(f * count + g + 1) * CHUNK] for g in range(count)]
            top = functools.reduce(jnp.maximum, row)
            raised = [jnp.exp2(item - top) for item in row]
            mass = functools.reduce(jnp.add, raised)
            for g in range(count):
                weight = raised[g] / mass
                prob_ref[f * count + g, place] = weight
                at = (f * count + g) * CHUNK
                weight_s[at:at + CHUNK] = weight.astype(jnp.bfloat16)
        wide = contract(weight_s[...], spread_ref[...], (1, 0))
        for f in range(count):
            total = 0.0
            for g in range(count):
                at = (f * count + g) * CHUNK
                total = total + wide[at:at + CHUNK] * values[g]
            outs[f][place] = total.astype(jnp.bfloat16)
        return carry
    lax.fori_loop(0, part // CHUNK, chunk_step, 0)

def time_forward(slots, time_packed, vec):
    count = len(slots)
    part, features = slots[0].shape
    gather = head_map(features)
    low, full = jnp.bfloat16, jnp.float32
    shape = jax.ShapeDtypeStruct
    vmem = pl.BlockSpec(memory_space=pltpu.VMEM)
    results = pl.pallas_call(
        functools.partial(time_forward_kernel, count, (features // HEADS) ** -0.5),
        grid=(1,),
        in_specs=[pl.BlockSpec((part, features), lambda i: (0, 0))] * count + [pl.BlockSpec((features, 3 * features), lambda i: (0, 0)), vmem, vmem, vmem],
        out_specs=[vmem] * (count + 3),
        out_shape=[shape((part, features), low)] * count + [shape((count * part, 3 * features), low), shape((count * count, part, 128), full), shape((count * part, features), low)],
        scratch_shapes=[pltpu.VMEM((count * count * CHUNK, features), low), pltpu.VMEM((count * count * CHUNK, 128), low)],
        compiler_params=pltpu.CompilerParams(vmem_limit_bytes=56 << 20),
    )(*slots, time_packed, vec, gather, gather.T)
    return results[:count], results[count], results[count + 1], results[count + 2]

def time_backward_kernel(count, scale, *refs):
    grads, (qkv_ref, prob_ref, a1_ref, gather_ref, spread_ref) = refs[:count], refs[count:count + 5]
    dqkv_ref, gtp_ref, sums_ref, pair_s, weight_s = refs[count + 5:]
    part, features = grads[0].shape
    def chunk_step(index, carry):
        place = pl.ds(pl.multiple_of(index * CHUNK, CHUNK), CHUNK)
        def rows_of(s, third):
            start = pl.multiple_of(s * part + index * CHUNK, CHUNK)
            return qkv_ref[pl.ds(start, CHUNK), third * features:(third + 1) * features].astype(jnp.float32)
        queries, keys, values = ([rows_of(s, third) for s in range(count)] for third in range(3))
        outer = [grads[s][place].astype(jnp.float32) for s in range(count)]
        slopes = pair_sums(outer, values, gather_ref, pair_s)
        size = count * count * CHUNK
        for f in range(count):
            row = [slopes[(f * count + g) * CHUNK:(f * count + g + 1) * CHUNK] for g in range(count)]
            weights = [prob_ref[f * count + g, place] for g in range(count)]
            delta = functools.reduce(jnp.add, [w * s for w, s in zip(weights, row)])
            for g in range(count):
                at = (f * count + g) * CHUNK
                weight_s[at:at + CHUNK] = weights[g].astype(jnp.bfloat16)
                weight_s[size + at:size + at + CHUNK] = (weights[g] * (row[g] - delta)).astype(jnp.bfloat16)
        wide = contract(weight_s[...], spread_ref[...], (1, 0))
        for s in range(count):
            dq, dk, dv = 0.0, 0.0, 0.0
            for t in range(count):
                forth, back = (s * count + t) * CHUNK, (t * count + s) * CHUNK
                dq = dq + wide[size + forth:size + forth + CHUNK] * keys[t]
                dk = dk + wide[size + back:size + back + CHUNK] * queries[t]
                dv = dv + wide[back:back + CHUNK] * outer[t]
            start = pl.ds(pl.multiple_of(s * part + index * CHUNK, CHUNK), CHUNK)
            for third, value in enumerate((dq * scale, dk * scale, dv)):
                dqkv_ref[start, third * features:(third + 1) * features] = value.astype(jnp.bfloat16)
        return carry
    lax.fori_loop(0, part // CHUNK, chunk_step, 0)
    a1t = a1_ref[...].T
    for third in range(3):
        span = slice(third * features, (third + 1) * features)
        gtp_ref[:, span] = contract(a1t, dqkv_ref[:, span], (1, 0)).astype(gtp_ref.dtype)
    sums_ref[0:1] = column_sum(dqkv_ref[:, :features].astype(jnp.float32))
    sums_ref[1:2] = column_sum(dqkv_ref[:, 2 * features:].astype(jnp.float32))
    sums_ref[2:8] = jnp.zeros((6, features), jnp.float32)

def time_backward(grads, qkv, prob, a1):
    count = len(grads)
    part, features = grads[0].shape
    gather = head_map(features)
    shape = jax.ShapeDtypeStruct
    vmem = pl.BlockSpec(memory_space=pltpu.VMEM)
    return pl.pallas_call(
        functools.partial(time_backward_kernel, count, (features // HEADS) ** -0.5),
        in_specs=[vmem] * (count + 5),
        out_specs=[vmem] * 3,
        out_shape=[shape(qkv.shape, jnp.bfloat16), shape((features, 3 * features), jnp.bfloat16), shape((8, features), jnp.float32)],
        scratch_shapes=[pltpu.VMEM((count * count * CHUNK, features), jnp.bfloat16), pltpu.VMEM((2 * count * count * CHUNK, 128), jnp.bfloat16)],
        compiler_params=pltpu.CompilerParams(vmem_limit_bytes=56 << 20),
    )(*grads, qkv, prob, a1, gather, gather.T)

def time_input_kernel(count, *refs):
    slots, (dqkv_ref, tp_ref, vec_ref) = refs[:count], refs[count:count + 3]
    outs, sums_ref = refs[count + 3:2 * count + 3], refs[2 * count + 3]
    part, features = slots[0].shape
    grad = contract(dqkv_ref[...], tp_ref[...], (1, 1))
    gain, shift = 0.0, 0.0
    for s in range(count):
        piece = grad[s * part:(s + 1) * part]
        normed, spread = norm_parts(slots[s][...].astype(jnp.float32))
        outs[s][...] = norm_back(piece, normed, spread, vec_ref[0:1]).astype(jnp.bfloat16)
        gain = gain + column_sum(piece * normed)
        shift = shift + column_sum(piece)
    sums_ref[0:1] = gain
    sums_ref[1:2] = shift
    sums_ref[2:8] = jnp.zeros((6, features), jnp.float32)

def time_input(slots, dqkv, time_packed, vec):
    count = len(slots)
    part, features = slots[0].shape
    shape = jax.ShapeDtypeStruct
    vmem = pl.BlockSpec(memory_space=pltpu.VMEM)
    results = pl.pallas_call(
        functools.partial(time_input_kernel, count),
        grid=(1,),
        in_specs=[pl.BlockSpec((part, features), lambda i: (0, 0))] * count + [vmem, pl.BlockSpec((features, 3 * features), lambda i: (0, 0)), vmem],
        out_specs=[vmem] * (count + 1),
        out_shape=[shape((part, features), jnp.bfloat16)] * count + [shape((8, features), jnp.float32)],
        compiler_params=pltpu.CompilerParams(vmem_limit_bytes=56 << 20),
    )(*slots, dqkv, time_packed, vec)
    return results[:count], results[count]

def body(
    tokens,
    size_tag,
    cotangent,
    time_project,
    time_output,
    time_vector,
    space_project,
    space_output,
    space_vector,
    feed_inner,
    feed_bias,
    feed_outer,
    feed_vector,
):
    frame_count = lax.axis_size("frame")
    batch_count = lax.axis_size("batch")
    frame_index = lax.axis_index("frame")
    batch_index = lax.axis_index("batch")
    features = tokens.shape[2]
    row_count = tokens.shape[1]
    part = round_up(-(-PATCHES // frame_count), 16)
    padded = part * frame_count
    token_rows = jnp.pad(tokens[0], ((0, padded - row_count), (0, 0)))
    grad_result = jnp.pad(cotangent[0], ((0, padded - row_count), (0, 0)))

    vectors = jnp.concatenate(
        [time_vector, space_vector, feed_vector, feed_bias.reshape(-1, time_vector.shape[1])], axis=0
    )
    vectors = lax.all_gather(vectors, "batch", axis=0)
    vec = vectors[:, :13].transpose(1, 0, 2).reshape(13, features).astype(jnp.float32)
    vec = jnp.pad(vec, ((0, 3), (0, 0)))
    feed_bias_row = vectors[:, 13:].reshape(1, -1).astype(jnp.float32)
    time_packed = lax.all_gather(
        jnp.concatenate([time_project, time_output], axis=1), "batch", axis=0, tiled=True
    )
    space_packed = lax.all_gather(
        jnp.concatenate([space_project, space_output], axis=1), "batch", axis=0, tiled=True
    )
    feed_inner_full = lax.all_gather(feed_inner, "batch", axis=0, tiled=True)
    feed_outer_full = lax.all_gather(feed_outer, "batch", axis=0, tiled=True)

    slots = rows_to_frames(token_rows, frame_count, frame_index)
    mixture_slots, qkv_time, prob_time, first_input = time_forward(slots, time_packed, vec)
    mixture_time = frames_to_rows(mixture_slots, frame_count, frame_index)
    after_time, second_input, qkv_space = middle_forward(
        token_rows, mixture_time, time_packed, space_packed, vec
    )
    clip = jnp.concatenate(
        [
            jnp.arange(PATCHES, dtype=jnp.int32) // size_tag[0],
            jnp.arange(UNITS, dtype=jnp.int32),
            jnp.full((padded - PATCHES - UNITS,), -1, jnp.int32),
        ]
    )
    mixture_space, total_space = space_forward(qkv_space, clip, features)
    (
        block_out,
        grad_second,
        grad_branch,
        grad_mixture,
        grad_feed_inner,
        grad_feed_outer,
        grad_feed_bias,
        grad_space_output,
        feed_sums,
    ) = feed_block(
        after_time,
        mixture_space,
        grad_result,
        space_packed,
        feed_inner_full,
        feed_outer_full,
        feed_bias_row,
        vec,
        tile=features,
        chunks=2,
    )
    grad_query, grad_keys, grad_values = space_backward(
        qkv_space, mixture_space, total_space, grad_mixture, clip, features
    )
    grad_first, grad_patch, grad_mixture_time, space_sums = middle_backward(
        grad_query, grad_keys, grad_values, after_time, grad_second, time_packed, space_packed, vec
    )
    grad_slots = rows_to_frames(grad_mixture_time, frame_count, frame_index)
    grad_space_project, grad_time_output = middle_weights(
        second_input, grad_query, grad_keys, grad_values, mixture_time, grad_patch
    )
    grad_joined_time, grad_time_project, time_sums = time_backward(
        grad_slots, qkv_time, prob_time, first_input
    )
    input_slots, input_sums = time_input(slots, grad_joined_time, time_packed, vec)
    grad_tokens = grad_first + frames_to_rows(input_slots, frame_count, frame_index).astype(
        jnp.float32
    )

    sizes = (batch_count, frame_count)
    indices = (batch_index, frame_index)
    vector_grads = jnp.concatenate(
        [
            input_sums[0:2],
            time_sums[0:2],
            space_sums[4:5],
            space_sums[0:4],
            feed_sums[3:4],
            feed_sums[0:3],
            grad_feed_bias.reshape(-1, features),
        ]
    )
    vector_grads = lax.psum(vector_grads, ("batch", "frame"))
    grad_feed_inner, grad_feed_outer = lax.psum(
        (grad_feed_inner, grad_feed_outer), ("batch", "frame")
    )
    (space_sum,) = sum_everywhere(
        [jnp.concatenate([grad_space_project, grad_space_output], axis=1)], sizes, indices
    )
    (time_sum,) = sum_everywhere(
        [jnp.concatenate([grad_time_project, grad_time_output], axis=1)], sizes, indices
    )
    space_sum = space_sum.astype(jnp.float32)
    time_sum = time_sum.astype(jnp.float32)
    return (
        block_out[None, :row_count],
        grad_tokens[None, :row_count],
        time_sum[:, : 3 * features],
        time_sum[:, 3 * features :],
        vector_grads[0:5],
        space_sum[:, : 3 * features],
        space_sum[:, 3 * features :],
        vector_grads[5:10],
        grad_feed_inner.astype(jnp.float32),
        vector_grads[13:].reshape(-1),
        grad_feed_outer.astype(jnp.float32),
        vector_grads[10:13],
    )


def solution(mesh):
    placed = (
        P("frame", "batch", None),
        P("batch"),
        P("frame", "batch", None),
        P("batch", None),
        P("batch", None),
        P(None, "batch"),
        P("batch", None),
        P("batch", None),
        P(None, "batch"),
        P("batch", None),
        P("batch"),
        P("batch", None),
        P(None, "batch"),
    )
    return jax.shard_map(
        body,
        mesh=mesh,
        in_specs=placed,
        out_specs=(
            P("frame", "batch", None),
            P("frame", "batch", None),
            P(),
            P(),
            P(),
            P(),
            P(),
            P(),
            P(),
            P(),
            P(),
            P(),
        ),
        check_vma=False,
    )
```

time: 833 us -> 704 us (0.85)
  matrix products: 283 us -> 0 us
  Pallas kernels: 0 us -> 168 us
  waiting for transfers between devices: 182 us -> 301 us
  local copies, waits for them, and re-layouts: 129 us -> 55.1 us
  other arithmetic: 118 us -> 52.6 us
  blocking collectives: 49.5 us -> 63.8 us
    dot_general x30 -> x0, matrix products: 283 us -> none  [the longest x6 55.3 us: forward_dot(): return jnp.dot(operand, partner, preferred_element_type=jnp.float32)]
    pallas_call x0 -> x9, Pallas kernels: none -> 168 us  [the longest x1 42.5 us: feed_block(): pl.pallas_call(functools.partial(feed_kernel, chunks), grid=(hidden // ti...]
    psum x1, waiting for transfers between devices: 0.01 us -> 68 us  [body(): lax.psum((grad_feed_inner, grad_feed_outer), ('batch', 'frame'))]
    another operation x26 -> x2, local copies, waits for them, and re-layouts: 46.9 us -> 1.21 us  [the longest x9 19.9 us: body(): mixture_time = frames_to_rows(list(mixture), frame_count, frame_index)]
    all_gather x1, waiting for transfers between devices: 0.01 us -> 40.7 us  [body(): feed_outer_full = lax.all_gather(feed_outer, 'batch', axis=0, tiled=True)]
    convert_element_type x8 -> x3, other arithmetic: 37 us -> 1.59 us  [the longest x2 1.58 us: head_map(): (head[:, None] == jnp.arange(lanes, dtype=jnp.int32)[None]).astype(jnp.bf...]
    reduce_sum x11 -> x0, other arithmetic: 32.8 us -> none  [the longest x1 16.1 us: body(): space_total = jax.nn.logsumexp(scores, axis=-1)]
    convert_element_type x10 -> x4, local copies, waits for them, and re-layouts: 24.3 us -> 0.81 us  [the longest x1 0.69 us: body(): feed_bias_row = vectors[:, 13:].reshape(1, -1).astype(jnp.float32)]
  transfers between devices with their start and end apart: 37 -> 37, of which waited for: 16 -> 21; matrix products, arithmetic and copies ran while one was open for 43% -> 11% of each run, Pallas kernels for 0% -> 12%
where the time goes in v2:
time: 704 us; the launch traced here: 698 us
  waiting for transfers between devices  301 us (43%)
  Pallas kernels  168 us (24%)
  blocking collectives  63.8 us (9%)
  local copies, waits for them, and re-layouts  55.1 us (8%)
  other arithmetic  52.6 us (7%)
  starting transfers between devices  41.7 us (6%)
  between operations  15.5 us (2%)
    ppermute x20, waiting for transfers between devices, swap_bit(): return lax.ppermute(block, axis, pairs)  144 us
    psum x1, waiting for transfers between devices, body(): lax.psum((grad_feed_inner, grad_feed_outer), ('batch', 'frame'))  68 us
    psum x1, blocking collectives, body(): vector_grads = lax.psum(vector_grads, ('batch', 'frame'))  54.6 us
    pallas_call x1, Pallas kernels, feed_block(): pl.pallas_call(functools.partial(feed_kernel, chunks), grid=(hidden // ti...  42.5 us
    all_gather x1, waiting for transfers between devices, body(): feed_outer_full = lax.all_gather(feed_outer, 'batch', axis=0, tiled=True)  40.7 us
    ppermute x12, waiting for transfers between devices, shift_frames(): return lax.ppermute(block, 'frame', pairs)  34.7 us
    pallas_call x1, Pallas kernels, space_backward(): pl.pallas_call(functools.partial(space_backward_kernel, scale, tile), gri...  29.9 us
    ppermute x20, starting transfers between devices, swap_bit(): return lax.ppermute(block, axis, pairs)  21.7 us
  transfers between devices with their start and end apart: 37, of which 21 were waited for; matrix products, arithmetic and copies ran while one was open for 11% of the time, Pallas kernels for 12%

profile of v2, /device:TPU:0, one launch (start us, length us, event | category | flops | bytes accessed | tf_op | source)
XLA Modules:
  0.0 697.8 jit_solution(5930637630239967752)
XLA Ops:
  21.2 9.2 %all-gather.1 = bf16[8,17,96]{2,1,0:T(8,128)(2,1)S(1)} all-gather(bf16[1,17,96]{2,1,0:T(8,128)(2,1)S(1)} %maximum_bitcast_fusion), channel_id=2, replica_groups=mesh['batch'=8,'frame'=4] {'batch'}, dimensions={0}, use_global_device_ids=true | all-gather | bytes 29376 | tf_op jit(solution)/shard_map/all_gather | solution.py:595
  40.5 11.7 %all-gather.7.cloned.1.call-done.refs_4_.to_ref.refs_5_ = bf16[768,3072]{1,0:T(8,128)(2,1)} async-done(((bf16[96,3072]{1,0:T(8,128)(2,1)}), bf16[768,3072]{1,0:T(8,128)(2,1)}) %all-gather.7.cloned.1.call-update) | async-done | bytes 4718608 | tf_op jit(solution)/shard_map/all_gather | solution.py:599
  52.3 16.7 %shard_map.220 = (bf16[208,768]{1,0:T(8,128)(2,1)}, bf16[208,768]{1,0:T(8,128)(2,1)}, bf16[208,768]{1,0:T(8,128)(2,1)}, bf16[208,768]{1,0:T(8,128)(2,1)}, bf16[8...) custom-call(bf16[208,768]{1,0:T(8,128)(2,1)} %get-tuple-element.137.refs_0_, ...), custom_call_target="tpu_custom_call" | custom-call | tf_op jit(solution)/shard_map/pallas_call | solution.py:467
  81.5 18.9 %collective-permute-done.4 = bf16[208,768]{1,0:T(8,128)(2,1)} collective-permute-done((bf16[208,768]{1,0:T(8,128)(2,1)}, bf16[208,768]{1,0:T(8,128)(2,1)}, u32[]{:S(2)}, u32[]{:S(2)}) %collective-permute-start.4) | collective-permute-done | bytes 319520 | tf_op jit(solution)/shard_map/ppermute | solution.py:24
  102.5 10.5 %shard_map.221 = (f32[832,768]{1,0:T(8,128)}, bf16[832,768]{1,0:T(8,128)(2,1)}, bf16[832,2304]{1,0:T(8,128)(2,1)}) custom-call(bf16[832,768]{1,0:T(8,128)(2,1)} %pad.18.token_ref, bf16[832,768]{1,0:T(8,128)(2,1)} %copy-done.9, bf16[768,3072]{1,0:T(8,128)(2,1)} %all-gather.7.cloned.1.call-done.refs_4_.to_ref.refs_5_, ...), custom_call_target="tpu_custom_call" | custom-call | tf_op jit(solution)/shard_map/pallas_call | solution.py:316
  113.0 18.8 %shard_map.222 = (bf16[832,768]{1,0:T(8,128)(2,1)S(1)}, f32[832,768]{1,0:T(8,128)S(1)}) custom-call(s32[832,1]{1,0:T(8,128)S(1)} %broadcast_in_dim.26.column_ref, s32[1,896]{1,0:T(1,128)S(1)} %broadcast_in_dim.23.row_ref, bf16[832,2304]{1,0:T(8,128)(2,1)} %get-tuple-element.54.q_ref.k_ref.v_ref, bf16[832,2304]{1,0:T(8,128)(2,1)} %get-tuple-element.54.q_ref.k_ref.v_ref, ...), custom_call_target="tpu_custom_call" | custom-call | tf_op jit(solution)/shard_map/pallas_call | solution.py:143
  134.5 40.7 %all-gather.13.cloned.1.call-done.fo_ref = bf16[3072,768]{1,0:T(8,128)(2,1)} async-done(((bf16[384,768]{1,0:T(8,128)(2,1)}), bf16[3072,768]{1,0:T(8,128)(2,1)}) %all-gather.13.cloned.1.call-update) | async-done | bytes 4718608 | tf_op jit(solution)/shard_map/all_gather | solution.py:606
  175.2 42.5 %shard_map.223 = (bf16[832,768]{1,0:T(8,128)(2,1)}, f32[832,768]{1,0:T(8,128)}, bf16[832,768]{1,0:T(8,128)(2,1)}, bf16[832,768]{1,0:T(8,128)(2,1)}, bf16[768,307...) custom-call(f32[832,768]{1,0:T(8,128)} %get-tuple-element.53.x1_ref,, ...), custom_call_target="tpu_custom_call" | custom-call | tf_op jit(solution)/shard_map/pallas_call | solution.py:283
  217.7 29.9 %shard_map.224 = (bf16[832,768]{1,0:T(8,128)(2,1)S(1)}, bf16[832,768]{1,0:T(8,128)(2,1)S(1)}, bf16[832,768]{1,0:T(8,128)(2,1)S(1)}) custom-call(s32[832,1]{1,0:T(8,128)S(1)} %broadcast_in_dim.26.column_ref, s32[1,896]{1,0:T(1,128)S(1)} %broadcast_in_dim.23.row_ref, bf16[832,2304]{1,0:T(8,128)(2,1)} %get-tuple-element.54.q_ref.k_ref.v_ref, ...), custom_call_target="tpu_custom_call" | custom-call | tf_op jit(solution)/shard_map/pallas_call | solution.py:202
  250.8 13.8 %shard_map.225 = (f32[832,768]{1,0:T(8,128)}, bf16[832,768]{1,0:T(8,128)(2,1)}, bf16[832,768]{1,0:T(8,128)(2,1)}, f32[8,768]{1,0:T(8,128)}) custom-call(bf16[832,768]{1,0:T(8,128)(2,1)} %copy-done.2, bf16[832,768]{1,0:T(8,128)(2,1)} %copy-done.3, bf16[832,768]{1,0:T(8,128)(2,1)} %copy-done.4, f32[832,768]{1,0:T(8,128)} %get-tuple-element.53.x1_ref, ...), custom_call_target="tpu_custom_call" | custom-call | tf_op jit(solution)/shard_map/pallas_call | solution.py:361
  272.0 9.7 %shard_map.228 = (bf16[768,2304]{1,0:T(8,128)(2,1)}, bf16[768,768]{1,0:T(8,128)(2,1)}) custom-call(bf16[832,768]{1,0:T(8,128)(2,1)} %get-tuple-element.74.a2_ref, bf16[832,768]{1,0:T(8,128)(2,1)} %copy-done.2, bf16[832,768]{1,0:T(8,128)(2,1)} %copy-done.3, bf16[832,768]{1,0:T(8,128)(2,1)} %copy-done.4, bf16[832,768]{1,0:T(8,128)(2,1)} %copy-done.9, ...), custom_call_target="tpu_custom_call" | custom-call | tf_op jit(solution)/shard_map/pallas_call | solution.py:394
  292.8 17.5 %shard_map.226 = (bf16[832,2304]{1,0:T(8,128)(2,1)}, bf16[768,2304]{1,0:T(8,128)(2,1)}, f32[8,768]{1,0:T(8,128)}) custom-call(bf16[208,768]{1,0:T(8,128)(2,1)} %get-tuple-element.135.refs_0_, bf16[208,768]{1,0:T(8,128)(2,1)} %copy-done.27, bf16[208,768]{1,0:T(8,128)(2,1)} %copy-done.28, bf16[208,768]{1,0:T(8,128)(2,1)} %copy-done.29, ...), custom_call_target="tpu_custom_call" | custom-call | tf_op jit(solution)/shard_map/pallas_call | solution.py:526
  327.4 21.1 %collective-permute-done.23 = bf16[192,3072]{1,0:T(8,128)(2,1)} collective-permute-done((bf16[192,3072]{1,0:T(8,128)(2,1)S(1)}, bf16[192,3072]{1,0:T(8,128)(2,1)}, u32[]{:S(2)}, u32[]{:S(2)}) %collective-permute-start.23) | collective-permute-done | bytes 1179680 | tf_op jit(solution)/shard_map/ppermute | solution.py:49
  351.6 21.8 %collective-permute-done.13 = bf16[192,3072]{1,0:T(8,128)(2,1)} collective-permute-done((bf16[192,3072]{1,0:T(8,128)(2,1)}, bf16[192,3072]{1,0:T(8,128)(2,1)}, u32[]{:S(2)}, u32[]{:S(2)}) %collective-permute-start.13) | collective-permute-done | bytes 1179680 | tf_op jit(solution)/shard_map/ppermute | solution.py:49
  375.3 7.3 %collective-permute-start.25 = (bf16[48,3072]{1,0:T(8,128)(2,1)S(1)}, bf16[48,3072]{1,0:T(8,128)(2,1)S(1)}, u32[]{:S(2)}, u32[]{:S(2)}) collective-permute-start(bf16[48,3072]{1,0:T(8,128)(2,1)S(1)} %constant_dynamic-slice_fusion.1), channel_id=1, source_target_pairs={{0,1},{1,0},{2,3},{3,2},{4,5},{5,4},{6,7},{7,6},{8,9},{9,8},{10,11... | collective-permute-start | bytes 884744 | tf_op jit(solution)/shard_map/ppermute | solution.py:49
  399.6 8.6 %collective-permute-done.15 = bf16[48,3072]{1,0:T(8,128)(2,1)S(1)} collective-permute-done((bf16[48,3072]{1,0:T(8,128)(2,1)S(1)}, bf16[48,3072]{1,0:T(8,128)(2,1)S(1)}, u32[]{:S(2)}, u32[]{:S(2)}) %collective-permute-start.15) | collective-permute-done | bytes 294944 | tf_op jit(solution)/shard_map/ppermute | solution.py:49
  408.7 8.4 %collective-permute-done.16 = bf16[24,3072]{1,0:T(8,128)(2,1)S(1)} collective-permute-done((bf16[24,3072]{1,0:T(8,128)(2,1)S(1)}, bf16[24,3072]{1,0:T(8,128)(2,1)S(1)}, u32[]{:S(2)}, u32[]{:S(2)}) %collective-permute-start.16) | collective-permute-done | bytes 147488 | tf_op jit(solution)/shard_map/ppermute | solution.py:49
  436.1 13.4 %collective-permute-done.29 = bf16[96,3072]{1,0:T(8,128)(2,1)S(1)} collective-permute-done((bf16[96,3072]{1,0:T(8,128)(2,1)S(1)}, bf16[96,3072]{1,0:T(8,128)(2,1)S(1)}, u32[]{:S(2)}, u32[]{:S(2)}) %collective-permute-start.29) | collective-permute-done | bytes 589856 | tf_op jit(solution)/shard_map/ppermute | solution.py:49
  451.4 13.2 %collective-permute-done.19 = bf16[96,3072]{1,0:T(8,128)(2,1)S(1)} collective-permute-done((bf16[96,3072]{1,0:T(8,128)(2,1)}, bf16[96,3072]{1,0:T(8,128)(2,1)S(1)}, u32[]{:S(2)}, u32[]{:S(2)}) %collective-permute-start.19) | collective-permute-done | bytes 589856 | tf_op jit(solution)/shard_map/ppermute | solution.py:49
  467.1 30.8 %collective-permute-done.30 = bf16[192,3072]{1,0:T(8,128)(2,1)} collective-permute-done((bf16[192,3072]{1,0:T(8,128)(2,1)S(1)}, bf16[192,3072]{1,0:T(8,128)(2,1)}, u32[]{:S(2)}, u32[]{:S(2)}) %collective-permute-start.30) | collective-permute-done | bytes 1179680 | tf_op jit(solution)/shard_map/ppermute | solution.py:49
  504.0 8.8 %shard_map.227 = (bf16[208,768]{1,0:T(8,128)(2,1)}, bf16[208,768]{1,0:T(8,128)(2,1)}, bf16[208,768]{1,0:T(8,128)(2,1)}, bf16[208,768]{1,0:T(8,128)(2,1)}, f32[8,768]{1,0:T(8,128)}) custom-call(bf16[208,768]{1,0:T(8,128)(2,1)} %get-tuple-element.137.refs_0_, bf16[208,768]{1,0:T(8,128)(2,1)} %copy-done.18, bf16[208,768]{1,0:T(8,128)(2,1)} %copy-done.19, ...), custom_call_target="tpu_custom_call" | custom-call | tf_op jit(solution)/shard_map/pallas_call | solution.py:556
  517.4 54.6 %psum.21 = f32[17,768]{1,0:T(8,128)S(1)} all-reduce(f32[17,768]{1,0:T(8,128)S(1)} %concatenate.61), channel_id=1, replica_groups=mesh['batch'=8,'frame'=4] {'batch','frame'}, use_global_device_ids=true, to_apply=%region_0.1 | all-reduce | flops 13056 | bytes 104448 | tf_op jit(solution)/shard_map/psum | solution.py:675
  592.6 68.0 %all-reduce.7.cloned.1.call-done = (bf16[768,3072]{1,0:T(8,128)(2,1)}, bf16[3072,768]{1,0:T(8,128)(2,1)}) async-done(((bf16[768,3072]{1,0:T(8,128)(2,1)}, bf16[3072,768]{1,0:T(8,128)(2,1)}), (bf16[768,3072]{1,0:T(8,128)(2,1)}, bf16[3072,768]{1,0:T(8,128)(2,1)})) %all-reduce.7.cloned.1.call-update) | async-done | bytes 9437200 | tf_op jit(solution)/shard_map/psum | solution.py:676
  660.6 7.5 %convert_element_type.171 = f32[768,3072]{1,0:T(8,128)} convert(bf16[768,3072]{1,0:T(8,128)(2,1)} %get-tuple-element.122) | non-fusion elementwise | flops 2359296 | bytes 14155776 | tf_op jit(solution)/shard_map/convert_element_type | solution.py:696
  (242 shorter events, 179.1 us)
Async XLA Ops:
  7.2 45.1 %all-gather.7.cloned.1.call-start = ((), (), s32[]{:S(2)}) async-start(), calls=%async_computation | async-start | bytes 5308416 | tf_op jit(solution)/shard_map/all_gather | solution.py:599
  9.3 92.2 %all-gather.9.cloned.1.call-start = ((), (), s32[]{:S(2)}) async-start(), calls=%async_computation.1 | async-start | bytes 5308416 | tf_op jit(solution)/shard_map/all_gather | solution.py:602
  11.3 123.2 %all-gather.11.cloned.1.call-start = ((), (), s32[]{:S(2)}) async-start(), calls=%async_computation.2 | async-start | bytes 5308416 | tf_op jit(solution)/shard_map/all_gather | solution.py:605
  12.1 163.1 %all-gather.13.cloned.1.call-start = ((), (), s32[]{:S(2)}) async-start(), calls=%async_computation.3 | async-start | bytes 5308416 | tf_op jit(solution)/shard_map/all_gather | solution.py:606
  12.7 648.0 %all-reduce.7.cloned.1.call-start = ((), (), s32[]{:S(2)}) async-start(), calls=%async_computation.4 | async-start | bytes 18874368 | tf_op jit(solution)/shard_map/psum | solution.py:676
  14.1 20.4 %collective-permute-start = (bf16[208,768]{1,0:T(8,128)(2,1)S(1)}, bf16[208,768]{1,0:T(8,128)(2,1)S(1)}, u32[]{:S(2)}, u32[]{:S(2)}) collective-permute-start(bf16[208,768]{1,0:T(8,128)(2,1)S(1)} %get-tuple-element.138), channel_id=1, source_target_pairs={{0,1},{1,2},{2,3},{3,0},{4,5},{5,6},{6,7},{7,4},{8,9},{9,10},{10,1... | collective-permute-start | bytes 958472 | tf_op jit(solution)/shard_map/ppermute | solution.py:24
  17.1 23.4 %collective-permute-start.1 = (bf16[208,768]{1,0:T(8,128)(2,1)S(1)}, bf16[208,768]{1,0:T(8,128)(2,1)S(1)}, u32[]{:S(2)}, u32[]{:S(2)}) collective-permute-start(bf16[208,768]{1,0:T(8,128)(2,1)S(1)} %get-tuple-element.139), channel_id=1, source_target_pairs={{0,2},{1,3},{2,0},{3,1},{4,6},{5,7},{6,4},{7,5},{8,10},{9,11},{10,... | collective-permute-start | bytes 958472 | tf_op jit(solution)/shard_map/ppermute | solution.py:24
  19.7 20.8 %collective-permute-start.2 = (bf16[208,768]{1,0:T(8,128)(2,1)S(1)}, bf16[208,768]{1,0:T(8,128)(2,1)S(1)}, u32[]{:S(2)}, u32[]{:S(2)}) collective-permute-start(bf16[208,768]{1,0:T(8,128)(2,1)S(1)} %get-tuple-element.136), channel_id=1, source_target_pairs={{0,3},{1,0},{2,1},{3,2},{4,7},{5,4},{6,5},{7,6},{8,11},{9,8},{10,9... | collective-permute-start | bytes 958472 | tf_op jit(solution)/shard_map/ppermute | solution.py:24
  72.4 28.0 %collective-permute-start.4 = (bf16[208,768]{1,0:T(8,128)(2,1)}, bf16[208,768]{1,0:T(8,128)(2,1)}, u32[]{:S(2)}, u32[]{:S(2)}) collective-permute-start(bf16[208,768]{1,0:T(8,128)(2,1)} %get-tuple-element.51), channel_id=1, source_target_pairs={{0,2},{1,3},{2,0},{3,1},{4,6},{5,7},{6,4},{7,5},{8,10},{9,11},{10,... | collective-permute-start | bytes 958472 | tf_op jit(solution)/shard_map/ppermute | solution.py:24
  74.7 26.7 %collective-permute-start.5 = (bf16[208,768]{1,0:T(8,128)(2,1)}, bf16[208,768]{1,0:T(8,128)(2,1)S(1)}, u32[]{:S(2)}, u32[]{:S(2)}) collective-permute-start(bf16[208,768]{1,0:T(8,128)(2,1)} %get-tuple-element.52), channel_id=1, source_target_pairs={{0,1},{1,2},{2,3},{3,0},{4,5},{5,6},{6,7},{7,4},{8,9},{9,10},{10,1... | collective-permute-start | bytes 958472 | tf_op jit(solution)/shard_map/ppermute | solution.py:24
  268.2 23.8 %collective-permute-start.7 = (bf16[208,768]{1,0:T(8,128)(2,1)S(1)}, bf16[208,768]{1,0:T(8,128)(2,1)S(1)}, u32[]{:S(2)}, u32[]{:S(2)}) collective-permute-start(bf16[208,768]{1,0:T(8,128)(2,1)S(1)} %get-tuple-element.133), channel_id=1, source_target_pairs={{0,2},{1,3},{2,0},{3,1},{4,6},{5,7},{6,4},{7,5},{8,10},{9,11},{10,... | collective-permute-start | bytes 958472 | tf_op jit(solution)/shard_map/ppermute | solution.py:24
  270.6 21.4 %collective-permute-start.8 = (bf16[208,768]{1,0:T(8,128)(2,1)S(1)}, bf16[208,768]{1,0:T(8,128)(2,1)S(1)}, u32[]{:S(2)}, u32[]{:S(2)}) collective-permute-start(bf16[208,768]{1,0:T(8,128)(2,1)S(1)} %get-tuple-element.132), channel_id=1, source_target_pairs={{0,3},{1,0},{2,1},{3,2},{4,7},{5,4},{6,5},{7,6},{8,11},{9,8},{10,9... | collective-permute-start | bytes 958472 | tf_op jit(solution)/shard_map/ppermute | solution.py:24
  286.6 29.4 %collective-permute-start.22 = (bf16[384,3072]{1,0:T(8,128)(2,1)S(1)}, bf16[384,3072]{1,0:T(8,128)(2,1)}, u32[]{:S(2)}, u32[]{:S(2)}) collective-permute-start(bf16[384,3072]{1,0:T(8,128)(2,1)S(1)} %constant_dynamic-slice_fusion.4), channel_id=1, source_target_pairs={{0,4},{4,0},{8,12},{12,8},{16,20},{20,16},{24,28},{28,24},{1,5},{5... | collective-permute-start | bytes 7077896 | tf_op jit(solution)/shard_map/ppermute | solution.py:49
  319.6 28.9 %collective-permute-start.23 = (bf16[192,3072]{1,0:T(8,128)(2,1)S(1)}, bf16[192,3072]{1,0:T(8,128)(2,1)}, u32[]{:S(2)}, u32[]{:S(2)}) collective-permute-start(bf16[192,3072]{1,0:T(8,128)(2,1)S(1)} %constant_dynamic-slice_fusion.3), channel_id=1, source_target_pairs={{0,8},{4,12},{8,0},{12,4},{16,24},{20,28},{24,16},{28,20},{1,9},{5... | collective-permute-start | bytes 3538952 | tf_op jit(solution)/shard_map/ppermute | solution.py:49
  326.1 47.2 %collective-permute-start.13 = (bf16[192,3072]{1,0:T(8,128)(2,1)}, bf16[192,3072]{1,0:T(8,128)(2,1)}, u32[]{:S(2)}, u32[]{:S(2)}) collective-permute-start(bf16[192,3072]{1,0:T(8,128)(2,1)} %constant_dynamic-slice_fusion.8), channel_id=1, source_target_pairs={{0,8},{4,12},{8,0},{12,4},{16,24},{20,28},{24,16},{28,20},{1,9},{5... | collective-permute-start | bytes 3538952 | tf_op jit(solution)/shard_map/ppermute | solution.py:49
  350.2 24.8 %collective-permute-start.24 = (bf16[96,3072]{1,0:T(8,128)(2,1)S(1)}, bf16[96,3072]{1,0:T(8,128)(2,1)S(1)}, u32[]{:S(2)}, u32[]{:S(2)}) collective-permute-start(bf16[96,3072]{1,0:T(8,128)(2,1)S(1)} %constant_dynamic-slice_fusion.2), channel_id=1, source_target_pairs={{0,16},{4,20},{8,24},{12,28},{16,0},{20,4},{24,8},{28,12},{1,17},{... | collective-permute-start | bytes 1769480 | tf_op jit(solution)/shard_map/ppermute | solution.py:49
  435.3 29.2 %collective-permute-start.19 = (bf16[96,3072]{1,0:T(8,128)(2,1)}, bf16[96,3072]{1,0:T(8,128)(2,1)S(1)}, u32[]{:S(2)}, u32[]{:S(2)}) collective-permute-start(bf16[96,3072]{1,0:T(8,128)(2,1)} %pad_maximum_fusion.6), channel_id=1, source_target_pairs={{0,16},{4,20},{8,24},{12,28},{16,0},{20,4},{24,8},{28,12},{1,17},{... | collective-permute-start | bytes 1769480 | tf_op jit(solution)/shard_map/ppermute | solution.py:49
  449.8 48.1 %collective-permute-start.30 = (bf16[192,3072]{1,0:T(8,128)(2,1)S(1)}, bf16[192,3072]{1,0:T(8,128)(2,1)}, u32[]{:S(2)}, u32[]{:S(2)}) collective-permute-start(bf16[192,3072]{1,0:T(8,128)(2,1)S(1)} %pad_maximum_fusion.3), channel_id=1, source_target_pairs={{0,8},{4,12},{8,0},{12,4},{16,24},{20,28},{24,16},{28,20},{1,9},{5... | collective-permute-start | bytes 3538952 | tf_op jit(solution)/shard_map/ppermute | solution.py:49
  466.0 106.7 %collective-permute-start.20 = (bf16[192,3072]{1,0:T(8,128)(2,1)}, bf16[192,3072]{1,0:T(8,128)(2,1)}, u32[]{:S(2)}, u32[]{:S(2)}) collective-permute-start(bf16[192,3072]{1,0:T(8,128)(2,1)} %pad_maximum_fusion.2), channel_id=1, source_target_pairs={{0,8},{4,12},{8,0},{12,4},{16,24},{20,28},{24,16},{28,20},{1,9},{5... | collective-permute-start | bytes 3538952 | tf_op jit(solution)/shard_map/ppermute | solution.py:49
  501.4 171.3 %collective-permute-start.31 = (bf16[384,3072]{1,0:T(8,128)(2,1)}, bf16[384,3072]{1,0:T(8,128)(2,1)}, u32[]{:S(2)}, u32[]{:S(2)}) collective-permute-start(bf16[384,3072]{1,0:T(8,128)(2,1)} %pad_maximum_fusion.1), channel_id=1, source_target_pairs={{0,4},{4,0},{8,12},{12,8},{16,20},{20,16},{24,28},{28,24},{1,5},{5... | collective-permute-start | bytes 7077896 | tf_op jit(solution)/shard_map/ppermute | solution.py:49
  514.3 67.0 %collective-permute-start.9 = (bf16[208,768]{1,0:T(8,128)(2,1)}, bf16[208,768]{1,0:T(8,128)(2,1)}, u32[]{:S(2)}, u32[]{:S(2)}) collective-permute-start(bf16[208,768]{1,0:T(8,128)(2,1)} %get-tuple-element.70), channel_id=1, source_target_pairs={{0,3},{1,0},{2,1},{3,2},{4,7},{5,4},{6,5},{7,6},{8,11},{9,8},{10,9... | collective-permute-start | bytes 958472 | tf_op jit(solution)/shard_map/ppermute | solution.py:24
  514.9 68.0 %collective-permute-start.10 = (bf16[208,768]{1,0:T(8,128)(2,1)}, bf16[208,768]{1,0:T(8,128)(2,1)}, u32[]{:S(2)}, u32[]{:S(2)}) collective-permute-start(bf16[208,768]{1,0:T(8,128)(2,1)} %get-tuple-element.71), channel_id=1, source_target_pairs={{0,2},{1,3},{2,0},{3,1},{4,6},{5,7},{6,4},{7,5},{8,10},{9,11},{10,... | collective-permute-start | bytes 958472 | tf_op jit(solution)/shard_map/ppermute | solution.py:24
  515.8 68.9 %collective-permute-start.11 = (bf16[208,768]{1,0:T(8,128)(2,1)}, bf16[208,768]{1,0:T(8,128)(2,1)}, u32[]{:S(2)}, u32[]{:S(2)}) collective-permute-start(bf16[208,768]{1,0:T(8,128)(2,1)} %get-tuple-element.72), channel_id=1, source_target_pairs={{0,1},{1,2},{2,3},{3,0},{4,5},{5,6},{6,7},{7,4},{8,9},{9,10},{10,1... | collective-permute-start | bytes 958472 | tf_op jit(solution)/shard_map/ppermute | solution.py:24
  576.6 101.7 %collective-permute-start.21 = (bf16[384,3072]{1,0:T(8,128)(2,1)}, bf16[384,3072]{1,0:T(8,128)(2,1)}, u32[]{:S(2)}, u32[]{:S(2)}) collective-permute-start(bf16[384,3072]{1,0:T(8,128)(2,1)} %pad_maximum_fusion), channel_id=1, source_target_pairs={{0,4},{4,0},{8,12},{12,8},{16,20},{20,16},{24,28},{28,24},{1,5},{5... | collective-permute-start | bytes 7077896 | tf_op jit(solution)/shard_map/ppermute | solution.py:49
  (51 other events, 406.3 us)
Sparse Core Ops, SparseCore 0:
  10.5 41.7 all-gather.6
  54.7 38.9 all-gather.8
  95.6 38.9 all-gather.10
  136.2 38.9 all-gather.12
  451.5 209.1 all-reduce.6

commit v3 on v2

v3 whole, which is shorter than its diff:
```python
import functools
import math

import jax
import jax.numpy as jnp
from jax import lax
from jax.experimental import pallas as pl
from jax.experimental.pallas import tpu as pltpu
from jax.sharding import PartitionSpec as P

HEADS = 12
UNITS = 4
PATCHES = 784
LOG2E = 1.4426950408889634
ROW_TILE = 16


def round_up(count, step):
    return -(-count // step) * step


def struct(shape, dtype):
    return jax.ShapeDtypeStruct(shape, dtype)


VMEM = pl.BlockSpec(memory_space=pltpu.VMEM)
SMEM = pl.BlockSpec(memory_space=pltpu.SMEM)


class Order:
    def __init__(self, flags):
        self.flags = flags
        self.token = None

    def run(self, kernel, operands, in_specs, out_specs, out_shape, grid=(), scratch=(), prefetch=0):
        token = [] if self.token is None else [self.token]
        inputs, outputs, ordered = len(operands), len(out_shape), len(token)

        def body(*refs):
            refs = refs[:prefetch] + refs[prefetch + ordered :]
            token_ref = refs[inputs + outputs]
            token_ref[...] = jnp.zeros(token_ref.shape, token_ref.dtype)
            kernel(*refs[: inputs + outputs], *refs[inputs + outputs + 1 :])

        token_spec = pl.BlockSpec((8, 128), lambda *index: (0, 0))
        results = pl.pallas_call(
            body,
            grid_spec=pltpu.PrefetchScalarGridSpec(
                num_scalar_prefetch=prefetch,
                grid=grid,
                in_specs=[pl.BlockSpec(memory_space=pl.ANY)] * ordered + list(in_specs),
                out_specs=list(out_specs) + [token_spec],
                scratch_shapes=list(scratch),
            ),
            out_shape=list(out_shape) + [struct((8, 128), jnp.float32)],
            compiler_params=pltpu.CompilerParams(vmem_limit_bytes=56 << 20),
        )(*operands[:prefetch], *token, *operands[prefetch:])
        self.token = results[-1]
        return results[:-1]


def shift_frames(block, frame_count, shift):
    if shift % frame_count == 0:
        return block
    pairs = [(index, (index + shift) % frame_count) for index in range(frame_count)]
    return lax.ppermute(block, "frame", pairs)


def rows_to_frames(rows, frame_count, frame_index):
    part = rows.shape[0] // frame_count
    slots = []
    for shift in range(frame_count):
        owner = (frame_index + shift) % frame_count
        block = lax.dynamic_slice_in_dim(rows, owner * part, part, 0)
        slots.append(shift_frames(block, frame_count, shift))
    return slots


def send_back(slots):
    return [shift_frames(slot, len(slots), -shift) for shift, slot in enumerate(slots)]


def swap_bit(block, axis, size, bit):
    pairs = [(index, index ^ (1 << bit)) for index in range(size)]
    return lax.ppermute(block, axis, pairs)


def shuffle_kernel(plan, source_count, flags_ref, *refs):
    sources, outputs = refs[:source_count], refs[source_count:]

    def emit(output, at, rows, terms):
        steps = [step for step in range(ROW_TILE, 65, ROW_TILE) if rows % step == 0]
        step = max(steps, default=rows)

        def some(index, carry):
            def load(term):
                source, start = term
                if steps:
                    return sources[source][pl.ds(pl.multiple_of(start + index * step, ROW_TILE), step)]
                return sources[source][start : start + step]

            value = load(terms[0])
            if len(terms) > 1:
                total = value.astype(jnp.float32)
                for term in terms[1:]:
                    total = total + load(term).astype(jnp.float32)
                value = total.astype(output.dtype)
            if steps:
                output[pl.ds(pl.multiple_of(at + index * step, ROW_TILE), step)] = value
            else:
                output[at : at + step] = value
            return carry

        if rows // step == 1:
            some(0, 0)
        else:
            lax.fori_loop(0, rows // step, some, 0)

    for output, segments in zip(outputs, plan):
        at = 0
        for rows, flag, *choices in segments:
            for value, terms in enumerate(choices):

                @pl.when(flags_ref[flag] == value)
                def _():
                    emit(output, at, rows, terms)

            at += rows


def shuffle(order, requests):
    sources, plan, counts = [], [], []
    for own_sources, own_plan in requests:
        base = len(sources)

        def lift(terms):
            return tuple((source + base, start) for source, start in terms)

        plan += [
            [(rows, flag, lift(low), lift(high)) for rows, flag, low, high in out] for out in own_plan
        ]
        sources += own_sources
        counts.append(len(own_plan))
    features = sources[0].shape[1]
    shapes = [struct((sum(segment[0] for segment in out), features), jnp.bfloat16) for out in plan]
    results = order.run(
        functools.partial(shuffle_kernel, plan, len(sources)),
        [order.flags, *sources],
        [SMEM] + [VMEM] * len(sources),
        [VMEM] * len(plan),
        shapes,
    )
    outputs = []
    for count in counts:
        outputs.append(results[:count])
        results = results[count:]
    return outputs


def split_plan(rows, flag, left, right):
    half = rows // 2
    low = ((left[0], left[1]), (right[0], right[1]))
    high = ((left[0], left[1] + half), (right[0], right[1] + half))
    return [[(half, flag, high, low)], [(half, flag, low, high)]]


def join_plan(rows, flag, own, arrived):
    return [(rows, flag, (own,), (arrived,)), (rows, flag, (arrived,), (own,))]


def sum_order(piece, sizes, rows):
    batch_bits, frame_bits = (size.bit_length() - 1 for size in sizes)
    batch, frame = divmod(piece, sizes[1])
    wide = list(range(1, batch_bits))
    size = rows // 4
    start = (batch & 1) * 2 * size + (frame & 1) * size
    for bit in wide[::-1] if frame & 1 else wide:
        size //= 2
        start += ((batch >> bit) & 1) * size
    for bit in range(1, frame_bits):
        size //= 2
        start += ((frame >> bit) & 1) * size
    return start


def sum_steps(kept, sent, sizes, spread):
    batch_bits, frame_bits = (size.bit_length() - 1 for size in sizes)
    wide = list(range(1, batch_bits))
    ways = (wide, wide[::-1])

    def over_batch(block, bit):
        return swap_bit(block, "batch", sizes[0], bit)

    def over_frame(block, bit):
        return swap_bit(block, "frame", sizes[1], bit)

    (arrived,) = yield [over_batch(sent, 0)]
    rows = kept.shape[0] // 2
    sources = [kept, arrived]
    pairs = [((0, 0), (1, 0)), ((0, rows), (1, rows))]
    for level in range(len(wide)):
        plan = []
        for (left, right), way in zip(pairs, ways):
            plan += split_plan(rows, way[level], left, right)
        first_out, first_kept, second_out, second_kept = yield sources, plan
        moved = yield [over_batch(first_out, ways[0][level]), over_batch(second_out, ways[1][level])]
        sources = [first_kept, moved[0], second_kept, moved[1]]
        pairs = [((0, 0), (1, 0)), ((2, 0), (3, 0))]
        rows //= 2
    flag = batch_bits
    plan = [[(rows, flag, pairs[1], pairs[0])], [(rows, flag, pairs[0], pairs[1])]]
    for bit in range(frame_bits):
        if bit:
            rows //= 2
            plan = split_plan(2 * rows, flag + bit, (0, 0), (1, 0))
        sent, kept = yield sources, plan
        (arrived,) = yield [over_frame(sent, bit)]
        sources = [kept, arrived]
    (block,) = yield sources, [[(rows, flag, ((0, 0), (1, 0)), ((0, 0), (1, 0)))]]
    if not spread:
        return block
    for bit in range(frame_bits)[:0:-1]:
        (arrived,) = yield [over_frame(block, bit)]
        (block,) = yield [block, arrived], [join_plan(rows, flag + bit, (0, 0), (1, 0))]
        rows *= 2
    (arrived,) = yield [over_frame(block, 0)]
    plan = [[(rows, flag, ((0, 0),), ((1, 0),))], [(rows, flag, ((1, 0),), ((0, 0),))]]
    blocks = yield [block, arrived], plan
    for level in range(len(wide))[::-1]:
        moved = yield [over_batch(block, way[level]) for block, way in zip(blocks, ways)]
        sources = [blocks[0], moved[0], blocks[1], moved[1]]
        plan = [join_plan(rows, ways[0][level], (0, 0), (1, 0))]
        plan += [join_plan(rows, ways[1][level], (2, 0), (3, 0))]
        if level == 0:
            plan = [plan[0] + plan[1]]
        blocks = yield sources, plan
        rows *= 2
    (arrived,) = yield [over_batch(blocks[0], 0)]
    return blocks[0], arrived


class Flight:
    def __init__(self, steps):
        self.steps, self.result = steps, None
        self.moved = next(steps)

    def send(self, value):
        try:
            return self.steps.send(value)
        except StopIteration as stop:
            self.result = stop.value
            return None


def advance(order, *flights):
    active, requests = [], []
    for flight in flights:
        request = flight.send(flight.moved) if flight.result is None else None
        if request is not None:
            active.append(flight)
            requests.append(request)
    if requests:
        for flight, outputs in zip(active, shuffle(order, requests)):
            flight.moved = flight.send(outputs)


def deliver_kernel(ranges, count, flags_ref, *refs):
    own_ref, arrived_ref = refs[0], refs[1]
    outputs = refs[len(refs) - len(ranges) :]
    whole = len(refs) - len(ranges) == 1
    step = pl.program_id(0)
    own = (step < count // 2) == (flags_ref[0] == 0)
    for output, (first, last, _) in zip(outputs, ranges):
        here = (step >= first) & (step < last)

        @pl.when(here if whole else here & own)
        def _():
            output[...] = own_ref[...].astype(output.dtype)

        if not whole:

            @pl.when(here & jnp.logical_not(own))
            def _():
                output[...] = arrived_ref[...].astype(output.dtype)


def deliver(order, sources, ranges, block):
    features = sources[0].shape[1]
    count = sum(source.shape[0] for source in sources) // block
    half = count // 2
    per = features // block

    def place(core, step):
        if len(sources) == 1:
            return step
        return jnp.where(core == 0, jnp.minimum(step, half - 1), jnp.maximum(step - half, 0))

    def spot(first, last, wide):
        def index(step, flags):
            at = jnp.clip(step - first, 0, last - first - 1)
            return (at % per, at // per) if wide else (at, 0)

        return pl.BlockSpec((block, features), index)

    def shape(first, last, wide):
        rows = (last - first) * block
        return (features, rows) if wide else (rows, features)

    specs = [
        pl.BlockSpec((block, features), lambda step, flags: (place(flags[0], step), 0)),
        pl.BlockSpec((block, features), lambda step, flags: (place(1 - flags[0], step), 0)),
    ]
    return order.run(
        functools.partial(deliver_kernel, ranges, count),
        [order.flags, *sources],
        specs[: len(sources)],
        [spot(*item) for item in ranges],
        [struct(shape(*item), jnp.float32) for item in ranges],
        grid=(count,),
        prefetch=1,
    )


def contract(x,y,dims):
    return lax.dot_general(x,y,((dims[0:1],dims[1:2]),((),())),preferred_element_type=jnp.float32)

def widen_rows(values, wide):
    rows, width = values.shape
    if wide == rows:
        return values
    return jnp.concatenate([values, jnp.zeros((wide - rows, width), values.dtype)])


def head_halves(width):
    lane = lax.broadcasted_iota(jnp.int32, (1, width), 1)
    return [lane < width // 2, lane >= width // 2]

def space_forward_kernel(scale, tile, column_ref, row_ref, q_ref, k_ref, v_ref, mixture_ref, total_ref, bias_ref, k_wide, v_wide):
    rows, width = q_ref.shape
    wide = k_wide.shape[0]
    @pl.when(pl.program_id(0) == 0)
    def _():
        bias_ref[...] = jnp.where(column_ref[...] == row_ref[...], 0.0, -1e30)
        if wide > rows:
            k_wide[rows:] = jnp.zeros((wide - rows, width), k_wide.dtype)
            v_wide[rows:] = jnp.zeros((wide - rows, width), v_wide.dtype)
    k_wide[:rows] = k_ref[...]
    v_wide[:rows] = v_ref[...]
    halves = head_halves(width)
    zero, one = jnp.zeros((), q_ref.dtype), jnp.ones((), q_ref.dtype)
    filled = [jnp.where(half, v_wide[...], one) for half in halves]
    for start in range(0, rows, tile):
        span = slice(start, start + tile)
        outs, tops = [], []
        for half, values in zip(halves, filled):
            queries = jnp.where(half, q_ref[span], zero)
            scores = contract(queries, k_wide[...], (1, 1)) * (scale * LOG2E) + bias_ref[span]
            top = jnp.max(scores, axis=1, keepdims=True)
            weights = jnp.exp2(scores - top)
            outs.append(contract(weights.astype(jnp.bfloat16), values, (1, 0)))
            tops.append(top)
        mass = pltpu.roll(jnp.where(halves[0], outs[1], outs[0]), width // 2, 1)
        mixture = jnp.where(halves[0], outs[0], outs[1]) / mass
        mixture_ref[span] = mixture.astype(mixture_ref.dtype)
        total_ref[span] = jnp.where(halves[0], tops[0], tops[1]) + jnp.log2(mass)


def space_specs(rows, features):
    pairs = HEADS // 2
    width = features // pairs
    wide = round_up(rows, 128)
    fixed = [pl.BlockSpec((rows, 1), lambda i: (0, 0)), pl.BlockSpec((1, wide), lambda i: (0, 0))]
    blocks = [pl.BlockSpec((rows, width), lambda i, o=o: (0, o + i)) for o in (0, pairs, 2 * pairs)]
    out = pl.BlockSpec((rows, width), lambda i: (0, i))
    scratch = [pltpu.VMEM((rows, wide), jnp.float32)]
    scratch += [pltpu.VMEM((wide, width), jnp.bfloat16)] * 2
    return pairs, (features // HEADS) ** -0.5, fixed + blocks, out, scratch


def clip_lines(clip):
    rows = clip.shape[0]
    row = jnp.pad(clip, (0, round_up(rows, 128) - rows), constant_values=-2)
    return clip[:, None], row[None]


def space_forward(order, qkv, clip, features):
    rows = qkv.shape[0]
    pairs, scale, specs, out, scratch = space_specs(rows, features)
    return order.run(
        functools.partial(space_forward_kernel, scale, rows),
        [*clip_lines(clip), qkv, qkv, qkv],
        specs,
        [out, out],
        [struct((rows, features), jnp.bfloat16), struct((rows, features), jnp.float32)],
        grid=(pairs,),
        scratch=scratch,
    )


def space_backward_kernel(scale, tile, column_ref, row_ref, q_ref, k_ref, v_ref, mixture_ref, total_ref, grad_ref, dq_ref, dk_ref, dv_ref, bias_ref, q_wide, g_wide):
    rows, width = q_ref.shape
    wide = q_wide.shape[0]
    @pl.when(pl.program_id(0) == 0)
    def _():
        bias_ref[...] = jnp.where(column_ref[...] == row_ref[...], 0.0, -1e30)
        if wide > rows:
            q_wide[rows:] = jnp.zeros((wide - rows, width), q_wide.dtype)
            g_wide[rows:] = jnp.zeros((wide - rows, width), g_wide.dtype)
    q_wide[:rows] = q_ref[...]
    g_wide[:rows] = grad_ref[...]
    halves = head_halves(width)
    zero = jnp.zeros((), q_ref.dtype)
    product = grad_ref[...].astype(jnp.float32) * mixture_ref[...].astype(jnp.float32)
    sums = [jnp.sum(jnp.where(half, product, 0.0), axis=1, keepdims=True) for half in halves]
    delta = widen_rows(jnp.where(halves[0], sums[0], sums[1]), wide).T
    total = widen_rows(total_ref[...], wide).T
    dq_parts = [None, None]
    for start in range(0, rows, tile):
        span = slice(start, start + tile)
        dk, dv = [], []
        for index, half in enumerate(halves):
            at = index * (width // 2)
            keys = jnp.where(half, k_ref[span], zero)
            values = jnp.where(half, v_ref[span], zero)
            scores = contract(keys, q_wide[...], (1, 1)) * (scale * LOG2E)
            weights = jnp.exp2(scores + (bias_ref[span] - total[at:at + 1]))
            slopes = contract(values, g_wide[...], (1, 1))
            slopes = (weights * (slopes - delta[at:at + 1])).astype(jnp.bfloat16)
            dv.append(contract(weights.astype(jnp.bfloat16), g_wide[...], (1, 0)))
            dk.append(contract(slopes, q_wide[...], (1, 0)))
            part = contract(slopes, keys, (0, 0))
            dq_parts[index] = part if start == 0 else dq_parts[index] + part
        dk_ref[span] = (jnp.where(halves[0], dk[0], dk[1]) * scale).astype(dk_ref.dtype)
        dv_ref[span] = jnp.where(halves[0], dv[0], dv[1]).astype(dv_ref.dtype)
    dq_ref[...] = ((dq_parts[0] + dq_parts[1])[:rows] * scale).astype(dq_ref.dtype)

def space_backward(order, qkv, mixture, total, grad, clip, features):
    rows = qkv.shape[0]
    pairs, scale, specs, out, scratch = space_specs(rows, features)
    return order.run(
        functools.partial(space_backward_kernel, scale, rows),
        [*clip_lines(clip), qkv, qkv, qkv, mixture, total, grad],
        specs + [out] * 3,
        [out] * 3,
        [struct((rows, features), jnp.bfloat16)] * 3,
        grid=(pairs,),
        scratch=scratch,
    )


def norm_parts(values):
    average = jnp.mean(values, axis=1, keepdims=True)
    centered = values - average
    spread = lax.rsqrt(jnp.mean(centered * centered, axis=1, keepdims=True) + 1e-06)
    return centered * spread, spread
def norm_back(grad, normed, spread, gain):
    scaled = grad * gain
    return spread * (scaled - jnp.mean(scaled, axis=1, keepdims=True) - normed * jnp.mean(scaled * normed, axis=1, keepdims=True))
def column_sum(values):
    return jnp.sum(values, axis=0, keepdims=True)

def feed_kernel(chunks, x1_ref, mixture_ref, dz_ref, so_ref, fi_ref, fo_ref, fb_ref, vec_ref,
                out_ref, dx2_ref, dys_ref, dos_ref, grad_ref, gfb_ref, gvec_ref,
                x2_s, a3_s, a3t_s, acc_s, da_s, g_s, dh_s):
    step = pl.program_id(0)
    rows = x1_ref.shape[0]
    @pl.when(step == 0)
    def _():
        x2 = x1_ref[...] + contract(mixture_ref[...], so_ref[...], (1, 0)) + vec_ref[9:10]
        x2_s[...] = x2
        normed, _ = norm_parts(x2)
        a3 = (normed * vec_ref[10:11] + vec_ref[11:12]).astype(jnp.bfloat16)
        a3_s[...] = a3
        a3t_s[...] = a3.T
        acc_s[...] = x2 + vec_ref[12:13]
        da_s[...] = jnp.zeros_like(da_s)
    part = rows // chunks
    for chunk in range(chunks):
        span = slice(chunk * part, (chunk + 1) * part)
        hidden = contract(a3_s[span], fi_ref[...], (1, 0)) + fb_ref[...]
        cdf = 0.5 + 0.5 * lax.erf(hidden * math.sqrt(0.5))
        slope = cdf + hidden * jnp.exp(hidden * hidden * -0.5) * (1.0 / math.sqrt(2.0 * math.pi))
        active = (hidden * cdf).astype(jnp.bfloat16)
        g_s[span] = active
        dh = (contract(dz_ref[span], fo_ref[...], (1, 1)) * slope).astype(jnp.bfloat16)
        dh_s[span] = dh
        acc_s[span] += contract(active, fo_ref[...], (1, 0))
        da_s[span] += contract(dh, fi_ref[...], (1, 1))
    grad_ref[0] = contract(a3t_s[...], dh_s[...], (1, 0)).astype(grad_ref.dtype)
    grad_ref[1] = contract(g_s[...], dz_ref[...], (0, 0)).astype(grad_ref.dtype)
    gfb_ref[...] = column_sum(dh_s[...].astype(jnp.float32))
    @pl.when(step == pl.num_programs(0) - 1)
    def _():
        out_ref[...] = acc_s[...].astype(out_ref.dtype)
        normed, spread = norm_parts(x2_s[...])
        grad = da_s[...]
        dz = dz_ref[...].astype(jnp.float32)
        dx2 = dz + norm_back(grad, normed, spread, vec_ref[10:11])
        dx2_ref[...] = dx2
        dys = dx2.astype(jnp.bfloat16)
        dys_ref[...] = dys
        dos_ref[...] = contract(dys, so_ref[...], (1, 1)).astype(dos_ref.dtype)
        gvec_ref[0:1] = column_sum(grad * normed)
        gvec_ref[1:2] = column_sum(grad)
        gvec_ref[2:3] = column_sum(dz)
        gvec_ref[3:4] = column_sum(dys.astype(jnp.float32))
        gvec_ref[4:8] = jnp.zeros((4, gvec_ref.shape[1]), jnp.float32)

def feed_block(order, x1, mixture, dz, space_packed, fi, fo, fb, vec, tile, chunks):
    rows, features = x1.shape
    hidden = fi.shape[1]
    whole = pl.BlockSpec((rows, features), lambda j: (0, 0))
    fi_spec = pl.BlockSpec((features, tile), lambda j: (0, j))
    fo_spec = pl.BlockSpec((tile, features), lambda j: (j, 0))
    fb_spec = pl.BlockSpec((1, tile), lambda j: (0, j))
    last = space_packed.shape[1] // features - 1
    low, full = jnp.bfloat16, jnp.float32
    return order.run(
        functools.partial(feed_kernel, chunks),
        [x1, mixture, dz, space_packed, fi, fo, fb, vec],
        [whole, whole, whole]
        + [pl.BlockSpec((features, features), lambda j: (0, last)), fi_spec, fo_spec, fb_spec]
        + [pl.BlockSpec(vec.shape, lambda j: (0, 0))],
        [whole] * 4
        + [pl.BlockSpec((2, tile, features), lambda j: (0, j, 0)), fb_spec]
        + [pl.BlockSpec((8, features), lambda j: (0, 0))],
        [
            struct((rows, features), low),
            struct((rows, features), full),
            struct((rows, features), low),
            struct((rows, features), low),
            struct((2, *fo.shape), low),
            struct((1, hidden), full),
            struct((8, features), full),
        ],
        grid=(hidden // tile,),
        scratch=[
            pltpu.VMEM((rows, features), full),
            pltpu.VMEM((rows, features), low),
            pltpu.VMEM((features, rows), low),
            pltpu.VMEM((rows, features), full),
            pltpu.VMEM((rows, features), full),
            pltpu.VMEM((rows, tile), low),
            pltpu.VMEM((rows, tile), low),
        ],
    )


def gather_rows(count, frame, slots, rows_s):
    part = slots[0].shape[0]
    for shift in range(count):
        owner = lax.rem(frame + shift, count)
        rows_s[pl.ds(pl.multiple_of(owner * part, ROW_TILE), part)] = slots[shift][...]


def middle_kernel(count, frame_flag, flags_ref, token_ref, *refs):
    slots, (to_ref, sp_ref, vec_ref) = refs[:count], refs[count : count + 3]
    mixture_ref, x1_ref, a2_ref, qkv_ref = refs[count + 3 :]
    rows, features = token_ref.shape
    gather_rows(count, flags_ref[frame_flag], slots, mixture_ref)
    number = lax.broadcasted_iota(jnp.int32, (rows, 1), 0)
    branch = contract(mixture_ref[...], to_ref[...], (1, 0)) + vec_ref[4:5]
    x1 = token_ref[...].astype(jnp.float32) + jnp.where(number < PATCHES, branch, 0.0)
    x1_ref[...] = x1
    normed, _ = norm_parts(x1)
    a2 = (normed * vec_ref[5:6] + vec_ref[6:7]).astype(jnp.bfloat16)
    a2_ref[...] = a2
    for third in range(3):
        span = slice(third * features, (third + 1) * features)
        joined = contract(a2, sp_ref[:, span], (1, 0))
        if third != 1:
            joined = joined + vec_ref[7 + third // 2 : 8 + third // 2]
        qkv_ref[:, span] = joined.astype(jnp.bfloat16)


def project_specs(features, vec):
    return [
        pl.BlockSpec((features, features), lambda i: (0, 3)),
        pl.BlockSpec((features, 3 * features), lambda i: (0, 0)),
        pl.BlockSpec(vec.shape, lambda i: (0, 0)),
    ]


def middle_forward(order, tokens, slots, time_packed, space_packed, vec):
    rows, features = tokens.shape
    low = jnp.bfloat16
    return order.run(
        functools.partial(middle_kernel, len(slots), order.flags.shape[0] - 1),
        [order.flags, tokens, *slots, time_packed, space_packed, vec],
        [SMEM] + [VMEM] * (len(slots) + 1) + project_specs(features, vec),
        [VMEM] * 4,
        [
            struct((rows, features), low),
            struct((rows, features), jnp.float32),
            struct((rows, features), low),
            struct((rows, 3 * features), low),
        ],
        grid=(1,),
    )


def middle_back_kernel(
    count, frame_flag, flags_ref, dq_ref, dk_ref, dv_ref, x1_ref, dx2_ref, to_ref, sp_ref, vec_ref, *refs
):
    dx1_ref, dyt_ref, sums_ref = refs[:3]
    slots, rows_s = refs[3 : 3 + count], refs[3 + count]
    rows, features = x1_ref.shape
    grad = 0.0
    for third, piece in enumerate((dq_ref, dk_ref, dv_ref)):
        span = slice(third * features, (third + 1) * features)
        grad = grad + contract(piece[...], sp_ref[:, span], (1, 1))
    normed, spread = norm_parts(x1_ref[...])
    dx1 = dx2_ref[...] + norm_back(grad, normed, spread, vec_ref[5:6])
    dx1_ref[...] = dx1
    number = lax.broadcasted_iota(jnp.int32, (rows, 1), 0)
    dyt = jnp.where(number < PATCHES, dx1, 0.0).astype(jnp.bfloat16)
    dyt_ref[...] = dyt
    rows_s[...] = contract(dyt, to_ref[...], (1, 1)).astype(rows_s.dtype)
    part = rows // count
    for shift in range(count):
        owner = lax.rem(flags_ref[frame_flag] + shift, count)
        slots[shift][...] = rows_s[pl.ds(pl.multiple_of(owner * part, ROW_TILE), part)]
    sums_ref[0:1] = column_sum(grad * normed)
    sums_ref[1:2] = column_sum(grad)
    sums_ref[2:3] = column_sum(dq_ref[...].astype(jnp.float32))
    sums_ref[3:4] = column_sum(dv_ref[...].astype(jnp.float32))
    sums_ref[4:5] = column_sum(dyt.astype(jnp.float32))
    sums_ref[5:8] = jnp.zeros((3, features), jnp.float32)


def middle_backward(order, count, dq, dk, dv, x1, dx2, time_packed, space_packed, vec):
    rows, features = x1.shape
    low, full = jnp.bfloat16, jnp.float32
    results = order.run(
        functools.partial(middle_back_kernel, count, order.flags.shape[0] - 1),
        [order.flags, dq, dk, dv, x1, dx2, time_packed, space_packed, vec],
        [SMEM] + [VMEM] * 5 + project_specs(features, vec),
        [VMEM] * (3 + count),
        [struct((rows, features), full), struct((rows, features), low), struct((8, features), full)]
        + [struct((rows // count, features), low)] * count,
        grid=(1,),
        scratch=[pltpu.VMEM((rows, features), low)],
    )
    return results[0], results[1], results[2], results[3:]


def put_rows(core_ref, kept_ref, sent_ref, sizes, at, value):
    half = kept_ref.shape[0]
    low = value.astype(kept_ref.dtype)
    part = 2 * half // (sizes[0] * sizes[1]) if sizes else math.gcd(half, low.shape[0])
    for offset in range(0, low.shape[0], part):
        start = at + offset
        if sizes:
            start = sum_order(start // part, sizes, 2 * half)
        piece = low[offset : offset + part]
        span = slice(start % half, start % half + part)

        @pl.when(core_ref[0] == start // half)
        def _():
            kept_ref[span] = piece

        @pl.when(core_ref[0] != start // half)
        def _():
            sent_ref[span] = piece


def fill_rows(pieces, rows, features):
    used = sum(piece.shape[0] for piece in pieces)
    return jnp.concatenate([*pieces, jnp.zeros((rows - used, features), jnp.float32)])


def middle_weights_kernel(
    sizes, flags_ref, a2_ref, dq_ref, dk_ref, dv_ref, time_ref, dyt_ref, space_ref, dys_ref, sums_ref, feed_ref,
    bias_ref, kept_ref, sent_ref
):
    features = a2_ref.shape[1]
    turned = a2_ref[...].T
    put = functools.partial(put_rows, flags_ref, kept_ref, sent_ref, sizes)
    for third, piece in enumerate((dq_ref, dk_ref, dv_ref)):
        put(third * features, contract(turned, piece[...], (1, 0)))
    put(3 * features, contract(time_ref[...], dyt_ref[...], (0, 0)))
    put(4 * features, contract(space_ref[...], dys_ref[...], (0, 0)))
    bias = bias_ref[...]
    lines = [bias[:, at : at + features] for at in range(0, bias.shape[1], features)]
    pieces = [sums_ref[0:4], feed_ref[3:4], feed_ref[0:3], *lines]
    put(5 * features, fill_rows(pieces, 2 * kept_ref.shape[0] - 5 * features, features))


def middle_weights(order, sizes, *operands):
    features = operands[0].shape[1]
    half = struct((round_up(5 * features + 16, 512) // 2, features), jnp.bfloat16)
    return order.run(
        functools.partial(middle_weights_kernel, sizes),
        [order.flags, *operands],
        [SMEM] + [VMEM] * len(operands),
        [VMEM] * 2,
        [half, half],
    )


CHUNK = 16
def head_map(features, lanes=128):
    head = jnp.arange(features, dtype=jnp.int32) // (features // HEADS)
    return (head[:, None] == jnp.arange(lanes, dtype=jnp.int32)[None]).astype(jnp.bfloat16)

def pair_sums(left, right, gather_ref, pair_s):
    count = len(left)
    for f in range(count):
        for g in range(count):
            at = (f * count + g) * CHUNK
            pair_s[at:at + CHUNK] = (left[f] * right[g]).astype(jnp.bfloat16)
    return contract(pair_s[...], gather_ref[...], (1, 0))

def time_forward_kernel(count, scale, *refs):
    slots, (tp_ref, vec_ref, gather_ref, spread_ref) = refs[:count], refs[count:count + 4]
    outs, (qkv_ref, prob_ref, a1_ref) = refs[count + 4:2 * count + 4], refs[2 * count + 4:2 * count + 7]
    pair_s, weight_s = refs[2 * count + 7:]
    part, features = slots[0].shape
    for s in range(count):
        normed, _ = norm_parts(slots[s][...].astype(jnp.float32))
        a1_ref[s * part:(s + 1) * part] = (normed * vec_ref[0:1] + vec_ref[1:2]).astype(jnp.bfloat16)
    for third in range(3):
        span = slice(third * features, (third + 1) * features)
        joined = contract(a1_ref[...], tp_ref[:, span], (1, 0))
        if third != 1:
            joined = joined + vec_ref[2 + third // 2:3 + third // 2]
        qkv_ref[:, span] = joined.astype(jnp.bfloat16)

    def chunk_step(index, carry):
        def rows_of(s, third):
            start = pl.multiple_of(s * part + index * CHUNK, CHUNK)
            return qkv_ref[pl.ds(start, CHUNK), third * features:(third + 1) * features].astype(jnp.float32)
        queries, keys, values = ([rows_of(s, third) for s in range(count)] for third in range(3))
        scores = pair_sums(queries, keys, gather_ref, pair_s) * (scale * LOG2E)
        place = pl.ds(pl.multiple_of(index * CHUNK, CHUNK), CHUNK)
        for f in range(count):
            row = [scores[(f * count + g) * CHUNK:(f * count + g + 1) * CHUNK] for g in range(count)]
            top = functools.reduce(jnp.maximum, row)
            raised = [jnp.exp2(item - top) for item in row]
            mass = functools.reduce(jnp.add, raised)
            for g in range(count):
                weight = raised[g] / mass
                prob_ref[f * count + g, place] = weight
                at = (f * count + g) * CHUNK
                weight_s[at:at + CHUNK] = weight.astype(jnp.bfloat16)
        wide = contract(weight_s[...], spread_ref[...], (1, 0))
        for f in range(count):
            total = 0.0
            for g in range(count):
                at = (f * count + g) * CHUNK
                total = total + wide[at:at + CHUNK] * values[g]
            outs[f][place] = total.astype(jnp.bfloat16)
        return carry
    lax.fori_loop(0, part // CHUNK, chunk_step, 0)

def time_forward(order, slots, time_packed, vec):
    count = len(slots)
    part, features = slots[0].shape
    gather = head_map(features)
    low, full = jnp.bfloat16, jnp.float32
    results = order.run(
        functools.partial(time_forward_kernel, count, (features // HEADS) ** -0.5),
        [*slots, time_packed, vec, gather, gather.T],
        [VMEM] * count + [pl.BlockSpec((features, 3 * features), lambda i: (0, 0)), VMEM, VMEM, VMEM],
        [VMEM] * (count + 3),
        [struct((part, features), low)] * count
        + [
            struct((count * part, 3 * features), low),
            struct((count * count, part, 128), full),
            struct((count * part, features), low),
        ],
        grid=(1,),
        scratch=[
            pltpu.VMEM((count * count * CHUNK, features), low),
            pltpu.VMEM((count * count * CHUNK, 128), low),
        ],
    )
    return results[:count], results[count], results[count + 1], results[count + 2]


def time_backward_kernel(count, scale, flags_ref, *refs):
    grads, slots = refs[:count], refs[count : 2 * count]
    qkv_ref, prob_ref, a1_ref, gather_ref, spread_ref, tp_ref, vec_ref, other_ref = refs[2 * count : 2 * count + 8]
    refs = refs[2 * count + 8 :]
    outs, (kept_ref, sent_ref, dqkv_ref, pair_s, weight_s) = refs[:count], refs[count:]
    part, features = grads[0].shape
    def chunk_step(index, carry):
        place = pl.ds(pl.multiple_of(index * CHUNK, CHUNK), CHUNK)
        def rows_of(s, third):
            start = pl.multiple_of(s * part + index * CHUNK, CHUNK)
            return qkv_ref[pl.ds(start, CHUNK), third * features:(third + 1) * features].astype(jnp.float32)
        queries, keys, values = ([rows_of(s, third) for s in range(count)] for third in range(3))
        outer = [grads[s][place].astype(jnp.float32) for s in range(count)]
        slopes = pair_sums(outer, values, gather_ref, pair_s)
        size = count * count * CHUNK
        for f in range(count):
            row = [slopes[(f * count + g) * CHUNK:(f * count + g + 1) * CHUNK] for g in range(count)]
            weights = [prob_ref[f * count + g, place] for g in range(count)]
            delta = functools.reduce(jnp.add, [w * s for w, s in zip(weights, row)])
            for g in range(count):
                at = (f * count + g) * CHUNK
                weight_s[at:at + CHUNK] = weights[g].astype(jnp.bfloat16)
                weight_s[size + at:size + at + CHUNK] = (weights[g] * (row[g] - delta)).astype(jnp.bfloat16)
        wide = contract(weight_s[...], spread_ref[...], (1, 0))
        for s in range(count):
            dq, dk, dv = 0.0, 0.0, 0.0
            for t in range(count):
                forth, back = (s * count + t) * CHUNK, (t * count + s) * CHUNK
                dq = dq + wide[size + forth:size + forth + CHUNK] * keys[t]
                dk = dk + wide[size + back:size + back + CHUNK] * queries[t]
                dv = dv + wide[back:back + CHUNK] * outer[t]
            start = pl.ds(pl.multiple_of(s * part + index * CHUNK, CHUNK), CHUNK)
            for third, value in enumerate((dq * scale, dk * scale, dv)):
                dqkv_ref[start, third * features:(third + 1) * features] = value.astype(jnp.bfloat16)
        return carry
    lax.fori_loop(0, part // CHUNK, chunk_step, 0)
    a1t = a1_ref[...].T
    put = functools.partial(put_rows, flags_ref, kept_ref, sent_ref, None)
    for third in range(3):
        span = slice(third * features, (third + 1) * features)
        put(third * features, contract(a1t, dqkv_ref[:, span], (1, 0)))
    grad = contract(dqkv_ref[...], tp_ref[...], (1, 1))
    gain, shift = 0.0, 0.0
    for s in range(count):
        piece = grad[s * part : (s + 1) * part]
        normed, spread = norm_parts(slots[s][...].astype(jnp.float32))
        outs[s][...] = norm_back(piece, normed, spread, vec_ref[0:1]).astype(jnp.bfloat16)
        gain = gain + column_sum(piece * normed)
        shift = shift + column_sum(piece)
    sums = [
        gain,
        shift,
        column_sum(dqkv_ref[:, :features].astype(jnp.float32)),
        column_sum(dqkv_ref[:, 2 * features :].astype(jnp.float32)),
        other_ref[4:5],
    ]
    put(3 * features, fill_rows(sums, 2 * kept_ref.shape[0] - 3 * features, features))


def time_backward(order, grads, slots, qkv, prob, a1, time_packed, vec, other):
    count = len(grads)
    part, features = grads[0].shape
    gather = head_map(features)
    low = jnp.bfloat16
    half = struct((round_up(3 * features + 16, 512) // 2, features), low)
    results = order.run(
        functools.partial(time_backward_kernel, count, (features // HEADS) ** -0.5),
        [order.flags, *grads, *slots, qkv, prob, a1, gather, gather.T, time_packed, vec, other],
        [SMEM] + [VMEM] * (2 * count + 5)
        + [pl.BlockSpec((features, 3 * features), lambda i: (0, 0)), VMEM, VMEM],
        [VMEM] * (count + 2),
        [struct((part, features), low)] * count + [half, half],
        grid=(1,),
        scratch=[
            pltpu.VMEM(qkv.shape, low),
            pltpu.VMEM((count * count * CHUNK, features), low),
            pltpu.VMEM((2 * count * count * CHUNK, 128), low),
        ],
    )
    return results[:count], results[count], results[count + 1]


def last_kernel(count, frame_flag, flags_ref, first_ref, *refs):
    slots, out_ref, rows_s = refs[:count], refs[count], refs[count + 1]
    gather_rows(count, flags_ref[frame_flag], slots, rows_s)
    rows = out_ref.shape[1]
    out_ref[0] = (first_ref[...] + rows_s[...].astype(jnp.float32))[:rows]


def add_branch(order, first, slots, row_count):
    features = first.shape[1]
    return order.run(
        functools.partial(last_kernel, len(slots), order.flags.shape[0] - 1),
        [order.flags, first, *slots],
        [SMEM] + [VMEM] * (len(slots) + 1),
        [VMEM],
        [struct((1, row_count, features), jnp.float32)],
        scratch=[pltpu.VMEM(first.shape, jnp.bfloat16)],
    )[0]


def body(
    tokens,
    size_tag,
    cotangent,
    time_project,
    time_output,
    time_vector,
    space_project,
    space_output,
    space_vector,
    feed_inner,
    feed_bias,
    feed_outer,
    feed_vector,
):
    frame_count = lax.axis_size("frame")
    batch_count = lax.axis_size("batch")
    sizes = (batch_count, frame_count)
    frame_index = lax.axis_index("frame")
    batch_index = lax.axis_index("batch")
    flags = [(batch_index >> bit) & 1 for bit in range(batch_count.bit_length() - 1)]
    flags += [(frame_index >> bit) & 1 for bit in range(frame_count.bit_length() - 1)]
    order = Order(jnp.stack([*flags, frame_index]).astype(jnp.int32))
    features = tokens.shape[2]
    row_count = tokens.shape[1]
    part = round_up(-(-PATCHES // frame_count), ROW_TILE)
    padded = part * frame_count
    token_rows = jnp.pad(tokens[0], ((0, padded - row_count), (0, 0)))
    grad_result = jnp.pad(cotangent[0], ((0, padded - row_count), (0, 0)))

    vectors = jnp.concatenate(
        [time_vector, space_vector, feed_vector, feed_bias.reshape(-1, time_vector.shape[1])], axis=0
    )
    vectors = lax.all_gather(vectors, "batch", axis=0)
    vec = vectors[:, :13].transpose(1, 0, 2).reshape(13, features).astype(jnp.float32)
    vec = jnp.pad(vec, ((0, 3), (0, 0)))
    feed_bias_row = vectors[:, 13:].reshape(1, -1).astype(jnp.float32)
    time_packed = lax.all_gather(
        jnp.concatenate([time_project, time_output], axis=1), "batch", axis=0, tiled=True
    )
    space_packed = lax.all_gather(
        jnp.concatenate([space_project, space_output], axis=1), "batch", axis=0, tiled=True
    )
    feed_inner_full = lax.all_gather(feed_inner, "batch", axis=0, tiled=True)
    feed_outer_full = lax.all_gather(feed_outer, "batch", axis=0, tiled=True)
    clip = jnp.concatenate(
        [
            jnp.arange(PATCHES, dtype=jnp.int32) // size_tag[0],
            jnp.arange(UNITS, dtype=jnp.int32),
            jnp.full((padded - PATCHES - UNITS,), -1, jnp.int32),
        ]
    )

    slots = rows_to_frames(token_rows, frame_count, frame_index)
    mixture_slots, qkv_time, prob_time, first_input = time_forward(order, slots, time_packed, vec)
    mixture_time, after_time, second_input, qkv_space = middle_forward(
        order, token_rows, send_back(mixture_slots), time_packed, space_packed, vec
    )
    mixture_space, total_space = space_forward(order, qkv_space, clip, features)
    (
        block_out,
        grad_second,
        grad_branch,
        grad_mixture,
        feed_grads,
        grad_feed_bias,
        feed_sums,
    ) = feed_block(
        order,
        after_time,
        mixture_space,
        grad_result,
        space_packed,
        feed_inner_full,
        feed_outer_full,
        feed_bias_row,
        vec,
        tile=features,
        chunks=2,
    )
    feed_total = lax.psum(feed_grads.reshape(-1, features), ("batch", "frame"))
    grad_query, grad_keys, grad_values = space_backward(
        order, qkv_space, mixture_space, total_space, grad_mixture, clip, features
    )
    grad_first, grad_patch, space_sums, grad_slots = middle_backward(
        order,
        frame_count,
        grad_query,
        grad_keys,
        grad_values,
        after_time,
        grad_second,
        time_packed,
        space_packed,
        vec,
    )
    grad_slots = [
        shift_frames(slot, frame_count, shift) for shift, slot in enumerate(grad_slots)
    ]
    space_kept, space_sent = middle_weights(
        order,
        sizes,
        second_input,
        grad_query,
        grad_keys,
        grad_values,
        mixture_time,
        grad_patch,
        mixture_space,
        grad_branch,
        space_sums,
        feed_sums,
        grad_feed_bias,
    )
    space_flight = Flight(sum_steps(space_kept, space_sent, sizes, False))
    input_slots, time_kept, time_sent = time_backward(
        order,
        grad_slots,
        slots,
        qkv_time,
        prob_time,
        first_input,
        time_packed,
        vec,
        space_sums,
    )
    time_flight = Flight(sum_steps(time_kept, time_sent, sizes, True))
    input_slots = send_back(input_slots)
    while space_flight.result is None:
        advance(order, time_flight, space_flight)
    space_total = lax.all_gather(space_flight.result, ("batch", "frame"), axis=0, tiled=True)
    advance(order, time_flight)
    grad_tokens = add_branch(order, grad_first, input_slots, row_count)
    while time_flight.result is None:
        advance(order, time_flight)
    block = 256
    per = features // block
    grad_feed_inner, grad_feed_outer = deliver(
        order, [feed_total], [(0, 4 * per, True), (4 * per, 8 * per, False)], block
    )
    count = 2 * time_flight.result[0].shape[0] // block
    grad_time_project, time_vectors = deliver(
        order, time_flight.result, [(0, 3 * per, True), (3 * per, count, False)], block
    )
    count = space_total.shape[0] // block
    grad_space_project, grad_time_output, grad_space_output, some_vectors = deliver(
        order,
        [space_total],
        [
            (0, 3 * per, True),
            (3 * per, 4 * per, False),
            (4 * per, 5 * per, False),
            (5 * per, count, False),
        ],
        block,
    )
    return (
        block_out[None, :row_count],
        grad_tokens,
        grad_time_project,
        grad_time_output,
        time_vectors[0:5],
        grad_space_project,
        grad_space_output,
        some_vectors[0:5],
        grad_feed_inner,
        some_vectors[8:12].reshape(-1),
        grad_feed_outer,
        some_vectors[5:8],
    )


def solution(mesh):
    placed = (
        P("frame", "batch", None),
        P("batch"),
        P("frame", "batch", None),
        P("batch", None),
        P("batch", None),
        P(None, "batch"),
        P("batch", None),
        P("batch", None),
        P(None, "batch"),
        P("batch", None),
        P("batch"),
        P("batch", None),
        P(None, "batch"),
    )
    return jax.shard_map(
        body,
        mesh=mesh,
        in_specs=placed,
        out_specs=(
            P("frame", "batch", None),
            P("frame", "batch", None),
            P(),
            P(),
            P(),
            P(),
            P(),
            P(),
            P(),
            P(),
            P(),
            P(),
        ),
        check_vma=False,
    )
```

time: 704 us -> 651 us (0.925)
  Pallas kernels: 168 us -> 251 us
  blocking collectives: 63.8 us -> 9.18 us
  other arithmetic: 52.6 us -> 5.31 us
  local copies, waits for them, and re-layouts: 55.1 us -> 30.7 us
  waiting for transfers between devices: 301 us -> 289 us
    pallas_call x9 -> x21, Pallas kernels: 168 us -> 251 us  [run(): pl.pallas_call(body, grid_spec=pltpu.PrefetchScalarGridSpec(num_scalar_pr...]
    psum x1, waiting for transfers between devices: 68 us -> 0.01 us  [body(): feed_total = lax.psum(feed_grads.reshape(-1, features), ('batch', 'frame'))]
    psum x1 -> x0, blocking collectives: 54.6 us -> none  [body(): vector_grads = lax.psum(vector_grads, ('batch', 'frame'))]
    ppermute x12, waiting for transfers between devices: 34.7 us -> 86.2 us  [shift_frames(): return lax.ppermute(block, 'frame', pairs)]
    ppermute x20 -> x21, waiting for transfers between devices: 144 us -> 118 us  [swap_bit(): return lax.ppermute(block, axis, pairs)]
    convert_element_type x14 -> x0, other arithmetic: 24.3 us -> none  [the longest x10 9.82 us: halve_sum(): (kept.astype(jnp.float32) + arrived.astype(jnp.float32)).astype(jnp.bfloa...]
    all_gather x0 -> x1, waiting for transfers between devices: none -> 18.8 us  [body(): lax.all_gather(space_flight.result, ('batch', 'frame'), axis=0, tiled=True)]
    all_gather x1, waiting for transfers between devices: 0.02 us -> 15.1 us  [body(): lax.all_gather(jnp.concatenate([space_project, space_output], axis=1), 'b...]
  transfers between devices with their start and end apart: 37 -> 39, of which waited for: 21 -> 24; matrix products, arithmetic and copies ran while one was open for 11% -> 3% of each run, Pallas kernels for 12% -> 21%
where the time goes in v3:
time: 651 us; the launch traced here: 644 us
  waiting for transfers between devices  289 us (44%)
  Pallas kernels  251 us (39%)
  starting transfers between devices  43.2 us (7%)
  local copies, waits for them, and re-layouts  30.7 us (5%)
  between operations  15.4 us (2%)
  blocking collectives  9.18 us (1%)
    pallas_call x21, Pallas kernels, run(): pl.pallas_call(body, grid_spec=pltpu.PrefetchScalarGridSpec(num_scalar_pr...  251 us
    ppermute x21, waiting for transfers between devices, swap_bit(): return lax.ppermute(block, axis, pairs)  118 us
    ppermute x12, waiting for transfers between devices, shift_frames(): return lax.ppermute(block, 'frame', pairs)  86.2 us
    all_gather x1, waiting for transfers between devices, body(): feed_outer_full = lax.all_gather(feed_outer, 'batch', axis=0, tiled=True)  40.7 us
    ppermute x21, starting transfers between devices, swap_bit(): return lax.ppermute(block, axis, pairs)  21.9 us
    ppermute x12, starting transfers between devices, shift_frames(): return lax.ppermute(block, 'frame', pairs)  21 us
    all_gather x1, waiting for transfers between devices, body(): lax.all_gather(space_flight.result, ('batch', 'frame'), axis=0, tiled=True)  18.8 us
    unnamed x95, local copies, waits for them, and re-layouts  17.6 us
  transfers between devices with their start and end apart: 39, of which 24 were waited for; matrix products, arithmetic and copies ran while one was open for 3% of the time, Pallas kernels for 21%

profile of v3, /device:TPU:0, one launch (start us, length us, event | category | flops | bytes accessed | tf_op | source)
XLA Modules:
  0.0 644.1 jit_solution(2879044834841404203)
XLA Ops:
  19.9 9.2 %all-gather.1 = bf16[8,17,96]{2,1,0:T(8,128)(2,1)S(1)} all-gather(bf16[1,17,96]{2,1,0:T(8,128)(2,1)S(1)} %maximum_bitcast_fusion), channel_id=2, replica_groups=mesh['batch'=8,'frame'=4] {'batch'}, dimensions={0}, use_global_device_ids=true | all-gather | bytes 29376 | tf_op jit(solution)/shard_map/all_gather | solution.py:915
  33.9 11.4 %collective-permute-done.1.refs_2_.refs_8_ = bf16[208,768]{1,0:T(8,128)(2,1)S(1)} collective-permute-done((bf16[208,768]{1,0:T(8,128)(2,1)S(1)}, bf16[208,768]{1,0:T(8,128)(2,1)S(1)}, u32[]{:S(2)}, u32[]{:S(2)}) %collective-permute-start.1) | collective-permute-done | bytes 319520 | tf_op jit(solution)/shard_map/ppermute | solution.py:66
  52.3 16.5 %shard_map.220 = (bf16[208,768]{1,0:T(8,128)(2,1)}, bf16[208,768]{1,0:T(8,128)(2,1)}, bf16[208,768]{1,0:T(8,128)(2,1)}, bf16[208,768]{1,0:T(8,128)(2,1)}, bf16[8...) custom-call(bf16[208,768]{1,0:T(8,128)(2,1)} %get-tuple-element.247.refs_0_.refs_6_,, ...), custom_call_target="tpu_custom_call" | custom-call | tf_op jit(solution)/shard_map/pallas_call | solution.py:46
  78.6 15.1 %all-gather.10.cloned.1.call-done.refs_8_.refs_4_ = bf16[768,3072]{1,0:T(8,128)(2,1)} async-done(((bf16[96,3072]{1,0:T(8,128)(2,1)}), bf16[768,3072]{1,0:T(8,128)(2,1)}) %all-gather.10.cloned.1.call-update) | async-done | bytes 4718608 | tf_op jit(solution)/shard_map/all_gather | solution.py:922
  101.1 10.8 %shard_map.221 = (bf16[832,768]{1,0:T(8,128)(2,1)}, f32[832,768]{1,0:T(8,128)}, bf16[832,768]{1,0:T(8,128)(2,1)}, bf16[832,2304]{1,0:T(8,128)(2,1)}, f32[8,128]{1,0:T(8,128)}) custom-call(f32[8,128]{1,0:T(8,128)} %get-tuple-element.111.refs_0_, s32[6]{0:T(128)} %stack.27.refs_1_.refs_0_, bf16[832,768]{1,0:T(8,128)(2,1)} %pad.18.refs_2_, ...), custom_call_target="tpu_custom_call" | custom-call | tf_op jit(solution)/shard_map/pallas_call | solution.py:46
  111.9 19.7 %shard_map.222 = (bf16[832,768]{1,0:T(8,128)(2,1)}, f32[832,768]{1,0:T(8,128)}, f32[8,128]{1,0:T(8,128)}) custom-call(f32[8,128]{1,0:T(8,128)} %get-tuple-element.116.refs_0_, s32[832,1]{1,0:T(8,128)} %broadcast_in_dim.22.refs_1_, s32[1,896]{1,0:T(1,128)} %broadcast_in_dim.20.refs_2_, bf16[832,2304]{1,0:T(8,128)(2,1)} %get-tuple-element.117.refs_3_.refs_4_.refs_5_, ...), custom_call_target="tpu_custom_call" | custom-call | tf_op jit(solution)/shard_map/pallas_call | solution.py:46
  134.5 40.7 %all-gather.14.cloned.1.call-done.refs_6_ = bf16[3072,768]{1,0:T(8,128)(2,1)} async-done(((bf16[384,768]{1,0:T(8,128)(2,1)}), bf16[3072,768]{1,0:T(8,128)(2,1)}) %all-gather.14.cloned.1.call-update) | async-done | bytes 4718608 | tf_op jit(solution)/shard_map/all_gather | solution.py:926
  175.2 40.9 %shard_map.223 = (bf16[832,768]{1,0:T(8,128)(2,1)}, f32[832,768]{1,0:T(8,128)}, bf16[832,768]{1,0:T(8,128)(2,1)}, bf16[832,768]{1,0:T(8,128)(2,1)}, bf16[2,3072,...) custom-call(f32[8,128]{1,0:T(8,128)} %get-tuple-element.118.refs_0_, ...), custom_call_target="tpu_custom_call" | custom-call | tf_op jit(solution)/shard_map/pallas_call | solution.py:46
  216.1 30.5 %shard_map.224 = (bf16[832,768]{1,0:T(8,128)(2,1)}, bf16[832,768]{1,0:T(8,128)(2,1)}, bf16[832,768]{1,0:T(8,128)(2,1)}, f32[8,128]{1,0:T(8,128)}) custom-call(f32[8,128]{1,0:T(8,128)} %get-tuple-element.122.refs_0_, s32[832,1]{1,0:T(8,128)} %broadcast_in_dim.22.refs_1_, s32[1,896]{1,0:T(1,128)} %broadcast_in_dim.20.refs_2_, ...), custom_call_target="tpu_custom_call" | custom-call | tf_op jit(solution)/shard_map/pallas_call | solution.py:46
  246.6 13.8 %shard_map.225 = (f32[832,768]{1,0:T(8,128)}, bf16[832,768]{1,0:T(8,128)(2,1)}, f32[8,768]{1,0:T(8,128)}, bf16[208,768]{1,0:T(8,128)(2,1)}, bf16[208,768]{1,0:T(...) custom-call(f32[8,128]{1,0:T(8,128)} %get-tuple-element.125.refs_0_, ...), custom_call_target="tpu_custom_call" | custom-call | tf_op jit(solution)/shard_map/pallas_call | solution.py:46
  260.4 16.4 %shard_map.226 = (bf16[2048,768]{1,0:T(8,128)(2,1)}, bf16[2048,768]{1,0:T(8,128)(2,1)}, f32[8,128]{1,0:T(8,128)}) custom-call(f32[8,128]{1,0:T(8,128)} %get-tuple-element.130.refs_0_, s32[6]{0:T(128)} %stack.27.refs_1_.refs_0_, bf16[832,768]{1,0:T(8,128)(2,1)} %get-tuple-element.131.refs_2_, bf16[832,768]{1,0:T(8,128)(2,1)} %get-tuple-element.126.refs_2_.refs_3_, ...), custom_call_target="tpu_custom_call" | custom-call | tf_op jit(solution)/shard_map/pallas_call | solution.py:46
  282.5 10.0 %collective-permute-done.6.refs_3_ = bf16[208,768]{1,0:T(8,128)(2,1)S(1)} collective-permute-done((bf16[208,768]{1,0:T(8,128)(2,1)}, bf16[208,768]{1,0:T(8,128)(2,1)S(1)}, u32[]{:S(2)}, u32[]{:S(2)}) %collective-permute-start.6) | collective-permute-done | bytes 319520 | tf_op jit(solution)/shard_map/ppermute | solution.py:66
  292.6 17.0 %collective-permute-done.7.refs_4_ = bf16[208,768]{1,0:T(8,128)(2,1)S(1)} collective-permute-done((bf16[208,768]{1,0:T(8,128)(2,1)}, bf16[208,768]{1,0:T(8,128)(2,1)S(1)}, u32[]{:S(2)}, u32[]{:S(2)}) %collective-permute-start.7) | collective-permute-done | bytes 319520 | tf_op jit(solution)/shard_map/ppermute | solution.py:66
  314.0 26.6 %shard_map.227 = (bf16[208,768]{1,0:T(8,128)(2,1)}, bf16[208,768]{1,0:T(8,128)(2,1)}, bf16[208,768]{1,0:T(8,128)(2,1)}, bf16[208,768]{1,0:T(8,128)(2,1)}, bf16[1...) custom-call(f32[8,128]{1,0:T(8,128)} %get-tuple-element.138.refs_0_, s32[6]{0:T(128)} %stack.27.refs_1_.refs_0_, ...), custom_call_target="tpu_custom_call" | custom-call | tf_op jit(solution)/shard_map/pallas_call | solution.py:46
  347.1 8.0 %shard_map.228 = (bf16[320,768]{1,0:T(8,128)(2,1)}, bf16[320,768]{1,0:T(8,128)(2,1)}, bf16[320,768]{1,0:T(8,128)(2,1)}, bf16[320,768]{1,0:T(8,128)(2,1)}, bf16[5...) custom-call(f32[8,128]{1,0:T(8,128)} %get-tuple-element.146.refs_0_,, ...), custom_call_target="tpu_custom_call" | custom-call | tf_op jit(solution)/shard_map/pallas_call | solution.py:46
  359.2 34.1 %collective-permute-done.11.refs_3_ = bf16[320,768]{1,0:T(8,128)(2,1)S(1)} collective-permute-done((bf16[320,768]{1,0:T(8,128)(2,1)}, bf16[320,768]{1,0:T(8,128)(2,1)S(1)}, u32[]{:S(2)}, u32[]{:S(2)}) %collective-permute-start.11) | collective-permute-done | bytes 491552 | tf_op jit(solution)/shard_map/ppermute | solution.py:85
  406.3 15.1 %collective-permute-done.15.refs_3_ = bf16[160,768]{1,0:T(8,128)(2,1)S(1)} collective-permute-done((bf16[160,768]{1,0:T(8,128)(2,1)}, bf16[160,768]{1,0:T(8,128)(2,1)S(1)}, u32[]{:S(2)}, u32[]{:S(2)}) %collective-permute-start.15) | collective-permute-done | bytes 245792 | tf_op jit(solution)/shard_map/ppermute | solution.py:85
  430.1 22.3 %collective-permute-done.19.refs_3_ = bf16[160,768]{1,0:T(8,128)(2,1)S(1)} collective-permute-done((bf16[160,768]{1,0:T(8,128)(2,1)}, bf16[160,768]{1,0:T(8,128)(2,1)S(1)}, u32[]{:S(2)}, u32[]{:S(2)}) %collective-permute-start.19) | collective-permute-done | bytes 245792 | tf_op jit(solution)/shard_map/ppermute | solution.py:85
  458.6 19.4 %collective-permute-done.21.refs_3_ = bf16[80,768]{1,0:T(8,128)(2,1)S(1)} collective-permute-done((bf16[80,768]{1,0:T(8,128)(2,1)}, bf16[80,768]{1,0:T(8,128)(2,1)S(1)}, u32[]{:S(2)}, u32[]{:S(2)}) %collective-permute-start.21) | collective-permute-done | bytes 122912 | tf_op jit(solution)/shard_map/ppermute | solution.py:85
  500.5 31.4 %collective-permute-done.25.refs_5_ = bf16[208,768]{1,0:T(8,128)(2,1)S(1)} collective-permute-done((bf16[208,768]{1,0:T(8,128)(2,1)S(1)}, bf16[208,768]{1,0:T(8,128)(2,1)S(1)}, u32[]{:S(2)}, u32[]{:S(2)}) %collective-permute-start.25) | collective-permute-done | bytes 319520 | tf_op jit(solution)/shard_map/ppermute | solution.py:66
  570.0 18.7 %shard_map.238 = (f32[768,3072]{1,0:T(8,128)}, f32[3072,768]{1,0:T(8,128)}, f32[8,128]{1,0:T(8,128)}) custom-call(s32[6]{0:T(128)} %stack.27.refs_1_.refs_0_, f32[8,128]{1,0:T(8,128)} %get-tuple-element.196.refs_1_, bf16[6144,768]{1,0:T(8,128)(2,1)} %all-reduce.6.cloned.1.call-done.refs_2_), custom_call_target="tpu_custom_call" | custom-call | tf_op jit(solution)/shard_map/pallas_call | solution.py:46
  589.9 9.3 %shard_map.239 = (f32[768,2304]{1,0:T(8,128)}, f32[256,768]{1,0:T(8,128)}, f32[8,128]{1,0:T(8,128)}) custom-call(s32[6]{0:T(128)} %stack.27.refs_1_.refs_0_, f32[8,128]{1,0:T(8,128)} %get-tuple-element.198.refs_1_, bf16[1280,768]{1,0:T(8,128)(2,1)} %get-tuple-element.199.refs_2_, bf16[1280,768]{1,0:T(8,128)(2,1)} %copy-done.4), custom_call_target="tpu_custom_call" | custom-call | tf_op jit(solution)/shard_map/pallas_call | solution.py:46
  600.6 18.8 %all-gather.16.cloned.1.call-done.refs_2_ = bf16[4096,768]{1,0:T(8,128)(2,1)} async-done(((bf16[128,768]{1,0:T(8,128)(2,1)}), bf16[4096,768]{1,0:T(8,128)(2,1)}) %all-gather.16.cloned.1.call-update) | async-done | bytes 6291472 | tf_op jit(solution)/shard_map/all_gather | solution.py:1012
  619.3 13.6 %shard_map.240 = (f32[768,2304]{1,0:T(8,128)}, f32[768,768]{1,0:T(8,128)}, f32[768,768]{1,0:T(8,128)}, f32[256,768]{1,0:T(8,128)}, f32[8,128]{1,0:T(8,128)}) custom-call(s32[6]{0:T(128)} %stack.27.refs_1_.refs_0_, f32[8,128]{1,0:T(8,128)} %get-tuple-element.201.refs_1_, bf16[4096,768]{1,0:T(8,128)(2,1)} %all-gather.16.cloned.1.call-done.refs_2_), custom_call_target="tpu_custom_call" | custom-call | tf_op jit(solution)/shard_map/pallas_call | solution.py:46
  (207 shorter events, 159.3 us)
Async XLA Ops:
  7.2 45.1 %all-gather.8.cloned.1.call-start = ((), (), s32[]{:S(2)}) async-start(), calls=%async_computation | async-start | bytes 5308416 | tf_op jit(solution)/shard_map/all_gather | solution.py:919
  9.3 84.4 %all-gather.10.cloned.1.call-start = ((), (), s32[]{:S(2)}) async-start(), calls=%async_computation.1 | async-start | bytes 5308416 | tf_op jit(solution)/shard_map/all_gather | solution.py:922
  10.2 124.3 %all-gather.12.cloned.1.call-start = ((), (), s32[]{:S(2)}) async-start(), calls=%async_computation.2 | async-start | bytes 5308416 | tf_op jit(solution)/shard_map/all_gather | solution.py:925
  11.0 164.2 %all-gather.14.cloned.1.call-start = ((), (), s32[]{:S(2)}) async-start(), calls=%async_computation.3 | async-start | bytes 5308416 | tf_op jit(solution)/shard_map/all_gather | solution.py:926
  11.6 558.3 %all-reduce.6.cloned.1.call-start = ((), (), s32[]{:S(2)}) async-start(), calls=%async_computation.4 | async-start | bytes 18874368 | tf_op jit(solution)/shard_map/psum | solution.py:962
  18.1 27.2 %collective-permute-start.1 = (bf16[208,768]{1,0:T(8,128)(2,1)S(1)}, bf16[208,768]{1,0:T(8,128)(2,1)S(1)}, u32[]{:S(2)}, u32[]{:S(2)}) collective-permute-start(bf16[208,768]{1,0:T(8,128)(2,1)S(1)} %get-tuple-element.249), channel_id=1, source_target_pairs={{0,2},{1,3},{2,0},{3,1},{4,6},{5,7},{6,4},{7,5},{8,10},{9,11},{10,... | collective-permute-start | bytes 958472 | tf_op jit(solution)/shard_map/ppermute | solution.py:66
  68.8 24.9 %collective-permute-start.3 = (bf16[208,768]{1,0:T(8,128)(2,1)}, bf16[208,768]{1,0:T(8,128)(2,1)S(1)}, u32[]{:S(2)}, u32[]{:S(2)}) collective-permute-start(bf16[208,768]{1,0:T(8,128)(2,1)} %get-tuple-element.113), channel_id=1, source_target_pairs={{0,3},{1,0},{2,1},{3,2},{4,7},{5,4},{6,5},{7,6},{8,11},{9,8},{10,9... | collective-permute-start | bytes 958472 | tf_op jit(solution)/shard_map/ppermute | solution.py:66
  72.2 28.1 %collective-permute-start.4 = (bf16[208,768]{1,0:T(8,128)(2,1)}, bf16[208,768]{1,0:T(8,128)(2,1)S(1)}, u32[]{:S(2)}, u32[]{:S(2)}) collective-permute-start(bf16[208,768]{1,0:T(8,128)(2,1)} %get-tuple-element.114), channel_id=1, source_target_pairs={{0,2},{1,3},{2,0},{3,1},{4,6},{5,7},{6,4},{7,5},{8,10},{9,11},{10,... | collective-permute-start | bytes 958472 | tf_op jit(solution)/shard_map/ppermute | solution.py:66
  72.2 28.1 %collective-permute-start.5 = (bf16[208,768]{1,0:T(8,128)(2,1)}, bf16[208,768]{1,0:T(8,128)(2,1)S(1)}, u32[]{:S(2)}, u32[]{:S(2)}) collective-permute-start(bf16[208,768]{1,0:T(8,128)(2,1)} %get-tuple-element.115), channel_id=1, source_target_pairs={{0,1},{1,2},{2,3},{3,0},{4,5},{5,6},{6,7},{7,4},{8,9},{9,10},{10,1... | collective-permute-start | bytes 958472 | tf_op jit(solution)/shard_map/ppermute | solution.py:66
  276.8 68.1 %collective-permute-start.10 = (bf16[2048,768]{1,0:T(8,128)(2,1)}, bf16[2048,768]{1,0:T(8,128)(2,1)S(1)}, u32[]{:S(2)}, u32[]{:S(2)}) collective-permute-start(bf16[2048,768]{1,0:T(8,128)(2,1)} %get-tuple-element.150), channel_id=1, source_target_pairs={{0,4},{4,0},{8,12},{12,8},{16,20},{20,16},{24,28},{28,24},{1,5},{5... | collective-permute-start | bytes 9437192 | tf_op jit(solution)/shard_map/ppermute | solution.py:85
  277.1 342.3 %all-gather.16.cloned.1.call-start = ((), (), s32[]{:S(2)}) async-start(), calls=%async_computation.5 | async-start | bytes 6488064 | tf_op jit(solution)/shard_map/all_gather | solution.py:1012
  278.7 30.9 %collective-permute-start.7 = (bf16[208,768]{1,0:T(8,128)(2,1)}, bf16[208,768]{1,0:T(8,128)(2,1)S(1)}, u32[]{:S(2)}, u32[]{:S(2)}) collective-permute-start(bf16[208,768]{1,0:T(8,128)(2,1)} %get-tuple-element.141), channel_id=1, source_target_pairs={{0,2},{1,3},{2,0},{3,1},{4,6},{5,7},{6,4},{7,5},{8,10},{9,11},{10,... | collective-permute-start | bytes 958472 | tf_op jit(solution)/shard_map/ppermute | solution.py:66
  281.1 32.2 %collective-permute-start.8 = (bf16[208,768]{1,0:T(8,128)(2,1)S(1)}, bf16[208,768]{1,0:T(8,128)(2,1)S(1)}, u32[]{:S(2)}, u32[]{:S(2)}) collective-permute-start(bf16[208,768]{1,0:T(8,128)(2,1)S(1)} %copy-done.46), channel_id=1, source_target_pairs={{0,3},{1,0},{2,1},{3,2},{4,7},{5,4},{6,5},{7,6},{8,11},{9,8},{10,9... | collective-permute-start | bytes 958472 | tf_op jit(solution)/shard_map/ppermute | solution.py:66
  355.1 41.0 %collective-permute-start.13 = (bf16[512,768]{1,0:T(8,128)(2,1)}, bf16[512,768]{1,0:T(8,128)(2,1)S(1)}, u32[]{:S(2)}, u32[]{:S(2)}) collective-permute-start(bf16[512,768]{1,0:T(8,128)(2,1)} %get-tuple-element.157), channel_id=1, source_target_pairs={{0,8},{4,12},{8,0},{12,4},{16,24},{20,28},{24,16},{28,20},{1,9},{5... | collective-permute-start | bytes 2359304 | tf_op jit(solution)/shard_map/ppermute | solution.py:85
  356.6 39.5 %collective-permute-start.14 = (bf16[512,768]{1,0:T(8,128)(2,1)}, bf16[512,768]{1,0:T(8,128)(2,1)S(1)}, u32[]{:S(2)}, u32[]{:S(2)}) collective-permute-start(bf16[512,768]{1,0:T(8,128)(2,1)} %get-tuple-element.159), channel_id=1, source_target_pairs={{0,16},{4,20},{8,24},{12,28},{16,0},{20,4},{24,8},{28,12},{1,17},{... | collective-permute-start | bytes 2359304 | tf_op jit(solution)/shard_map/ppermute | solution.py:85
  357.1 36.2 %collective-permute-start.11 = (bf16[320,768]{1,0:T(8,128)(2,1)}, bf16[320,768]{1,0:T(8,128)(2,1)S(1)}, u32[]{:S(2)}, u32[]{:S(2)}) collective-permute-start(bf16[320,768]{1,0:T(8,128)(2,1)} %get-tuple-element.153), channel_id=1, source_target_pairs={{0,8},{4,12},{8,0},{12,4},{16,24},{20,28},{24,16},{28,20},{1,9},{5... | collective-permute-start | bytes 1474568 | tf_op jit(solution)/shard_map/ppermute | solution.py:85
  358.4 37.7 %collective-permute-start.12 = (bf16[320,768]{1,0:T(8,128)(2,1)}, bf16[320,768]{1,0:T(8,128)(2,1)S(1)}, u32[]{:S(2)}, u32[]{:S(2)}) collective-permute-start(bf16[320,768]{1,0:T(8,128)(2,1)} %get-tuple-element.155), channel_id=1, source_target_pairs={{0,16},{4,20},{8,24},{12,28},{16,0},{20,4},{24,8},{28,12},{1,17},{... | collective-permute-start | bytes 1474568 | tf_op jit(solution)/shard_map/ppermute | solution.py:85
  425.8 26.6 %collective-permute-start.20 = (bf16[256,768]{1,0:T(8,128)(2,1)}, bf16[256,768]{1,0:T(8,128)(2,1)S(1)}, u32[]{:S(2)}, u32[]{:S(2)}) collective-permute-start(bf16[256,768]{1,0:T(8,128)(2,1)} %get-tuple-element.173), channel_id=1, source_target_pairs={{0,1},{1,0},{2,3},{3,2},{4,5},{5,4},{6,7},{7,6},{8,9},{9,8},{10,11... | collective-permute-start | bytes 1179656 | tf_op jit(solution)/shard_map/ppermute | solution.py:85
  430.0 22.4 %collective-permute-start.19 = (bf16[160,768]{1,0:T(8,128)(2,1)}, bf16[160,768]{1,0:T(8,128)(2,1)S(1)}, u32[]{:S(2)}, u32[]{:S(2)}) collective-permute-start(bf16[160,768]{1,0:T(8,128)(2,1)} %get-tuple-element.171), channel_id=1, source_target_pairs={{0,1},{1,0},{2,3},{3,2},{4,5},{5,4},{6,7},{7,6},{8,9},{9,8},{10,11... | collective-permute-start | bytes 737288 | tf_op jit(solution)/shard_map/ppermute | solution.py:85
  455.7 22.3 %collective-permute-start.22 = (bf16[128,768]{1,0:T(8,128)(2,1)}, bf16[128,768]{1,0:T(8,128)(2,1)S(1)}, u32[]{:S(2)}, u32[]{:S(2)}) collective-permute-start(bf16[128,768]{1,0:T(8,128)(2,1)} %get-tuple-element.178), channel_id=1, source_target_pairs={{0,2},{1,3},{2,0},{3,1},{4,6},{5,7},{6,4},{7,5},{8,10},{9,11},{10,... | collective-permute-start | bytes 589832 | tf_op jit(solution)/shard_map/ppermute | solution.py:85
  483.2 48.7 %collective-permute-start.25 = (bf16[208,768]{1,0:T(8,128)(2,1)S(1)}, bf16[208,768]{1,0:T(8,128)(2,1)S(1)}, u32[]{:S(2)}, u32[]{:S(2)}) collective-permute-start(bf16[208,768]{1,0:T(8,128)(2,1)S(1)} %copy-done.44), channel_id=1, source_target_pairs={{0,2},{1,3},{2,0},{3,1},{4,6},{5,7},{6,4},{7,5},{8,10},{9,11},{10,... | collective-permute-start | bytes 958472 | tf_op jit(solution)/shard_map/ppermute | solution.py:66
  485.2 46.8 %collective-permute-start.26 = (bf16[208,768]{1,0:T(8,128)(2,1)S(1)}, bf16[208,768]{1,0:T(8,128)(2,1)S(1)}, u32[]{:S(2)}, u32[]{:S(2)}) collective-permute-start(bf16[208,768]{1,0:T(8,128)(2,1)S(1)} %copy-done.43), channel_id=1, source_target_pairs={{0,1},{1,2},{2,3},{3,0},{4,5},{5,6},{6,7},{7,4},{8,9},{9,10},{10,1... | collective-permute-start | bytes 958472 | tf_op jit(solution)/shard_map/ppermute | solution.py:66
  494.8 42.0 %collective-permute-start.27 = (bf16[160,768]{1,0:T(8,128)(2,1)}, bf16[160,768]{1,0:T(8,128)(2,1)S(1)}, u32[]{:S(2)}, u32[]{:S(2)}) collective-permute-start(bf16[160,768]{1,0:T(8,128)(2,1)} %get-tuple-element.189.refs_2_), channel_id=1, source_target_pairs={{0,1},{1,0},{2,3},{3,2},{4,5},{5,4},{6,7},{7,6},{8,9},{9,8},{10,11... | collective-permute-start | bytes 737288 | tf_op jit(solution)/shard_map/ppermute | solution.py:85
  563.9 24.7 %collective-permute-start.32 = (bf16[1280,768]{1,0:T(8,128)(2,1)}, bf16[1280,768]{1,0:T(8,128)(2,1)S(1)}, u32[]{:S(2)}, u32[]{:S(2)}) collective-permute-start(bf16[1280,768]{1,0:T(8,128)(2,1)} %get-tuple-element.199.refs_2_), channel_id=1, source_target_pairs={{0,4},{4,0},{8,12},{12,8},{16,20},{20,16},{24,28},{28,24},{1,5},{5... | collective-permute-start | bytes 5898248 | tf_op jit(solution)/shard_map/ppermute | solution.py:85
  (62 other events, 597.7 us)
Sparse Core Ops, SparseCore 0:
  10.5 41.7 all-gather.7
  54.7 38.9 all-gather.9
  95.6 38.9 all-gather.11
  136.3 38.9 all-gather.13
  277.2 269.1 all-reduce.5
  549.5 69.8 all-gather.15

commit v4 on v3

--- a/solution.py
+++ b/solution.py
@@ -13,6 +13,7 @@
 PATCHES = 784
 LOG2E = 1.4426950408889634
 ROW_TILE = 16
+FEED_BLOCKS = 8
 
 
 def round_up(count, step):
@@ -32,8 +33,10 @@
         self.flags = flags
         self.token = None
 
-    def run(self, kernel, operands, in_specs, out_specs, out_shape, grid=(), scratch=(), prefetch=0):
-        token = [] if self.token is None else [self.token]
+    def run(
+        self, kernel, operands, in_specs, out_specs, out_shape, grid=(), scratch=(), prefetch=0, after=()
+    ):
+        token = [*after] if self.token is None else [self.token, *after]
         inputs, outputs, ordered = len(operands), len(out_shape), len(token)
 
         def body(*refs):
@@ -128,7 +131,7 @@
             at += rows
 
 
-def shuffle(order, requests):
+def shuffle(order, requests, after):
     sources, plan, counts = [], [], []
     for own_sources, own_plan in requests:
         base = len(sources)
@@ -137,7 +140,7 @@
             return tuple((source + base, start) for source, start in terms)
 
         plan += [
-            [(rows, flag, lift(low), lift(high)) for rows, flag, low, high in out] for out in own_plan
+            [(rows, flag, *map(lift, choices)) for rows, flag, *choices in out] for out in own_plan
         ]
         sources += own_sources
         counts.append(len(own_plan))
@@ -149,6 +152,7 @@
         [SMEM] + [VMEM] * len(sources),
         [VMEM] * len(plan),
         shapes,
+        after=after,
     )
     outputs = []
     for count in counts:
@@ -168,31 +172,58 @@
     return [(rows, flag, (own,), (arrived,)), (rows, flag, (arrived,), (own,))]
 
 
-def sum_order(piece, sizes, rows):
-    batch_bits, frame_bits = (size.bit_length() - 1 for size in sizes)
-    batch, frame = divmod(piece, sizes[1])
-    wide = list(range(1, batch_bits))
-    size = rows // 4
-    start = (batch & 1) * 2 * size + (frame & 1) * size
-    for bit in wide[::-1] if frame & 1 else wide:
-        size //= 2
-        start += ((batch >> bit) & 1) * size
-    for bit in range(1, frame_bits):
-        size //= 2
-        start += ((frame >> bit) & 1) * size
-    return start
-
-
-def sum_steps(kept, sent, sizes, spread):
-    batch_bits, frame_bits = (size.bit_length() - 1 for size in sizes)
-    wide = list(range(1, batch_bits))
+def frame_parts(rows, frame_count, flag, terms_at):
+    part = rows // frame_count
+    return [
+        [
+            (part, flag)
+            + tuple(terms_at((frame + shift) % frame_count * part) for frame in range(frame_count))
+        ]
+        for shift in range(frame_count)
+    ]
+
+
+def send_parts(parts):
+    return [shift_frames(part, len(parts), shift) for shift, part in enumerate(parts)]
+
+
+def add_parts(rows, flag, frame_count):
+    terms = tuple((source, 0) for source in range(frame_count))
+    return [[(rows // frame_count, flag, *[terms] * frame_count)]]
+
+
+def frame_steps(block, frame_count, flag):
+    (block,) = yield [block]
+    rows = block.shape[0]
+    parts = yield [block], frame_parts(rows, frame_count, flag, lambda at: ((0, at),))
+    parts = yield send_parts(parts)
+    return list(parts), add_parts(rows, flag, frame_count)
+
+
+def core_steps(pairs, batch_size):
+    moved = yield [swap_bit(sent, "batch", batch_size, 0) for _, sent in pairs]
+    sources, segments = [], []
+    for (kept, _), arrived in zip(pairs, moved):
+        terms = ((len(sources), 0), (len(sources) + 1, 0))
+        segments.append((kept.shape[0], 0, terms, terms))
+        sources += [kept, arrived]
+    return sources, [segments]
+
+
+def sum_chips(block, batch_size):
+    groups = [list(range(core, batch_size, 2)) for core in range(2)]
+    return lax.psum_scatter(
+        block, "batch", scatter_dimension=0, axis_index_groups=groups, tiled=True
+    )
+
+
+def sum_steps(kept, sent, sizes, flag):
+    wide = list(range(1, sizes[0].bit_length() - 1))
     ways = (wide, wide[::-1])
+    frame_count = sizes[1]
 
     def over_batch(block, bit):
         return swap_bit(block, "batch", sizes[0], bit)
-
-    def over_frame(block, bit):
-        return swap_bit(block, "frame", sizes[1], bit)
 
     (arrived,) = yield [over_batch(sent, 0)]
     rows = kept.shape[0] // 2
@@ -207,25 +238,21 @@
         sources = [first_kept, moved[0], second_kept, moved[1]]
         pairs = [((0, 0), (1, 0)), ((2, 0), (3, 0))]
         rows //= 2
-    flag = batch_bits
-    plan = [[(rows, flag, pairs[1], pairs[0])], [(rows, flag, pairs[0], pairs[1])]]
-    for bit in range(frame_bits):
-        if bit:
-            rows //= 2
-            plan = split_plan(2 * rows, flag + bit, (0, 0), (1, 0))
-        sent, kept = yield sources, plan
-        (arrived,) = yield [over_frame(sent, bit)]
-        sources = [kept, arrived]
-    (block,) = yield sources, [[(rows, flag, ((0, 0), (1, 0)), ((0, 0), (1, 0)))]]
-    if not spread:
-        return block
-    for bit in range(frame_bits)[:0:-1]:
-        (arrived,) = yield [over_frame(block, bit)]
-        (block,) = yield [block, arrived], [join_plan(rows, flag + bit, (0, 0), (1, 0))]
-        rows *= 2
-    (arrived,) = yield [over_frame(block, 0)]
-    plan = [[(rows, flag, ((0, 0),), ((1, 0),))], [(rows, flag, ((1, 0),), ((0, 0),))]]
-    blocks = yield [block, arrived], plan
+
+    def terms_at(start):
+        (left, right), at = pairs[start // rows], start % rows
+        return (left[0], left[1] + at), (right[0], right[1] + at)
+
+    parts = yield sources, frame_parts(2 * rows, frame_count, flag, terms_at)
+    parts = yield send_parts(parts)
+    (part,) = yield parts, add_parts(2 * rows, flag, frame_count)
+    parts = yield [shift_frames(part, frame_count, shift) for shift in range(frame_count)]
+    size = 2 * rows // frame_count
+    segments = [
+        (size, flag) + tuple((((frame - owner) % frame_count, 0),) for frame in range(frame_count))
+        for owner in range(frame_count)
+    ]
+    blocks = yield parts, [segments[: frame_count // 2], segments[frame_count // 2 :]]
     for level in range(len(wide))[::-1]:
         moved = yield [over_batch(block, way[level]) for block, way in zip(blocks, ways)]
         sources = [blocks[0], moved[0], blocks[1], moved[1]]
@@ -239,6 +266,44 @@
     return blocks[0], arrived
 
 
+def gather_steps(shard, batch_size):
+    wide = list(range(1, batch_size.bit_length() - 1))
+    ways = (wide, wide[::-1])
+    half = shard.shape[0] // 2
+
+    def over_batch(block, bit):
+        return swap_bit(block, "batch", batch_size, bit)
+
+    blocks = [shard[:half], shard[half:]]
+    done = [[], []]
+    for level in range(len(wide)):
+        moved = yield [over_batch(block, way[level]) for block, way in zip(blocks, ways)]
+        plan = []
+        for index, way in enumerate(ways):
+            bit, before = way[level], done[index]
+            done[index] = sorted([*before, bit])
+            segments = []
+            for place in range(2 ** len(done[index])):
+                value = {one: (place >> at) & 1 for at, one in enumerate(done[index])}
+                row = half * sum(value[one] << at for at, one in enumerate(before))
+                own, other = ((2 * index, row),), ((2 * index + 1, row),)
+                segments.append((half, bit, *((other, own) if value[bit] else (own, other))))
+            plan.append(segments)
+        if level == len(wide) - 1:
+            plan = [plan[0] + plan[1]]
+        blocks = yield [blocks[0], moved[0], blocks[1], moved[1]], plan
+    (block,) = blocks
+    (arrived,) = yield [over_batch(block, 0)]
+    segments = []
+    for place in range(batch_size):
+        for index in range(2):
+            row = (index * batch_size // 2 + (place >> 1)) * half
+            own, other = ((0, row),), ((1, row),)
+            segments.append((half, 0, *((other, own) if place & 1 else (own, other))))
+    (whole,) = yield [block, arrived], [segments]
+    return whole
+
+
 class Flight:
     def __init__(self, steps):
         self.steps, self.result = steps, None
@@ -252,72 +317,138 @@
             return None
 
 
-def advance(order, *flights):
+def advance(order, *flights, after=()):
     active, requests = [], []
     for flight in flights:
-        request = flight.send(flight.moved) if flight.result is None else None
+        if flight.result is not None:
+            continue
+        request = flight.send(flight.moved)
+        if request is None and isinstance(flight.result[0], list):
+            request = flight.result
         if request is not None:
             active.append(flight)
             requests.append(request)
     if requests:
-        for flight, outputs in zip(active, shuffle(order, requests)):
-            flight.moved = flight.send(outputs)
-
-
-def deliver_kernel(ranges, count, flags_ref, *refs):
-    own_ref, arrived_ref = refs[0], refs[1]
-    outputs = refs[len(refs) - len(ranges) :]
-    whole = len(refs) - len(ranges) == 1
-    step = pl.program_id(0)
-    own = (step < count // 2) == (flags_ref[0] == 0)
-    for output, (first, last, _) in zip(outputs, ranges):
-        here = (step >= first) & (step < last)
-
-        @pl.when(here if whole else here & own)
+        for flight, outputs in zip(active, shuffle(order, requests, after)):
+            if flight.result is None:
+                flight.moved = flight.send(outputs)
+            else:
+                flight.result = outputs
+
+
+def finish_together(order, *flights):
+    sources, segments = [], []
+    for flight in flights:
+        if flight.result is None:
+            flight.send(flight.moved)
+            parts, ((segment,),) = flight.result
+        else:
+            parts = flight.result
+            segment = (parts[0].shape[0], 0, ((0, 0),), ((0, 0),))
+        rows, flag, *choices = segment
+        base = len(sources)
+        segments.append(
+            (rows, flag, *[tuple((source + base, at) for source, at in terms) for terms in choices])
+        )
+        sources += parts
+    ((whole,),) = shuffle(order, [(sources, [segments])], ())
+    return whole
+
+
+def deliver_kernel(flags_ref, own_ref, arrived_ref, out_ref, rest_ref):
+    half, features = own_ref.shape
+    columns = out_ref.shape[1] // features
+    for core in range(2):
+
+        @pl.when(flags_ref[0] == core)
         def _():
-            output[...] = own_ref[...].astype(output.dtype)
-
-        if not whole:
-
-            @pl.when(here & jnp.logical_not(own))
-            def _():
-                output[...] = arrived_ref[...].astype(output.dtype)
-
-
-def deliver(order, sources, ranges, block):
-    features = sources[0].shape[1]
-    count = sum(source.shape[0] for source in sources) // block
-    half = count // 2
-    per = features // block
-
-    def place(core, step):
-        if len(sources) == 1:
-            return step
-        return jnp.where(core == 0, jnp.minimum(step, half - 1), jnp.maximum(step - half, 0))
+            for index in range(columns + 1):
+                first = index * features
+                height = features if index < columns else rest_ref.shape[0]
+                while height:
+                    owner, at = divmod(first, half)
+                    size = min(height, half - at)
+                    piece = (own_ref if owner == core else arrived_ref)[at : at + size]
+                    piece = piece.astype(jnp.float32)
+                    row = first % features
+                    if index < columns:
+                        span = slice(index * features, (index + 1) * features)
+                        out_ref[row : row + size, span] = piece
+                    else:
+                        rest_ref[row : row + size] = piece
+                    first, height = first + size, height - size
+
+
+def deliver_halves(order, own, arrived):
+    half, features = own.shape
+    columns = 2 * half // features
+    return order.run(
+        deliver_kernel,
+        [order.flags, own, arrived],
+        [SMEM, VMEM, VMEM],
+        [VMEM, VMEM],
+        [struct((features, columns * features), jnp.float32), struct((8, features), jnp.float32)],
+    )
+
+
+def deliver_parts_kernel(outputs, counts, *refs):
+    steps = pl.program_id(0)
+    feed_refs, space_refs = refs[: counts[0]], refs[counts[0] : sum(counts)]
+    for output, (first, last, _) in zip(refs[sum(counts) :], outputs):
+
+        @pl.when((steps >= first) & (steps < last))
+        def _():
+            sources = feed_refs if last <= FEED_BLOCKS else space_refs
+            rows = sources[0].shape[1]
+            for piece in range(sources[0].shape[0]):
+                for index, source in enumerate(sources):
+                    at = (piece * len(sources) + index) * rows
+                    output[at : at + rows] = source[piece].astype(output.dtype)
+
+
+def deliver_parts(order, gathered, space_part):
+    _, part, features = gathered.shape
+    feed_part = part - space_part
+    unit = math.gcd(space_part, feed_part)
+
+    def source(rows, first, step_of, index):
+        def place(step):
+            return step_of(step), first // unit + index, 0
+
+        return pl.BlockSpec((features // rows, unit, features), place)
+
+    counts = (feed_part // unit, space_part // unit)
+    feed_specs = [
+        source(feed_part, space_part, lambda step: jnp.minimum(step, FEED_BLOCKS - 1), index)
+        for index in range(counts[0])
+    ]
+    space_specs_ = [
+        source(space_part, 0, lambda step: jnp.maximum(step - FEED_BLOCKS, 0), index)
+        for index in range(counts[1])
+    ]
+    half = FEED_BLOCKS // 2
+    outputs = [(0, half, True), (half, FEED_BLOCKS, False)]
+    for first, last, wide in ((0, 3, True), (3, 4, False), (4, 5, False)):
+        outputs.append((FEED_BLOCKS + first, FEED_BLOCKS + last, wide))
 
     def spot(first, last, wide):
-        def index(step, flags):
+        def index(step):
             at = jnp.clip(step - first, 0, last - first - 1)
-            return (at % per, at // per) if wide else (at, 0)
-
-        return pl.BlockSpec((block, features), index)
+            return (0, at) if wide else (at, 0)
+
+        return pl.BlockSpec((features, features), index)
 
     def shape(first, last, wide):
-        rows = (last - first) * block
-        return (features, rows) if wide else (rows, features)
-
-    specs = [
-        pl.BlockSpec((block, features), lambda step, flags: (place(flags[0], step), 0)),
-        pl.BlockSpec((block, features), lambda step, flags: (place(1 - flags[0], step), 0)),
-    ]
+        rows = (last - first) * features
+        return struct((features, rows) if wide else (rows, features), jnp.float32)
+
     return order.run(
-        functools.partial(deliver_kernel, ranges, count),
-        [order.flags, *sources],
-        specs[: len(sources)],
-        [spot(*item) for item in ranges],
-        [struct(shape(*item), jnp.float32) for item in ranges],
-        grid=(count,),
-        prefetch=1,
+        functools.partial(deliver_parts_kernel, outputs, counts),
+        [gathered] * sum(counts),
+        feed_specs + space_specs_,
+        [spot(*item) for item in outputs],
+        [shape(*item) for item in outputs],
+        grid=(outputs[-1][1],),
     )
 
 
@@ -459,6 +590,15 @@
 def column_sum(values):
     return jnp.sum(values, axis=0, keepdims=True)
 
+def square_spec(packed, index):
+    batch_count, _, features = packed.shape
+    return pl.BlockSpec((batch_count, features // batch_count, features), lambda i: (0, index, 0))
+
+
+def square(ref):
+    return ref[...].reshape(-1, ref.shape[-1])
+
+
 def feed_kernel(chunks, x1_ref, mixture_ref, dz_ref, so_ref, fi_ref, fo_ref, fb_ref, vec_ref,
                 out_ref, dx2_ref, dys_ref, dos_ref, grad_ref, gfb_ref, gvec_ref,
                 x2_s, a3_s, a3t_s, acc_s, da_s, g_s, dh_s):
@@ -466,7 +606,7 @@
     rows = x1_ref.shape[0]
     @pl.when(step == 0)
     def _():
-        x2 = x1_ref[...] + contract(mixture_ref[...], so_ref[...], (1, 0)) + vec_ref[9:10]
+        x2 = x1_ref[...] + contract(mixture_ref[...], square(so_ref), (1, 0)) + vec_ref[9:10]
         x2_s[...] = x2
         normed, _ = norm_parts(x2)
         a3 = (normed * vec_ref[10:11] + vec_ref[11:12]).astype(jnp.bfloat16)
@@ -474,24 +614,25 @@
         a3t_s[...] = a3.T
         acc_s[...] = x2 + vec_ref[12:13]
         da_s[...] = jnp.zeros_like(da_s)
+    inner, outer = square(fi_ref), square(fo_ref)
     part = rows // chunks
     for chunk in range(chunks):
         span = slice(chunk * part, (chunk + 1) * part)
-        hidden = contract(a3_s[span], fi_ref[...], (1, 0)) + fb_ref[...]
+        hidden = contract(a3_s[span], inner, (1, 0)) + fb_ref[...]
         cdf = 0.5 + 0.5 * lax.erf(hidden * math.sqrt(0.5))
         slope = cdf + hidden * jnp.exp(hidden * hidden * -0.5) * (1.0 / math.sqrt(2.0 * math.pi))
         active = (hidden * cdf).astype(jnp.bfloat16)
         g_s[span] = active
-        dh = (contract(dz_ref[span], fo_ref[...], (1, 1)) * slope).astype(jnp.bfloat16)
+        dh = (contract(dz_ref[span], outer, (1, 1)) * slope).astype(jnp.bfloat16)
         dh_s[span] = dh
-        acc_s[span] += contract(active, fo_ref[...], (1, 0))
-        da_s[span] += contract(dh, fi_ref[...], (1, 1))
+        acc_s[span] += contract(active, outer, (1, 0))
+        da_s[span] += contract(dh, inner, (1, 1))
     grad_ref[0] = contract(a3t_s[...], dh_s[...], (1, 0)).astype(grad_ref.dtype)
     grad_ref[1] = contract(g_s[...], dz_ref[...], (0, 0)).astype(grad_ref.dtype)
     gfb_ref[...] = column_sum(dh_s[...].astype(jnp.float32))
     @pl.when(step == pl.num_programs(0) - 1)
     def _():
-        out_ref[...] = acc_s[...].astype(out_ref.dtype)
+        out_ref[0] = acc_s[: out_ref.shape[1]].astype(out_ref.dtype)
         normed, spread = norm_parts(x2_s[...])
         grad = da_s[...]
         dz = dz_ref[...].astype(jnp.float32)
@@ -499,49 +640,61 @@
         dx2_ref[...] = dx2
         dys = dx2.astype(jnp.bfloat16)
         dys_ref[...] = dys
-        dos_ref[...] = contract(dys, so_ref[...], (1, 1)).astype(dos_ref.dtype)
+        dos_ref[...] = contract(dys, square(so_ref), (1, 1)).astype(dos_ref.dtype)
         gvec_ref[0:1] = column_sum(grad * normed)
         gvec_ref[1:2] = column_sum(grad)
         gvec_ref[2:3] = column_sum(dz)
         gvec_ref[3:4] = column_sum(dys.astype(jnp.float32))
         gvec_ref[4:8] = jnp.zeros((4, gvec_ref.shape[1]), jnp.float32)
 
-def feed_block(order, x1, mixture, dz, space_packed, fi, fo, fb, vec, tile, chunks):
+def feed_block(order, row_count, x1, mixture, dz, packed, feed_packed, bias, vec, chunks):
     rows, features = x1.shape
-    hidden = fi.shape[1]
+    batch_count = feed_packed.shape[0]
+    hidden = bias.shape[1]
     whole = pl.BlockSpec((rows, features), lambda j: (0, 0))
-    fi_spec = pl.BlockSpec((features, tile), lambda j: (0, j))
-    fo_spec = pl.BlockSpec((tile, features), lambda j: (j, 0))
-    fb_spec = pl.BlockSpec((1, tile), lambda j: (0, j))
-    last = space_packed.shape[1] // features - 1
+    line = pl.BlockSpec((1, features), lambda j: (0, j))
+    shard = hidden // batch_count
     low, full = jnp.bfloat16, jnp.float32
     return order.run(
         functools.partial(feed_kernel, chunks),
-        [x1, mixture, dz, space_packed, fi, fo, fb, vec],
-        [whole, whole, whole]
-        + [pl.BlockSpec((features, features), lambda j: (0, last)), fi_spec, fo_spec, fb_spec]
-        + [pl.BlockSpec(vec.shape, lambda j: (0, 0))],
-        [whole] * 4
-        + [pl.BlockSpec((2, tile, features), lambda j: (0, j, 0)), fb_spec]
-        + [pl.BlockSpec((8, features), lambda j: (0, 0))],
+        [x1, mixture, dz, packed, feed_packed, feed_packed, bias, vec],
         [
-            struct((rows, features), low),
+            whole,
+            whole,
+            whole,
+            square_spec(packed, 4),
+            pl.BlockSpec((batch_count, features // batch_count, features), lambda j: (0, j, 0)),
+            pl.BlockSpec((features // shard, shard, features), lambda j: (j, 1, 0)),
+            line,
+            pl.BlockSpec(vec.shape, lambda j: (0, 0)),
+        ],
+        [
+            pl.BlockSpec((1, row_count, features), lambda j: (0, 0, 0)),
+            whole,
+            whole,
+            whole,
+            pl.BlockSpec((2, features, features), lambda j: (0, j, 0)),
+            line,
+            pl.BlockSpec((8, features), lambda j: (0, 0)),
+        ],
+        [
+            struct((1, row_count, features), low),
             struct((rows, features), full),
             struct((rows, features), low),
             struct((rows, features), low),
-            struct((2, *fo.shape), low),
+            struct((2, hidden, features), low),
             struct((1, hidden), full),
             struct((8, features), full),
         ],
-        grid=(hidden // tile,),
+        grid=(hidden // features,),
         scratch=[
             pltpu.VMEM((rows, features), full),
             pltpu.VMEM((rows, features), low),
             pltpu.VMEM((features, rows), low),
             pltpu.VMEM((rows, features), full),
             pltpu.VMEM((rows, features), full),
-            pltpu.VMEM((rows, tile), low),
-            pltpu.VMEM((rows, tile), low),
+            pltpu.VMEM((rows, features), low),
+            pltpu.VMEM((rows, features), low),
         ],
     )
 
@@ -554,12 +707,12 @@
 
 
 def middle_kernel(count, frame_flag, flags_ref, token_ref, *refs):
-    slots, (to_ref, sp_ref, vec_ref) = refs[:count], refs[count : count + 3]
-    mixture_ref, x1_ref, a2_ref, qkv_ref = refs[count + 3 :]
+    slots, (to_ref, *sp_refs, vec_ref) = refs[:count], refs[count : count + 5]
+    mixture_ref, x1_ref, a2_ref, qkv_ref = refs[count + 5 :]
     rows, features = token_ref.shape
     gather_rows(count, flags_ref[frame_flag], slots, mixture_ref)
     number = lax.broadcasted_iota(jnp.int32, (rows, 1), 0)
-    branch = contract(mixture_ref[...], to_ref[...], (1, 0)) + vec_ref[4:5]
+    branch = contract(mixture_ref[...], square(to_ref), (1, 0)) + vec_ref[4:5]
     x1 = token_ref[...].astype(jnp.float32) + jnp.where(number < PATCHES, branch, 0.0)
     x1_ref[...] = x1
     normed, _ = norm_parts(x1)
@@ -567,27 +720,25 @@
     a2_ref[...] = a2
     for third in range(3):
         span = slice(third * features, (third + 1) * features)
-        joined = contract(a2, sp_ref[:, span], (1, 0))
+        joined = contract(a2, square(sp_refs[third]), (1, 0))
         if third != 1:
             joined = joined + vec_ref[7 + third // 2 : 8 + third // 2]
         qkv_ref[:, span] = joined.astype(jnp.bfloat16)
 
 
-def project_specs(features, vec):
-    return [
-        pl.BlockSpec((features, features), lambda i: (0, 3)),
-        pl.BlockSpec((features, 3 * features), lambda i: (0, 0)),
-        pl.BlockSpec(vec.shape, lambda i: (0, 0)),
+def project_specs(packed, vec):
+    return [square_spec(packed, index) for index in range(4)] + [
+        pl.BlockSpec(vec.shape, lambda i: (0, 0))
     ]
 
 
-def middle_forward(order, tokens, slots, time_packed, space_packed, vec):
+def middle_forward(order, tokens, slots, packed, vec):
     rows, features = tokens.shape
     low = jnp.bfloat16
     return order.run(
         functools.partial(middle_kernel, len(slots), order.flags.shape[0] - 1),
-        [order.flags, tokens, *slots, time_packed, space_packed, vec],
-        [SMEM] + [VMEM] * (len(slots) + 1) + project_specs(features, vec),
+        [order.flags, tokens, *slots, *[packed] * 4, vec],
+        [SMEM] + [VMEM] * (len(slots) + 1) + project_specs(packed, vec),
         [VMEM] * 4,
         [
             struct((rows, features), low),
@@ -600,68 +751,75 @@
 
 
 def middle_back_kernel(
-    count, frame_flag, flags_ref, dq_ref, dk_ref, dv_ref, x1_ref, dx2_ref, to_ref, sp_ref, vec_ref, *refs
+    sizes, part, flags_ref, dq_ref, dk_ref, dv_ref, x1_ref, dx2_ref, to_ref, *refs
 ):
-    dx1_ref, dyt_ref, sums_ref = refs[:3]
-    slots, rows_s = refs[3 : 3 + count], refs[3 + count]
+    *sp_refs, vec_ref, time_ref, feed_ref, bias_ref = refs[:7]
+    dx1_ref, sums_ref, kept_ref, sent_ref = refs[7:11]
+    count = sizes[1]
+    slots, rows_s = refs[11 : 11 + count], refs[11 + count]
     rows, features = x1_ref.shape
     grad = 0.0
     for third, piece in enumerate((dq_ref, dk_ref, dv_ref)):
-        span = slice(third * features, (third + 1) * features)
-        grad = grad + contract(piece[...], sp_ref[:, span], (1, 1))
+        grad = grad + contract(piece[...], square(sp_refs[third]), (1, 1))
     normed, spread = norm_parts(x1_ref[...])
     dx1 = dx2_ref[...] + norm_back(grad, normed, spread, vec_ref[5:6])
     dx1_ref[...] = dx1
     number = lax.broadcasted_iota(jnp.int32, (rows, 1), 0)
     dyt = jnp.where(number < PATCHES, dx1, 0.0).astype(jnp.bfloat16)
-    dyt_ref[...] = dyt
-    rows_s[...] = contract(dyt, to_ref[...], (1, 1)).astype(rows_s.dtype)
-    part = rows // count
+    rows_s[...] = contract(dyt, square(to_ref), (1, 1)).astype(rows_s.dtype)
+    block = rows // count
     for shift in range(count):
-        owner = lax.rem(flags_ref[frame_flag] + shift, count)
-        slots[shift][...] = rows_s[pl.ds(pl.multiple_of(owner * part, ROW_TILE), part)]
+        owner = lax.rem(flags_ref[flags_ref.shape[0] - 1] + shift, count)
+        slots[shift][...] = rows_s[pl.ds(pl.multiple_of(owner * block, ROW_TILE), block)]
     sums_ref[0:1] = column_sum(grad * normed)
     sums_ref[1:2] = column_sum(grad)
     sums_ref[2:3] = column_sum(dq_ref[...].astype(jnp.float32))
     sums_ref[3:4] = column_sum(dv_ref[...].astype(jnp.float32))
     sums_ref[4:5] = column_sum(dyt.astype(jnp.float32))
     sums_ref[5:8] = jnp.zeros((3, features), jnp.float32)
-
-
-def middle_backward(order, count, dq, dk, dv, x1, dx2, time_packed, space_packed, vec):
+    first = 4 * features
+    put = functools.partial(put_parts, flags_ref, kept_ref, sent_ref, sizes, part, first)
+    put(first, contract(time_ref[...], dyt, (0, 0)))
+    bias = bias_ref[...]
+    lines = [bias[:, at : at + features] for at in range(0, bias.shape[1], features)]
+    pieces = [sums_ref[0:4], feed_ref[3:4], feed_ref[0:3], *lines]
+    put(first + features, fill_rows(pieces, 2 * kept_ref.shape[0] - features, features))
+
+
+def middle_backward(order, sizes, dq, dk, dv, x1, dx2, packed, vec, mixture, feed_sums, bias):
     rows, features = x1.shape
+    count = sizes[1]
     low, full = jnp.bfloat16, jnp.float32
+    total, part = space_rows(sizes, features)
+    half = struct(((total - 4 * features) // 2, features), low)
     results = order.run(
-        functools.partial(middle_back_kernel, count, order.flags.shape[0] - 1),
-        [order.flags, dq, dk, dv, x1, dx2, time_packed, space_packed, vec],
-        [SMEM] + [VMEM] * 5 + project_specs(features, vec),
-        [VMEM] * (3 + count),
-        [struct((rows, features), full), struct((rows, features), low), struct((8, features), full)]
+        functools.partial(middle_back_kernel, sizes, part),
+        [order.flags, dq, dk, dv, x1, dx2, *[packed] * 4, vec, mixture, feed_sums, bias],
+        [SMEM] + [VMEM] * 5 + project_specs(packed, vec) + [VMEM] * 3,
+        [VMEM] * (4 + count),
+        [struct((rows, features), full), struct((8, features), full), half, half]
         + [struct((rows // count, features), low)] * count,
         grid=(1,),
         scratch=[pltpu.VMEM((rows, features), low)],
     )
-    return results[0], results[1], results[2], results[3:]
-
-
-def put_rows(core_ref, kept_ref, sent_ref, sizes, at, value):
+    return results[0], results[1], results[2:4], results[4:]
+
+
+def put_half(core_ref, kept_ref, sent_ref, at, value):
     half = kept_ref.shape[0]
     low = value.astype(kept_ref.dtype)
-    part = 2 * half // (sizes[0] * sizes[1]) if sizes else math.gcd(half, low.shape[0])
+    part = math.gcd(half, low.shape[0])
     for offset in range(0, low.shape[0], part):
-        start = at + offset
-        if sizes:
-            start = sum_order(start // part, sizes, 2 * half)
+        owner, first = divmod(at + offset, half)
         piece = low[offset : offset + part]
-        span = slice(start % half, start % half + part)
-
-        @pl.when(core_ref[0] == start // half)
+
+        @pl.when(core_ref[0] == owner)
         def _():
-            kept_ref[span] = piece
-
-        @pl.when(core_ref[0] != start // half)
+            kept_ref[first : first + part] = piece
+
+        @pl.when(core_ref[0] != owner)
         def _():
-            sent_ref[span] = piece
+            sent_ref[first : first + part] = piece
 
 
 def fill_rows(pieces, rows, features):
@@ -669,28 +827,44 @@
     return jnp.concatenate([*pieces, jnp.zeros((rows - used, features), jnp.float32)])
 
 
-def middle_weights_kernel(
-    sizes, flags_ref, a2_ref, dq_ref, dk_ref, dv_ref, time_ref, dyt_ref, space_ref, dys_ref, sums_ref, feed_ref,
-    bias_ref, kept_ref, sent_ref
+def put_parts(core_ref, kept_ref, sent_ref, sizes, part, first, at, value):
+    low = value.astype(kept_ref.dtype)
+    for offset in range(0, low.shape[0], part):
+        batch, frame = divmod((at + offset) // part, sizes[1])
+        start = ((batch >> 1) * sizes[1] + frame) * part - first // 2
+        piece = low[offset : offset + part]
+
+        @pl.when(core_ref[0] == batch & 1)
+        def _():
+            kept_ref[start : start + part] = piece
+
+        @pl.when(core_ref[0] != batch & 1)
+        def _():
+            sent_ref[start : start + part] = piece
+
+
+def space_rows(sizes, features):
+    rows = round_up(5 * features + ROW_TILE, sizes[0] * sizes[1] * ROW_TILE)
+    return rows, rows // (sizes[0] * sizes[1])
+
+
+def space_weights_kernel(
+    sizes, part, flags_ref, a2_ref, dq_ref, dk_ref, dv_ref, mixture_ref, dys_ref, kept_ref, sent_ref
 ):
     features = a2_ref.shape[1]
+    put = functools.partial(put_parts, flags_ref, kept_ref, sent_ref, sizes, part, 0)
     turned = a2_ref[...].T
-    put = functools.partial(put_rows, flags_ref, kept_ref, sent_ref, sizes)
     for third, piece in enumerate((dq_ref, dk_ref, dv_ref)):
         put(third * features, contract(turned, piece[...], (1, 0)))
-    put(3 * features, contract(time_ref[...], dyt_ref[...], (0, 0)))
-    put(4 * features, contract(space_ref[...], dys_ref[...], (0, 0)))
-    bias = bias_ref[...]
-    lines = [bias[:, at : at + features] for at in range(0, bias.shape[1], features)]
-    pieces = [sums_ref[0:4], feed_ref[3:4], feed_ref[0:3], *lines]
-    put(5 * features, fill_rows(pieces, 2 * kept_ref.shape[0] - 5 * features, features))
-
-
-def middle_weights(order, sizes, *operands):
+    put(3 * features, contract(mixture_ref[...], dys_ref[...], (0, 0)))
+
+
+def space_weights(order, sizes, *operands):
     features = operands[0].shape[1]
-    half = struct((round_up(5 * features + 16, 512) // 2, features), jnp.bfloat16)
+    part = space_rows(sizes, features)[1]
+    half = struct((2 * features, features), jnp.bfloat16)
     return order.run(
-        functools.partial(middle_weights_kernel, sizes),
+        functools.partial(space_weights_kernel, sizes, part),
         [order.flags, *operands],
         [SMEM] + [VMEM] * len(operands),
         [VMEM] * 2,
@@ -753,14 +927,14 @@
         return carry
     lax.fori_loop(0, part // CHUNK, chunk_step, 0)
 
-def time_forward(order, slots, time_packed, vec):
+def time_forward(order, slots, time_weight, vec):
     count = len(slots)
     part, features = slots[0].shape
     gather = head_map(features)
     low, full = jnp.bfloat16, jnp.float32
     results = order.run(
         functools.partial(time_forward_kernel, count, (features // HEADS) ** -0.5),
-        [*slots, time_packed, vec, gather, gather.T],
+        [*slots, time_weight, vec, gather, gather.T],
         [VMEM] * count + [pl.BlockSpec((features, 3 * features), lambda i: (0, 0)), VMEM, VMEM, VMEM],
         [VMEM] * (count + 3),
         [struct((part, features), low)] * count
@@ -815,7 +989,7 @@
         return carry
     lax.fori_loop(0, part // CHUNK, chunk_step, 0)
     a1t = a1_ref[...].T
-    put = functools.partial(put_rows, flags_ref, kept_ref, sent_ref, None)
+    put = functools.partial(put_half, flags_ref, kept_ref, sent_ref)
     for third in range(3):
         span = slice(third * features, (third + 1) * features)
         put(third * features, contract(a1t, dqkv_ref[:, span], (1, 0)))
@@ -837,7 +1011,7 @@
     put(3 * features, fill_rows(sums, 2 * kept_ref.shape[0] - 3 * features, features))
 
 
-def time_backward(order, grads, slots, qkv, prob, a1, time_packed, vec, other):
+def time_backward(order, grads, slots, qkv, prob, a1, time_weight, vec, other):
     count = len(grads)
     part, features = grads[0].shape
     gather = head_map(features)
@@ -845,7 +1019,7 @@
     half = struct((round_up(3 * features + 16, 512) // 2, features), low)
     results = order.run(
         functools.partial(time_backward_kernel, count, (features // HEADS) ** -0.5),
-        [order.flags, *grads, *slots, qkv, prob, a1, gather, gather.T, time_packed, vec, other],
+        [order.flags, *grads, *slots, qkv, prob, a1, gather, gather.T, time_weight, vec, other],
         [SMEM] + [VMEM] * (2 * count + 5)
         + [pl.BlockSpec((features, 3 * features), lambda i: (0, 0)), VMEM, VMEM],
         [VMEM] * (count + 2),
@@ -860,22 +1034,18 @@
     return results[:count], results[count], results[count + 1]
 
 
-def last_kernel(count, frame_flag, flags_ref, first_ref, *refs):
-    slots, out_ref, rows_s = refs[:count], refs[count], refs[count + 1]
-    gather_rows(count, flags_ref[frame_flag], slots, rows_s)
-    rows = out_ref.shape[1]
-    out_ref[0] = (first_ref[...] + rows_s[...].astype(jnp.float32))[:rows]
-
-
-def add_branch(order, first, slots, row_count):
-    features = first.shape[1]
+def place_kernel(count, flags_ref, *refs):
+    gather_rows(count, flags_ref[flags_ref.shape[0] - 1], refs[:count], refs[count])
+
+
+def place_slots(order, slots):
+    part, features = slots[0].shape
     return order.run(
-        functools.partial(last_kernel, len(slots), order.flags.shape[0] - 1),
-        [order.flags, first, *slots],
-        [SMEM] + [VMEM] * (len(slots) + 1),
+        functools.partial(place_kernel, len(slots)),
+        [order.flags, *slots],
+        [SMEM] + [VMEM] * len(slots),
         [VMEM],
-        [struct((1, row_count, features), jnp.float32)],
-        scratch=[pltpu.VMEM(first.shape, jnp.bfloat16)],
+        [struct((len(slots) * part, features), slots[0].dtype)],
     )[0]
 
 
@@ -900,15 +1070,17 @@
     frame_index = lax.axis_index("frame")
     batch_index = lax.axis_index("batch")
     flags = [(batch_index >> bit) & 1 for bit in range(batch_count.bit_length() - 1)]
-    flags += [(frame_index >> bit) & 1 for bit in range(frame_count.bit_length() - 1)]
+    frame_flag = len(flags)
     order = Order(jnp.stack([*flags, frame_index]).astype(jnp.int32))
     features = tokens.shape[2]
     row_count = tokens.shape[1]
     part = round_up(-(-PATCHES // frame_count), ROW_TILE)
     padded = part * frame_count
+
+    time_weight = lax.all_gather(time_project, "batch", axis=0, tiled=True)
     token_rows = jnp.pad(tokens[0], ((0, padded - row_count), (0, 0)))
     grad_result = jnp.pad(cotangent[0], ((0, padded - row_count), (0, 0)))
-
+    slots = rows_to_frames(token_rows, frame_count, frame_index)
     vectors = jnp.concatenate(
         [time_vector, space_vector, feed_vector, feed_bias.reshape(-1, time_vector.shape[1])], axis=0
     )
@@ -916,14 +1088,13 @@
     vec = vectors[:, :13].transpose(1, 0, 2).reshape(13, features).astype(jnp.float32)
     vec = jnp.pad(vec, ((0, 3), (0, 0)))
     feed_bias_row = vectors[:, 13:].reshape(1, -1).astype(jnp.float32)
-    time_packed = lax.all_gather(
-        jnp.concatenate([time_project, time_output], axis=1), "batch", axis=0, tiled=True
-    )
-    space_packed = lax.all_gather(
-        jnp.concatenate([space_project, space_output], axis=1), "batch", axis=0, tiled=True
-    )
-    feed_inner_full = lax.all_gather(feed_inner, "batch", axis=0, tiled=True)
-    feed_outer_full = lax.all_gather(feed_outer, "batch", axis=0, tiled=True)
+
+    def stack_columns(weight):
+        return [weight[:, at : at + features] for at in range(0, weight.shape[1], features)]
+
+    packed = jnp.concatenate([time_output, *stack_columns(space_project), space_output], axis=0)
+    feed_packed = jnp.concatenate([*stack_columns(feed_inner), feed_outer], axis=0)
+    feed_packed = lax.all_gather(feed_packed, "batch", axis=0)
     clip = jnp.concatenate(
         [
             jnp.arange(PATCHES, dtype=jnp.int32) // size_tag[0],
@@ -932,10 +1103,15 @@
         ]
     )
 
-    slots = rows_to_frames(token_rows, frame_count, frame_index)
-    mixture_slots, qkv_time, prob_time, first_input = time_forward(order, slots, time_packed, vec)
+    weight_flight = Flight(gather_steps(packed, batch_count))
+    advance(order, weight_flight)
+    mixture_slots, qkv_time, prob_time, first_input = time_forward(order, slots, time_weight, vec)
+    mixture_slots = send_back(mixture_slots)
+    while weight_flight.result is None:
+        advance(order, weight_flight)
+    packed = weight_flight.result.reshape(batch_count, -1, features)
     mixture_time, after_time, second_input, qkv_space = middle_forward(
-        order, token_rows, send_back(mixture_slots), time_packed, space_packed, vec
+        order, token_rows, mixture_slots, packed, vec
     )
     mixture_space, total_space = space_forward(order, qkv_space, clip, features)
     (
@@ -948,52 +1124,54 @@
         feed_sums,
     ) = feed_block(
         order,
+        row_count,
         after_time,
         mixture_space,
         grad_result,
-        space_packed,
-        feed_inner_full,
-        feed_outer_full,
+        packed,
+        feed_packed,
         feed_bias_row,
         vec,
-        tile=features,
         chunks=2,
     )
-    feed_total = lax.psum(feed_grads.reshape(-1, features), ("batch", "frame"))
+
+    def sum_batch(block):
+        return lax.psum_scatter(block, "batch", scatter_dimension=0, tiled=True)
+
+    feed_part = sum_batch(feed_grads.reshape(-1, features))
     grad_query, grad_keys, grad_values = space_backward(
         order, qkv_space, mixture_space, total_space, grad_mixture, clip, features
     )
-    grad_first, grad_patch, space_sums, grad_slots = middle_backward(
-        order,
-        frame_count,
-        grad_query,
-        grad_keys,
-        grad_values,
-        after_time,
-        grad_second,
-        time_packed,
-        space_packed,
-        vec,
-    )
-    grad_slots = [
-        shift_frames(slot, frame_count, shift) for shift, slot in enumerate(grad_slots)
-    ]
-    space_kept, space_sent = middle_weights(
+    space_pair = space_weights(
         order,
         sizes,
         second_input,
         grad_query,
         grad_keys,
         grad_values,
-        mixture_time,
-        grad_patch,
         mixture_space,
         grad_branch,
-        space_sums,
+    )
+    grad_first, space_sums, other_pair, grad_slots = middle_backward(
+        order,
+        sizes,
+        grad_query,
+        grad_keys,
+        grad_values,
+        after_time,
+        grad_second,
+        packed,
+        vec,
+        mixture_time,
         feed_sums,
         grad_feed_bias,
     )
-    space_flight = Flight(sum_steps(space_kept, space_sent, sizes, False))
+    grad_slots = send_parts(grad_slots)
+    core_flight = Flight(core_steps([space_pair, other_pair], batch_count))
+    advance(order, core_flight)
+    space_part = sum_chips(core_flight.result[0], batch_count)
+    feed_flight = Flight(frame_steps(feed_part, frame_count, frame_flag))
+    advance(order, feed_flight, after=grad_slots[1:])
     input_slots, time_kept, time_sent = time_backward(
         order,
         grad_slots,
@@ -1001,42 +1179,32 @@
         qkv_time,
         prob_time,
         first_input,
-        time_packed,
+        time_weight,
         vec,
         space_sums,
     )
-    time_flight = Flight(sum_steps(time_kept, time_sent, sizes, True))
+    time_flight = Flight(sum_steps(time_kept, time_sent, sizes, frame_flag))
     input_slots = send_back(input_slots)
-    while space_flight.result is None:
-        advance(order, time_flight, space_flight)
-    space_total = lax.all_gather(space_flight.result, ("batch", "frame"), axis=0, tiled=True)
-    advance(order, time_flight)
-    grad_tokens = add_branch(order, grad_first, input_slots, row_count)
+    space_flight = Flight(frame_steps(space_part, frame_count, frame_flag))
+    advance(order, feed_flight, space_flight)
+    whole = finish_together(order, space_flight, feed_flight)
+    whole = lax.all_gather(whole, ("batch", "frame"), axis=0)
     while time_flight.result is None:
         advance(order, time_flight)
-    block = 256
-    per = features // block
-    grad_feed_inner, grad_feed_outer = deliver(
-        order, [feed_total], [(0, 4 * per, True), (4 * per, 8 * per, False)], block
-    )
-    count = 2 * time_flight.result[0].shape[0] // block
-    grad_time_project, time_vectors = deliver(
-        order, time_flight.result, [(0, 3 * per, True), (3 * per, count, False)], block
-    )
-    count = space_total.shape[0] // block
-    grad_space_project, grad_time_output, grad_space_output, some_vectors = deliver(
-        order,
-        [space_total],
-        [
-            (0, 3 * per, True),
-            (3 * per, 4 * per, False),
-            (4 * per, 5 * per, False),
-            (5 * per, count, False),
-        ],
-        block,
-    )
+    grad_time_project, time_vectors = deliver_halves(order, *time_flight.result)
+    space_part_rows = space_part.shape[0] // frame_count
+    (
+        grad_feed_inner,
+        grad_feed_outer,
+        grad_space_project,
+        grad_space_output,
+        grad_time_output,
+    ) = deliver_parts(order, whole, space_part_rows)
+    some_vectors = whole[5 * features // space_part_rows, :ROW_TILE].astype(jnp.float32)
+    input_rows = place_slots(order, input_slots)
+    grad_tokens = (grad_first[:row_count] + input_rows[:row_count].astype(jnp.float32))[None]
     return (
-        block_out[None, :row_count],
+        block_out,
         grad_tokens,
         grad_time_project,
         grad_time_output,

time: 651 us -> 526 us (0.81)
  waiting for transfers between devices: 289 us -> 145 us
  starting transfers between devices: 43.2 us -> 61.3 us
    all_gather x5 -> x3, waiting for transfers between devices: 84.4 us -> 6.21 us  [the longest x1 6.2 us: body(): time_weight = lax.all_gather(time_project, 'batch', axis=0, tiled=True)]
    ppermute x21 -> x17, waiting for transfers between devices: 118 us -> 49.1 us  [swap_bit(): return lax.ppermute(block, axis, pairs)]
    ppermute x12 -> x24, starting transfers between devices: 21 us -> 44.5 us  [shift_frames(): return lax.ppermute(block, 'frame', pairs)]
    unnamed x95 -> x123, local copies, waits for them, and re-layouts: 17.6 us -> 24.1 us
    ppermute x21 -> x17, starting transfers between devices: 21.9 us -> 16.6 us  [swap_bit(): return lax.ppermute(block, axis, pairs)]
    ppermute x12 -> x24, waiting for transfers between devices: 86.2 us -> 89.2 us  [shift_frames(): return lax.ppermute(block, 'frame', pairs)]
    pallas_call x21 -> x25, Pallas kernels: 251 us -> 248 us  [run(): pl.pallas_call(body, grid_spec=pltpu.PrefetchScalarGridSpec(num_scalar_pr...]
  transfers between devices with their start and end apart: 39 -> 46, of which waited for: 24 -> 21; matrix products, arithmetic and copies ran while one was open for 3% -> 3% of each run, Pallas kernels for 21% -> 39%
where the time goes in v4:
time: 526 us; the launch traced here: 519 us
  Pallas kernels  248 us (47%)
  waiting for transfers between devices  145 us (28%)
  starting transfers between devices  61.3 us (12%)
  local copies, waits for them, and re-layouts  32.1 us (6%)
  between operations  15.2 us (3%)
  blocking collectives  11.5 us (2%)
  other arithmetic  5.39 us (1%)
    pallas_call x25, Pallas kernels, run(): pl.pallas_call(body, grid_spec=pltpu.PrefetchScalarGridSpec(num_scalar_pr...  248 us
    ppermute x24, waiting for transfers between devices, shift_frames(): return lax.ppermute(block, 'frame', pairs)  89.2 us
    ppermute x17, waiting for transfers between devices, swap_bit(): return lax.ppermute(block, axis, pairs)  49.1 us
    ppermute x24, starting transfers between devices, shift_frames(): return lax.ppermute(block, 'frame', pairs)  44.5 us
    unnamed x123, local copies, waits for them, and re-layouts  24.1 us
    ppermute x17, starting transfers between devices, swap_bit(): return lax.ppermute(block, axis, pairs)  16.6 us
    all_gather x1, blocking collectives, body(): vectors = lax.all_gather(vectors, 'batch', axis=0)  11.5 us
  transfers between devices with their start and end apart: 46, of which 21 were waited for; matrix products, arithmetic and copies ran while one was open for 3% of the time, Pallas kernels for 39%

profile of v4, /device:TPU:0, one launch (start us, length us, event | category | flops | bytes accessed | tf_op | source)
XLA Modules:
  0.0 519.1 jit_solution(2996395861293569537)
XLA Ops:
  23.9 11.5 %all-gather.3 = bf16[8,17,96]{2,1,0:T(8,128)(2,1)S(1)} all-gather(bf16[1,17,96]{2,1,0:T(8,128)(2,1)S(1)} %maximum_bitcast_fusion), channel_id=2, replica_groups=mesh['batch'=8,'frame'=4] {'batch'}, dimensions={0}, use_global_device_ids=true | all-gather | bytes 29376 | tf_op jit(solution)/shard_map/all_gather | solution.py:1087
  43.7 5.9 %collective-permute-done.3.refs_3_.refs_8_ = bf16[208,768]{1,0:T(8,128)(2,1)S(1)} collective-permute-done((bf16[208,768]{1,0:T(8,128)(2,1)}, bf16[208,768]{1,0:T(8,128)(2,1)S(1)}, u32[]{:S(2)}, u32[]{:S(2)}) %collective-permute-start.3) | collective-permute-done | bytes 319520 | tf_op jit(solution)/shard_map/ppermute | solution.py:69
  49.6 6.2 %all-gather.8.cloned.1.call-done.refs_5_.refs_15_ = bf16[768,2304]{1,0:T(8,128)(2,1)} async-done(((bf16[96,2304]{1,0:T(8,128)(2,1)}), bf16[768,2304]{1,0:T(8,128)(2,1)}) %all-gather.8.cloned.1.call-update) | async-done | bytes 3538960 | tf_op jit(solution)/shard_map/all_gather | solution.py:1080
  55.9 16.5 %shard_map.221 = (bf16[208,768]{1,0:T(8,128)(2,1)}, bf16[208,768]{1,0:T(8,128)(2,1)}, bf16[208,768]{1,0:T(8,128)(2,1)}, bf16[208,768]{1,0:T(8,128)(2,1)}, bf16[8...) custom-call(f32[8,128]{1,0:T(8,128)} %get-tuple-element.116.refs_0_, ...), custom_call_target="tpu_custom_call" | custom-call | tf_op jit(solution)/shard_map/pallas_call | solution.py:49
  87.1 7.9 %shard_map.223 = (bf16[3840,768]{1,0:T(8,128)(2,1)}, f32[8,128]{1,0:T(8,128)}) custom-call(f32[8,128]{1,0:T(8,128)} %get-tuple-element.120.refs_0_, s32[4]{0:T(128)} %pad_add_fusion.1.refs_0_.refs_1_.refs_4_, bf16[1920,768]{1,0:T(8,128)(2,1)} %get-tuple-element.121.refs_2_, bf16[1920,768]{1,0:T(8,128)(2,1)} %collective-permute-done.7.refs_3_), custom_call_target="tpu_custom_call" | custom-call | tf_op jit(solution)/shard_map/pallas_call | solution.py:49
  95.0 14.5 %collective-permute-done.9.refs_5_ = bf16[208,768]{1,0:T(8,128)(2,1)S(1)} collective-permute-done((bf16[208,768]{1,0:T(8,128)(2,1)}, bf16[208,768]{1,0:T(8,128)(2,1)S(1)}, u32[]{:S(2)}, u32[]{:S(2)}) %collective-permute-start.9) | collective-permute-done | bytes 319520 | tf_op jit(solution)/shard_map/ppermute | solution.py:69
  110.3 10.2 %shard_map.224 = (bf16[832,768]{1,0:T(8,128)(2,1)}, f32[832,768]{1,0:T(8,128)}, bf16[832,768]{1,0:T(8,128)(2,1)}, bf16[832,2304]{1,0:T(8,128)(2,1)}, f32[8,128]{1,0:T(8,128)}) custom-call(f32[8,128]{1,0:T(8,128)} %get-tuple-element.122.refs_0_, s32[4]{0:T(128)} %pad_add_fusion.1.refs_0_.refs_1_.refs_4_, bf16[832,768]{1,0:T(8,128)(2,1)} %pad.18.refs_2_, ...), custom_call_target="tpu_custom_call" | custom-call | tf_op jit(solution)/shard_map/pallas_call | solution.py:49
  120.6 19.7 %shard_map.225 = (bf16[832,768]{1,0:T(8,128)(2,1)}, f32[832,768]{1,0:T(8,128)}, f32[8,128]{1,0:T(8,128)}) custom-call(f32[8,128]{1,0:T(8,128)} %get-tuple-element.128.refs_0_, s32[832,1]{1,0:T(8,128)} %broadcast_in_dim.22.refs_1_, s32[1,896]{1,0:T(1,128)} %broadcast_in_dim.20.refs_2_, bf16[832,2304]{1,0:T(8,128)(2,1)} %get-tuple-element.129.refs_3_.refs_4_.refs_5_, ...), custom_call_target="tpu_custom_call" | custom-call | tf_op jit(solution)/shard_map/pallas_call | solution.py:49
  140.3 40.1 %shard_map.226 = (bf16[1,788,768]{2,1,0:T(8,128)(2,1)}, f32[832,768]{1,0:T(8,128)}, bf16[832,768]{1,0:T(8,128)(2,1)}, bf16[832,768]{1,0:T(8,128)(2,1)}, bf16[2,3...) custom-call(f32[8,128]{1,0:T(8,128)} %get-tuple-element.130.refs_0_, ...), custom_call_target="tpu_custom_call" | custom-call | tf_op jit(solution)/shard_map/pallas_call | solution.py:49
  180.4 30.5 %shard_map.227 = (bf16[832,768]{1,0:T(8,128)(2,1)}, bf16[832,768]{1,0:T(8,128)(2,1)}, bf16[832,768]{1,0:T(8,128)(2,1)}, f32[8,128]{1,0:T(8,128)}) custom-call(f32[8,128]{1,0:T(8,128)} %get-tuple-element.134.refs_0_, s32[832,1]{1,0:T(8,128)} %broadcast_in_dim.22.refs_1_, s32[1,896]{1,0:T(1,128)} %broadcast_in_dim.20.refs_2_, ...), custom_call_target="tpu_custom_call" | custom-call | tf_op jit(solution)/shard_map/pallas_call | solution.py:49
  210.9 13.7 %shard_map.228 = (bf16[1536,768]{1,0:T(8,128)(2,1)}, bf16[1536,768]{1,0:T(8,128)(2,1)}, f32[8,128]{1,0:T(8,128)}) custom-call(f32[8,128]{1,0:T(8,128)} %get-tuple-element.137.refs_0_, s32[4]{0:T(128)} %pad_add_fusion.1.refs_0_.refs_1_.refs_4_, bf16[832,768]{1,0:T(8,128)(2,1)} %get-tuple-element.138.refs_2_, ...), custom_call_target="tpu_custom_call" | custom-call | tf_op jit(solution)/shard_map/pallas_call | solution.py:49
  224.7 16.2 %shard_map.229 = (f32[832,768]{1,0:T(8,128)}, f32[8,768]{1,0:T(8,128)}, bf16[512,768]{1,0:T(8,128)(2,1)}, bf16[512,768]{1,0:T(8,128)(2,1)}, bf16[208,768]{1,0:T(...) custom-call(f32[8,128]{1,0:T(8,128)} %get-tuple-element.143.refs_0_,, ...), custom_call_target="tpu_custom_call" | custom-call | tf_op jit(solution)/shard_map/pallas_call | solution.py:49
  257.0 6.8 %collective-permute-done.13.refs_1_.refs_3_ = bf16[208,768]{1,0:T(8,128)(2,1)S(1)} collective-permute-done((bf16[208,768]{1,0:T(8,128)(2,1)S(1)}, bf16[208,768]{1,0:T(8,128)(2,1)S(1)}, u32[]{:S(2)}, u32[]{:S(2)}) %collective-permute-start.13) | collective-permute-done | bytes 319520 | tf_op jit(solution)/shard_map/ppermute | solution.py:69
  263.8 13.2 %collective-permute-done.14.refs_2_.refs_4_ = bf16[208,768]{1,0:T(8,128)(2,1)S(1)} collective-permute-done((bf16[208,768]{1,0:T(8,128)(2,1)S(1)}, bf16[208,768]{1,0:T(8,128)(2,1)S(1)}, u32[]{:S(2)}, u32[]{:S(2)}) %collective-permute-start.14) | collective-permute-done | bytes 319520 | tf_op jit(solution)/shard_map/ppermute | solution.py:69
  280.4 6.7 %collective-permute-start.16 = (bf16[192,768]{1,0:T(8,128)(2,1)}, bf16[192,768]{1,0:T(8,128)(2,1)S(1)}, u32[]{:S(2)}, u32[]{:S(2)}) collective-permute-start(bf16[192,768]{1,0:T(8,128)(2,1)} %get-tuple-element.167), channel_id=1, source_target_pairs={{0,1},{1,2},{2,3},{3,0},{4,5},{5,6},{6,7},{7,4},{8,9},{9,10},{10,1... | collective-permute-start | bytes 884744 | tf_op jit(solution)/shard_map/ppermute | solution.py:69
  289.5 26.9 %shard_map.232 = (bf16[208,768]{1,0:T(8,128)(2,1)}, bf16[208,768]{1,0:T(8,128)(2,1)}, bf16[208,768]{1,0:T(8,128)(2,1)}, bf16[208,768]{1,0:T(8,128)(2,1)}, bf16[1...) custom-call(f32[8,128]{1,0:T(8,128)} %get-tuple-element.159.refs_0_, ...), custom_call_target="tpu_custom_call" | custom-call | tf_op jit(solution)/shard_map/pallas_call | solution.py:49
  330.3 6.3 %collective-permute-done.20.refs_4_ = bf16[128,768]{1,0:T(8,128)(2,1)S(1)} collective-permute-done((bf16[128,768]{1,0:T(8,128)(2,1)}, bf16[128,768]{1,0:T(8,128)(2,1)S(1)}, u32[]{:S(2)}, u32[]{:S(2)}) %collective-permute-start.20) | collective-permute-done | bytes 196640 | tf_op jit(solution)/shard_map/ppermute | solution.py:69
  351.3 15.2 %collective-permute-done.23.refs_3_ = bf16[320,768]{1,0:T(8,128)(2,1)S(1)} collective-permute-done((bf16[320,768]{1,0:T(8,128)(2,1)}, bf16[320,768]{1,0:T(8,128)(2,1)S(1)}, u32[]{:S(2)}, u32[]{:S(2)}) %collective-permute-start.23) | collective-permute-done | bytes 491552 | tf_op jit(solution)/shard_map/ppermute | solution.py:88
  372.2 11.4 %collective-permute-done.25.refs_3_ = bf16[160,768]{1,0:T(8,128)(2,1)S(1)} collective-permute-done((bf16[160,768]{1,0:T(8,128)(2,1)}, bf16[160,768]{1,0:T(8,128)(2,1)S(1)}, u32[]{:S(2)}, u32[]{:S(2)}) %collective-permute-start.25) | collective-permute-done | bytes 245792 | tf_op jit(solution)/shard_map/ppermute | solution.py:88
  397.4 8.2 %collective-permute-done.28.refs_4_ = bf16[80,768]{1,0:T(8,128)(2,1)S(1)} collective-permute-done((bf16[80,768]{1,0:T(8,128)(2,1)}, bf16[80,768]{1,0:T(8,128)(2,1)S(1)}, u32[]{:S(2)}, u32[]{:S(2)}) %collective-permute-start.28) | collective-permute-done | bytes 122912 | tf_op jit(solution)/shard_map/ppermute | solution.py:69
  408.1 6.8 %collective-permute-start.32 = (bf16[80,768]{1,0:T(8,128)(2,1)}, bf16[80,768]{1,0:T(8,128)(2,1)S(1)}, u32[]{:S(2)}, u32[]{:S(2)}) collective-permute-start(bf16[80,768]{1,0:T(8,128)(2,1)} %get-tuple-element.196.refs_2_), channel_id=1, source_target_pairs={{0,3},{1,0},{2,1},{3,2},{4,7},{5,4},{6,5},{7,6},{8,11},{9,8},{10,9... | collective-permute-start | bytes 368648 | tf_op jit(solution)/shard_map/ppermute | solution.py:69
  421.1 18.8 %collective-permute-done.31.refs_4_ = bf16[80,768]{1,0:T(8,128)(2,1)S(1)} collective-permute-done((bf16[80,768]{1,0:T(8,128)(2,1)}, bf16[80,768]{1,0:T(8,128)(2,1)S(1)}, u32[]{:S(2)}, u32[]{:S(2)}) %collective-permute-start.31) | collective-permute-done | bytes 122912 | tf_op jit(solution)/shard_map/ppermute | solution.py:69
  456.5 8.7 %collective-permute-done.35.refs_3_ = bf16[320,768]{1,0:T(8,128)(2,1)S(1)} collective-permute-done((bf16[320,768]{1,0:T(8,128)(2,1)}, bf16[320,768]{1,0:T(8,128)(2,1)S(1)}, u32[]{:S(2)}, u32[]{:S(2)}) %collective-permute-start.35) | collective-permute-done | bytes 491552 | tf_op jit(solution)/shard_map/ppermute | solution.py:88
  483.2 19.6 %shard_map.243 = (f32[768,3072]{1,0:T(8,128)}, f32[3072,768]{1,0:T(8,128)}, f32[768,2304]{1,0:T(8,128)}, f32[768,768]{1,0:T(8,128)}, f32[768,768]{1,0:T(8,128)}, /*index=5*/f32[8,128]{1,0:T(8,128)}) custom-call(f32[8,128]{1,0:T(8,128)} %get-tuple-element.205.refs_0_, bf16[32,320,768]{2,1,0:T(8,128)(2,1)} %bitcast.34, bf16[32,320,768]{2,1,0:T(8,128)(2,1)} %bitcast.35, ...), custom_call_target="tpu_custom_call" | custom-call | tf_op jit(solution)/shard_map/pallas_call | solution.py:49
  (253 shorter events, 162.2 us)
Async XLA Ops:
  7.2 48.7 %all-gather.8.cloned.1.call-start = ((), (), s32[]{:S(2)}) async-start(), calls=%async_computation.2 | async-start | bytes 3981312 | tf_op jit(solution)/shard_map/all_gather | solution.py:1080
  7.9 132.4 %all-gather.10.cloned.1.call-start = ((), (), s32[]{:S(2)}) async-start(), calls=%async_computation.5 | async-start | bytes 10616832 | tf_op jit(solution)/shard_map/all_gather | solution.py:1097
  12.8 264.2 %reduce-scatter.3.cloned.1.call-start = ((), (), s32[]{:S(2)}) async-start(), calls=%async_computation.3 | async-start | bytes 10616832 | tf_op jit(solution)/shard_map/reduce_scatter | solution.py:1139
  13.2 22.9 %collective-permute-start.1 = (bf16[240,768]{1,0:T(8,128)(2,1)S(1)}, bf16[240,768]{1,0:T(8,128)(2,1)S(1)}, u32[]{:S(2)}, u32[]{:S(2)}) collective-permute-start(bf16[240,768]{1,0:T(8,128)(2,1)S(1)} %get-tuple-element.263.refs_3_), channel_id=1, source_target_pairs={{0,16},{4,20},{8,24},{12,28},{16,0},{20,4},{24,8},{28,12},{1,17},{... | collective-permute-start | bytes 1105928 | tf_op jit(solution)/shard_map/ppermute | solution.py:88
  16.2 19.8 %collective-permute-start = (bf16[240,768]{1,0:T(8,128)(2,1)S(1)}, bf16[240,768]{1,0:T(8,128)(2,1)}, u32[]{:S(2)}, u32[]{:S(2)}) collective-permute-start(bf16[240,768]{1,0:T(8,128)(2,1)S(1)} %get-tuple-element.264.refs_1_), channel_id=1, source_target_pairs={{0,8},{4,12},{8,0},{12,4},{16,24},{20,28},{24,16},{28,20},{1,9},{5... | collective-permute-start | bytes 1105928 | tf_op jit(solution)/shard_map/ppermute | solution.py:88
  19.2 24.6 %collective-permute-start.4 = (bf16[208,768]{1,0:T(8,128)(2,1)}, bf16[208,768]{1,0:T(8,128)(2,1)S(1)}, u32[]{:S(2)}, u32[]{:S(2)}) collective-permute-start(bf16[208,768]{1,0:T(8,128)(2,1)} %get-tuple-element.256), channel_id=1, source_target_pairs={{0,3},{1,0},{2,1},{3,2},{4,7},{5,4},{6,5},{7,6},{8,11},{9,8},{10,9... | collective-permute-start | bytes 958472 | tf_op jit(solution)/shard_map/ppermute | solution.py:69
  22.8 21.0 %collective-permute-start.2 = (bf16[208,768]{1,0:T(8,128)(2,1)}, bf16[208,768]{1,0:T(8,128)(2,1)S(1)}, u32[]{:S(2)}, u32[]{:S(2)}) collective-permute-start(bf16[208,768]{1,0:T(8,128)(2,1)} %get-tuple-element.258), channel_id=1, source_target_pairs={{0,1},{1,2},{2,3},{3,0},{4,5},{5,6},{6,7},{7,4},{8,9},{9,10},{10,1... | collective-permute-start | bytes 958472 | tf_op jit(solution)/shard_map/ppermute | solution.py:69
  22.8 26.9 %collective-permute-start.3 = (bf16[208,768]{1,0:T(8,128)(2,1)}, bf16[208,768]{1,0:T(8,128)(2,1)S(1)}, u32[]{:S(2)}, u32[]{:S(2)}) collective-permute-start(bf16[208,768]{1,0:T(8,128)(2,1)} %get-tuple-element.259), channel_id=1, source_target_pairs={{0,2},{1,3},{2,0},{3,1},{4,6},{5,7},{6,4},{7,5},{8,10},{9,11},{10,... | collective-permute-start | bytes 958472 | tf_op jit(solution)/shard_map/ppermute | solution.py:69
  39.4 33.0 %collective-permute-start.5 = (bf16[480,768]{1,0:T(8,128)(2,1)}, bf16[480,768]{1,0:T(8,128)(2,1)S(1)}, u32[]{:S(2)}, u32[]{:S(2)}) collective-permute-start(bf16[480,768]{1,0:T(8,128)(2,1)} %get-tuple-element.118.refs_2_), channel_id=1, source_target_pairs={{0,16},{4,20},{8,24},{12,28},{16,0},{20,4},{24,8},{28,12},{1,17},{... | collective-permute-start | bytes 2211848 | tf_op jit(solution)/shard_map/ppermute | solution.py:88
  40.0 32.5 %collective-permute-start.6 = (bf16[480,768]{1,0:T(8,128)(2,1)}, bf16[480,768]{1,0:T(8,128)(2,1)}, u32[]{:S(2)}, u32[]{:S(2)}) collective-permute-start(bf16[480,768]{1,0:T(8,128)(2,1)} %get-tuple-element.119.refs_4_), channel_id=1, source_target_pairs={{0,8},{4,12},{8,0},{12,4},{16,24},{20,28},{24,16},{28,20},{1,9},{5... | collective-permute-start | bytes 2211848 | tf_op jit(solution)/shard_map/ppermute | solution.py:88
  81.3 28.2 %collective-permute-start.9 = (bf16[208,768]{1,0:T(8,128)(2,1)}, bf16[208,768]{1,0:T(8,128)(2,1)S(1)}, u32[]{:S(2)}, u32[]{:S(2)}) collective-permute-start(bf16[208,768]{1,0:T(8,128)(2,1)} %get-tuple-element.125), channel_id=1, source_target_pairs={{0,2},{1,3},{2,0},{3,1},{4,6},{5,7},{6,4},{7,5},{8,10},{9,11},{10,... | collective-permute-start | bytes 958472 | tf_op jit(solution)/shard_map/ppermute | solution.py:69
  81.3 28.2 %collective-permute-start.10 = (bf16[208,768]{1,0:T(8,128)(2,1)}, bf16[208,768]{1,0:T(8,128)(2,1)S(1)}, u32[]{:S(2)}, u32[]{:S(2)}) collective-permute-start(bf16[208,768]{1,0:T(8,128)(2,1)} %get-tuple-element.126), channel_id=1, source_target_pairs={{0,1},{1,2},{2,3},{3,0},{4,5},{5,6},{6,7},{7,4},{8,9},{9,10},{10,1... | collective-permute-start | bytes 958472 | tf_op jit(solution)/shard_map/ppermute | solution.py:69
  180.4 136.0 %reduce-scatter.5.cloned.1.call-start = ((), (), s32[]{:S(2)}) async-start(), calls=%async_computation.4 | async-start | bytes 3932160 | tf_op jit(solution)/shard_map/reduce_scatter | solution.py:215
  250.6 230.7 %all-gather.12.cloned.1.call-start = ((), (), s32[]{:S(2)}) async-start(), calls=%async_computation.6 | async-start | bytes 16220160 | tf_op jit(solution)/shard_map/all_gather | solution.py:1191
  252.2 24.8 %collective-permute-start.14 = (bf16[208,768]{1,0:T(8,128)(2,1)S(1)}, bf16[208,768]{1,0:T(8,128)(2,1)S(1)}, u32[]{:S(2)}, u32[]{:S(2)}) collective-permute-start(bf16[208,768]{1,0:T(8,128)(2,1)S(1)} %copy-done.57), channel_id=1, source_target_pairs={{0,2},{1,3},{2,0},{3,1},{4,6},{5,7},{6,4},{7,5},{8,10},{9,11},{10,... | collective-permute-start | bytes 958472 | tf_op jit(solution)/shard_map/ppermute | solution.py:69
  254.2 22.8 %collective-permute-start.15 = (bf16[208,768]{1,0:T(8,128)(2,1)S(1)}, bf16[208,768]{1,0:T(8,128)(2,1)S(1)}, u32[]{:S(2)}, u32[]{:S(2)}) collective-permute-start(bf16[208,768]{1,0:T(8,128)(2,1)S(1)} %copy-done.56), channel_id=1, source_target_pairs={{0,3},{1,0},{2,1},{3,2},{4,7},{5,4},{6,5},{7,6},{8,11},{9,8},{10,9... | collective-permute-start | bytes 958472 | tf_op jit(solution)/shard_map/ppermute | solution.py:69
  280.4 36.0 %collective-permute-start.16 = (bf16[192,768]{1,0:T(8,128)(2,1)}, bf16[192,768]{1,0:T(8,128)(2,1)S(1)}, u32[]{:S(2)}, u32[]{:S(2)}) collective-permute-start(bf16[192,768]{1,0:T(8,128)(2,1)} %get-tuple-element.167), channel_id=1, source_target_pairs={{0,1},{1,2},{2,3},{3,0},{4,5},{5,6},{6,7},{7,4},{8,9},{9,10},{10,1... | collective-permute-start | bytes 884744 | tf_op jit(solution)/shard_map/ppermute | solution.py:69
  287.1 29.3 %collective-permute-start.17 = (bf16[192,768]{1,0:T(8,128)(2,1)}, bf16[192,768]{1,0:T(8,128)(2,1)S(1)}, u32[]{:S(2)}, u32[]{:S(2)}) collective-permute-start(bf16[192,768]{1,0:T(8,128)(2,1)} %get-tuple-element.168), channel_id=1, source_target_pairs={{0,2},{1,3},{2,0},{3,1},{4,6},{5,7},{6,4},{7,5},{8,10},{9,11},{10,... | collective-permute-start | bytes 884744 | tf_op jit(solution)/shard_map/ppermute | solution.py:69
  289.4 27.0 %collective-permute-start.18 = (bf16[192,768]{1,0:T(8,128)(2,1)}, bf16[192,768]{1,0:T(8,128)(2,1)S(1)}, u32[]{:S(2)}, u32[]{:S(2)}) collective-permute-start(bf16[192,768]{1,0:T(8,128)(2,1)} %get-tuple-element.169), channel_id=1, source_target_pairs={{0,3},{1,0},{2,1},{3,2},{4,7},{5,4},{6,5},{7,6},{8,11},{9,8},{10,9... | collective-permute-start | bytes 884744 | tf_op jit(solution)/shard_map/ppermute | solution.py:69
  414.9 25.1 %collective-permute-start.31 = (bf16[80,768]{1,0:T(8,128)(2,1)}, bf16[80,768]{1,0:T(8,128)(2,1)S(1)}, u32[]{:S(2)}, u32[]{:S(2)}) collective-permute-start(bf16[80,768]{1,0:T(8,128)(2,1)} %get-tuple-element.196.refs_2_), channel_id=1, source_target_pairs={{0,2},{1,3},{2,0},{3,1},{4,6},{5,7},{6,4},{7,5},{8,10},{9,11},{10,... | collective-permute-start | bytes 368648 | tf_op jit(solution)/shard_map/ppermute | solution.py:69
  415.4 24.6 %collective-permute-start.30 = (bf16[80,768]{1,0:T(8,128)(2,1)}, bf16[80,768]{1,0:T(8,128)(2,1)S(1)}, u32[]{:S(2)}, u32[]{:S(2)}) collective-permute-start(bf16[80,768]{1,0:T(8,128)(2,1)} %get-tuple-element.196.refs_2_), channel_id=1, source_target_pairs={{0,1},{1,2},{2,3},{3,0},{4,5},{5,6},{6,7},{7,4},{8,9},{9,10},{10,1... | collective-permute-start | bytes 368648 | tf_op jit(solution)/shard_map/ppermute | solution.py:69
  469.7 33.8 %collective-permute-start.38 = (bf16[208,768]{1,0:T(8,128)(2,1)S(1)}, bf16[208,768]{1,0:T(8,128)(2,1)S(1)}, u32[]{:S(2)}, u32[]{:S(2)}) collective-permute-start(bf16[208,768]{1,0:T(8,128)(2,1)S(1)} %copy-done.55), channel_id=1, source_target_pairs={{0,3},{1,0},{2,1},{3,2},{4,7},{5,4},{6,5},{7,6},{8,11},{9,8},{10,9... | collective-permute-start | bytes 958472 | tf_op jit(solution)/shard_map/ppermute | solution.py:69
  469.8 33.7 %collective-permute-start.39 = (bf16[208,768]{1,0:T(8,128)(2,1)S(1)}, bf16[208,768]{1,0:T(8,128)(2,1)S(1)}, u32[]{:S(2)}, u32[]{:S(2)}) collective-permute-start(bf16[208,768]{1,0:T(8,128)(2,1)S(1)} %copy-done.54), channel_id=1, source_target_pairs={{0,2},{1,3},{2,0},{3,1},{4,6},{5,7},{6,4},{7,5},{8,10},{9,11},{10,... | collective-permute-start | bytes 958472 | tf_op jit(solution)/shard_map/ppermute | solution.py:69
  471.9 31.6 %collective-permute-start.40 = (bf16[208,768]{1,0:T(8,128)(2,1)S(1)}, bf16[208,768]{1,0:T(8,128)(2,1)S(1)}, u32[]{:S(2)}, u32[]{:S(2)}) collective-permute-start(bf16[208,768]{1,0:T(8,128)(2,1)S(1)} %copy-done.53), channel_id=1, source_target_pairs={{0,1},{1,2},{2,3},{3,0},{4,5},{5,6},{6,7},{7,4},{8,9},{9,10},{10,1... | collective-permute-start | bytes 958472 | tf_op jit(solution)/shard_map/ppermute | solution.py:69
  (81 other events, 532.7 us)
Sparse Core Ops, SparseCore 0:
  9.9 45.9 all-gather.7
  58.3 59.2 all-gather.9
  180.5 76.4 reduce-scatter.2
  260.5 43.9 reduce-scatter.4
  339.7 132.3 all-gather.11

commit v5 on v4

--- a/solution.py
+++ b/solution.py
@@ -466,60 +466,62 @@
     lane = lax.broadcasted_iota(jnp.int32, (1, width), 1)
     return [lane < width // 2, lane >= width // 2]
 
-def space_forward_kernel(scale, tile, column_ref, row_ref, q_ref, k_ref, v_ref, mixture_ref, total_ref, bias_ref, k_wide, v_wide):
+def space_forward_kernel(
+    scale, mark_q_ref, mark_k_ref, q_ref, k_ref, v_ref, mixture_ref, total_ref, k_wide, v_wide
+):
     rows, width = q_ref.shape
     wide = k_wide.shape[0]
-    @pl.when(pl.program_id(0) == 0)
-    def _():
-        bias_ref[...] = jnp.where(column_ref[...] == row_ref[...], 0.0, -1e30)
-        if wide > rows:
+    if wide > rows:
+
+        @pl.when(pl.program_id(0) == 0)
+        def _():
             k_wide[rows:] = jnp.zeros((wide - rows, width), k_wide.dtype)
             v_wide[rows:] = jnp.zeros((wide - rows, width), v_wide.dtype)
+
     k_wide[:rows] = k_ref[...]
     v_wide[:rows] = v_ref[...]
     halves = head_halves(width)
-    zero, one = jnp.zeros((), q_ref.dtype), jnp.ones((), q_ref.dtype)
-    filled = [jnp.where(half, v_wide[...], one) for half in halves]
-    for start in range(0, rows, tile):
-        span = slice(start, start + tile)
-        outs, tops = [], []
-        for half, values in zip(halves, filled):
-            queries = jnp.where(half, q_ref[span], zero)
-            scores = contract(queries, k_wide[...], (1, 1)) * (scale * LOG2E) + bias_ref[span]
-            top = jnp.max(scores, axis=1, keepdims=True)
-            weights = jnp.exp2(scores - top)
-            outs.append(contract(weights.astype(jnp.bfloat16), values, (1, 0)))
-            tops.append(top)
-        mass = pltpu.roll(jnp.where(halves[0], outs[1], outs[0]), width // 2, 1)
-        mixture = jnp.where(halves[0], outs[0], outs[1]) / mass
-        mixture_ref[span] = mixture.astype(mixture_ref.dtype)
-        total_ref[span] = jnp.where(halves[0], tops[0], tops[1]) + jnp.log2(mass)
+    one = jnp.ones((), q_ref.dtype)
+    outs, tops = [], []
+    for half in halves:
+        queries = jnp.where(half, q_ref[...], mark_q_ref[:rows])
+        keys = jnp.where(half, k_wide[...], mark_k_ref[...])
+        scores = contract(queries, keys, (1, 1)) * (scale * LOG2E)
+        top = jnp.max(scores, axis=1, keepdims=True)
+        weights = jnp.exp2(scores - top)
+        values = jnp.where(half, v_wide[...], one)
+        outs.append(contract(weights.astype(jnp.bfloat16), values, (1, 0)))
+        tops.append(top)
+    mass = pltpu.roll(jnp.where(halves[0], outs[1], outs[0]), width // 2, 1)
+    mixture = jnp.where(halves[0], outs[0], outs[1]) / mass
+    mixture_ref[...] = mixture.astype(mixture_ref.dtype)
+    total_ref[...] = jnp.where(halves[0], tops[0], tops[1]) + jnp.log2(mass)
 
 
 def space_specs(rows, features):
     pairs = HEADS // 2
     width = features // pairs
     wide = round_up(rows, 128)
-    fixed = [pl.BlockSpec((rows, 1), lambda i: (0, 0)), pl.BlockSpec((1, wide), lambda i: (0, 0))]
+    fixed = [pl.BlockSpec((wide, width), lambda i: (0, 0))] * 2
     blocks = [pl.BlockSpec((rows, width), lambda i, o=o: (0, o + i)) for o in (0, pairs, 2 * pairs)]
     out = pl.BlockSpec((rows, width), lambda i: (0, i))
-    scratch = [pltpu.VMEM((rows, wide), jnp.float32)]
-    scratch += [pltpu.VMEM((wide, width), jnp.bfloat16)] * 2
+    scratch = [pltpu.VMEM((wide, width), jnp.bfloat16)] * 2
     return pairs, (features // HEADS) ** -0.5, fixed + blocks, out, scratch
 
 
-def clip_lines(clip):
+def clip_marks(clip, width):
     rows = clip.shape[0]
-    row = jnp.pad(clip, (0, round_up(rows, 128) - rows), constant_values=-2)
-    return clip[:, None], row[None]
+    clip = jnp.pad(clip, (0, round_up(rows, 128) - rows), constant_values=-2)
+    same = (clip[:, None] + 2) == jnp.arange(width, dtype=jnp.int32)[None] % (width // 2)
+    return same.astype(jnp.bfloat16), jnp.where(same, 0.0, -1e30).astype(jnp.bfloat16)
 
 
 def space_forward(order, qkv, clip, features):
     rows = qkv.shape[0]
     pairs, scale, specs, out, scratch = space_specs(rows, features)
     return order.run(
-        functools.partial(space_forward_kernel, scale, rows),
-        [*clip_lines(clip), qkv, qkv, qkv],
+        functools.partial(space_forward_kernel, scale),
+        [*clip_marks(clip, features // pairs), qkv, qkv, qkv],
         specs,
         [out, out],
         [struct((rows, features), jnp.bfloat16), struct((rows, features), jnp.float32)],
@@ -528,15 +530,19 @@
     )
 
 
-def space_backward_kernel(scale, tile, column_ref, row_ref, q_ref, k_ref, v_ref, mixture_ref, total_ref, grad_ref, dq_ref, dk_ref, dv_ref, bias_ref, q_wide, g_wide):
+def space_backward_kernel(
+    scale, mark_q_ref, mark_k_ref, q_ref, k_ref, v_ref, mixture_ref, total_ref, grad_ref, dq_ref, dk_ref, dv_ref,
+    q_wide, g_wide
+):
     rows, width = q_ref.shape
     wide = q_wide.shape[0]
-    @pl.when(pl.program_id(0) == 0)
-    def _():
-        bias_ref[...] = jnp.where(column_ref[...] == row_ref[...], 0.0, -1e30)
-        if wide > rows:
+    if wide > rows:
+
+        @pl.when(pl.program_id(0) == 0)
+        def _():
             q_wide[rows:] = jnp.zeros((wide - rows, width), q_wide.dtype)
             g_wide[rows:] = jnp.zeros((wide - rows, width), g_wide.dtype)
+
     q_wide[:rows] = q_ref[...]
     g_wide[:rows] = grad_ref[...]
     halves = head_halves(width)
@@ -545,32 +551,30 @@
     sums = [jnp.sum(jnp.where(half, product, 0.0), axis=1, keepdims=True) for half in halves]
     delta = widen_rows(jnp.where(halves[0], sums[0], sums[1]), wide).T
     total = widen_rows(total_ref[...], wide).T
-    dq_parts = [None, None]
-    for start in range(0, rows, tile):
-        span = slice(start, start + tile)
-        dk, dv = [], []
-        for index, half in enumerate(halves):
-            at = index * (width // 2)
-            keys = jnp.where(half, k_ref[span], zero)
-            values = jnp.where(half, v_ref[span], zero)
-            scores = contract(keys, q_wide[...], (1, 1)) * (scale * LOG2E)
-            weights = jnp.exp2(scores + (bias_ref[span] - total[at:at + 1]))
-            slopes = contract(values, g_wide[...], (1, 1))
-            slopes = (weights * (slopes - delta[at:at + 1])).astype(jnp.bfloat16)
-            dv.append(contract(weights.astype(jnp.bfloat16), g_wide[...], (1, 0)))
-            dk.append(contract(slopes, q_wide[...], (1, 0)))
-            part = contract(slopes, keys, (0, 0))
-            dq_parts[index] = part if start == 0 else dq_parts[index] + part
-        dk_ref[span] = (jnp.where(halves[0], dk[0], dk[1]) * scale).astype(dk_ref.dtype)
-        dv_ref[span] = jnp.where(halves[0], dv[0], dv[1]).astype(dv_ref.dtype)
-    dq_ref[...] = ((dq_parts[0] + dq_parts[1])[:rows] * scale).astype(dq_ref.dtype)
+    dq, dk, dv = [], [], []
+    for index, half in enumerate(halves):
+        at = index * (width // 2)
+        queries = jnp.where(half, q_wide[...], mark_q_ref[...])
+        keys = jnp.where(half, k_ref[...], mark_k_ref[:rows])
+        values = jnp.where(half, v_ref[...], zero)
+        scores = contract(keys, queries, (1, 1)) * (scale * LOG2E)
+        weights = jnp.exp2(scores - total[at : at + 1])
+        slopes = contract(values, g_wide[...], (1, 1))
+        slopes = (weights * (slopes - delta[at : at + 1])).astype(jnp.bfloat16)
+        dv.append(contract(weights.astype(jnp.bfloat16), g_wide[...], (1, 0)))
+        dk.append(contract(slopes, q_wide[...], (1, 0)))
+        dq.append(contract(slopes, k_ref[...], (0, 0)))
+    dk_ref[...] = (jnp.where(halves[0], dk[0], dk[1]) * scale).astype(dk_ref.dtype)
+    dv_ref[...] = jnp.where(halves[0], dv[0], dv[1]).astype(dv_ref.dtype)
+    dq_ref[...] = (jnp.where(halves[0], dq[0], dq[1])[:rows] * scale).astype(dq_ref.dtype)
+
 
 def space_backward(order, qkv, mixture, total, grad, clip, features):
     rows = qkv.shape[0]
     pairs, scale, specs, out, scratch = space_specs(rows, features)
     return order.run(
-        functools.partial(space_backward_kernel, scale, rows),
-        [*clip_lines(clip), qkv, qkv, qkv, mixture, total, grad],
+        functools.partial(space_backward_kernel, scale),
+        [*clip_marks(clip, features // pairs), qkv, qkv, qkv, mixture, total, grad],
         specs + [out] * 3,
         [out] * 3,
         [struct((rows, features), jnp.bfloat16)] * 3,
@@ -647,7 +651,7 @@
         gvec_ref[3:4] = column_sum(dys.astype(jnp.float32))
         gvec_ref[4:8] = jnp.zeros((4, gvec_ref.shape[1]), jnp.float32)
 
-def feed_block(order, row_count, x1, mixture, dz, packed, feed_packed, bias, vec, chunks):
+def feed_block(order, row_count, x1, mixture, dz, feed_packed, bias, vec, chunks):
     rows, features = x1.shape
     batch_count = feed_packed.shape[0]
     hidden = bias.shape[1]
@@ -657,12 +661,12 @@
     low, full = jnp.bfloat16, jnp.float32
     return order.run(
         functools.partial(feed_kernel, chunks),
-        [x1, mixture, dz, packed, feed_packed, feed_packed, bias, vec],
+        [x1, mixture, dz, feed_packed, feed_packed, feed_packed, bias, vec],
         [
             whole,
             whole,
             whole,
-            square_spec(packed, 4),
+            square_spec(feed_packed, 2 * hidden // features),
             pl.BlockSpec((batch_count, features // batch_count, features), lambda j: (0, j, 0)),
             pl.BlockSpec((features // shard, shard, features), lambda j: (j, 1, 0)),
             line,
@@ -925,7 +929,7 @@
                 total = total + wide[at:at + CHUNK] * values[g]
             outs[f][place] = total.astype(jnp.bfloat16)
         return carry
-    lax.fori_loop(0, part // CHUNK, chunk_step, 0)
+    lax.fori_loop(0, part // CHUNK, chunk_step, 0, unroll=True)
 
 def time_forward(order, slots, time_weight, vec):
     count = len(slots)
@@ -987,7 +991,7 @@
             for third, value in enumerate((dq * scale, dk * scale, dv)):
                 dqkv_ref[start, third * features:(third + 1) * features] = value.astype(jnp.bfloat16)
         return carry
-    lax.fori_loop(0, part // CHUNK, chunk_step, 0)
+    lax.fori_loop(0, part // CHUNK, chunk_step, 0, unroll=True)
     a1t = a1_ref[...].T
     put = functools.partial(put_half, flags_ref, kept_ref, sent_ref)
     for third in range(3):
@@ -1034,18 +1038,27 @@
     return results[:count], results[count], results[count + 1]
 
 
-def place_kernel(count, flags_ref, *refs):
-    gather_rows(count, flags_ref[flags_ref.shape[0] - 1], refs[:count], refs[count])
-
-
-def place_slots(order, slots):
-    part, features = slots[0].shape
+def place_kernel(flags_ref, first_ref, *refs):
+    slots, out_ref, rows_s = refs[:-2], refs[-2], refs[-1]
+    gather_rows(len(slots), flags_ref[flags_ref.shape[0] - 1], slots, rows_s)
+    lanes = out_ref.shape[1]
+    parts = first_ref.shape[1] // lanes
+    rows = out_ref.shape[0] // parts
+    for index in range(parts):
+        span = slice(index * lanes, (index + 1) * lanes)
+        total = first_ref[:rows, span] + rows_s[:rows, span].astype(jnp.float32)
+        out_ref[pl.ds(index, rows, stride=parts)] = total
+
+
+def add_slots(order, first, slots, row_count):
+    features = first.shape[1]
     return order.run(
-        functools.partial(place_kernel, len(slots)),
-        [order.flags, *slots],
-        [SMEM] + [VMEM] * len(slots),
+        place_kernel,
+        [order.flags, first, *slots],
+        [SMEM] + [VMEM] * (len(slots) + 1),
         [VMEM],
-        [struct((len(slots) * part, features), slots[0].dtype)],
+        [struct((row_count * features // 128, 128), jnp.float32)],
+        scratch=[pltpu.VMEM(first.shape, slots[0].dtype)],
     )[0]
 
 
@@ -1092,8 +1105,7 @@
     def stack_columns(weight):
         return [weight[:, at : at + features] for at in range(0, weight.shape[1], features)]
 
-    packed = jnp.concatenate([time_output, *stack_columns(space_project), space_output], axis=0)
-    feed_packed = jnp.concatenate([*stack_columns(feed_inner), feed_outer], axis=0)
+    feed_packed = jnp.concatenate([*stack_columns(feed_inner), feed_outer, space_output], axis=0)
     feed_packed = lax.all_gather(feed_packed, "batch", axis=0)
     clip = jnp.concatenate(
         [
@@ -1103,6 +1115,7 @@
         ]
     )
 
+    packed = jnp.concatenate([time_output, *stack_columns(space_project)], axis=0)
     weight_flight = Flight(gather_steps(packed, batch_count))
     advance(order, weight_flight)
     mixture_slots, qkv_time, prob_time, first_input = time_forward(order, slots, time_weight, vec)
@@ -1128,7 +1141,6 @@
         after_time,
         mixture_space,
         grad_result,
-        packed,
         feed_packed,
         feed_bias_row,
         vec,
@@ -1191,7 +1203,6 @@
     whole = lax.all_gather(whole, ("batch", "frame"), axis=0)
     while time_flight.result is None:
         advance(order, time_flight)
-    grad_time_project, time_vectors = deliver_halves(order, *time_flight.result)
     space_part_rows = space_part.shape[0] // frame_count
     (
         grad_feed_inner,
@@ -1200,9 +1211,10 @@
         grad_space_output,
         grad_time_output,
     ) = deliver_parts(order, whole, space_part_rows)
+    grad_time_project, time_vectors = deliver_halves(order, *time_flight.result)
     some_vectors = whole[5 * features // space_part_rows, :ROW_TILE].astype(jnp.float32)
-    input_rows = place_slots(order, input_slots)
-    grad_tokens = (grad_first[:row_count] + input_rows[:row_count].astype(jnp.float32))[None]
+    grad_tokens = add_slots(order, grad_first, input_slots, row_count)
+    grad_tokens = grad_tokens.reshape(1, row_count, features)
     return (
         block_out,
         grad_tokens,

time: 526 us -> 518 us (0.985)
  Pallas kernels: 248 us -> 238 us
  waiting for transfers between devices: 145 us -> 151 us
    pallas_call x25, Pallas kernels: 248 us -> 238 us  [run(): pl.pallas_call(body, grid_spec=pltpu.PrefetchScalarGridSpec(num_scalar_pr...]
    ppermute x24, waiting for transfers between devices: 89.2 us -> 94.9 us  [shift_frames(): return lax.ppermute(block, 'frame', pairs)]
    unnamed x123 -> x121, local copies, waits for them, and re-layouts: 24.1 us -> 20.8 us
  transfers between devices with their start and end apart: 46 -> 46, of which waited for: 21 -> 22; matrix products, arithmetic and copies ran while one was open for 3% -> 3% of each run, Pallas kernels for 39% -> 37%
where the time goes in v5:
time: 518 us; the launch traced here: 509 us
  Pallas kernels  238 us (46%)
  waiting for transfers between devices  151 us (29%)
  starting transfers between devices  62.3 us (12%)
  local copies, waits for them, and re-layouts  27.3 us (5%)
  between operations  15.2 us (3%)
  blocking collectives  9.33 us (2%)
  other arithmetic  5.53 us (1%)
    pallas_call x25, Pallas kernels, run(): pl.pallas_call(body, grid_spec=pltpu.PrefetchScalarGridSpec(num_scalar_pr...  238 us
    ppermute x24, waiting for transfers between devices, shift_frames(): return lax.ppermute(block, 'frame', pairs)  94.9 us
    ppermute x17, waiting for transfers between devices, swap_bit(): return lax.ppermute(block, axis, pairs)  47.8 us
    ppermute x24, starting transfers between devices, shift_frames(): return lax.ppermute(block, 'frame', pairs)  45.6 us
    unnamed x121, local copies, waits for them, and re-layouts  20.8 us
    ppermute x17, starting transfers between devices, swap_bit(): return lax.ppermute(block, axis, pairs)  16.4 us
  transfers between devices with their start and end apart: 46, of which 22 were waited for; matrix products, arithmetic and copies ran while one was open for 3% of the time, Pallas kernels for 37%

profile of v5, /device:TPU:0, one launch (start us, length us, event | category | flops | bytes accessed | tf_op | source)
XLA Modules:
  0.0 509.1 jit_solution(8770191941529996817)
XLA Ops:
  23.9 9.3 %all-gather.3 = bf16[8,17,96]{2,1,0:T(8,128)(2,1)S(1)} all-gather(bf16[1,17,96]{2,1,0:T(8,128)(2,1)S(1)} %maximum_bitcast_fusion), channel_id=2, replica_groups=mesh['batch'=8,'frame'=4] {'batch'}, dimensions={0}, use_global_device_ids=true | all-gather | bytes 29376 | tf_op jit(solution)/shard_map/all_gather | solution.py:1100
  42.0 7.6 %collective-permute-done.3.refs_3_.refs_8_ = bf16[208,768]{1,0:T(8,128)(2,1)S(1)} collective-permute-done((bf16[208,768]{1,0:T(8,128)(2,1)}, bf16[208,768]{1,0:T(8,128)(2,1)S(1)}, u32[]{:S(2)}, u32[]{:S(2)}) %collective-permute-start.3) | collective-permute-done | bytes 319520 | tf_op jit(solution)/shard_map/ppermute | solution.py:69
  54.9 13.7 %shard_map.221 = (bf16[208,768]{1,0:T(8,128)(2,1)}, bf16[208,768]{1,0:T(8,128)(2,1)}, bf16[208,768]{1,0:T(8,128)(2,1)}, bf16[208,768]{1,0:T(8,128)(2,1)}, bf16[8...) custom-call(f32[8,128]{1,0:T(8,128)} %get-tuple-element.116.refs_0_, ...), custom_call_target="tpu_custom_call" | custom-call | tf_op jit(solution)/shard_map/pallas_call | solution.py:49
  88.7 17.4 %collective-permute-done.9.refs_5_ = bf16[208,768]{1,0:T(8,128)(2,1)S(1)} collective-permute-done((bf16[208,768]{1,0:T(8,128)(2,1)}, bf16[208,768]{1,0:T(8,128)(2,1)S(1)}, u32[]{:S(2)}, u32[]{:S(2)}) %collective-permute-start.9) | collective-permute-done | bytes 319520 | tf_op jit(solution)/shard_map/ppermute | solution.py:69
  106.9 10.2 %shard_map.224 = (bf16[832,768]{1,0:T(8,128)(2,1)}, f32[832,768]{1,0:T(8,128)}, bf16[832,768]{1,0:T(8,128)(2,1)}, bf16[832,2304]{1,0:T(8,128)(2,1)}, f32[8,128]{1,0:T(8,128)}) custom-call(f32[8,128]{1,0:T(8,128)} %get-tuple-element.122.refs_0_, s32[4]{0:T(128)} %pad_add_fusion.2.refs_0_.refs_1_.refs_4_, bf16[832,768]{1,0:T(8,128)(2,1)} %pad.18.refs_2_, ...), custom_call_target="tpu_custom_call" | custom-call | tf_op jit(solution)/shard_map/pallas_call | solution.py:49
  117.1 18.9 %shard_map.225 = (bf16[832,768]{1,0:T(8,128)(2,1)}, f32[832,768]{1,0:T(8,128)}, f32[8,128]{1,0:T(8,128)}) custom-call(f32[8,128]{1,0:T(8,128)} %get-tuple-element.128.refs_0_, bf16[896,128]{1,0:T(8,128)(2,1)} %compare_convert_fusion.refs_1_, bf16[896,128]{1,0:T(8,128)(2,1)} %fusion.refs_2_, bf16[832,2304]{1,0:T(8,128)(2,1)} %get-tuple-element.129.refs_3_.refs_4_.refs_5_, ...), custom_call_target="tpu_custom_call" | custom-call | tf_op jit(solution)/shard_map/pallas_call | solution.py:49
  136.0 39.9 %shard_map.226 = (bf16[1,788,768]{2,1,0:T(8,128)(2,1)}, f32[832,768]{1,0:T(8,128)}, bf16[832,768]{1,0:T(8,128)(2,1)}, bf16[832,768]{1,0:T(8,128)(2,1)}, bf16[2,3...) custom-call(f32[8,128]{1,0:T(8,128)} %get-tuple-element.130.refs_0_, ...), custom_call_target="tpu_custom_call" | custom-call | tf_op jit(solution)/shard_map/pallas_call | solution.py:49
  176.0 30.1 %shard_map.227 = (bf16[832,768]{1,0:T(8,128)(2,1)}, bf16[832,768]{1,0:T(8,128)(2,1)}, bf16[832,768]{1,0:T(8,128)(2,1)}, f32[8,128]{1,0:T(8,128)}) custom-call(f32[8,128]{1,0:T(8,128)} %get-tuple-element.134.refs_0_, bf16[896,128]{1,0:T(8,128)(2,1)} %compare_convert_fusion.refs_1_, bf16[896,128]{1,0:T(8,128)(2,1)} %fusion.refs_2_, ...), custom_call_target="tpu_custom_call" | custom-call | tf_op jit(solution)/shard_map/pallas_call | solution.py:49
  206.1 13.7 %shard_map.228 = (bf16[1536,768]{1,0:T(8,128)(2,1)}, bf16[1536,768]{1,0:T(8,128)(2,1)}, f32[8,128]{1,0:T(8,128)}) custom-call(f32[8,128]{1,0:T(8,128)} %get-tuple-element.137.refs_0_, s32[4]{0:T(128)} %pad_add_fusion.2.refs_0_.refs_1_.refs_4_, bf16[832,768]{1,0:T(8,128)(2,1)} %get-tuple-element.138.refs_2_, ...), custom_call_target="tpu_custom_call" | custom-call | tf_op jit(solution)/shard_map/pallas_call | solution.py:49
  219.8 16.1 %shard_map.229 = (f32[832,768]{1,0:T(8,128)}, f32[8,768]{1,0:T(8,128)}, bf16[512,768]{1,0:T(8,128)(2,1)}, bf16[512,768]{1,0:T(8,128)(2,1)}, bf16[208,768]{1,0:T(...) custom-call(f32[8,128]{1,0:T(8,128)} %get-tuple-element.143.refs_0_,, ...), custom_call_target="tpu_custom_call" | custom-call | tf_op jit(solution)/shard_map/pallas_call | solution.py:49
  252.5 6.4 %collective-permute-done.13.refs_1_.refs_3_ = bf16[208,768]{1,0:T(8,128)(2,1)S(1)} collective-permute-done((bf16[208,768]{1,0:T(8,128)(2,1)S(1)}, bf16[208,768]{1,0:T(8,128)(2,1)S(1)}, u32[]{:S(2)}, u32[]{:S(2)}) %collective-permute-start.13) | collective-permute-done | bytes 319520 | tf_op jit(solution)/shard_map/ppermute | solution.py:69
  258.9 13.2 %collective-permute-done.14.refs_2_.refs_4_ = bf16[208,768]{1,0:T(8,128)(2,1)S(1)} collective-permute-done((bf16[208,768]{1,0:T(8,128)(2,1)S(1)}, bf16[208,768]{1,0:T(8,128)(2,1)S(1)}, u32[]{:S(2)}, u32[]{:S(2)}) %collective-permute-start.14) | collective-permute-done | bytes 319520 | tf_op jit(solution)/shard_map/ppermute | solution.py:69
  275.5 7.1 %collective-permute-start.16 = (bf16[192,768]{1,0:T(8,128)(2,1)}, bf16[192,768]{1,0:T(8,128)(2,1)S(1)}, u32[]{:S(2)}, u32[]{:S(2)}) collective-permute-start(bf16[192,768]{1,0:T(8,128)(2,1)} %get-tuple-element.166), channel_id=1, source_target_pairs={{0,1},{1,2},{2,3},{3,0},{4,5},{5,6},{6,7},{7,4},{8,9},{9,10},{10,1... | collective-permute-start | bytes 884744 | tf_op jit(solution)/shard_map/ppermute | solution.py:69
  285.2 23.7 %shard_map.232 = (bf16[208,768]{1,0:T(8,128)(2,1)}, bf16[208,768]{1,0:T(8,128)(2,1)}, bf16[208,768]{1,0:T(8,128)(2,1)}, bf16[208,768]{1,0:T(8,128)(2,1)}, bf16[1...) custom-call(f32[8,128]{1,0:T(8,128)} %get-tuple-element.158.refs_0_, ...), custom_call_target="tpu_custom_call" | custom-call | tf_op jit(solution)/shard_map/pallas_call | solution.py:49
  317.0 5.7 %collective-permute-done.19.refs_3_ = bf16[128,768]{1,0:T(8,128)(2,1)S(1)} collective-permute-done((bf16[128,768]{1,0:T(8,128)(2,1)}, bf16[128,768]{1,0:T(8,128)(2,1)S(1)}, u32[]{:S(2)}, u32[]{:S(2)}) %collective-permute-start.19) | collective-permute-done | bytes 196640 | tf_op jit(solution)/shard_map/ppermute | solution.py:69
  322.7 6.6 %collective-permute-done.20.refs_4_ = bf16[128,768]{1,0:T(8,128)(2,1)S(1)} collective-permute-done((bf16[128,768]{1,0:T(8,128)(2,1)}, bf16[128,768]{1,0:T(8,128)(2,1)S(1)}, u32[]{:S(2)}, u32[]{:S(2)}) %collective-permute-start.20) | collective-permute-done | bytes 196640 | tf_op jit(solution)/shard_map/ppermute | solution.py:69
  344.4 15.2 %collective-permute-done.23.refs_3_ = bf16[320,768]{1,0:T(8,128)(2,1)S(1)} collective-permute-done((bf16[320,768]{1,0:T(8,128)(2,1)}, bf16[320,768]{1,0:T(8,128)(2,1)S(1)}, u32[]{:S(2)}, u32[]{:S(2)}) %collective-permute-start.23) | collective-permute-done | bytes 491552 | tf_op jit(solution)/shard_map/ppermute | solution.py:88
  365.3 11.5 %collective-permute-done.25.refs_3_ = bf16[160,768]{1,0:T(8,128)(2,1)S(1)} collective-permute-done((bf16[160,768]{1,0:T(8,128)(2,1)}, bf16[160,768]{1,0:T(8,128)(2,1)S(1)}, u32[]{:S(2)}, u32[]{:S(2)}) %collective-permute-start.25) | collective-permute-done | bytes 245792 | tf_op jit(solution)/shard_map/ppermute | solution.py:88
  391.2 8.5 %collective-permute-done.28.refs_4_ = bf16[80,768]{1,0:T(8,128)(2,1)S(1)} collective-permute-done((bf16[80,768]{1,0:T(8,128)(2,1)}, bf16[80,768]{1,0:T(8,128)(2,1)S(1)}, u32[]{:S(2)}, u32[]{:S(2)}) %collective-permute-start.28) | collective-permute-done | bytes 122912 | tf_op jit(solution)/shard_map/ppermute | solution.py:69
  402.3 5.8 %collective-permute-start.32 = (bf16[80,768]{1,0:T(8,128)(2,1)}, bf16[80,768]{1,0:T(8,128)(2,1)S(1)}, u32[]{:S(2)}, u32[]{:S(2)}) collective-permute-start(bf16[80,768]{1,0:T(8,128)(2,1)} %get-tuple-element.195.refs_2_), channel_id=1, source_target_pairs={{0,3},{1,0},{2,1},{3,2},{4,7},{5,4},{6,5},{7,6},{8,11},{9,8},{10,9... | collective-permute-start | bytes 368648 | tf_op jit(solution)/shard_map/ppermute | solution.py:69
  414.3 20.8 %collective-permute-done.31.refs_4_ = bf16[80,768]{1,0:T(8,128)(2,1)S(1)} collective-permute-done((bf16[80,768]{1,0:T(8,128)(2,1)}, bf16[80,768]{1,0:T(8,128)(2,1)S(1)}, u32[]{:S(2)}, u32[]{:S(2)}) %collective-permute-start.31) | collective-permute-done | bytes 122912 | tf_op jit(solution)/shard_map/ppermute | solution.py:69
  451.0 7.5 %collective-permute-done.35.refs_3_ = bf16[320,768]{1,0:T(8,128)(2,1)S(1)} collective-permute-done((bf16[320,768]{1,0:T(8,128)(2,1)}, bf16[320,768]{1,0:T(8,128)(2,1)S(1)}, u32[]{:S(2)}, u32[]{:S(2)}) %collective-permute-start.35) | collective-permute-done | bytes 491552 | tf_op jit(solution)/shard_map/ppermute | solution.py:88
  470.6 19.5 %shard_map.242 = (f32[768,3072]{1,0:T(8,128)}, f32[3072,768]{1,0:T(8,128)}, f32[768,2304]{1,0:T(8,128)}, f32[768,768]{1,0:T(8,128)}, f32[768,768]{1,0:T(8,128)}, /*index=5*/f32[8,128]{1,0:T(8,128)}) custom-call(f32[8,128]{1,0:T(8,128)} %get-tuple-element.202.refs_0_, bf16[32,320,768]{2,1,0:T(8,128)(2,1)} %bitcast.24, bf16[32,320,768]{2,1,0:T(8,128)(2,1)} %bitcast.25, ...), custom_call_target="tpu_custom_call" | custom-call | tf_op jit(solution)/shard_map/pallas_call | solution.py:49
  491.3 5.6 %shard_map.243 = (f32[768,2304]{1,0:T(8,128)}, f32[8,768]{1,0:T(8,128)}, f32[8,128]{1,0:T(8,128)}) custom-call(f32[8,128]{1,0:T(8,128)} %get-tuple-element.204.refs_0_, s32[4]{0:T(128)} %pad_add_fusion.2.refs_0_.refs_1_.refs_4_, bf16[1280,768]{1,0:T(8,128)(2,1)} %get-tuple-element.205.refs_2_, bf16[1280,768]{1,0:T(8,128)(2,1)} %copy-done.2), custom_call_target="tpu_custom_call" | custom-call | tf_op jit(solution)/shard_map/pallas_call | solution.py:49
  (252 shorter events, 160.0 us)
Async XLA Ops:
  7.2 47.7 %all-gather.8.cloned.1.call-start = ((), (), s32[]{:S(2)}) async-start(), calls=%async_computation.2 | async-start | bytes 3981312 | tf_op jit(solution)/shard_map/all_gather | solution.py:1093
  7.9 128.1 %all-gather.10.cloned.1.call-start = ((), (), s32[]{:S(2)}) async-start(), calls=%async_computation.5 | async-start | bytes 11943936 | tf_op jit(solution)/shard_map/all_gather | solution.py:1109
  12.9 259.2 %reduce-scatter.3.cloned.1.call-start = ((), (), s32[]{:S(2)}) async-start(), calls=%async_computation.3 | async-start | bytes 10616832 | tf_op jit(solution)/shard_map/reduce_scatter | solution.py:1151
  13.0 20.8 %collective-permute-start = (bf16[192,768]{1,0:T(8,128)(2,1)S(1)}, bf16[192,768]{1,0:T(8,128)(2,1)S(1)}, u32[]{:S(2)}, u32[]{:S(2)}) collective-permute-start(bf16[192,768]{1,0:T(8,128)(2,1)S(1)} %pad_maximum_fusion.refs_1_), channel_id=1, source_target_pairs={{0,8},{4,12},{8,0},{12,4},{16,24},{20,28},{24,16},{28,20},{1,9},{5... | collective-permute-start | bytes 884744 | tf_op jit(solution)/shard_map/ppermute | solution.py:88
  19.1 22.8 %collective-permute-start.4 = (bf16[208,768]{1,0:T(8,128)(2,1)}, bf16[208,768]{1,0:T(8,128)(2,1)S(1)}, u32[]{:S(2)}, u32[]{:S(2)}) collective-permute-start(bf16[208,768]{1,0:T(8,128)(2,1)} %get-tuple-element.256), channel_id=1, source_target_pairs={{0,3},{1,0},{2,1},{3,2},{4,7},{5,4},{6,5},{7,6},{8,11},{9,8},{10,9... | collective-permute-start | bytes 958472 | tf_op jit(solution)/shard_map/ppermute | solution.py:69
  22.7 19.3 %collective-permute-start.2 = (bf16[208,768]{1,0:T(8,128)(2,1)}, bf16[208,768]{1,0:T(8,128)(2,1)S(1)}, u32[]{:S(2)}, u32[]{:S(2)}) collective-permute-start(bf16[208,768]{1,0:T(8,128)(2,1)} %get-tuple-element.258), channel_id=1, source_target_pairs={{0,1},{1,2},{2,3},{3,0},{4,5},{5,6},{6,7},{7,4},{8,9},{9,10},{10,1... | collective-permute-start | bytes 958472 | tf_op jit(solution)/shard_map/ppermute | solution.py:69
  22.7 26.9 %collective-permute-start.3 = (bf16[208,768]{1,0:T(8,128)(2,1)}, bf16[208,768]{1,0:T(8,128)(2,1)S(1)}, u32[]{:S(2)}, u32[]{:S(2)}) collective-permute-start(bf16[208,768]{1,0:T(8,128)(2,1)} %get-tuple-element.259), channel_id=1, source_target_pairs={{0,2},{1,3},{2,0},{3,1},{4,6},{5,7},{6,4},{7,5},{8,10},{9,11},{10,... | collective-permute-start | bytes 958472 | tf_op jit(solution)/shard_map/ppermute | solution.py:69
  37.7 30.9 %collective-permute-start.5 = (bf16[384,768]{1,0:T(8,128)(2,1)}, bf16[384,768]{1,0:T(8,128)(2,1)S(1)}, u32[]{:S(2)}, u32[]{:S(2)}) collective-permute-start(bf16[384,768]{1,0:T(8,128)(2,1)} %get-tuple-element.118.refs_2_), channel_id=1, source_target_pairs={{0,16},{4,20},{8,24},{12,28},{16,0},{20,4},{24,8},{28,12},{1,17},{... | collective-permute-start | bytes 1769480 | tf_op jit(solution)/shard_map/ppermute | solution.py:88
  38.0 30.6 %collective-permute-start.6 = (bf16[384,768]{1,0:T(8,128)(2,1)}, bf16[384,768]{1,0:T(8,128)(2,1)S(1)}, u32[]{:S(2)}, u32[]{:S(2)}) collective-permute-start(bf16[384,768]{1,0:T(8,128)(2,1)} %get-tuple-element.119.refs_4_), channel_id=1, source_target_pairs={{0,8},{4,12},{8,0},{12,4},{16,24},{20,28},{24,16},{28,20},{1,9},{5... | collective-permute-start | bytes 1769480 | tf_op jit(solution)/shard_map/ppermute | solution.py:88
  78.2 27.8 %collective-permute-start.9 = (bf16[208,768]{1,0:T(8,128)(2,1)}, bf16[208,768]{1,0:T(8,128)(2,1)S(1)}, u32[]{:S(2)}, u32[]{:S(2)}) collective-permute-start(bf16[208,768]{1,0:T(8,128)(2,1)} %get-tuple-element.125), channel_id=1, source_target_pairs={{0,2},{1,3},{2,0},{3,1},{4,6},{5,7},{6,4},{7,5},{8,10},{9,11},{10,... | collective-permute-start | bytes 958472 | tf_op jit(solution)/shard_map/ppermute | solution.py:69
  78.2 27.8 %collective-permute-start.10 = (bf16[208,768]{1,0:T(8,128)(2,1)}, bf16[208,768]{1,0:T(8,128)(2,1)S(1)}, u32[]{:S(2)}, u32[]{:S(2)}) collective-permute-start(bf16[208,768]{1,0:T(8,128)(2,1)} %get-tuple-element.126), channel_id=1, source_target_pairs={{0,1},{1,2},{2,3},{3,0},{4,5},{5,6},{6,7},{7,4},{8,9},{9,10},{10,1... | collective-permute-start | bytes 958472 | tf_op jit(solution)/shard_map/ppermute | solution.py:69
  175.9 132.9 %reduce-scatter.5.cloned.1.call-start = ((), (), s32[]{:S(2)}) async-start(), calls=%async_computation.4 | async-start | bytes 3932160 | tf_op jit(solution)/shard_map/reduce_scatter | solution.py:215
  245.7 222.9 %all-gather.12.cloned.1.call-start = ((), (), s32[]{:S(2)}) async-start(), calls=%async_computation.6 | async-start | bytes 16220160 | tf_op jit(solution)/shard_map/all_gather | solution.py:1203
  247.8 24.3 %collective-permute-start.14 = (bf16[208,768]{1,0:T(8,128)(2,1)S(1)}, bf16[208,768]{1,0:T(8,128)(2,1)S(1)}, u32[]{:S(2)}, u32[]{:S(2)}) collective-permute-start(bf16[208,768]{1,0:T(8,128)(2,1)S(1)} %copy-done.56), channel_id=1, source_target_pairs={{0,2},{1,3},{2,0},{3,1},{4,6},{5,7},{6,4},{7,5},{8,10},{9,11},{10,... | collective-permute-start | bytes 958472 | tf_op jit(solution)/shard_map/ppermute | solution.py:69
  249.6 22.5 %collective-permute-start.15 = (bf16[208,768]{1,0:T(8,128)(2,1)S(1)}, bf16[208,768]{1,0:T(8,128)(2,1)S(1)}, u32[]{:S(2)}, u32[]{:S(2)}) collective-permute-start(bf16[208,768]{1,0:T(8,128)(2,1)S(1)} %copy-done.55), channel_id=1, source_target_pairs={{0,3},{1,0},{2,1},{3,2},{4,7},{5,4},{6,5},{7,6},{8,11},{9,8},{10,9... | collective-permute-start | bytes 958472 | tf_op jit(solution)/shard_map/ppermute | solution.py:69
  275.5 33.3 %collective-permute-start.16 = (bf16[192,768]{1,0:T(8,128)(2,1)}, bf16[192,768]{1,0:T(8,128)(2,1)S(1)}, u32[]{:S(2)}, u32[]{:S(2)}) collective-permute-start(bf16[192,768]{1,0:T(8,128)(2,1)} %get-tuple-element.166), channel_id=1, source_target_pairs={{0,1},{1,2},{2,3},{3,0},{4,5},{5,6},{6,7},{7,4},{8,9},{9,10},{10,1... | collective-permute-start | bytes 884744 | tf_op jit(solution)/shard_map/ppermute | solution.py:69
  282.6 26.2 %collective-permute-start.17 = (bf16[192,768]{1,0:T(8,128)(2,1)}, bf16[192,768]{1,0:T(8,128)(2,1)S(1)}, u32[]{:S(2)}, u32[]{:S(2)}) collective-permute-start(bf16[192,768]{1,0:T(8,128)(2,1)} %get-tuple-element.167), channel_id=1, source_target_pairs={{0,2},{1,3},{2,0},{3,1},{4,6},{5,7},{6,4},{7,5},{8,10},{9,11},{10,... | collective-permute-start | bytes 884744 | tf_op jit(solution)/shard_map/ppermute | solution.py:69
  284.8 24.1 %collective-permute-start.18 = (bf16[192,768]{1,0:T(8,128)(2,1)}, bf16[192,768]{1,0:T(8,128)(2,1)S(1)}, u32[]{:S(2)}, u32[]{:S(2)}) collective-permute-start(bf16[192,768]{1,0:T(8,128)(2,1)} %get-tuple-element.168), channel_id=1, source_target_pairs={{0,3},{1,0},{2,1},{3,2},{4,7},{5,4},{6,5},{7,6},{8,11},{9,8},{10,9... | collective-permute-start | bytes 884744 | tf_op jit(solution)/shard_map/ppermute | solution.py:69
  408.1 27.0 %collective-permute-start.31 = (bf16[80,768]{1,0:T(8,128)(2,1)}, bf16[80,768]{1,0:T(8,128)(2,1)S(1)}, u32[]{:S(2)}, u32[]{:S(2)}) collective-permute-start(bf16[80,768]{1,0:T(8,128)(2,1)} %get-tuple-element.195.refs_2_), channel_id=1, source_target_pairs={{0,2},{1,3},{2,0},{3,1},{4,6},{5,7},{6,4},{7,5},{8,10},{9,11},{10,... | collective-permute-start | bytes 368648 | tf_op jit(solution)/shard_map/ppermute | solution.py:69
  409.9 25.2 %collective-permute-start.30 = (bf16[80,768]{1,0:T(8,128)(2,1)}, bf16[80,768]{1,0:T(8,128)(2,1)S(1)}, u32[]{:S(2)}, u32[]{:S(2)}) collective-permute-start(bf16[80,768]{1,0:T(8,128)(2,1)} %get-tuple-element.195.refs_2_), channel_id=1, source_target_pairs={{0,1},{1,2},{2,3},{3,0},{4,5},{5,6},{6,7},{7,4},{8,9},{9,10},{10,1... | collective-permute-start | bytes 368648 | tf_op jit(solution)/shard_map/ppermute | solution.py:69
  463.5 26.5 %collective-permute-start.37 = (bf16[1280,768]{1,0:T(8,128)(2,1)}, bf16[1280,768]{1,0:T(8,128)(2,1)S(1)}, u32[]{:S(2)}, u32[]{:S(2)}) collective-permute-start(bf16[1280,768]{1,0:T(8,128)(2,1)} %get-tuple-element.205.refs_2_), channel_id=1, source_target_pairs={{0,4},{4,0},{8,12},{12,8},{16,20},{20,16},{24,28},{28,24},{1,5},{5... | collective-permute-start | bytes 5898248 | tf_op jit(solution)/shard_map/ppermute | solution.py:88
  463.5 34.0 %collective-permute-start.38 = (bf16[208,768]{1,0:T(8,128)(2,1)}, bf16[208,768]{1,0:T(8,128)(2,1)S(1)}, u32[]{:S(2)}, u32[]{:S(2)}) collective-permute-start(bf16[208,768]{1,0:T(8,128)(2,1)} %get-tuple-element.209), channel_id=1, source_target_pairs={{0,3},{1,0},{2,1},{3,2},{4,7},{5,4},{6,5},{7,6},{8,11},{9,8},{10,9... | collective-permute-start | bytes 958472 | tf_op jit(solution)/shard_map/ppermute | solution.py:69
  463.5 34.0 %collective-permute-start.39 = (bf16[208,768]{1,0:T(8,128)(2,1)}, bf16[208,768]{1,0:T(8,128)(2,1)S(1)}, u32[]{:S(2)}, u32[]{:S(2)}) collective-permute-start(bf16[208,768]{1,0:T(8,128)(2,1)} %get-tuple-element.210), channel_id=1, source_target_pairs={{0,2},{1,3},{2,0},{3,1},{4,6},{5,7},{6,4},{7,5},{8,10},{9,11},{10,... | collective-permute-start | bytes 958472 | tf_op jit(solution)/shard_map/ppermute | solution.py:69
  464.9 32.6 %collective-permute-start.40 = (bf16[208,768]{1,0:T(8,128)(2,1)S(1)}, bf16[208,768]{1,0:T(8,128)(2,1)S(1)}, u32[]{:S(2)}, u32[]{:S(2)}) collective-permute-start(bf16[208,768]{1,0:T(8,128)(2,1)S(1)} %copy-done.54), channel_id=1, source_target_pairs={{0,1},{1,2},{2,3},{3,0},{4,5},{5,6},{6,7},{7,4},{8,9},{9,10},{10,1... | collective-permute-start | bytes 958472 | tf_op jit(solution)/shard_map/ppermute | solution.py:69
  (80 other events, 505.6 us)
Sparse Core Ops, SparseCore 0:
  9.9 44.9 all-gather.7
  57.3 64.7 all-gather.9
  176.1 77.0 reduce-scatter.2
  256.6 43.9 reduce-scatter.4
  332.5 136.0 all-gather.11

commit v6 on v5

--- a/solution.py
+++ b/solution.py
@@ -14,6 +14,8 @@
 LOG2E = 1.4426950408889634
 ROW_TILE = 16
 FEED_BLOCKS = 8
+LIMIT = 56
+ROOM = 64
 
 
 def round_up(count, step):
@@ -22,6 +24,11 @@
 
 def struct(shape, dtype):
     return jax.ShapeDtypeStruct(shape, dtype)
+
+
+def block_bytes(array, spec):
+    shape = spec.block_shape or array.shape
+    return math.prod(shape) * jnp.dtype(array.dtype).itemsize
 
 
 VMEM = pl.BlockSpec(memory_space=pltpu.VMEM)
@@ -34,7 +41,17 @@
         self.token = None
 
     def run(
-        self, kernel, operands, in_specs, out_specs, out_shape, grid=(), scratch=(), prefetch=0, after=()
+        self,
+        kernel,
+        operands,
+        in_specs,
+        out_specs,
+        out_shape,
+        grid=(),
+        scratch=(),
+        prefetch=0,
+        after=(),
+        room=ROOM,
     ):
         token = [*after] if self.token is None else [self.token, *after]
         inputs, outputs, ordered = len(operands), len(out_shape), len(token)
@@ -45,6 +62,10 @@
             token_ref[...] = jnp.zeros(token_ref.shape, token_ref.dtype)
             kernel(*refs[: inputs + outputs], *refs[inputs + outputs + 1 :])
 
+        pairs = [*zip(operands[prefetch:], in_specs), *zip(out_shape, out_specs)]
+        limit = sum(block_bytes(*pair) for pair in pairs) * (2 if math.prod(grid) > 1 else 1)
+        limit += sum(math.prod(item.shape) * item.dtype.itemsize for item in scratch)
+        limit = min(limit + (room << 20), LIMIT << 20)
         token_spec = pl.BlockSpec((8, 128), lambda *index: (0, 0))
         results = pl.pallas_call(
             body,
@@ -56,7 +77,7 @@
                 scratch_shapes=list(scratch),
             ),
             out_shape=list(out_shape) + [struct((8, 128), jnp.float32)],
-            compiler_params=pltpu.CompilerParams(vmem_limit_bytes=56 << 20),
+            compiler_params=pltpu.CompilerParams(vmem_limit_bytes=limit),
         )(*operands[:prefetch], *token, *operands[prefetch:])
         self.token = results[-1]
         return results[:-1]
@@ -131,7 +152,7 @@
             at += rows
 
 
-def shuffle(order, requests, after):
+def shuffle(order, requests, after, room):
     sources, plan, counts = [], [], []
     for own_sources, own_plan in requests:
         base = len(sources)
@@ -153,6 +174,7 @@
         [VMEM] * len(plan),
         shapes,
         after=after,
+        room=room,
     )
     outputs = []
     for count in counts:
@@ -317,7 +339,7 @@
             return None
 
 
-def advance(order, *flights, after=()):
+def advance(order, *flights, after=(), room=ROOM):
     active, requests = [], []
     for flight in flights:
         if flight.result is not None:
@@ -329,7 +351,7 @@
             active.append(flight)
             requests.append(request)
     if requests:
-        for flight, outputs in zip(active, shuffle(order, requests, after)):
+        for flight, outputs in zip(active, shuffle(order, requests, after, room)):
             if flight.result is None:
                 flight.moved = flight.send(outputs)
             else:
@@ -351,7 +373,7 @@
             (rows, flag, *[tuple((source + base, at) for source, at in terms) for terms in choices])
         )
         sources += parts
-    ((whole,),) = shuffle(order, [(sources, [segments])], ())
+    ((whole,),) = shuffle(order, [(sources, [segments])], (), 4)
     return whole
 
 
@@ -392,13 +414,13 @@
 
 
 def deliver_parts_kernel(outputs, counts, *refs):
-    steps = pl.program_id(0)
+    step = pl.program_id(0)
     feed_refs, space_refs = refs[: counts[0]], refs[counts[0] : sum(counts)]
-    for output, (first, last, _) in zip(refs[sum(counts) :], outputs):
-
-        @pl.when((steps >= first) & (steps < last))
+    for number, (output, (first, last, _)) in enumerate(zip(refs[sum(counts) :], outputs)):
+        sources = feed_refs if number < 2 else space_refs
+
+        @pl.when((step >= first) & (step < last))
         def _():
-            sources = feed_refs if last <= FEED_BLOCKS else space_refs
             rows = sources[0].shape[1]
             for piece in range(sources[0].shape[0]):
                 for index, source in enumerate(sources):
@@ -423,13 +445,13 @@
         for index in range(counts[0])
     ]
     space_specs_ = [
-        source(space_part, 0, lambda step: jnp.maximum(step - FEED_BLOCKS, 0), index)
+        source(space_part, 0, lambda step: jnp.minimum(step, 4), index)
         for index in range(counts[1])
     ]
     half = FEED_BLOCKS // 2
     outputs = [(0, half, True), (half, FEED_BLOCKS, False)]
     for first, last, wide in ((0, 3, True), (3, 4, False), (4, 5, False)):
-        outputs.append((FEED_BLOCKS + first, FEED_BLOCKS + last, wide))
+        outputs.append((first, last, wide))
 
     def spot(first, last, wide):
         def index(step):
@@ -448,7 +470,7 @@
         feed_specs + space_specs_,
         [spot(*item) for item in outputs],
         [shape(*item) for item in outputs],
-        grid=(outputs[-1][1],),
+        grid=(FEED_BLOCKS,),
     )
 
 
@@ -551,7 +573,7 @@
     sums = [jnp.sum(jnp.where(half, product, 0.0), axis=1, keepdims=True) for half in halves]
     delta = widen_rows(jnp.where(halves[0], sums[0], sums[1]), wide).T
     total = widen_rows(total_ref[...], wide).T
-    dq, dk, dv = [], [], []
+    parts = [[], [], [], [], []]
     for index, half in enumerate(halves):
         at = index * (width // 2)
         queries = jnp.where(half, q_wide[...], mark_q_ref[...])
@@ -561,12 +583,22 @@
         weights = jnp.exp2(scores - total[at : at + 1])
         slopes = contract(values, g_wide[...], (1, 1))
         slopes = (weights * (slopes - delta[at : at + 1])).astype(jnp.bfloat16)
-        dv.append(contract(weights.astype(jnp.bfloat16), g_wide[...], (1, 0)))
-        dk.append(contract(slopes, q_wide[...], (1, 0)))
-        dq.append(contract(slopes, k_ref[...], (0, 0)))
-    dk_ref[...] = (jnp.where(halves[0], dk[0], dk[1]) * scale).astype(dk_ref.dtype)
-    dv_ref[...] = jnp.where(halves[0], dv[0], dv[1]).astype(dv_ref.dtype)
-    dq_ref[...] = (jnp.where(halves[0], dq[0], dq[1])[:rows] * scale).astype(dq_ref.dtype)
+        own = (
+            weights.astype(jnp.bfloat16),
+            slopes,
+            jnp.where(half, g_wide[...], zero),
+            jnp.where(half, q_wide[...], zero),
+            jnp.where(half, k_ref[...], zero),
+        )
+        for part, value in zip(parts, own):
+            part.append(value)
+    weights, slopes, grads, queries, keys = parts
+    grads, queries, keys = (jnp.concatenate(part, axis=0) for part in (grads, queries, keys))
+    dv_ref[...] = contract(jnp.concatenate(weights, axis=1), grads, (1, 0)).astype(dv_ref.dtype)
+    dk = contract(jnp.concatenate(slopes, axis=1), queries, (1, 0))
+    dk_ref[...] = (dk * scale).astype(dk_ref.dtype)
+    dq = contract(jnp.concatenate(slopes, axis=0), keys, (0, 0))
+    dq_ref[...] = (dq[:rows] * scale).astype(dq_ref.dtype)
 
 
 def space_backward(order, qkv, mixture, total, grad, clip, features):
@@ -805,6 +837,7 @@
         + [struct((rows // count, features), low)] * count,
         grid=(1,),
         scratch=[pltpu.VMEM((rows, features), low)],
+        room=14,
     )
     return results[0], results[1], results[2:4], results[4:]
 
@@ -1180,10 +1213,10 @@
     )
     grad_slots = send_parts(grad_slots)
     core_flight = Flight(core_steps([space_pair, other_pair], batch_count))
-    advance(order, core_flight)
+    advance(order, core_flight, room=4)
     space_part = sum_chips(core_flight.result[0], batch_count)
     feed_flight = Flight(frame_steps(feed_part, frame_count, frame_flag))
-    advance(order, feed_flight, after=grad_slots[1:])
+    advance(order, feed_flight, after=grad_slots[1:], room=4)
     input_slots, time_kept, time_sent = time_backward(
         order,
         grad_slots,
@@ -1198,7 +1231,7 @@
     time_flight = Flight(sum_steps(time_kept, time_sent, sizes, frame_flag))
     input_slots = send_back(input_slots)
     space_flight = Flight(frame_steps(space_part, frame_count, frame_flag))
-    advance(order, feed_flight, space_flight)
+    advance(order, feed_flight, space_flight, room=4)
     whole = finish_together(order, space_flight, feed_flight)
     whole = lax.all_gather(whole, ("batch", "frame"), axis=0)
     while time_flight.result is None:

time: 518 us -> 506 us (0.977)
  Pallas kernels: 238 us -> 223 us
    pallas_call x25, Pallas kernels: 238 us -> 223 us  [run(): pl.pallas_call(body, grid_spec=pltpu.PrefetchScalarGridSpec(num_scalar_pr...]
    unnamed x121 -> x147, local copies, waits for them, and re-layouts: 20.8 us -> 23.3 us
  transfers between devices with their start and end apart: 46 -> 46, of which waited for: 22 -> 22; matrix products, arithmetic and copies ran while one was open for 3% -> 3% of each run, Pallas kernels for 37% -> 36%
where the time goes in v6:
time: 506 us; the launch traced here: 497 us
  Pallas kernels  223 us (44%)
  waiting for transfers between devices  150 us (30%)
  starting transfers between devices  63.7 us (13%)
  local copies, waits for them, and re-layouts  29.8 us (6%)
  between operations  15.4 us (3%)
  blocking collectives  9.33 us (2%)
  other arithmetic  5.61 us (1%)
    pallas_call x25, Pallas kernels, run(): pl.pallas_call(body, grid_spec=pltpu.PrefetchScalarGridSpec(num_scalar_pr...  223 us
    ppermute x24, waiting for transfers between devices, shift_frames(): return lax.ppermute(block, 'frame', pairs)  95.1 us
    ppermute x24, starting transfers between devices, shift_frames(): return lax.ppermute(block, 'frame', pairs)  48.9 us
    ppermute x17, waiting for transfers between devices, swap_bit(): return lax.ppermute(block, axis, pairs)  48.2 us
    unnamed x147, local copies, waits for them, and re-layouts  23.3 us
    ppermute x17, starting transfers between devices, swap_bit(): return lax.ppermute(block, axis, pairs)  14.5 us
  transfers between devices with their start and end apart: 46, of which 22 were waited for; matrix products, arithmetic and copies ran while one was open for 3% of the time, Pallas kernels for 36%

profile of v6, /device:TPU:0, one launch (start us, length us, event | category | flops | bytes accessed | tf_op | source)
XLA Modules:
  0.0 496.8 jit_solution(8509350983766896711)
XLA Ops:
  23.9 9.3 %all-gather.3 = bf16[8,17,96]{2,1,0:T(8,128)(2,1)S(1)} all-gather(bf16[1,17,96]{2,1,0:T(8,128)(2,1)S(1)} %maximum_bitcast_fusion), channel_id=2, replica_groups=mesh['batch'=8,'frame'=4] {'batch'}, dimensions={0}, use_global_device_ids=true | all-gather | bytes 29376 | tf_op jit(solution)/shard_map/all_gather | solution.py:1133
  42.1 7.5 %collective-permute-done.3.refs_3_.refs_8_ = bf16[208,768]{1,0:T(8,128)(2,1)S(1)} collective-permute-done((bf16[208,768]{1,0:T(8,128)(2,1)}, bf16[208,768]{1,0:T(8,128)(2,1)S(1)}, u32[]{:S(2)}, u32[]{:S(2)}) %collective-permute-start.3) | collective-permute-done | bytes 319520 | tf_op jit(solution)/shard_map/ppermute | solution.py:90
  54.9 13.7 %shard_map.221 = (bf16[208,768]{1,0:T(8,128)(2,1)}, bf16[208,768]{1,0:T(8,128)(2,1)}, bf16[208,768]{1,0:T(8,128)(2,1)}, bf16[208,768]{1,0:T(8,128)(2,1)}, bf16[8...) custom-call(f32[8,128]{1,0:T(8,128)} %get-tuple-element.116.refs_0_, ...), custom_call_target="tpu_custom_call" | custom-call | tf_op jit(solution)/shard_map/pallas_call | solution.py:70
  88.7 17.4 %collective-permute-done.9.refs_5_ = bf16[208,768]{1,0:T(8,128)(2,1)S(1)} collective-permute-done((bf16[208,768]{1,0:T(8,128)(2,1)}, bf16[208,768]{1,0:T(8,128)(2,1)S(1)}, u32[]{:S(2)}, u32[]{:S(2)}) %collective-permute-start.9) | collective-permute-done | bytes 319520 | tf_op jit(solution)/shard_map/ppermute | solution.py:90
  106.9 10.2 %shard_map.224 = (bf16[832,768]{1,0:T(8,128)(2,1)}, f32[832,768]{1,0:T(8,128)}, bf16[832,768]{1,0:T(8,128)(2,1)}, bf16[832,2304]{1,0:T(8,128)(2,1)}, f32[8,128]{1,0:T(8,128)}) custom-call(f32[8,128]{1,0:T(8,128)} %get-tuple-element.122.refs_0_, s32[4]{0:T(128)} %pad_add_fusion.2.refs_0_.refs_1_.refs_4_, bf16[832,768]{1,0:T(8,128)(2,1)} %pad.18.refs_2_, ...), custom_call_target="tpu_custom_call" | custom-call | tf_op jit(solution)/shard_map/pallas_call | solution.py:70
  117.1 18.9 %shard_map.225 = (bf16[832,768]{1,0:T(8,128)(2,1)}, f32[832,768]{1,0:T(8,128)}, f32[8,128]{1,0:T(8,128)}) custom-call(f32[8,128]{1,0:T(8,128)} %get-tuple-element.128.refs_0_, bf16[896,128]{1,0:T(8,128)(2,1)} %compare_convert_fusion.refs_1_, bf16[896,128]{1,0:T(8,128)(2,1)} %fusion.refs_2_, bf16[832,2304]{1,0:T(8,128)(2,1)} %get-tuple-element.129.refs_3_.refs_4_.refs_5_, ...), custom_call_target="tpu_custom_call" | custom-call | tf_op jit(solution)/shard_map/pallas_call | solution.py:70
  136.0 39.9 %shard_map.226 = (bf16[1,788,768]{2,1,0:T(8,128)(2,1)}, f32[832,768]{1,0:T(8,128)}, bf16[832,768]{1,0:T(8,128)(2,1)}, bf16[832,768]{1,0:T(8,128)(2,1)}, bf16[2,3...) custom-call(f32[8,128]{1,0:T(8,128)} %get-tuple-element.130.refs_0_, ...), custom_call_target="tpu_custom_call" | custom-call | tf_op jit(solution)/shard_map/pallas_call | solution.py:70
  176.0 29.3 %shard_map.227 = (bf16[832,768]{1,0:T(8,128)(2,1)}, bf16[832,768]{1,0:T(8,128)(2,1)}, bf16[832,768]{1,0:T(8,128)(2,1)}, f32[8,128]{1,0:T(8,128)}) custom-call(f32[8,128]{1,0:T(8,128)} %get-tuple-element.134.refs_0_, bf16[896,128]{1,0:T(8,128)(2,1)} %compare_convert_fusion.refs_1_, bf16[896,128]{1,0:T(8,128)(2,1)} %fusion.refs_2_, ...), custom_call_target="tpu_custom_call" | custom-call | tf_op jit(solution)/shard_map/pallas_call | solution.py:70
  205.4 13.8 %shard_map.228 = (bf16[1536,768]{1,0:T(8,128)(2,1)}, bf16[1536,768]{1,0:T(8,128)(2,1)}, f32[8,128]{1,0:T(8,128)}) custom-call(f32[8,128]{1,0:T(8,128)} %get-tuple-element.137.refs_0_, s32[4]{0:T(128)} %pad_add_fusion.2.refs_0_.refs_1_.refs_4_, bf16[832,768]{1,0:T(8,128)(2,1)} %get-tuple-element.138.refs_2_, ...), custom_call_target="tpu_custom_call" | custom-call | tf_op jit(solution)/shard_map/pallas_call | solution.py:70
  221.7 10.9 %shard_map.229 = (f32[832,768]{1,0:T(8,128)S(1)}, f32[8,768]{1,0:T(8,128)S(1)}, bf16[512,768]{1,0:T(8,128)(2,1)S(1)}, bf16[512,768]{1,0:T(8,128)(2,1)S(1)}, bf16...) custom-call(f32[8,128]{1,0:T(8,128)S(1)} %copy-done.22, ...), custom_call_target="tpu_custom_call" | custom-call | tf_op jit(solution)/shard_map/pallas_call | solution.py:70
  245.2 6.4 %collective-permute-done.13.refs_1_.refs_3_ = bf16[208,768]{1,0:T(8,128)(2,1)S(1)} collective-permute-done((bf16[208,768]{1,0:T(8,128)(2,1)S(1)}, bf16[208,768]{1,0:T(8,128)(2,1)S(1)}, u32[]{:S(2)}, u32[]{:S(2)}) %collective-permute-start.13) | collective-permute-done | bytes 319520 | tf_op jit(solution)/shard_map/ppermute | solution.py:90
  251.6 13.1 %collective-permute-done.14.refs_2_.refs_4_ = bf16[208,768]{1,0:T(8,128)(2,1)S(1)} collective-permute-done((bf16[208,768]{1,0:T(8,128)(2,1)S(1)}, bf16[208,768]{1,0:T(8,128)(2,1)S(1)}, u32[]{:S(2)}, u32[]{:S(2)}) %collective-permute-start.14) | collective-permute-done | bytes 319520 | tf_op jit(solution)/shard_map/ppermute | solution.py:90
  267.1 7.3 %collective-permute-start.16 = (bf16[192,768]{1,0:T(8,128)(2,1)S(1)}, bf16[192,768]{1,0:T(8,128)(2,1)S(1)}, u32[]{:S(2)}, u32[]{:S(2)}) collective-permute-start(bf16[192,768]{1,0:T(8,128)(2,1)S(1)} %get-tuple-element.166), channel_id=1, source_target_pairs={{0,1},{1,2},{2,3},{3,0},{4,5},{5,6},{6,7},{7,4},{8,9},{9,10},{10,1... | collective-permute-start | bytes 884744 | tf_op jit(solution)/shard_map/ppermute | solution.py:90
  277.0 23.3 %shard_map.232 = (bf16[208,768]{1,0:T(8,128)(2,1)}, bf16[208,768]{1,0:T(8,128)(2,1)}, bf16[208,768]{1,0:T(8,128)(2,1)}, bf16[208,768]{1,0:T(8,128)(2,1)}, bf16[1...) custom-call(f32[8,128]{1,0:T(8,128)} %copy-done.21, s32[4]{0:T(128)} %pad_add_fusion.2.refs_0_.refs_1_.refs_4_, ...), custom_call_target="tpu_custom_call" | custom-call | tf_op jit(solution)/shard_map/pallas_call | solution.py:70
  313.1 7.3 %collective-permute-done.20.refs_4_ = bf16[128,768]{1,0:T(8,128)(2,1)S(1)} collective-permute-done((bf16[128,768]{1,0:T(8,128)(2,1)S(1)}, bf16[128,768]{1,0:T(8,128)(2,1)S(1)}, u32[]{:S(2)}, u32[]{:S(2)}) %collective-permute-start.20) | collective-permute-done | bytes 196640 | tf_op jit(solution)/shard_map/ppermute | solution.py:90
  334.1 15.0 %collective-permute-done.23.refs_3_ = bf16[320,768]{1,0:T(8,128)(2,1)S(1)} collective-permute-done((bf16[320,768]{1,0:T(8,128)(2,1)}, bf16[320,768]{1,0:T(8,128)(2,1)S(1)}, u32[]{:S(2)}, u32[]{:S(2)}) %collective-permute-start.23) | collective-permute-done | bytes 491552 | tf_op jit(solution)/shard_map/ppermute | solution.py:109
  355.8 10.1 %collective-permute-done.25.refs_3_ = bf16[160,768]{1,0:T(8,128)(2,1)S(1)} collective-permute-done((bf16[160,768]{1,0:T(8,128)(2,1)}, bf16[160,768]{1,0:T(8,128)(2,1)S(1)}, u32[]{:S(2)}, u32[]{:S(2)}) %collective-permute-start.25) | collective-permute-done | bytes 245792 | tf_op jit(solution)/shard_map/ppermute | solution.py:109
  382.0 8.5 %collective-permute-done.28.refs_4_ = bf16[80,768]{1,0:T(8,128)(2,1)S(1)} collective-permute-done((bf16[80,768]{1,0:T(8,128)(2,1)}, bf16[80,768]{1,0:T(8,128)(2,1)S(1)}, u32[]{:S(2)}, u32[]{:S(2)}) %collective-permute-start.28) | collective-permute-done | bytes 122912 | tf_op jit(solution)/shard_map/ppermute | solution.py:90
  393.0 5.6 %collective-permute-start.32 = (bf16[80,768]{1,0:T(8,128)(2,1)}, bf16[80,768]{1,0:T(8,128)(2,1)S(1)}, u32[]{:S(2)}, u32[]{:S(2)}) collective-permute-start(bf16[80,768]{1,0:T(8,128)(2,1)} %get-tuple-element.195.refs_2_), channel_id=1, source_target_pairs={{0,3},{1,0},{2,1},{3,2},{4,7},{5,4},{6,5},{7,6},{8,11},{9,8},{10,9... | collective-permute-start | bytes 368648 | tf_op jit(solution)/shard_map/ppermute | solution.py:90
  405.4 20.0 %collective-permute-done.31.refs_4_ = bf16[80,768]{1,0:T(8,128)(2,1)S(1)} collective-permute-done((bf16[80,768]{1,0:T(8,128)(2,1)}, bf16[80,768]{1,0:T(8,128)(2,1)S(1)}, u32[]{:S(2)}, u32[]{:S(2)}) %collective-permute-start.31) | collective-permute-done | bytes 122912 | tf_op jit(solution)/shard_map/ppermute | solution.py:90
  429.3 5.7 %collective-permute-done.33.refs_3_ = bf16[160,768]{1,0:T(8,128)(2,1)S(1)} collective-permute-done((bf16[160,768]{1,0:T(8,128)(2,1)}, bf16[160,768]{1,0:T(8,128)(2,1)S(1)}, u32[]{:S(2)}, u32[]{:S(2)}) %collective-permute-start.33) | collective-permute-done | bytes 245792 | tf_op jit(solution)/shard_map/ppermute | solution.py:109
  440.3 9.2 %collective-permute-done.35.refs_3_ = bf16[320,768]{1,0:T(8,128)(2,1)S(1)} collective-permute-done((bf16[320,768]{1,0:T(8,128)(2,1)}, bf16[320,768]{1,0:T(8,128)(2,1)S(1)}, u32[]{:S(2)}, u32[]{:S(2)}) %collective-permute-start.35) | collective-permute-done | bytes 491552 | tf_op jit(solution)/shard_map/ppermute | solution.py:109
  460.4 17.3 %shard_map.242 = (f32[768,3072]{1,0:T(8,128)}, f32[3072,768]{1,0:T(8,128)}, f32[768,2304]{1,0:T(8,128)}, f32[768,768]{1,0:T(8,128)}, f32[768,768]{1,0:T(8,128)}, /*index=5*/f32[8,128]{1,0:T(8,128)}) custom-call(f32[8,128]{1,0:T(8,128)} %get-tuple-element.202.refs_0_, bf16[32,320,768]{2,1,0:T(8,128)(2,1)} %bitcast.24, bf16[32,320,768]{2,1,0:T(8,128)(2,1)} %bitcast.25, ...), custom_call_target="tpu_custom_call" | custom-call | tf_op jit(solution)/shard_map/pallas_call | solution.py:70
  478.9 5.6 %shard_map.243 = (f32[768,2304]{1,0:T(8,128)}, f32[8,768]{1,0:T(8,128)}, f32[8,128]{1,0:T(8,128)}) custom-call(f32[8,128]{1,0:T(8,128)} %get-tuple-element.204.refs_0_, s32[4]{0:T(128)} %pad_add_fusion.2.refs_0_.refs_1_.refs_4_, bf16[1280,768]{1,0:T(8,128)(2,1)} %get-tuple-element.205.refs_2_, bf16[1280,768]{1,0:T(8,128)(2,1)} %copy-done.29), custom_call_target="tpu_custom_call" | custom-call | tf_op jit(solution)/shard_map/pallas_call | solution.py:70
  (278 shorter events, 156.1 us)
Async XLA Ops:
  7.2 47.7 %all-gather.8.cloned.1.call-start = ((), (), s32[]{:S(2)}) async-start(), calls=%async_computation.2 | async-start | bytes 3981312 | tf_op jit(solution)/shard_map/all_gather | solution.py:1126
  7.9 128.1 %all-gather.10.cloned.1.call-start = ((), (), s32[]{:S(2)}) async-start(), calls=%async_computation.5 | async-start | bytes 11943936 | tf_op jit(solution)/shard_map/all_gather | solution.py:1142
  12.9 251.9 %reduce-scatter.3.cloned.1.call-start = ((), (), s32[]{:S(2)}) async-start(), calls=%async_computation.3 | async-start | bytes 10616832 | tf_op jit(solution)/shard_map/reduce_scatter | solution.py:1184
  13.0 20.8 %collective-permute-start = (bf16[192,768]{1,0:T(8,128)(2,1)S(1)}, bf16[192,768]{1,0:T(8,128)(2,1)S(1)}, u32[]{:S(2)}, u32[]{:S(2)}) collective-permute-start(bf16[192,768]{1,0:T(8,128)(2,1)S(1)} %pad_maximum_fusion.refs_1_), channel_id=1, source_target_pairs={{0,8},{4,12},{8,0},{12,4},{16,24},{20,28},{24,16},{28,20},{1,9},{5... | collective-permute-start | bytes 884744 | tf_op jit(solution)/shard_map/ppermute | solution.py:109
  19.1 22.9 %collective-permute-start.4 = (bf16[208,768]{1,0:T(8,128)(2,1)}, bf16[208,768]{1,0:T(8,128)(2,1)S(1)}, u32[]{:S(2)}, u32[]{:S(2)}) collective-permute-start(bf16[208,768]{1,0:T(8,128)(2,1)} %get-tuple-element.256), channel_id=1, source_target_pairs={{0,3},{1,0},{2,1},{3,2},{4,7},{5,4},{6,5},{7,6},{8,11},{9,8},{10,9... | collective-permute-start | bytes 958472 | tf_op jit(solution)/shard_map/ppermute | solution.py:90
  22.7 19.3 %collective-permute-start.2 = (bf16[208,768]{1,0:T(8,128)(2,1)}, bf16[208,768]{1,0:T(8,128)(2,1)S(1)}, u32[]{:S(2)}, u32[]{:S(2)}) collective-permute-start(bf16[208,768]{1,0:T(8,128)(2,1)} %get-tuple-element.258), channel_id=1, source_target_pairs={{0,1},{1,2},{2,3},{3,0},{4,5},{5,6},{6,7},{7,4},{8,9},{9,10},{10,1... | collective-permute-start | bytes 958472 | tf_op jit(solution)/shard_map/ppermute | solution.py:90
  22.7 26.9 %collective-permute-start.3 = (bf16[208,768]{1,0:T(8,128)(2,1)}, bf16[208,768]{1,0:T(8,128)(2,1)S(1)}, u32[]{:S(2)}, u32[]{:S(2)}) collective-permute-start(bf16[208,768]{1,0:T(8,128)(2,1)} %get-tuple-element.259), channel_id=1, source_target_pairs={{0,2},{1,3},{2,0},{3,1},{4,6},{5,7},{6,4},{7,5},{8,10},{9,11},{10,... | collective-permute-start | bytes 958472 | tf_op jit(solution)/shard_map/ppermute | solution.py:90
  37.7 30.8 %collective-permute-start.5 = (bf16[384,768]{1,0:T(8,128)(2,1)}, bf16[384,768]{1,0:T(8,128)(2,1)S(1)}, u32[]{:S(2)}, u32[]{:S(2)}) collective-permute-start(bf16[384,768]{1,0:T(8,128)(2,1)} %get-tuple-element.118.refs_2_), channel_id=1, source_target_pairs={{0,16},{4,20},{8,24},{12,28},{16,0},{20,4},{24,8},{28,12},{1,17},{... | collective-permute-start | bytes 1769480 | tf_op jit(solution)/shard_map/ppermute | solution.py:109
  38.1 30.5 %collective-permute-start.6 = (bf16[384,768]{1,0:T(8,128)(2,1)}, bf16[384,768]{1,0:T(8,128)(2,1)S(1)}, u32[]{:S(2)}, u32[]{:S(2)}) collective-permute-start(bf16[384,768]{1,0:T(8,128)(2,1)} %get-tuple-element.119.refs_4_), channel_id=1, source_target_pairs={{0,8},{4,12},{8,0},{12,4},{16,24},{20,28},{24,16},{28,20},{1,9},{5... | collective-permute-start | bytes 1769480 | tf_op jit(solution)/shard_map/ppermute | solution.py:109
  78.2 27.8 %collective-permute-start.9 = (bf16[208,768]{1,0:T(8,128)(2,1)}, bf16[208,768]{1,0:T(8,128)(2,1)S(1)}, u32[]{:S(2)}, u32[]{:S(2)}) collective-permute-start(bf16[208,768]{1,0:T(8,128)(2,1)} %get-tuple-element.125), channel_id=1, source_target_pairs={{0,2},{1,3},{2,0},{3,1},{4,6},{5,7},{6,4},{7,5},{8,10},{9,11},{10,... | collective-permute-start | bytes 958472 | tf_op jit(solution)/shard_map/ppermute | solution.py:90
  78.2 27.9 %collective-permute-start.10 = (bf16[208,768]{1,0:T(8,128)(2,1)}, bf16[208,768]{1,0:T(8,128)(2,1)S(1)}, u32[]{:S(2)}, u32[]{:S(2)}) collective-permute-start(bf16[208,768]{1,0:T(8,128)(2,1)} %get-tuple-element.126), channel_id=1, source_target_pairs={{0,1},{1,2},{2,3},{3,0},{4,5},{5,6},{6,7},{7,4},{8,9},{9,10},{10,1... | collective-permute-start | bytes 958472 | tf_op jit(solution)/shard_map/ppermute | solution.py:90
  175.9 124.6 %reduce-scatter.5.cloned.1.call-start = ((), (), s32[]{:S(2)}) async-start(), calls=%async_computation.4 | async-start | bytes 3932160 | tf_op jit(solution)/shard_map/reduce_scatter | solution.py:237
  238.4 220.0 %all-gather.12.cloned.1.call-start = ((), (), s32[]{:S(2)}) async-start(), calls=%async_computation.6 | async-start | bytes 16220160 | tf_op jit(solution)/shard_map/all_gather | solution.py:1236
  240.6 24.1 %collective-permute-start.14 = (bf16[208,768]{1,0:T(8,128)(2,1)S(1)}, bf16[208,768]{1,0:T(8,128)(2,1)S(1)}, u32[]{:S(2)}, u32[]{:S(2)}) collective-permute-start(bf16[208,768]{1,0:T(8,128)(2,1)S(1)} %copy-done.25), channel_id=1, source_target_pairs={{0,2},{1,3},{2,0},{3,1},{4,6},{5,7},{6,4},{7,5},{8,10},{9,11},{10,... | collective-permute-start | bytes 958472 | tf_op jit(solution)/shard_map/ppermute | solution.py:90
  242.3 22.4 %collective-permute-start.15 = (bf16[208,768]{1,0:T(8,128)(2,1)S(1)}, bf16[208,768]{1,0:T(8,128)(2,1)S(1)}, u32[]{:S(2)}, u32[]{:S(2)}) collective-permute-start(bf16[208,768]{1,0:T(8,128)(2,1)S(1)} %get-tuple-element.156), channel_id=1, source_target_pairs={{0,3},{1,0},{2,1},{3,2},{4,7},{5,4},{6,5},{7,6},{8,11},{9,8},{10,9... | collective-permute-start | bytes 958472 | tf_op jit(solution)/shard_map/ppermute | solution.py:90
  267.1 33.5 %collective-permute-start.16 = (bf16[192,768]{1,0:T(8,128)(2,1)S(1)}, bf16[192,768]{1,0:T(8,128)(2,1)S(1)}, u32[]{:S(2)}, u32[]{:S(2)}) collective-permute-start(bf16[192,768]{1,0:T(8,128)(2,1)S(1)} %get-tuple-element.166), channel_id=1, source_target_pairs={{0,1},{1,2},{2,3},{3,0},{4,5},{5,6},{6,7},{7,4},{8,9},{9,10},{10,1... | collective-permute-start | bytes 884744 | tf_op jit(solution)/shard_map/ppermute | solution.py:90
  274.4 26.2 %collective-permute-start.17 = (bf16[192,768]{1,0:T(8,128)(2,1)S(1)}, bf16[192,768]{1,0:T(8,128)(2,1)S(1)}, u32[]{:S(2)}, u32[]{:S(2)}) collective-permute-start(bf16[192,768]{1,0:T(8,128)(2,1)S(1)} %get-tuple-element.167), channel_id=1, source_target_pairs={{0,2},{1,3},{2,0},{3,1},{4,6},{5,7},{6,4},{7,5},{8,10},{9,11},{10,... | collective-permute-start | bytes 884744 | tf_op jit(solution)/shard_map/ppermute | solution.py:90
  276.5 24.0 %collective-permute-start.18 = (bf16[192,768]{1,0:T(8,128)(2,1)S(1)}, bf16[192,768]{1,0:T(8,128)(2,1)S(1)}, u32[]{:S(2)}, u32[]{:S(2)}) collective-permute-start(bf16[192,768]{1,0:T(8,128)(2,1)S(1)} %get-tuple-element.168), channel_id=1, source_target_pairs={{0,3},{1,0},{2,1},{3,2},{4,7},{5,4},{6,5},{7,6},{8,11},{9,8},{10,9... | collective-permute-start | bytes 884744 | tf_op jit(solution)/shard_map/ppermute | solution.py:90
  398.6 26.8 %collective-permute-start.31 = (bf16[80,768]{1,0:T(8,128)(2,1)}, bf16[80,768]{1,0:T(8,128)(2,1)S(1)}, u32[]{:S(2)}, u32[]{:S(2)}) collective-permute-start(bf16[80,768]{1,0:T(8,128)(2,1)} %get-tuple-element.195.refs_2_), channel_id=1, source_target_pairs={{0,2},{1,3},{2,0},{3,1},{4,6},{5,7},{6,4},{7,5},{8,10},{9,11},{10,... | collective-permute-start | bytes 368648 | tf_op jit(solution)/shard_map/ppermute | solution.py:90
  400.2 25.2 %collective-permute-start.30 = (bf16[80,768]{1,0:T(8,128)(2,1)}, bf16[80,768]{1,0:T(8,128)(2,1)S(1)}, u32[]{:S(2)}, u32[]{:S(2)}) collective-permute-start(bf16[80,768]{1,0:T(8,128)(2,1)} %get-tuple-element.195.refs_2_), channel_id=1, source_target_pairs={{0,1},{1,2},{2,3},{3,0},{4,5},{5,6},{6,7},{7,4},{8,9},{9,10},{10,1... | collective-permute-start | bytes 368648 | tf_op jit(solution)/shard_map/ppermute | solution.py:90
  453.4 24.2 %collective-permute-start.37 = (bf16[1280,768]{1,0:T(8,128)(2,1)}, bf16[1280,768]{1,0:T(8,128)(2,1)S(1)}, u32[]{:S(2)}, u32[]{:S(2)}) collective-permute-start(bf16[1280,768]{1,0:T(8,128)(2,1)} %get-tuple-element.205.refs_2_), channel_id=1, source_target_pairs={{0,4},{4,0},{8,12},{12,8},{16,20},{20,16},{24,28},{28,24},{1,5},{5... | collective-permute-start | bytes 5898248 | tf_op jit(solution)/shard_map/ppermute | solution.py:109
  453.4 31.7 %collective-permute-start.38 = (bf16[208,768]{1,0:T(8,128)(2,1)}, bf16[208,768]{1,0:T(8,128)(2,1)S(1)}, u32[]{:S(2)}, u32[]{:S(2)}) collective-permute-start(bf16[208,768]{1,0:T(8,128)(2,1)} %get-tuple-element.209), channel_id=1, source_target_pairs={{0,3},{1,0},{2,1},{3,2},{4,7},{5,4},{6,5},{7,6},{8,11},{9,8},{10,9... | collective-permute-start | bytes 958472 | tf_op jit(solution)/shard_map/ppermute | solution.py:90
  453.4 31.8 %collective-permute-start.39 = (bf16[208,768]{1,0:T(8,128)(2,1)}, bf16[208,768]{1,0:T(8,128)(2,1)S(1)}, u32[]{:S(2)}, u32[]{:S(2)}) collective-permute-start(bf16[208,768]{1,0:T(8,128)(2,1)} %get-tuple-element.210), channel_id=1, source_target_pairs={{0,2},{1,3},{2,0},{3,1},{4,6},{5,7},{6,4},{7,5},{8,10},{9,11},{10,... | collective-permute-start | bytes 958472 | tf_op jit(solution)/shard_map/ppermute | solution.py:90
  456.6 28.7 %collective-permute-start.40 = (bf16[208,768]{1,0:T(8,128)(2,1)S(1)}, bf16[208,768]{1,0:T(8,128)(2,1)S(1)}, u32[]{:S(2)}, u32[]{:S(2)}) collective-permute-start(bf16[208,768]{1,0:T(8,128)(2,1)S(1)} %copy-done.70), channel_id=1, source_target_pairs={{0,1},{1,2},{2,3},{3,0},{4,5},{5,6},{6,7},{7,4},{8,9},{9,10},{10,1... | collective-permute-start | bytes 958472 | tf_op jit(solution)/shard_map/ppermute | solution.py:90
  (93 other events, 737.2 us)
Sparse Core Ops, SparseCore 0:
  9.9 44.8 all-gather.7
  57.3 64.6 all-gather.9
  176.1 77.0 reduce-scatter.2
  256.6 43.9 reduce-scatter.4
  322.6 135.7 all-gather.11

commit v7 on v6

--- a/solution.py
+++ b/solution.py
@@ -1092,6 +1092,7 @@
         [VMEM],
         [struct((row_count * features // 128, 128), jnp.float32)],
         scratch=[pltpu.VMEM(first.shape, slots[0].dtype)],
+        room=4,
     )[0]
 
 
@@ -1154,7 +1155,7 @@
     mixture_slots, qkv_time, prob_time, first_input = time_forward(order, slots, time_weight, vec)
     mixture_slots = send_back(mixture_slots)
     while weight_flight.result is None:
-        advance(order, weight_flight)
+        advance(order, weight_flight, room=4)
     packed = weight_flight.result.reshape(batch_count, -1, features)
     mixture_time, after_time, second_input, qkv_space = middle_forward(
         order, token_rows, mixture_slots, packed, vec

time: 506 us -> 502 us (level)
  Pallas kernels: 223 us -> 217 us
    pallas_call x25, Pallas kernels: 223 us -> 217 us  [run(): pl.pallas_call(body, grid_spec=pltpu.PrefetchScalarGridSpec(num_scalar_pr...]
    unnamed x147 -> x159, local copies, waits for them, and re-layouts: 23.3 us -> 24.9 us
  transfers between devices with their start and end apart: 46 -> 46, of which waited for: 22 -> 22; matrix products, arithmetic and copies ran while one was open for 3% -> 4% of each run, Pallas kernels for 36% -> 35%
where the time goes in v7:
time: 502 us; the launch traced here: 493 us
  Pallas kernels  217 us (43%)
  waiting for transfers between devices  147 us (29%)
  starting transfers between devices  65.1 us (13%)
  local copies, waits for them, and re-layouts  32.7 us (7%)
  between operations  15.5 us (3%)
  blocking collectives  9.43 us (2%)
  other arithmetic  6.26 us (1%)
    pallas_call x25, Pallas kernels, run(): pl.pallas_call(body, grid_spec=pltpu.PrefetchScalarGridSpec(num_scalar_pr...  217 us
    ppermute x24, waiting for transfers between devices, shift_frames(): return lax.ppermute(block, 'frame', pairs)  93.5 us
    ppermute x24, starting transfers between devices, shift_frames(): return lax.ppermute(block, 'frame', pairs)  50.7 us
    ppermute x17, waiting for transfers between devices, swap_bit(): return lax.ppermute(block, axis, pairs)  47.2 us
    unnamed x159, local copies, waits for them, and re-layouts  24.9 us
    ppermute x17, starting transfers between devices, swap_bit(): return lax.ppermute(block, axis, pairs)  14.2 us
  transfers between devices with their start and end apart: 46, of which 22 were waited for; matrix products, arithmetic and copies ran while one was open for 4% of the time, Pallas kernels for 35%

profile of v7, /device:TPU:0, one launch (start us, length us, event | category | flops | bytes accessed | tf_op | source)
XLA Modules:
  0.0 492.9 jit_solution(17729504335548719842)
XLA Ops:
  23.8 9.4 %all-gather.3 = bf16[8,17,96]{2,1,0:T(8,128)(2,1)S(1)} all-gather(bf16[1,17,96]{2,1,0:T(8,128)(2,1)S(1)} %maximum_bitcast_fusion), channel_id=2, replica_groups=mesh['batch'=8,'frame'=4] {'batch'}, dimensions={0}, use_global_device_ids=true | all-gather | bytes 29376 | tf_op jit(solution)/shard_map/all_gather | solution.py:1134
  42.0 7.5 %collective-permute-done.3.refs_3_.refs_8_ = bf16[208,768]{1,0:T(8,128)(2,1)S(1)} collective-permute-done((bf16[208,768]{1,0:T(8,128)(2,1)S(1)}, bf16[208,768]{1,0:T(8,128)(2,1)S(1)}, u32[]{:S(2)}, u32[]{:S(2)}) %collective-permute-start.3) | collective-permute-done | bytes 319520 | tf_op jit(solution)/shard_map/ppermute | solution.py:90
  49.5 5.4 %all-gather.8.cloned.1.call-done.refs_5_.refs_15_ = bf16[768,2304]{1,0:T(8,128)(2,1)} async-done(((bf16[96,2304]{1,0:T(8,128)(2,1)}), bf16[768,2304]{1,0:T(8,128)(2,1)}) %all-gather.8.cloned.1.call-update) | async-done | bytes 3538960 | tf_op jit(solution)/shard_map/all_gather | solution.py:1127
  54.9 13.7 %shard_map.221 = (bf16[208,768]{1,0:T(8,128)(2,1)}, bf16[208,768]{1,0:T(8,128)(2,1)}, bf16[208,768]{1,0:T(8,128)(2,1)}, bf16[208,768]{1,0:T(8,128)(2,1)}, bf16[8...) custom-call(f32[8,128]{1,0:T(8,128)} %get-tuple-element.116.refs_0_, ...), custom_call_target="tpu_custom_call" | custom-call | tf_op jit(solution)/shard_map/pallas_call | solution.py:70
  87.6 15.9 %collective-permute-done.9.refs_5_ = bf16[208,768]{1,0:T(8,128)(2,1)S(1)} collective-permute-done((bf16[208,768]{1,0:T(8,128)(2,1)}, bf16[208,768]{1,0:T(8,128)(2,1)S(1)}, u32[]{:S(2)}, u32[]{:S(2)}) %collective-permute-start.9) | collective-permute-done | bytes 319520 | tf_op jit(solution)/shard_map/ppermute | solution.py:90
  104.3 10.4 %shard_map.224 = (bf16[832,768]{1,0:T(8,128)(2,1)}, f32[832,768]{1,0:T(8,128)}, bf16[832,768]{1,0:T(8,128)(2,1)}, bf16[832,2304]{1,0:T(8,128)(2,1)}, f32[8,128]{1,0:T(8,128)}) custom-call(f32[8,128]{1,0:T(8,128)} %copy-done.32, s32[4]{0:T(128)} %pad_add_fusion.2.refs_0_.refs_1_.refs_4_, bf16[832,768]{1,0:T(8,128)(2,1)} %pad.18.refs_2_, ...), custom_call_target="tpu_custom_call" | custom-call | tf_op jit(solution)/shard_map/pallas_call | solution.py:70
  114.7 18.9 %shard_map.225 = (bf16[832,768]{1,0:T(8,128)(2,1)}, f32[832,768]{1,0:T(8,128)}, f32[8,128]{1,0:T(8,128)}) custom-call(f32[8,128]{1,0:T(8,128)} %get-tuple-element.128.refs_0_, bf16[896,128]{1,0:T(8,128)(2,1)} %compare_convert_fusion.refs_1_, bf16[896,128]{1,0:T(8,128)(2,1)} %fusion.refs_2_, bf16[832,2304]{1,0:T(8,128)(2,1)} %get-tuple-element.129.refs_3_.refs_4_.refs_5_, ...), custom_call_target="tpu_custom_call" | custom-call | tf_op jit(solution)/shard_map/pallas_call | solution.py:70
  133.6 39.9 %shard_map.226 = (bf16[1,788,768]{2,1,0:T(8,128)(2,1)}, f32[832,768]{1,0:T(8,128)}, bf16[832,768]{1,0:T(8,128)(2,1)}, bf16[832,768]{1,0:T(8,128)(2,1)}, bf16[2,3...) custom-call(f32[8,128]{1,0:T(8,128)} %get-tuple-element.130.refs_0_, ...), custom_call_target="tpu_custom_call" | custom-call | tf_op jit(solution)/shard_map/pallas_call | solution.py:70
  173.5 29.3 %shard_map.227 = (bf16[832,768]{1,0:T(8,128)(2,1)}, bf16[832,768]{1,0:T(8,128)(2,1)}, bf16[832,768]{1,0:T(8,128)(2,1)}, f32[8,128]{1,0:T(8,128)}) custom-call(f32[8,128]{1,0:T(8,128)} %get-tuple-element.134.refs_0_, bf16[896,128]{1,0:T(8,128)(2,1)} %compare_convert_fusion.refs_1_, bf16[896,128]{1,0:T(8,128)(2,1)} %fusion.refs_2_, ...), custom_call_target="tpu_custom_call" | custom-call | tf_op jit(solution)/shard_map/pallas_call | solution.py:70
  202.9 13.8 %shard_map.228 = (bf16[1536,768]{1,0:T(8,128)(2,1)}, bf16[1536,768]{1,0:T(8,128)(2,1)}, f32[8,128]{1,0:T(8,128)}) custom-call(f32[8,128]{1,0:T(8,128)} %get-tuple-element.137.refs_0_, s32[4]{0:T(128)} %pad_add_fusion.2.refs_0_.refs_1_.refs_4_, bf16[832,768]{1,0:T(8,128)(2,1)} %get-tuple-element.138.refs_2_, ...), custom_call_target="tpu_custom_call" | custom-call | tf_op jit(solution)/shard_map/pallas_call | solution.py:70
  219.3 11.0 %shard_map.229 = (f32[832,768]{1,0:T(8,128)S(1)}, f32[8,768]{1,0:T(8,128)S(1)}, bf16[512,768]{1,0:T(8,128)(2,1)S(1)}, bf16[512,768]{1,0:T(8,128)(2,1)S(1)}, bf16...) custom-call(f32[8,128]{1,0:T(8,128)S(1)} %copy-done.29, ...), custom_call_target="tpu_custom_call" | custom-call | tf_op jit(solution)/shard_map/pallas_call | solution.py:70
  242.8 6.4 %collective-permute-done.13.refs_1_.refs_3_ = bf16[208,768]{1,0:T(8,128)(2,1)S(1)} collective-permute-done((bf16[208,768]{1,0:T(8,128)(2,1)S(1)}, bf16[208,768]{1,0:T(8,128)(2,1)S(1)}, u32[]{:S(2)}, u32[]{:S(2)}) %collective-permute-start.13) | collective-permute-done | bytes 319520 | tf_op jit(solution)/shard_map/ppermute | solution.py:90
  249.2 13.1 %collective-permute-done.14.refs_2_.refs_4_ = bf16[208,768]{1,0:T(8,128)(2,1)S(1)} collective-permute-done((bf16[208,768]{1,0:T(8,128)(2,1)S(1)}, bf16[208,768]{1,0:T(8,128)(2,1)S(1)}, u32[]{:S(2)}, u32[]{:S(2)}) %collective-permute-start.14) | collective-permute-done | bytes 319520 | tf_op jit(solution)/shard_map/ppermute | solution.py:90
  264.6 7.2 %collective-permute-start.16 = (bf16[192,768]{1,0:T(8,128)(2,1)S(1)}, bf16[192,768]{1,0:T(8,128)(2,1)S(1)}, u32[]{:S(2)}, u32[]{:S(2)}) collective-permute-start(bf16[192,768]{1,0:T(8,128)(2,1)S(1)} %get-tuple-element.166), channel_id=1, source_target_pairs={{0,1},{1,2},{2,3},{3,0},{4,5},{5,6},{6,7},{7,4},{8,9},{9,10},{10,1... | collective-permute-start | bytes 884744 | tf_op jit(solution)/shard_map/ppermute | solution.py:90
  274.5 23.3 %shard_map.232 = (bf16[208,768]{1,0:T(8,128)(2,1)}, bf16[208,768]{1,0:T(8,128)(2,1)}, bf16[208,768]{1,0:T(8,128)(2,1)}, bf16[208,768]{1,0:T(8,128)(2,1)}, bf16[1...) custom-call(f32[8,128]{1,0:T(8,128)} %copy-done.28, s32[4]{0:T(128)} %pad_add_fusion.2.refs_0_.refs_1_.refs_4_, ...), custom_call_target="tpu_custom_call" | custom-call | tf_op jit(solution)/shard_map/pallas_call | solution.py:70
  310.7 7.3 %collective-permute-done.20.refs_4_ = bf16[128,768]{1,0:T(8,128)(2,1)S(1)} collective-permute-done((bf16[128,768]{1,0:T(8,128)(2,1)S(1)}, bf16[128,768]{1,0:T(8,128)(2,1)S(1)}, u32[]{:S(2)}, u32[]{:S(2)}) %collective-permute-start.20) | collective-permute-done | bytes 196640 | tf_op jit(solution)/shard_map/ppermute | solution.py:90
  331.7 15.0 %collective-permute-done.23.refs_3_ = bf16[320,768]{1,0:T(8,128)(2,1)S(1)} collective-permute-done((bf16[320,768]{1,0:T(8,128)(2,1)}, bf16[320,768]{1,0:T(8,128)(2,1)S(1)}, u32[]{:S(2)}, u32[]{:S(2)}) %collective-permute-start.23) | collective-permute-done | bytes 491552 | tf_op jit(solution)/shard_map/ppermute | solution.py:109
  353.4 10.7 %collective-permute-done.25.refs_3_ = bf16[160,768]{1,0:T(8,128)(2,1)S(1)} collective-permute-done((bf16[160,768]{1,0:T(8,128)(2,1)}, bf16[160,768]{1,0:T(8,128)(2,1)S(1)}, u32[]{:S(2)}, u32[]{:S(2)}) %collective-permute-start.25) | collective-permute-done | bytes 245792 | tf_op jit(solution)/shard_map/ppermute | solution.py:109
  379.6 8.5 %collective-permute-done.28.refs_4_ = bf16[80,768]{1,0:T(8,128)(2,1)S(1)} collective-permute-done((bf16[80,768]{1,0:T(8,128)(2,1)}, bf16[80,768]{1,0:T(8,128)(2,1)S(1)}, u32[]{:S(2)}, u32[]{:S(2)}) %collective-permute-start.28) | collective-permute-done | bytes 122912 | tf_op jit(solution)/shard_map/ppermute | solution.py:90
  390.6 5.6 %collective-permute-start.32 = (bf16[80,768]{1,0:T(8,128)(2,1)}, bf16[80,768]{1,0:T(8,128)(2,1)S(1)}, u32[]{:S(2)}, u32[]{:S(2)}) collective-permute-start(bf16[80,768]{1,0:T(8,128)(2,1)} %get-tuple-element.195.refs_2_), channel_id=1, source_target_pairs={{0,3},{1,0},{2,1},{3,2},{4,7},{5,4},{6,5},{7,6},{8,11},{9,8},{10,9... | collective-permute-start | bytes 368648 | tf_op jit(solution)/shard_map/ppermute | solution.py:90
  402.9 20.1 %collective-permute-done.31.refs_4_ = bf16[80,768]{1,0:T(8,128)(2,1)S(1)} collective-permute-done((bf16[80,768]{1,0:T(8,128)(2,1)}, bf16[80,768]{1,0:T(8,128)(2,1)S(1)}, u32[]{:S(2)}, u32[]{:S(2)}) %collective-permute-start.31) | collective-permute-done | bytes 122912 | tf_op jit(solution)/shard_map/ppermute | solution.py:90
  437.4 8.1 %collective-permute-done.35.refs_3_ = bf16[320,768]{1,0:T(8,128)(2,1)S(1)} collective-permute-done((bf16[320,768]{1,0:T(8,128)(2,1)}, bf16[320,768]{1,0:T(8,128)(2,1)S(1)}, u32[]{:S(2)}, u32[]{:S(2)}) %collective-permute-start.35) | collective-permute-done | bytes 491552 | tf_op jit(solution)/shard_map/ppermute | solution.py:109
  458.1 17.3 %shard_map.242 = (f32[768,3072]{1,0:T(8,128)}, f32[3072,768]{1,0:T(8,128)}, f32[768,2304]{1,0:T(8,128)}, f32[768,768]{1,0:T(8,128)}, f32[768,768]{1,0:T(8,128)}, /*index=5*/f32[8,128]{1,0:T(8,128)}) custom-call(f32[8,128]{1,0:T(8,128)} %get-tuple-element.202.refs_0_, bf16[32,320,768]{2,1,0:T(8,128)(2,1)} %bitcast.32, bf16[32,320,768]{2,1,0:T(8,128)(2,1)} %bitcast.33, ...), custom_call_target="tpu_custom_call" | custom-call | tf_op jit(solution)/shard_map/pallas_call | solution.py:70
  476.7 5.7 %shard_map.243 = (f32[768,2304]{1,0:T(8,128)}, f32[8,768]{1,0:T(8,128)}, f32[8,128]{1,0:T(8,128)}) custom-call(f32[8,128]{1,0:T(8,128)} %get-tuple-element.204.refs_0_, s32[4]{0:T(128)} %pad_add_fusion.2.refs_0_.refs_1_.refs_4_, bf16[1280,768]{1,0:T(8,128)(2,1)} %get-tuple-element.205.refs_2_, bf16[1280,768]{1,0:T(8,128)(2,1)} %copy-done.39), custom_call_target="tpu_custom_call" | custom-call | tf_op jit(solution)/shard_map/pallas_call | solution.py:70
  (290 shorter events, 153.9 us)
Async XLA Ops:
  7.2 47.7 %all-gather.8.cloned.1.call-start = ((), (), s32[]{:S(2)}) async-start(), calls=%async_computation.2 | async-start | bytes 3981312 | tf_op jit(solution)/shard_map/all_gather | solution.py:1127
  7.9 125.6 %all-gather.10.cloned.1.call-start = ((), (), s32[]{:S(2)}) async-start(), calls=%async_computation.5 | async-start | bytes 11943936 | tf_op jit(solution)/shard_map/all_gather | solution.py:1143
  12.9 249.4 %reduce-scatter.3.cloned.1.call-start = ((), (), s32[]{:S(2)}) async-start(), calls=%async_computation.3 | async-start | bytes 10616832 | tf_op jit(solution)/shard_map/reduce_scatter | solution.py:1185
  13.0 20.7 %collective-permute-start = (bf16[192,768]{1,0:T(8,128)(2,1)S(1)}, bf16[192,768]{1,0:T(8,128)(2,1)S(1)}, u32[]{:S(2)}, u32[]{:S(2)}) collective-permute-start(bf16[192,768]{1,0:T(8,128)(2,1)S(1)} %pad_maximum_fusion.refs_1_), channel_id=1, source_target_pairs={{0,8},{4,12},{8,0},{12,4},{16,24},{20,28},{24,16},{28,20},{1,9},{5... | collective-permute-start | bytes 884744 | tf_op jit(solution)/shard_map/ppermute | solution.py:109
  19.0 22.9 %collective-permute-start.4 = (bf16[208,768]{1,0:T(8,128)(2,1)}, bf16[208,768]{1,0:T(8,128)(2,1)S(1)}, u32[]{:S(2)}, u32[]{:S(2)}) collective-permute-start(bf16[208,768]{1,0:T(8,128)(2,1)} %get-tuple-element.256), channel_id=1, source_target_pairs={{0,3},{1,0},{2,1},{3,2},{4,7},{5,4},{6,5},{7,6},{8,11},{9,8},{10,9... | collective-permute-start | bytes 958472 | tf_op jit(solution)/shard_map/ppermute | solution.py:90
  22.6 19.3 %collective-permute-start.2 = (bf16[208,768]{1,0:T(8,128)(2,1)}, bf16[208,768]{1,0:T(8,128)(2,1)S(1)}, u32[]{:S(2)}, u32[]{:S(2)}) collective-permute-start(bf16[208,768]{1,0:T(8,128)(2,1)} %get-tuple-element.258), channel_id=1, source_target_pairs={{0,1},{1,2},{2,3},{3,0},{4,5},{5,6},{6,7},{7,4},{8,9},{9,10},{10,1... | collective-permute-start | bytes 958472 | tf_op jit(solution)/shard_map/ppermute | solution.py:90
  22.6 26.9 %collective-permute-start.3 = (bf16[208,768]{1,0:T(8,128)(2,1)S(1)}, bf16[208,768]{1,0:T(8,128)(2,1)S(1)}, u32[]{:S(2)}, u32[]{:S(2)}) collective-permute-start(bf16[208,768]{1,0:T(8,128)(2,1)S(1)} %get-tuple-element.259), channel_id=1, source_target_pairs={{0,2},{1,3},{2,0},{3,1},{4,6},{5,7},{6,4},{7,5},{8,10},{9,11},{10,... | collective-permute-start | bytes 958472 | tf_op jit(solution)/shard_map/ppermute | solution.py:90
  37.7 31.0 %collective-permute-start.5 = (bf16[384,768]{1,0:T(8,128)(2,1)}, bf16[384,768]{1,0:T(8,128)(2,1)S(1)}, u32[]{:S(2)}, u32[]{:S(2)}) collective-permute-start(bf16[384,768]{1,0:T(8,128)(2,1)} %get-tuple-element.118.refs_2_), channel_id=1, source_target_pairs={{0,16},{4,20},{8,24},{12,28},{16,0},{20,4},{24,8},{28,12},{1,17},{... | collective-permute-start | bytes 1769480 | tf_op jit(solution)/shard_map/ppermute | solution.py:109
  37.9 30.8 %collective-permute-start.6 = (bf16[384,768]{1,0:T(8,128)(2,1)}, bf16[384,768]{1,0:T(8,128)(2,1)S(1)}, u32[]{:S(2)}, u32[]{:S(2)}) collective-permute-start(bf16[384,768]{1,0:T(8,128)(2,1)} %get-tuple-element.119.refs_4_), channel_id=1, source_target_pairs={{0,8},{4,12},{8,0},{12,4},{16,24},{20,28},{24,16},{28,20},{1,9},{5... | collective-permute-start | bytes 1769480 | tf_op jit(solution)/shard_map/ppermute | solution.py:109
  75.7 27.8 %collective-permute-start.9 = (bf16[208,768]{1,0:T(8,128)(2,1)}, bf16[208,768]{1,0:T(8,128)(2,1)S(1)}, u32[]{:S(2)}, u32[]{:S(2)}) collective-permute-start(bf16[208,768]{1,0:T(8,128)(2,1)} %get-tuple-element.125), channel_id=1, source_target_pairs={{0,2},{1,3},{2,0},{3,1},{4,6},{5,7},{6,4},{7,5},{8,10},{9,11},{10,... | collective-permute-start | bytes 958472 | tf_op jit(solution)/shard_map/ppermute | solution.py:90
  75.7 27.8 %collective-permute-start.10 = (bf16[208,768]{1,0:T(8,128)(2,1)}, bf16[208,768]{1,0:T(8,128)(2,1)S(1)}, u32[]{:S(2)}, u32[]{:S(2)}) collective-permute-start(bf16[208,768]{1,0:T(8,128)(2,1)} %get-tuple-element.126), channel_id=1, source_target_pairs={{0,1},{1,2},{2,3},{3,0},{4,5},{5,6},{6,7},{7,4},{8,9},{9,10},{10,1... | collective-permute-start | bytes 958472 | tf_op jit(solution)/shard_map/ppermute | solution.py:90
  173.5 124.7 %reduce-scatter.5.cloned.1.call-start = ((), (), s32[]{:S(2)}) async-start(), calls=%async_computation.4 | async-start | bytes 3932160 | tf_op jit(solution)/shard_map/reduce_scatter | solution.py:237
  235.9 220.2 %all-gather.12.cloned.1.call-start = ((), (), s32[]{:S(2)}) async-start(), calls=%async_computation.6 | async-start | bytes 16220160 | tf_op jit(solution)/shard_map/all_gather | solution.py:1237
  238.1 24.2 %collective-permute-start.14 = (bf16[208,768]{1,0:T(8,128)(2,1)S(1)}, bf16[208,768]{1,0:T(8,128)(2,1)S(1)}, u32[]{:S(2)}, u32[]{:S(2)}) collective-permute-start(bf16[208,768]{1,0:T(8,128)(2,1)S(1)} %copy-done.35), channel_id=1, source_target_pairs={{0,2},{1,3},{2,0},{3,1},{4,6},{5,7},{6,4},{7,5},{8,10},{9,11},{10,... | collective-permute-start | bytes 958472 | tf_op jit(solution)/shard_map/ppermute | solution.py:90
  240.0 22.3 %collective-permute-start.15 = (bf16[208,768]{1,0:T(8,128)(2,1)S(1)}, bf16[208,768]{1,0:T(8,128)(2,1)S(1)}, u32[]{:S(2)}, u32[]{:S(2)}) collective-permute-start(bf16[208,768]{1,0:T(8,128)(2,1)S(1)} %get-tuple-element.156), channel_id=1, source_target_pairs={{0,3},{1,0},{2,1},{3,2},{4,7},{5,4},{6,5},{7,6},{8,11},{9,8},{10,9... | collective-permute-start | bytes 958472 | tf_op jit(solution)/shard_map/ppermute | solution.py:90
  264.6 33.5 %collective-permute-start.16 = (bf16[192,768]{1,0:T(8,128)(2,1)S(1)}, bf16[192,768]{1,0:T(8,128)(2,1)S(1)}, u32[]{:S(2)}, u32[]{:S(2)}) collective-permute-start(bf16[192,768]{1,0:T(8,128)(2,1)S(1)} %get-tuple-element.166), channel_id=1, source_target_pairs={{0,1},{1,2},{2,3},{3,0},{4,5},{5,6},{6,7},{7,4},{8,9},{9,10},{10,1... | collective-permute-start | bytes 884744 | tf_op jit(solution)/shard_map/ppermute | solution.py:90
  271.9 26.3 %collective-permute-start.17 = (bf16[192,768]{1,0:T(8,128)(2,1)S(1)}, bf16[192,768]{1,0:T(8,128)(2,1)S(1)}, u32[]{:S(2)}, u32[]{:S(2)}) collective-permute-start(bf16[192,768]{1,0:T(8,128)(2,1)S(1)} %get-tuple-element.167), channel_id=1, source_target_pairs={{0,2},{1,3},{2,0},{3,1},{4,6},{5,7},{6,4},{7,5},{8,10},{9,11},{10,... | collective-permute-start | bytes 884744 | tf_op jit(solution)/shard_map/ppermute | solution.py:90
  274.2 24.0 %collective-permute-start.18 = (bf16[192,768]{1,0:T(8,128)(2,1)S(1)}, bf16[192,768]{1,0:T(8,128)(2,1)S(1)}, u32[]{:S(2)}, u32[]{:S(2)}) collective-permute-start(bf16[192,768]{1,0:T(8,128)(2,1)S(1)} %get-tuple-element.168), channel_id=1, source_target_pairs={{0,3},{1,0},{2,1},{3,2},{4,7},{5,4},{6,5},{7,6},{8,11},{9,8},{10,9... | collective-permute-start | bytes 884744 | tf_op jit(solution)/shard_map/ppermute | solution.py:90
  396.2 26.8 %collective-permute-start.31 = (bf16[80,768]{1,0:T(8,128)(2,1)}, bf16[80,768]{1,0:T(8,128)(2,1)S(1)}, u32[]{:S(2)}, u32[]{:S(2)}) collective-permute-start(bf16[80,768]{1,0:T(8,128)(2,1)} %get-tuple-element.195.refs_2_), channel_id=1, source_target_pairs={{0,2},{1,3},{2,0},{3,1},{4,6},{5,7},{6,4},{7,5},{8,10},{9,11},{10,... | collective-permute-start | bytes 368648 | tf_op jit(solution)/shard_map/ppermute | solution.py:90
  397.8 25.2 %collective-permute-start.30 = (bf16[80,768]{1,0:T(8,128)(2,1)}, bf16[80,768]{1,0:T(8,128)(2,1)S(1)}, u32[]{:S(2)}, u32[]{:S(2)}) collective-permute-start(bf16[80,768]{1,0:T(8,128)(2,1)} %get-tuple-element.195.refs_2_), channel_id=1, source_target_pairs={{0,1},{1,2},{2,3},{3,0},{4,5},{5,6},{6,7},{7,4},{8,9},{9,10},{10,1... | collective-permute-start | bytes 368648 | tf_op jit(solution)/shard_map/ppermute | solution.py:90
  449.5 25.9 %collective-permute-start.37 = (bf16[1280,768]{1,0:T(8,128)(2,1)}, bf16[1280,768]{1,0:T(8,128)(2,1)S(1)}, u32[]{:S(2)}, u32[]{:S(2)}) collective-permute-start(bf16[1280,768]{1,0:T(8,128)(2,1)} %get-tuple-element.205.refs_2_), channel_id=1, source_target_pairs={{0,4},{4,0},{8,12},{12,8},{16,20},{20,16},{24,28},{28,24},{1,5},{5... | collective-permute-start | bytes 5898248 | tf_op jit(solution)/shard_map/ppermute | solution.py:109
  449.5 33.5 %collective-permute-start.38 = (bf16[208,768]{1,0:T(8,128)(2,1)}, bf16[208,768]{1,0:T(8,128)(2,1)S(1)}, u32[]{:S(2)}, u32[]{:S(2)}) collective-permute-start(bf16[208,768]{1,0:T(8,128)(2,1)} %get-tuple-element.209), channel_id=1, source_target_pairs={{0,3},{1,0},{2,1},{3,2},{4,7},{5,4},{6,5},{7,6},{8,11},{9,8},{10,9... | collective-permute-start | bytes 958472 | tf_op jit(solution)/shard_map/ppermute | solution.py:90
  449.5 33.5 %collective-permute-start.39 = (bf16[208,768]{1,0:T(8,128)(2,1)}, bf16[208,768]{1,0:T(8,128)(2,1)S(1)}, u32[]{:S(2)}, u32[]{:S(2)}) collective-permute-start(bf16[208,768]{1,0:T(8,128)(2,1)} %get-tuple-element.210), channel_id=1, source_target_pairs={{0,2},{1,3},{2,0},{3,1},{4,6},{5,7},{6,4},{7,5},{8,10},{9,11},{10,... | collective-permute-start | bytes 958472 | tf_op jit(solution)/shard_map/ppermute | solution.py:90
  454.1 28.9 %collective-permute-start.40 = (bf16[208,768]{1,0:T(8,128)(2,1)S(1)}, bf16[208,768]{1,0:T(8,128)(2,1)S(1)}, u32[]{:S(2)}, u32[]{:S(2)}) collective-permute-start(bf16[208,768]{1,0:T(8,128)(2,1)S(1)} %copy-done.76), channel_id=1, source_target_pairs={{0,1},{1,2},{2,3},{3,0},{4,5},{5,6},{6,7},{7,4},{8,9},{9,10},{10,1... | collective-permute-start | bytes 958472 | tf_op jit(solution)/shard_map/ppermute | solution.py:90
  (99 other events, 843.7 us)
Sparse Core Ops, SparseCore 0:
  9.9 44.9 all-gather.7
  57.4 64.7 all-gather.9
  173.6 77.1 reduce-scatter.2
  254.2 43.9 reduce-scatter.4
  320.2 135.3 all-gather.11
